TPU v7x, 128 devices: a whole 4x4x4 slice. The times are simulated.
128 devices in a mesh: grp: 8 (over z_lo, x), blk: 16 (over z_hi, y, core).
Axes of the slice: x: 4, y: 4, z: 4 (z_hi: 2, z_lo: 2; z = z_hi * 2 + z_lo), core: 2. Of those that a mesh axis runs over, the one named last changes fastest.
Arguments:
- features: float32 [131072, 128], P(('grp', 'blk')), may hold values from -6 to 6
- new_slot: int32 [1024], P(('grp', 'blk')), may hold values from 0 to 1023, as said below
- tile_values: float32 [8, 16, 16, 16, 128, 128], P('grp', 'blk'), may hold values from 0 to 0.04
- tile_dest: int32 [8, 16, 16, 16], P('grp', 'blk'), may hold values from -1 to 63, as said below
- tile_source: int32 [8, 16, 16, 16], P('grp', 'blk'), may hold values from -1 to 7, as said below
- weight: float32 [128, 128], replicated, may hold values from -0.5 to 0.5
- bias_vector: float32 [128], replicated, may hold values from -3 to 3
Outputs:
- activations: float32 [131072, 128], P(('grp', 'blk'))
Inputs may be any that keep to these rules, and one draw needn't show every extreme that they name: new_slot is a permutation of the block positions that keeps every block in its range of 128 blocks; the 8 blocks of one device go to at most 16 - 1 devices of its range, at most 1 to any one device, a count that some device reaches; every device's new positions receive exactly 8 blocks. tile_dest[g, b, k, t] is -1 exactly where the slot is empty; the live slots of each (g, b, k) come first, from 1 to 16 of them, and every (g, b) has some k with all 16 live. tile_source is -1 exactly where tile_dest is -1.
All inputs are finite; a program needn't handle non-finite values.
Results may differ from a plain program's by a relative error of at most 0.0003.
Values sent between devices are 32-bit elements; how exact they have to be, the bound alone decides.
No kernel may reach another device: no remote copies, remote signals or barrier semaphores. Data moves between devices by JAX's collectives and lax.ppermute only.
A program may use at most 128 MiB of HBM per device.

v0:
```python
import jax
import jax.numpy as jnp
from jax import lax
from jax.sharding import PartitionSpec as P

TILE = 128
FEAT = 128
BLOCKS_DEV = 8
TILE_SLOTS = 16


precise = lax.Precision.HIGHEST


def tile_products(values, targets, anchors, sources):
    shards = values.shape[0]
    rows_index = jnp.arange(shards)[:, None]
    picked = sources[rows_index, jnp.maximum(anchors, 0)]
    products = jnp.einsum(
        "kptr,kprf->kptf", values, picked, precision=precise, preferred_element_type=jnp.float32
    )
    live_mask = (targets >= 0).astype(jnp.float32)
    products = products * live_mask[:, :, None, None]
    return (products.reshape(-1, TILE, FEAT), jnp.maximum(targets, 0).reshape(-1))


def body(features, new_slot, tile_values, tile_dest, tile_source, weight, bias_vector):
    cycle_count = lax.axis_size("blk")
    group_count = lax.axis_size("grp")
    capacity = BLOCKS_DEV // (cycle_count - 1) + 1
    range_blocks = cycle_count * BLOCKS_DEV
    local_rows = group_count * BLOCKS_DEV
    values_all = tile_values.reshape(cycle_count, TILE_SLOTS, TILE, TILE)
    dest_all = tile_dest.reshape(cycle_count, TILE_SLOTS)
    source_all = tile_source.reshape(cycle_count, TILE_SLOTS)
    flat_blocks = features.reshape(BLOCKS_DEV, TILE * FEAT)
    target = new_slot % range_blocks // BLOCKS_DEV
    landing = new_slot % BLOCKS_DEV
    order_ids = jnp.arange(BLOCKS_DEV)
    earlier = (target[None, :] == target[:, None]) & (order_ids[None, :] < order_ids[:, None])
    rank_ids = jnp.sum(earlier.astype(jnp.int32), axis=1)
    position = target * capacity + rank_ids
    slot_ids = jnp.arange(cycle_count * capacity)
    packer = position[None, :] == slot_ids[:, None]
    packed = jnp.dot(
        packer.astype(jnp.float32),
        flat_blocks,
        precision=precise,
        preferred_element_type=jnp.float32,
    )
    labels = jnp.sum(jnp.where(packer, landing[None, :] + 1, 0), axis=1) - 1
    arrived, arrived_labels = (
        lax.all_to_all(
            packed.reshape(cycle_count, capacity, TILE * FEAT),
            "blk",
            split_axis=0,
            concat_axis=0,
            tiled=True,
        ),
        lax.all_to_all(
            labels.reshape(cycle_count, capacity), "blk", split_axis=0, concat_axis=0, tiled=True
        ),
    )
    placer = arrived_labels.reshape(-1)[None, :] == order_ids[:, None]
    owned_blocks = jnp.dot(
        placer.astype(jnp.float32),
        arrived.reshape(-1, TILE * FEAT),
        precision=precise,
        preferred_element_type=jnp.float32,
    )
    shards = lax.all_gather(owned_blocks.reshape(BLOCKS_DEV, TILE, FEAT), "blk", axis=0, tiled=True)
    amount = shards.shape[0] // BLOCKS_DEV
    products, dest_ids = tile_products(
        values_all, dest_all, source_all, shards.reshape(amount, BLOCKS_DEV, TILE, FEAT)
    )
    partial_value = jax.ops.segment_sum(products, dest_ids, num_segments=local_rows)
    summed = lax.psum_scatter(partial_value, "grp", scatter_dimension=0, tiled=True)
    hidden = jnp.dot(
        summed.reshape(-1, FEAT), weight, precision=precise, preferred_element_type=jnp.float32
    )
    return jax.nn.relu(hidden + bias_vector[None, :])


def solution(mesh):
    return jax.shard_map(
        body,
        mesh=mesh,
        in_specs=(
            P(("grp", "blk"), None),
            P(("grp", "blk")),
            P("grp", "blk", None, None, None, None),
            P("grp", "blk", None, None),
            P("grp", "blk", None, None),
            P(),
            P(),
        ),
        out_specs=P(("grp", "blk"), None),
        check_vma=False,
    )
```

profile of v0, /device:TPU:0, one launch (start us, length us, event | category | flops | bytes accessed | tf_op | source)
XLA Modules:
  0.0 319.6 jit_solution(16681363062597375283)
XLA Ops:
  6.5 0.0 copy-start
  6.5 0.7 fusion.13
  7.2 0.2 convert_reduce_fusion
  7.4 0.1 select_reduce_fusion
  7.5 0.7 copy.25
  8.2 8.0 %all-to-all-start = ((s32[16,1,1]{2,1,0:T(1,128)}), s32[16,1,1]{2,1,0:T(1,128)S(1)}, u32[]{:S(2)}, u32[]{:S(2)}) async-start(s32[16,1,1]{2,1,0:T(1,128)} %copy.25), calls=%async_computation | async-start | bytes 16384 | tf_op jit(solution)/shard_map/all_to_all | solution.py:60
  16.2 1.1 reshape.82
  17.3 0.7 convolution_bitcast_fusion
  18.0 2.1 copy.26
  20.1 3.6 %all-to-all-done = s32[16,1,1]{2,1,0:T(1,128)S(1)} async-done(((s32[16,1,1]{2,1,0:T(1,128)}), s32[16,1,1]{2,1,0:T(1,128)S(1)}, u32[]{:S(2)}, u32[]{:S(2)}) %all-to-all-start) | async-done | bytes 96 | tf_op jit(solution)/shard_map/all_to_all | solution.py:60
  23.7 3.7 %all-to-all-start.1 = ((f32[16,1,16384]{2,1,0:T(1,128)}), f32[16,1,16384]{2,1,0:T(1,128)S(1)}, u32[]{:S(2)}, u32[]{:S(2)}) async-start(f32[16,1,16384]{2,1,0:T(1,128)} %copy.26), calls=%async_computation.1 | async-start | bytes 2097152 | tf_op jit(solution)/shard_map/all_to_all | solution.py:53
  27.3 0.0 all-gather.2.cloned.1.call-start
  27.4 0.4 reduce
  27.8 17.5 %all-to-all-done.1 = f32[16,1,16384]{2,1,0:T(1,128)S(1)} async-done(((f32[16,1,16384]{2,1,0:T(1,128)}), f32[16,1,16384]{2,1,0:T(1,128)S(1)}, u32[]{:S(2)}, u32[]{:S(2)}) %all-to-all-start.1) | async-done | bytes 1048608 | tf_op jit(solution)/shard_map/all_to_all | solution.py:53
  45.3 1.9 fusion.5
  47.2 0.0 all-gather.2.cloned.1.call-update
  47.2 0.0 reduce-scatter.2.cloned.1.call-start
  47.3 0.7 bitcast_or_fusion
  48.0 0.1 reshape.90
  48.1 0.7 broadcast_maximum_fusion
  48.8 0.1 reshape.98
  48.8 0.7 convert_bitcast_fusion
  49.5 74.9 %all-gather.2.cloned.1.call-done = f32[128,128,128]{2,0,1:T(8,128)} async-done(((f32[8,128,128]{2,0,1:T(8,128)}), f32[128,128,128]{2,0,1:T(8,128)}) %all-gather.2.cloned.1.call-update) | async-done | bytes 8388624 | tf_op jit(solution)/shard_map/all_gather | solution.py:71
  124.5 11.5 %copy.28 = f32[16,8,128,128]{3,2,1,0:T(8,128)} copy(f32[16,8,128,128]{3,1,0,2:T(8,128)} %bitcast.42) | data formatting | bytes 16777216 | tf_op jit(solution)/shard_map/reshape | solution.py:74
  135.9 16.7 %gather_fusion = f32[256,128,128]{2,1,0:T(8,128)} fusion(f32[16,8,128,128]{3,2,1,0:T(8,128)} %copy.28, s32[256]{0:T(256)S(1)} %reshape.90), kind=kCustom, calls=%fused_computation | custom fusion | bytes 33556480 | tf_op jit(solution)/shard_map/gather | solution.py:18
  152.6 34.6 %broadcast_multiply_fusion = f32[16,16,128,128]{3,2,1,0:T(8,128)} fusion(f32[16,16]{1,0:T(8,128)S(1)} %convert_bitcast_fusion, f32[16,16,128,128]{3,2,1,0:T(8,128)} %bitcast.40, f32[1,1,16,16,128,128]{5,4,3,2,1,0:T(8,128)} %param.9), kind=kOutput, calls=%fused_computation.5 | convolution fusion | flops 6446645248 | bytes 50332672 | tf_op jit(solution)/shard_map/kptr,kprf->kptf/dot_general | solution.py:19
  187.3 17.5 %copy.30 = f32[256,128,128]{2,1,0:T(8,128)} copy(f32[256,128,128]{1,2,0:T(8,128)} %bitcast.41) | data formatting | bytes 33554432 | tf_op jit(solution)/shard_map/reshape | solution.py:24
  204.7 2.4 broadcast_in_dim.16
  207.2 0.0 copy-start.1
  207.2 52.3 %scatter_fusion = f32[64,128,128]{2,1,0:T(8,128)} fusion(f32[64,128,128]{2,1,0:T(8,128)} %broadcast_in_dim.16, s32[256]{0:T(256)S(1)} %reshape.98, f32[256,128,128]{2,1,0:T(8,128)} %copy.30), kind=kCustom, calls=%fused_computation.1 | custom fusion | flops 4194304 | bytes 50332672 | tf_op jit(solution)/shard_map/scatter-add | solution.py:76
  259.5 0.0 reduce-scatter.2.cloned.1.call-update
  259.5 50.9 %reduce-scatter.2.cloned.1.call-done = f32[8,128,128]{2,1,0:T(8,128)} async-done(((f32[64,128,128]{2,1,0:T(8,128)}), f32[8,128,128]{2,1,0:T(8,128)}) %reduce-scatter.2.cloned.1.call-update) | async-done | bytes 524304 | tf_op jit(solution)/shard_map/reduce_scatter | solution.py:77
  310.4 0.0 copy-done
  310.4 0.0 copy-done.1
  310.4 2.4 fusion.4
  (2 shorter events, 0.0 us)
Async XLA Ops:
  6.5 303.8 %copy-start = (f32[128,128]{1,0:T(8,128)S(1)}, f32[128,128]{1,0:T(8,128)}, u32[]{:S(2)}) copy-start(f32[128,128]{1,0:T(8,128)} %param.12) | copy-start | bytes 196612
  8.2 15.5 %all-to-all-start = ((s32[16,1,1]{2,1,0:T(1,128)}), s32[16,1,1]{2,1,0:T(1,128)S(1)}, u32[]{:S(2)}, u32[]{:S(2)}) async-start(s32[16,1,1]{2,1,0:T(1,128)} %copy.25), calls=%async_computation | async-start | bytes 16384 | tf_op jit(solution)/shard_map/all_to_all | solution.py:60
  23.7 21.6 %all-to-all-start.1 = ((f32[16,1,16384]{2,1,0:T(1,128)}), f32[16,1,16384]{2,1,0:T(1,128)S(1)}, u32[]{:S(2)}, u32[]{:S(2)}) async-start(f32[16,1,16384]{2,1,0:T(1,128)} %copy.26), calls=%async_computation.1 | async-start | bytes 2097152 | tf_op jit(solution)/shard_map/all_to_all | solution.py:53
  27.3 97.1 %all-gather.2.cloned.1.call-start = ((), (), s32[]{:S(2)}) async-start(), calls=%async_computation.3 | async-start | bytes 8912896 | tf_op jit(solution)/shard_map/all_gather | solution.py:71
  47.2 263.2 %reduce-scatter.2.cloned.1.call-start = ((), (), s32[]{:S(2)}) async-start(), calls=%async_computation.4 | async-start | bytes 4718592 | tf_op jit(solution)/shard_map/reduce_scatter | solution.py:77
  207.2 103.2 %copy-start.1 = (f32[128]{0:T(128)S(1)}, f32[128]{0:T(128)}, u32[]{:S(2)}) copy-start(f32[128]{0:T(128)} %param.13) | copy-start | bytes 1540
Sparse Core Ops, SparseCore 0:
  47.3 77.1 all-gather.1
  259.6 50.7 reduce-scatter.1
where the time goes:
time: 322 us; the launch traced here: 320 us
  waiting for transfers between devices  147 us (46%)
  other arithmetic  55.8 us (17%)
  local copies, waits for them, and re-layouts  52.1 us (16%)
  matrix products  39.6 us (12%)
  between operations  13.4 us (4%)
  starting transfers between devices  11.7 us (4%)
    all_gather x1, waiting for transfers between devices, body(): lax.all_gather(owned_blocks.reshape(BLOCKS_DEV, TILE, FEAT), 'blk', axis=...  74.9 us
    scatter-add x1, other arithmetic, body(): jax.ops.segment_sum(products, dest_ids, num_segments=local_rows)  52.3 us
    reduce_scatter x1, waiting for transfers between devices, body(): lax.psum_scatter(partial_value, 'grp', scatter_dimension=0, tiled=True)  50.9 us
    dot_general x1, matrix products, tile_products(): jnp.einsum('kptr,kprf->kptf', values, picked, precision=precise, preferre...  34.6 us
    all_to_all x1, waiting for transfers between devices, body(): lax.all_to_all(packed.reshape(cycle_count, capacity, TILE * FEAT), 'blk',...  17.5 us
    reshape x1, local copies, waits for them, and re-layouts, tile_products(): products.reshape(-1, TILE, FEAT)  17.5 us
    gather x1, local copies, waits for them, and re-layouts, tile_products(): picked = sources[rows_index, jnp.maximum(anchors, 0)]  16.7 us
    reshape x1, local copies, waits for them, and re-layouts, body(): shards.reshape(amount, BLOCKS_DEV, TILE, FEAT)  11.5 us
  transfers between devices with their start and end apart: 4, of which 4 were waited for; matrix products, arithmetic and copies ran while one was open for 2% of the time, Pallas kernels for 0%

commit v1 on v0

v1 whole, which is shorter than its diff:
```python
import functools

import jax
import jax.numpy as jnp
from jax import lax
from jax.experimental import pallas as pl
from jax.experimental.pallas import tpu as pltpu
from jax.sharding import Mesh, PartitionSpec as P

TILE = 128
FEAT = 128
BLOCKS = 8
SLOTS = 16
BUCKETS = 16
TILES = BUCKETS * SLOTS
UNROLL = 4
RING = 16
FIRST, SECOND, THIRD = 80, 24, 24
LIST = TILES + UNROLL
DUMMY = 64

AXES = ("z_lo", "x", "z_hi", "y", "core")
AHEAD = [(2 * i + c, 2 * ((i + 1 - 2 * c) % 4) + c) for i in range(4) for c in range(2)]
BACK = [(b, a) for a, b in AHEAD]
SWAP = [(0, 1), (1, 0)]

f32, bf16 = jnp.float32, jnp.bfloat16


def plan_kernel(where, slots, dest, source, lists, counts, table):
    z_lo, x, z_hi, y, core = (where[i] for i in range(5))

    def place(member, carry):
        dz = (member // 8) ^ z_hi
        dc = (member % 2) ^ core
        turn = 1 - 2 * (member % 2)
        dy = ((y - (member // 2) % 4) * turn) & 3
        near = (dy * 2 + dc) * BLOCKS
        side = FIRST - 2 * BLOCKS + dc * BLOCKS
        late = FIRST + dc * SECOND + (dy - 1) * BLOCKS
        base = jnp.where(dz == 0, near, jnp.where(dy == 0, side, late))
        for j in range(BLOCKS):
            table[slots[member * BLOCKS + j] & 127] = base + j
        return carry

    lax.fori_loop(0, BUCKETS, place, 0)

    def bucket(k, carry):
        def one(t, n):
            n0, n1, n2 = n
            at = k * SLOTS + t
            d = dest[at]
            live = d >= 0
            s = table[k * BLOCKS + jnp.maximum(source[at], 0)]
            g = jnp.maximum(d, 0) // BLOCKS
            rel = (((g // 4) ^ z_lo) * 4 + (((g % 4 - x) * (1 - 2 * core)) & 3)) * BLOCKS + (d & 7)
            word = at + s * 256 + rel * 65536
            a, b = s < FIRST, s < FIRST + SECOND
            pos = jnp.where(a, n0, jnp.where(b, LIST + n1, 2 * LIST + n2))
            lists[pos] = word
            inc = live.astype(jnp.int32)
            ia = jnp.where(a, inc, 0)
            ib = jnp.where(a, 0, jnp.where(b, inc, 0))
            return n0 + ia, n1 + ib, n2 + inc - ia - ib

        for t in range(SLOTS):
            carry = one(t, carry)
        return carry

    n = lax.fori_loop(0, BUCKETS, bucket, (0, 0, 0))
    for i in range(3):
        counts[i] = (n[i] + UNROLL - 1) // UNROLL
        for j in range(UNROLL):
            lists[i * LIST + n[i] + j] = (i * FIRST + (SECOND if i == 2 else 0) - (FIRST if i == 2 else 0)) * 256 + DUMMY * 65536


def split(v):
    hi = v.astype(bf16)
    return hi, (v - hi.astype(f32)).astype(bf16)


def product(a, b):
    ah, al = split(a)
    bh, bl = split(b)
    left = jnp.concatenate([ah, al], axis=1)
    right = jnp.concatenate([bh, bl], axis=1)
    both = jnp.dot(left, jnp.concatenate([right, right], axis=0), preferred_element_type=f32)
    return both[:, :FEAT] + both[:, FEAT:]


def tile_kernel(part, base, sizes, n_in, out_sizes, *refs):
    lists, counts, tiles = refs[:3]
    pieces = refs[3 : 3 + len(sizes)]
    refs = refs[3 + len(sizes) :]
    acc_in = refs[0] if n_in else None
    refs = refs[n_in:]
    outs = refs[: len(out_sizes)]
    acc, xs, ring, piece_sem, ring_sem, acc_sem, out_sem = refs[len(out_sizes) :]
    groups = counts[part]

    def fetch(group, slot):
        for j in range(UNROLL):
            at = lists[part * LIST + group * UNROLL + j] & 255
            pltpu.make_async_copy(
                tiles.at[at], ring.at[slot, j], ring_sem.at[slot, j]
            ).start()

    def landed(slot):
        for j in range(UNROLL):
            pltpu.make_async_copy(tiles.at[0], ring.at[slot, j], ring_sem.at[slot, j]).wait()

    depth = RING // UNROLL
    piece_copies = []
    at = 0
    for i, size in enumerate(sizes):
        copy = pltpu.make_async_copy(pieces[i], xs.at[pl.ds(at, size)], piece_sem.at[i])
        copy.start()
        piece_copies.append(copy)
        at += size
    for s in range(depth - 1):
        @pl.when(s < groups)
        def _(s=s):
            fetch(s, s)
    if n_in:
        first = pltpu.make_async_copy(acc_in, acc.at[pl.ds(0, DUMMY)], acc_sem)
        first.start()
    else:
        def clear(d, carry):
            acc[d] = jnp.zeros((TILE, FEAT), f32)
            return carry

        lax.fori_loop(0, DUMMY, clear, 0)
    acc[DUMMY] = jnp.zeros((TILE, FEAT), f32)
    for copy in piece_copies:
        copy.wait()
    if n_in:
        first.wait()

    def step(group, carry):
        slot = group % depth
        ahead = group + depth - 1

        @pl.when(ahead < groups)
        def _():
            fetch(ahead, ahead % depth)

        landed(slot)
        words = [lists[part * LIST + group * UNROLL + j] for j in range(UNROLL)]
        results = [
            product(ring[slot, j], xs[((words[j] >> 8) & 255) - base]) for j in range(UNROLL)
        ]
        for j in range(UNROLL):
            acc[words[j] >> 16] += results[j]
        return carry

    lax.fori_loop(0, groups, step, 0)
    copies = []
    at = 0
    for i, size in enumerate(out_sizes):
        copy = pltpu.make_async_copy(acc.at[pl.ds(at, size)], outs[i], out_sem.at[i])
        copy.start()
        copies.append(copy)
        at += size
    for copy in copies:
        copy.wait()


def tile_products(part, base, lists, counts, tiles, pieces, acc_in, out_sizes):
    sizes = [p.shape[0] for p in pieces]
    n_in = 0 if acc_in is None else 1
    smem = pl.BlockSpec(memory_space=pltpu.SMEM)
    anywhere = pl.BlockSpec(memory_space=pl.ANY)
    return pl.pallas_call(
        functools.partial(tile_kernel, part, base, sizes, n_in, out_sizes),
        out_shape=[jax.ShapeDtypeStruct((n, TILE, FEAT), f32) for n in out_sizes],
        in_specs=[smem, smem] + [anywhere] * (1 + len(sizes) + n_in),
        out_specs=[anywhere] * len(out_sizes),
        scratch_shapes=[
            pltpu.VMEM((DUMMY + 1, TILE, FEAT), f32),
            pltpu.VMEM((sum(sizes), TILE, FEAT), f32),
            pltpu.VMEM((RING // UNROLL, UNROLL, TILE, TILE), f32),
            pltpu.SemaphoreType.DMA((len(sizes),)),
            pltpu.SemaphoreType.DMA((RING // UNROLL, UNROLL)),
            pltpu.SemaphoreType.DMA,
            pltpu.SemaphoreType.DMA((len(out_sizes),)),
        ],
        compiler_params=pltpu.CompilerParams(vmem_limit_bytes=50 * 2**20),
        cost_estimate=pl.CostEstimate(
            flops=2 * TILE * TILE * FEAT * 4 * 60, bytes_accessed=8 * 2**20, transcendentals=0
        ),
    )(lists, counts, tiles, *pieces, *([] if acc_in is None else [acc_in]))


def finish_kernel(a, b, c, d, weight, bias, out):
    total = a[...] + b[...] + c[...] + d[...]
    hidden = product(total.reshape(BLOCKS * TILE, FEAT), weight[...])
    out[...] = jnp.maximum(hidden + bias[...], 0.0)


def after(value, other):
    anywhere = pl.BlockSpec(memory_space=pl.ANY)
    return pl.pallas_call(
        lambda v, o, out: None,
        out_shape=jax.ShapeDtypeStruct(value.shape, value.dtype),
        in_specs=[anywhere, anywhere],
        out_specs=anywhere,
        input_output_aliases={0: 0},
    )(value, other)


def body(features, new_slot, tile_values, tile_dest, tile_source, weight, bias_vector):
    move = lax.ppermute
    where = jnp.stack([lax.axis_index(a) for a in AXES]).astype(jnp.int32)
    own = features.reshape(BLOCKS, TILE, FEAT)
    prim = move(own, ("y", "core"), AHEAD)
    sec = move(own, ("y", "core"), BACK)
    far = move(own, "z_hi", SWAP)
    other = move(own, "core", SWAP)
    wide = new_slot[:, None] + 1024 * lax.broadcasted_iota(jnp.int32, (BLOCKS, 128), 1)
    slots = lax.all_gather(wide, ("z_hi", "y", "core"), axis=0, tiled=True)[:, 0]

    smem = pl.BlockSpec(memory_space=pltpu.SMEM)
    lists, counts = pl.pallas_call(
        plan_kernel,
        out_shape=[
            jax.ShapeDtypeStruct((3 * LIST,), jnp.int32),
            jax.ShapeDtypeStruct((3,), jnp.int32),
        ],
        in_specs=[smem] * 4,
        out_specs=[smem] * 2,
        scratch_shapes=[pltpu.SMEM((128,), jnp.int32)],
    )(where, slots, tile_dest.reshape(TILES), tile_source.reshape(TILES))
    prim = after(prim, lists)

    two = move(prim, ("y", "core"), AHEAD)
    prim_other, sec_other, far_other = [move(p, "core", SWAP) for p in (prim, sec, far)]
    far_prim = move(far, ("y", "core"), AHEAD)
    far_sec = move(far, ("y", "core"), BACK)
    far_two = move(two, "z_hi", SWAP)
    two_other = move(two, "core", SWAP)
    second = [far_prim, far_two, far_sec]
    third = [move(p, "core", SWAP) for p in second]

    tiles = tile_values.reshape(TILES, TILE, TILE)

    first = [own, other, prim, prim_other, two, two_other, sec, sec_other, far, far_other]
    [acc] = tile_products(0, 0, lists, counts, tiles, first, None, [DUMMY])
    [acc] = tile_products(1, FIRST, lists, counts, tiles, second, acc, [DUMMY])
    mine, prim, two, sec, z_mine, z_prim, z_two, z_sec = tile_products(
        2, FIRST + SECOND, lists, counts, tiles, third, acc, [BLOCKS] * 8
    )

    got_two = move(z_two, "z_lo", SWAP)
    got_prim = move(z_prim, ("x", "core"), AHEAD)
    got_sec = move(z_sec, ("x", "core"), BACK)
    got = move(two + got_two, ("x", "core"), AHEAD)
    end_sec = move(sec, ("x", "core"), BACK)
    end_z = move(z_mine + got_prim + got_sec, "z_lo", SWAP)
    end_prim = move(prim + got, ("x", "core"), AHEAD)

    return pl.pallas_call(
        finish_kernel,
        out_shape=jax.ShapeDtypeStruct((BLOCKS * TILE, FEAT), f32),
        compiler_params=pltpu.CompilerParams(vmem_limit_bytes=24 * 2**20),
    )(mine, end_prim, end_sec, end_z, weight, bias_vector.reshape(1, FEAT))


def solution(mesh):
    fine = Mesh(mesh.devices.reshape(2, 4, 2, 4, 2), AXES)
    grp, blk = AXES[:2], AXES[2:]
    return jax.shard_map(
        body,
        mesh=fine,
        in_specs=(
            P(AXES, None),
            P(AXES),
            P(grp, blk, None, None, None, None),
            P(grp, blk, None, None),
            P(grp, blk, None, None),
            P(),
            P(),
        ),
        out_specs=P(AXES, None),
        check_vma=False,
    )
```

time: 322 us -> 144 us (0.45)
  waiting for transfers between devices: 147 us -> 48.6 us
  other arithmetic: 55.8 us -> 0.95 us
  local copies, waits for them, and re-layouts: 52.1 us -> 10.7 us
  matrix products: 39.6 us -> 0 us
  Pallas kernels: 0 us -> 34.1 us
  blocking collectives: 0 us -> 20.9 us
  starting transfers between devices: 11.7 us -> 26 us
  between operations: 13.4 us -> 0.2 us
    all_gather x1 -> x0, waiting for transfers between devices: 74.9 us -> none  [body(): lax.all_gather(owned_blocks.reshape(BLOCKS_DEV, TILE, FEAT), 'blk', axis=...]
    scatter-add x1 -> x0, other arithmetic: 52.3 us -> none  [body(): jax.ops.segment_sum(products, dest_ids, num_segments=local_rows)]
    reduce_scatter x1 -> x0, waiting for transfers between devices: 50.9 us -> none  [body(): lax.psum_scatter(partial_value, 'grp', scatter_dimension=0, tiled=True)]
    ppermute x0 -> x22, waiting for transfers between devices: none -> 48.6 us  [the longest x1 9.99 us: body(): got = move(two + got_two, ('x', 'core'), AHEAD)]
    dot_general x4 -> x0, matrix products: 39.6 us -> none  [the longest x1 34.6 us: tile_products(): jnp.einsum('kptr,kprf->kptf', values, picked, precision=precise, preferre...]
    pallas_call x0 -> x6, Pallas kernels: none -> 34.1 us  [the longest x3 26.1 us: tile_products(): pl.pallas_call(functools.partial(tile_kernel, part, base, sizes, n_in, ou...]
    reshape x4 -> x2, local copies, waits for them, and re-layouts: 32.1 us -> 2.7 us  [the longest x1 1.36 us: body(): tile_source.reshape(TILES)]
    ppermute x0 -> x22, starting transfers between devices: none -> 26 us  [the longest x1 3.88 us: body(): far = move(own, 'z_hi', SWAP)]
  transfers between devices with their start and end apart: 4 -> 22, of which waited for: 4 -> 7; matrix products, arithmetic and copies ran while one was open for 2% -> 3% of each run, Pallas kernels for 0% -> 19%
where the time goes in v1:
time: 144 us; the launch traced here: 141 us
  waiting for transfers between devices  48.6 us (34%)
  Pallas kernels  34.1 us (24%)
  starting transfers between devices  26 us (18%)
  blocking collectives  20.9 us (15%)
  local copies, waits for them, and re-layouts  10.7 us (7%)
    pallas_call x3, Pallas kernels, tile_products(): pl.pallas_call(functools.partial(tile_kernel, part, base, sizes, n_in, ou...  26.1 us
    all_gather x1, blocking collectives, body(): lax.all_gather(wide, ('z_hi', 'y', 'core'), axis=0, tiled=True)[:, 0]  20.9 us
    ppermute x1, waiting for transfers between devices, body(): got = move(two + got_two, ('x', 'core'), AHEAD)  9.99 us
    ppermute x1, waiting for transfers between devices, body(): two = move(prim, ('y', 'core'), AHEAD)  9.69 us
    ppermute x1, waiting for transfers between devices, body(): got_two = move(z_two, 'z_lo', SWAP)  9.38 us
    ppermute x1, waiting for transfers between devices, body(): end_prim = move(prim + got, ('x', 'core'), AHEAD)  7.95 us
    pallas_call x1, Pallas kernels, body(): pl.pallas_call(plan_kernel, out_shape=[jax.ShapeDtypeStruct((3 * LIST,),...  6.83 us
    unnamed x26, local copies, waits for them, and re-layouts  6.74 us
  transfers between devices with their start and end apart: 22, of which 7 were waited for; matrix products, arithmetic and copies ran while one was open for 3% of the time, Pallas kernels for 19%

profile of v1, /device:TPU:0, one launch (start us, length us, event | category | flops | bytes accessed | tf_op | source)
XLA Modules:
  0.0 141.4 jit_solution(10931809111095568573)
XLA Ops:
  0.0 1.7 %collective-permute-start.3 = (f32[8,128,128]{2,1,0:T(8,128)}, f32[8,128,128]{2,1,0:T(8,128)S(1)}, u32[]{:S(2)}, u32[]{:S(2)}) collective-permute-start(f32[8,128,128]{2,1,0:T(8,128)} %bitcast.12), channel_id=1, source_target_pairs={{0,2},{1,7},{2,4},{3,1},{4,6},{5,3},{6,0},{7,5},{8,10},{9,15},{10,... | collective-permute-start | bytes 1572872 | tf_op jit(solution)/shard_map/ppermute | solution.py:215
  1.7 3.9 %collective-permute-start = (f32[8,128,128]{2,1,0:T(8,128)}, f32[8,128,128]{2,1,0:T(8,128)S(1)}, u32[]{:S(2)}, u32[]{:S(2)}) collective-permute-start(f32[8,128,128]{2,1,0:T(8,128)} %bitcast.13), channel_id=1, source_target_pairs={{0,8},{8,0},{1,9},{9,1},{2,10},{10,2},{3,11},{11,3},{4,12},{12,4},... | collective-permute-start | bytes 1572872 | tf_op jit(solution)/shard_map/ppermute | solution.py:217
  5.5 1.7 %collective-permute-start.12 = (f32[8,128,128]{2,1,0:T(8,128)}, f32[8,128,128]{2,1,0:T(8,128)S(1)}, u32[]{:S(2)}, u32[]{:S(2)}) collective-permute-start(f32[8,128,128]{2,1,0:T(8,128)} %bitcast.14), channel_id=1, source_target_pairs={{2,0},{7,1},{4,2},{1,3},{6,4},{3,5},{0,6},{5,7},{10,8},{15,9},{12,... | collective-permute-start | bytes 1572872 | tf_op jit(solution)/shard_map/ppermute | solution.py:216
  7.2 0.7 broadcast_add_fusion
  7.9 1.3 reshape.16.dest
  9.3 1.4 reshape.17.source
  10.6 0.7 stack.23.where
  11.3 20.9 %all_gather.3 = s32[128,128]{1,0:T(8,128)S(1)} all-gather(s32[8,128]{1,0:T(8,128)S(1)} %broadcast_add_fusion), channel_id=1, replica_groups=mesh['z_lo'=2,'x'=4,'z_hi'=2,'y'=4,'core'=2] {'z_hi','y','core'}, dimensions={0}, use_global_device_ids=true | all-gather | bytes 69632 | tf_op jit(solution)/shard_map/all_gather | solution.py:220
  32.2 0.6 slice_reduce_fusion.slots
  32.8 6.8 %shard_map.73 = (s32[780]{0:T(1024)}, s32[3]{0:T(128)}) custom-call(s32[5]{0:T(128)} %stack.23.where, s32[128]{0:T(128)} %slice_reduce_fusion.slots, s32[256]{0:T(256)} %reshape.16.dest, s32[256]{0:T(256)} %reshape.17.source), custom_call_target="tpu_custom_call" | custom-call | tf_op jit(solution)/shard_map/pallas_call | solution.py:223
  39.7 0.8 copy-done
  40.5 0.3 collective-permute-start.4
  40.8 0.0 collective-permute-start.10
  40.8 0.5 collective-permute-start.14
  41.3 1.4 collective-permute-start.1
  42.6 1.9 %collective-permute-start.7 = (f32[8,128,128]{2,1,0:T(8,128)S(1)}, f32[8,128,128]{2,1,0:T(8,128)S(1)}, u32[]{:S(2)}, u32[]{:S(2)}) collective-permute-start(f32[8,128,128]{2,1,0:T(8,128)S(1)} %collective-permute-done.refs_11_), channel_id=1, source_target_pairs={{2,0},{7,1},{4,2},{1,3},{6,4},{3,5},{0,6},{5,7},{10,8},{15,9},{12,... | collective-permute-start | bytes 1572872 | tf_op jit(solution)/shard_map/ppermute | solution.py:238
  44.5 9.7 %collective-permute-done.4.refs_7_ = f32[8,128,128]{2,1,0:T(8,128)S(1)} collective-permute-done((f32[8,128,128]{2,1,0:T(8,128)}, f32[8,128,128]{2,1,0:T(8,128)S(1)}, u32[]{:S(2)}, u32[]{:S(2)}) %collective-permute-start.4) | collective-permute-done | bytes 524320 | tf_op jit(solution)/shard_map/ppermute | solution.py:235
  54.2 3.6 %collective-permute-start.5 = (f32[8,128,128]{2,1,0:T(8,128)S(1)}, f32[8,128,128]{2,1,0:T(8,128)S(1)}, u32[]{:S(2)}, u32[]{:S(2)}) collective-permute-start(f32[8,128,128]{2,1,0:T(8,128)S(1)} %collective-permute-done.4.refs_7_), channel_id=1, source_target_pairs={{0,8},{8,0},{1,9},{9,1},{2,10},{10,2},{3,11},{11,3},{4,12},{12,4},... | collective-permute-start | bytes 1572872 | tf_op jit(solution)/shard_map/ppermute | solution.py:239
  57.8 0.5 collective-permute-start.11
  58.3 4.0 %collective-permute-done.1.refs_3_ = f32[8,128,128]{2,1,0:T(8,128)S(1)} collective-permute-done((f32[8,128,128]{2,1,0:T(8,128)S(1)}, f32[8,128,128]{2,1,0:T(8,128)S(1)}, u32[]{:S(2)}, u32[]{:S(2)}) %collective-permute-start.1) | collective-permute-done | bytes 524320 | tf_op jit(solution)/shard_map/ppermute | solution.py:237
  62.3 0.5 collective-permute-start.8
  62.8 5.1 %collective-permute-done.5.refs_4_ = f32[8,128,128]{2,1,0:T(8,128)S(1)} collective-permute-done((f32[8,128,128]{2,1,0:T(8,128)S(1)}, f32[8,128,128]{2,1,0:T(8,128)S(1)}, u32[]{:S(2)}, u32[]{:S(2)}) %collective-permute-start.5) | collective-permute-done | bytes 524320 | tf_op jit(solution)/shard_map/ppermute | solution.py:239
  68.0 0.8 copy-done.12
  68.8 1.0 copy-done.1
  69.8 1.0 copy-done.2
  70.9 0.7 copy-done.4
  71.5 0.7 copy-done.5
  72.2 12.3 %shard_map.75.refs_6_ = f32[64,128,128]{2,1,0:T(8,128)} custom-call(s32[780]{0:T(1024)S(1)} %copy-done.4, s32[3]{0:T(128)S(1)} %copy-done.5, f32[256,128,128]{2,1,0:T(8,128)} %bitcast.18, f32[8,128,128]{2,1,0:T(8,128)S(1)} %bitcast.16, f32[8,128,128]{2,1,0:T(8,128)S(1)} %collective-permute-done.9.refs_4_, f32[8,128,128]{2,1,0:T(8,128)S(1)} %copy-done.1, ...), custom_call_target="tpu_custom_call" | custom-call | flops 1006632960 | bytes 8388608 | tf_op jit(solution)/shard_map/pallas_call | solution.py:173
  84.5 7.5 %shard_map.76.refs_6_ = f32[64,128,128]{2,1,0:T(8,128)} custom-call(s32[780]{0:T(1024)S(1)} %copy-done.4, s32[3]{0:T(128)S(1)} %copy-done.5, f32[256,128,128]{2,1,0:T(8,128)} %bitcast.19, f32[8,128,128]{2,1,0:T(8,128)S(1)} %collective-permute-done.1.refs_3_, f32[8,128,128]{2,1,0:T(8,128)S(1)} %collective-permute-done.5.refs_4_, ...), custom_call_target="tpu_custom_call" | custom-call | flops 1006632960 | bytes 8388608 | tf_op jit(solution)/shard_map/pallas_call | solution.py:173
  92.1 0.8 copy-done.9
  92.8 0.2 copy-done.10
  93.0 0.8 copy-done.11
  93.8 6.3 %shard_map.77 = (f32[8,128,128]{2,1,0:T(8,128)S(1)}, f32[8,128,128]{2,1,0:T(8,128)S(1)}, f32[8,128,128]{2,1,0:T(8,128)S(1)}, f32[8,128,128]{2,1,0:T(8,128)S(1)},...) custom-call(s32[780]{0:T(1024)S(1)} %copy-done.4, ...), custom_call_target="tpu_custom_call" | custom-call | flops 1006632960 | bytes 8388608 | tf_op jit(solution)/shard_map/pallas_call | solution.py:173
  100.1 2.4 %collective-permute-start.15 = (f32[8,128,128]{2,1,0:T(8,128)S(1)}, f32[8,128,128]{2,1,0:T(8,128)S(1)}, u32[]{:S(2)}, u32[]{:S(2)}) collective-permute-start(f32[8,128,128]{2,1,0:T(8,128)S(1)} %get-tuple-element.20), channel_id=1, source_target_pairs={{0,64},{64,0},{1,65},{65,1},{2,66},{66,2},{3,67},{67,3},{4,68},{68... | collective-permute-start | bytes 1572872 | tf_op jit(solution)/shard_map/ppermute | solution.py:253
  102.5 2.7 %collective-permute-start.19 = (f32[8,128,128]{2,1,0:T(8,128)S(1)}, f32[8,128,128]{2,1,0:T(8,128)S(1)}, u32[]{:S(2)}, u32[]{:S(2)}) collective-permute-start(f32[8,128,128]{2,1,0:T(8,128)S(1)} %get-tuple-element.23), channel_id=1, source_target_pairs={{0,16},{1,49},{16,32},{17,1},{32,48},{33,17},{48,0},{49,33},{2,18}... | collective-permute-start | bytes 1572872 | tf_op jit(solution)/shard_map/ppermute | solution.py:254
  105.2 0.5 collective-permute-start.20
  105.8 9.4 %collective-permute-done.15 = f32[8,128,128]{2,1,0:T(8,128)S(1)} collective-permute-done((f32[8,128,128]{2,1,0:T(8,128)S(1)}, f32[8,128,128]{2,1,0:T(8,128)S(1)}, u32[]{:S(2)}, u32[]{:S(2)}) %collective-permute-start.15) | collective-permute-done | bytes 524320 | tf_op jit(solution)/shard_map/ppermute | solution.py:253
  115.1 0.1 add.22
  115.2 0.7 collective-permute-start.16
  115.9 2.6 %collective-permute-start.18 = (f32[8,128,128]{2,1,0:T(8,128)S(1)}, f32[8,128,128]{2,1,0:T(8,128)S(1)}, u32[]{:S(2)}, u32[]{:S(2)}) collective-permute-start(f32[8,128,128]{2,1,0:T(8,128)S(1)} %get-tuple-element.21), channel_id=1, source_target_pairs={{16,0},{49,1},{32,16},{1,17},{48,32},{17,33},{0,48},{33,49},{18,2}... | collective-permute-start | bytes 1572872 | tf_op jit(solution)/shard_map/ppermute | solution.py:257
  118.5 0.1 add_add_fusion
  118.6 1.2 collective-permute-start.21
  119.8 10.0 %collective-permute-done.16 = f32[8,128,128]{2,1,0:T(8,128)S(1)} collective-permute-done((f32[8,128,128]{2,1,0:T(8,128)S(1)}, f32[8,128,128]{2,1,0:T(8,128)S(1)}, u32[]{:S(2)}, u32[]{:S(2)}) %collective-permute-start.16) | collective-permute-done | bytes 524320 | tf_op jit(solution)/shard_map/ppermute | solution.py:256
  129.8 0.1 add.23
  129.8 0.1 collective-permute-start.17
  129.9 2.4 %collective-permute-done.21.d = f32[8,128,128]{2,1,0:T(8,128)S(1)} collective-permute-done((f32[8,128,128]{2,1,0:T(8,128)S(1)}, f32[8,128,128]{2,1,0:T(8,128)S(1)}, u32[]{:S(2)}, u32[]{:S(2)}) %collective-permute-start.21) | collective-permute-done | bytes 524320 | tf_op jit(solution)/shard_map/ppermute | solution.py:258
  132.4 8.0 %collective-permute-done.17.b = f32[8,128,128]{2,1,0:T(8,128)S(1)} collective-permute-done((f32[8,128,128]{2,1,0:T(8,128)S(1)}, f32[8,128,128]{2,1,0:T(8,128)S(1)}, u32[]{:S(2)}, u32[]{:S(2)}) %collective-permute-start.17) | collective-permute-done | bytes 524320 | tf_op jit(solution)/shard_map/ppermute | solution.py:259
  140.3 1.1 shard_map.78
  (38 shorter events, 0.1 us)
Async XLA Ops:
  0.0 39.6 %collective-permute-start.3 = (f32[8,128,128]{2,1,0:T(8,128)}, f32[8,128,128]{2,1,0:T(8,128)S(1)}, u32[]{:S(2)}, u32[]{:S(2)}) collective-permute-start(f32[8,128,128]{2,1,0:T(8,128)} %bitcast.12), channel_id=1, source_target_pairs={{0,2},{1,7},{2,4},{3,1},{4,6},{5,3},{6,0},{7,5},{8,10},{9,15},{10,... | collective-permute-start | bytes 1572872 | tf_op jit(solution)/shard_map/ppermute | solution.py:215
  1.7 39.1 %collective-permute-start = (f32[8,128,128]{2,1,0:T(8,128)}, f32[8,128,128]{2,1,0:T(8,128)S(1)}, u32[]{:S(2)}, u32[]{:S(2)}) collective-permute-start(f32[8,128,128]{2,1,0:T(8,128)} %bitcast.13), channel_id=1, source_target_pairs={{0,8},{8,0},{1,9},{9,1},{2,10},{10,2},{3,11},{11,3},{4,12},{12,4},... | collective-permute-start | bytes 1572872 | tf_op jit(solution)/shard_map/ppermute | solution.py:217
  5.5 35.8 %collective-permute-start.12 = (f32[8,128,128]{2,1,0:T(8,128)}, f32[8,128,128]{2,1,0:T(8,128)S(1)}, u32[]{:S(2)}, u32[]{:S(2)}) collective-permute-start(f32[8,128,128]{2,1,0:T(8,128)} %bitcast.14), channel_id=1, source_target_pairs={{2,0},{7,1},{4,2},{1,3},{6,4},{3,5},{0,6},{5,7},{10,8},{15,9},{12,... | collective-permute-start | bytes 1572872 | tf_op jit(solution)/shard_map/ppermute | solution.py:216
  7.2 35.4 %collective-permute-start.9 = (f32[8,128,128]{2,1,0:T(8,128)}, f32[8,128,128]{2,1,0:T(8,128)S(1)}, u32[]{:S(2)}, u32[]{:S(2)}) collective-permute-start(f32[8,128,128]{2,1,0:T(8,128)} %bitcast.15), channel_id=1, source_target_pairs={{0,1},{1,0},{2,3},{3,2},{4,5},{5,4},{6,7},{7,6},{8,9},{9,8},{10,11... | collective-permute-start | bytes 1572872 | tf_op jit(solution)/shard_map/ppermute | solution.py:218
  39.7 0.8 copy-start
  40.5 13.8 %collective-permute-start.4 = (f32[8,128,128]{2,1,0:T(8,128)}, f32[8,128,128]{2,1,0:T(8,128)S(1)}, u32[]{:S(2)}, u32[]{:S(2)}) collective-permute-start(f32[8,128,128]{2,1,0:T(8,128)} %shard_map.74.refs_5_), channel_id=1, source_target_pairs={{0,2},{1,7},{2,4},{3,1},{4,6},{5,3},{6,0},{7,5},{8,10},{9,15},{10,... | collective-permute-start | bytes 1572872 | tf_op jit(solution)/shard_map/ppermute | solution.py:235
  40.8 17.0 %collective-permute-start.10 = (f32[8,128,128]{2,1,0:T(8,128)}, f32[8,128,128]{2,1,0:T(8,128)S(1)}, u32[]{:S(2)}, u32[]{:S(2)}) collective-permute-start(f32[8,128,128]{2,1,0:T(8,128)} %shard_map.74.refs_5_), channel_id=1, source_target_pairs={{0,1},{1,0},{2,3},{3,2},{4,5},{5,4},{6,7},{7,6},{8,9},{9,8},{10,11... | collective-permute-start | bytes 1572872 | tf_op jit(solution)/shard_map/ppermute | solution.py:236
  40.8 27.2 %copy-start.7 = (f32[8,128,128]{2,1,0:T(8,128)}, f32[8,128,128]{2,1,0:T(8,128)S(1)}, u32[]{:S(2)}) copy-start(f32[8,128,128]{2,1,0:T(8,128)S(1)} %collective-permute-done.refs_11_) | copy-start | bytes 1572868
  40.8 17.0 %collective-permute-start.14 = (f32[8,128,128]{2,1,0:T(8,128)S(1)}, f32[8,128,128]{2,1,0:T(8,128)S(1)}, u32[]{:S(2)}, u32[]{:S(2)}) collective-permute-start(f32[8,128,128]{2,1,0:T(8,128)S(1)} %collective-permute-done.refs_11_), channel_id=1, source_target_pairs={{0,1},{1,0},{2,3},{3,2},{4,5},{5,4},{6,7},{7,6},{8,9},{9,8},{10,11... | collective-permute-start | bytes 1572872 | tf_op jit(solution)/shard_map/ppermute | solution.py:236
  41.3 21.0 %collective-permute-start.1 = (f32[8,128,128]{2,1,0:T(8,128)S(1)}, f32[8,128,128]{2,1,0:T(8,128)S(1)}, u32[]{:S(2)}, u32[]{:S(2)}) collective-permute-start(f32[8,128,128]{2,1,0:T(8,128)S(1)} %collective-permute-done.refs_11_), channel_id=1, source_target_pairs={{0,2},{1,7},{2,4},{3,1},{4,6},{5,3},{6,0},{7,5},{8,10},{9,15},{10,... | collective-permute-start | bytes 1572872 | tf_op jit(solution)/shard_map/ppermute | solution.py:237
  42.6 19.7 %collective-permute-start.7 = (f32[8,128,128]{2,1,0:T(8,128)S(1)}, f32[8,128,128]{2,1,0:T(8,128)S(1)}, u32[]{:S(2)}, u32[]{:S(2)}) collective-permute-start(f32[8,128,128]{2,1,0:T(8,128)S(1)} %collective-permute-done.refs_11_), channel_id=1, source_target_pairs={{2,0},{7,1},{4,2},{1,3},{6,4},{3,5},{0,6},{5,7},{10,8},{15,9},{12,... | collective-permute-start | bytes 1572872 | tf_op jit(solution)/shard_map/ppermute | solution.py:238
  54.2 13.7 %collective-permute-start.5 = (f32[8,128,128]{2,1,0:T(8,128)S(1)}, f32[8,128,128]{2,1,0:T(8,128)S(1)}, u32[]{:S(2)}, u32[]{:S(2)}) collective-permute-start(f32[8,128,128]{2,1,0:T(8,128)S(1)} %collective-permute-done.4.refs_7_), channel_id=1, source_target_pairs={{0,8},{8,0},{1,9},{9,1},{2,10},{10,2},{3,11},{11,3},{4,12},{12,4},... | collective-permute-start | bytes 1572872 | tf_op jit(solution)/shard_map/ppermute | solution.py:239
  57.8 10.1 %collective-permute-start.13 = (f32[8,128,128]{2,1,0:T(8,128)S(1)}, f32[8,128,128]{2,1,0:T(8,128)S(1)}, u32[]{:S(2)}, u32[]{:S(2)}) collective-permute-start(f32[8,128,128]{2,1,0:T(8,128)S(1)} %collective-permute-done.12.refs_9_), channel_id=1, source_target_pairs={{0,1},{1,0},{2,3},{3,2},{4,5},{5,4},{6,7},{7,6},{8,9},{9,8},{10,11... | collective-permute-start | bytes 1572872 | tf_op jit(solution)/shard_map/ppermute | solution.py:236
  57.8 10.2 %copy-start.8 = (f32[8,128,128]{2,1,0:T(8,128)}, f32[8,128,128]{2,1,0:T(8,128)S(1)}, u32[]{:S(2)}) copy-start(f32[8,128,128]{2,1,0:T(8,128)S(1)} %collective-permute-done.14.refs_12_) | copy-start | bytes 1572868
  57.8 10.1 %collective-permute-start.11 = (f32[8,128,128]{2,1,0:T(8,128)S(1)}, f32[8,128,128]{2,1,0:T(8,128)S(1)}, u32[]{:S(2)}, u32[]{:S(2)}) collective-permute-start(f32[8,128,128]{2,1,0:T(8,128)S(1)} %collective-permute-done.4.refs_7_), channel_id=1, source_target_pairs={{0,1},{1,0},{2,3},{3,2},{4,5},{5,4},{6,7},{7,6},{8,9},{9,8},{10,11... | collective-permute-start | bytes 1572872 | tf_op jit(solution)/shard_map/ppermute | solution.py:240
  62.3 29.7 %collective-permute-start.2 = (f32[8,128,128]{2,1,0:T(8,128)S(1)}, f32[8,128,128]{2,1,0:T(8,128)S(1)}, u32[]{:S(2)}, u32[]{:S(2)}) collective-permute-start(f32[8,128,128]{2,1,0:T(8,128)S(1)} %collective-permute-done.1.refs_3_), channel_id=1, source_target_pairs={{0,1},{1,0},{2,3},{3,2},{4,5},{5,4},{6,7},{7,6},{8,9},{9,8},{10,11... | collective-permute-start | bytes 1572872 | tf_op jit(solution)/shard_map/ppermute | solution.py:242
  62.3 29.8 %collective-permute-start.8 = (f32[8,128,128]{2,1,0:T(8,128)S(1)}, f32[8,128,128]{2,1,0:T(8,128)S(1)}, u32[]{:S(2)}, u32[]{:S(2)}) collective-permute-start(f32[8,128,128]{2,1,0:T(8,128)S(1)} %collective-permute-done.7.refs_5_), channel_id=1, source_target_pairs={{0,1},{1,0},{2,3},{3,2},{4,5},{5,4},{6,7},{7,6},{8,9},{9,8},{10,11... | collective-permute-start | bytes 1572872 | tf_op jit(solution)/shard_map/ppermute | solution.py:242
  67.9 24.1 %collective-permute-start.6 = (f32[8,128,128]{2,1,0:T(8,128)S(1)}, f32[8,128,128]{2,1,0:T(8,128)S(1)}, u32[]{:S(2)}, u32[]{:S(2)}) collective-permute-start(f32[8,128,128]{2,1,0:T(8,128)S(1)} %collective-permute-done.5.refs_4_), channel_id=1, source_target_pairs={{0,1},{1,0},{2,3},{3,2},{4,5},{5,4},{6,7},{7,6},{8,9},{9,8},{10,11... | collective-permute-start | bytes 1572872 | tf_op jit(solution)/shard_map/ppermute | solution.py:242
  68.0 0.8 copy-start.12
  68.8 1.0 copy-start.1
  69.8 1.0 copy-start.2
  70.9 0.7 copy-start.4
  71.5 0.7 copy-start.5
  92.0 0.8 copy-start.9
  92.1 0.9 copy-start.10
  93.0 0.8 copy-start.11
  100.1 40.2 %copy-start.3 = (f32[128,128]{1,0:T(8,128)S(1)}, f32[128,128]{1,0:T(8,128)}, u32[]{:S(2)}) copy-start(f32[128,128]{1,0:T(8,128)} %weight.1) | copy-start | bytes 196612
  100.1 40.2 %copy-start.6 = (f32[128]{0:T(128)S(1)}, f32[128]{0:T(128)}, u32[]{:S(2)}) copy-start(f32[128]{0:T(128)} %param.13) | copy-start | bytes 1540
  100.1 15.0 %collective-permute-start.15 = (f32[8,128,128]{2,1,0:T(8,128)S(1)}, f32[8,128,128]{2,1,0:T(8,128)S(1)}, u32[]{:S(2)}, u32[]{:S(2)}) collective-permute-start(f32[8,128,128]{2,1,0:T(8,128)S(1)} %get-tuple-element.20), channel_id=1, source_target_pairs={{0,64},{64,0},{1,65},{65,1},{2,66},{66,2},{3,67},{67,3},{4,68},{68... | collective-permute-start | bytes 1572872 | tf_op jit(solution)/shard_map/ppermute | solution.py:253
  102.5 16.0 %collective-permute-start.19 = (f32[8,128,128]{2,1,0:T(8,128)S(1)}, f32[8,128,128]{2,1,0:T(8,128)S(1)}, u32[]{:S(2)}, u32[]{:S(2)}) collective-permute-start(f32[8,128,128]{2,1,0:T(8,128)S(1)} %get-tuple-element.23), channel_id=1, source_target_pairs={{0,16},{1,49},{16,32},{17,1},{32,48},{33,17},{48,0},{49,33},{2,18}... | collective-permute-start | bytes 1572872 | tf_op jit(solution)/shard_map/ppermute | solution.py:254
  105.2 13.3 %collective-permute-start.20 = (f32[8,128,128]{2,1,0:T(8,128)}, f32[8,128,128]{2,1,0:T(8,128)S(1)}, u32[]{:S(2)}, u32[]{:S(2)}) collective-permute-start(f32[8,128,128]{2,1,0:T(8,128)} %get-tuple-element.24), channel_id=1, source_target_pairs={{16,0},{49,1},{32,16},{1,17},{48,32},{17,33},{0,48},{33,49},{18,2}... | collective-permute-start | bytes 1572872 | tf_op jit(solution)/shard_map/ppermute | solution.py:255
  115.2 14.6 %collective-permute-start.16 = (f32[8,128,128]{2,1,0:T(8,128)S(1)}, f32[8,128,128]{2,1,0:T(8,128)S(1)}, u32[]{:S(2)}, u32[]{:S(2)}) collective-permute-start(f32[8,128,128]{2,1,0:T(8,128)S(1)} %add.22), channel_id=1, source_target_pairs={{0,16},{1,49},{16,32},{17,1},{32,48},{33,17},{48,0},{49,33},{2,18}... | collective-permute-start | bytes 1572872 | tf_op jit(solution)/shard_map/ppermute | solution.py:256
  115.9 14.0 %collective-permute-start.18 = (f32[8,128,128]{2,1,0:T(8,128)S(1)}, f32[8,128,128]{2,1,0:T(8,128)S(1)}, u32[]{:S(2)}, u32[]{:S(2)}) collective-permute-start(f32[8,128,128]{2,1,0:T(8,128)S(1)} %get-tuple-element.21), channel_id=1, source_target_pairs={{16,0},{49,1},{32,16},{1,17},{48,32},{17,33},{0,48},{33,49},{18,2}... | collective-permute-start | bytes 1572872 | tf_op jit(solution)/shard_map/ppermute | solution.py:257
  118.6 13.7 %collective-permute-start.21 = (f32[8,128,128]{2,1,0:T(8,128)S(1)}, f32[8,128,128]{2,1,0:T(8,128)S(1)}, u32[]{:S(2)}, u32[]{:S(2)}) collective-permute-start(f32[8,128,128]{2,1,0:T(8,128)S(1)} %add_add_fusion), channel_id=1, source_target_pairs={{0,64},{64,0},{1,65},{65,1},{2,66},{66,2},{3,67},{67,3},{4,68},{68... | collective-permute-start | bytes 1572872 | tf_op jit(solution)/shard_map/ppermute | solution.py:258
  129.8 10.5 %collective-permute-start.17 = (f32[8,128,128]{2,1,0:T(8,128)S(1)}, f32[8,128,128]{2,1,0:T(8,128)S(1)}, u32[]{:S(2)}, u32[]{:S(2)}) collective-permute-start(f32[8,128,128]{2,1,0:T(8,128)S(1)} %add.23), channel_id=1, source_target_pairs={{0,16},{1,49},{16,32},{17,1},{32,48},{33,17},{48,0},{49,33},{2,18}... | collective-permute-start | bytes 1572872 | tf_op jit(solution)/shard_map/ppermute | solution.py:259

commit v2 on v1

v2 whole, which is shorter than its diff:
```python
import functools

import jax
import jax.numpy as jnp
from jax import lax
from jax.experimental import pallas as pl
from jax.experimental.pallas import tpu as pltpu
from jax.sharding import Mesh, PartitionSpec as P

TILE = 128
FEAT = 128
BLOCKS = 8
SLOTS = 16
BUCKETS = 16
TILES = BUCKETS * SLOTS
UNROLL = 4
RING = 16
FIRST, SECOND, THIRD = 80, 24, 24
LIST = TILES + UNROLL
DUMMY = 64

AXES = ("z_lo", "x", "z_hi", "y", "core")
AHEAD = [(2 * i + c, 2 * ((i + 1 - 2 * c) % 4) + c) for i in range(4) for c in range(2)]
BACK = [(b, a) for a, b in AHEAD]
SWAP = [(0, 1), (1, 0)]

f32, bf16 = jnp.float32, jnp.bfloat16


BASES = (
    (0, 8, 64, 72),
    (16, 56, 80, 120),
    (32, 40, 88, 112),
    (48, 24, 96, 104),
)


def plan_kernel(own, prim, two, sec, packed, lists, counts, table):
    for bases, slots in zip(BASES, (own, prim, two, sec)):
        for i, base in enumerate(bases):
            for j in range(BLOCKS):
                table[slots[i * BLOCKS + j] & 127] = base + j

    def bucket(k, n):
        n0, n1, n2 = n
        for t in range(SLOTS):
            word = packed[k * SLOTS + t]
            inc = (word >= 0).astype(jnp.int32)
            s = table[(word >> 8) & 127]
            a, b = s < FIRST, s < FIRST + SECOND
            lists[jnp.where(a, n0, jnp.where(b, LIST + n1, 2 * LIST + n2))] = (word & 0xFF00FF) | (s << 8)
            ia = jnp.where(a, inc, 0)
            ib = jnp.where(b, inc, 0)
            n0, n1, n2 = n0 + ia, n1 + ib - ia, n2 + inc - ib
        return n0, n1, n2

    n = lax.fori_loop(0, BUCKETS, bucket, (0, 0, 0))
    for i, base in enumerate((0, FIRST, FIRST + SECOND)):
        counts[i] = (n[i] + UNROLL - 1) // UNROLL
        for j in range(UNROLL):
            lists[i * LIST + n[i] + j] = base * 256 + DUMMY * 65536


def split(v):
    hi = v.astype(bf16)
    return hi, (v - hi.astype(f32)).astype(bf16)


def halves(v):
    return jnp.concatenate(split(v), axis=1)


def product(a, right):
    both = jnp.dot(halves(a), jnp.concatenate([right, right], axis=0), preferred_element_type=f32)
    return both[:, :FEAT] + both[:, FEAT:]


def tile_kernel(part, base, n_pieces, n_in, n_parts, *refs):
    lists, counts, tiles = refs[:3]
    pieces = refs[3 : 3 + n_pieces]
    *parts, acc, xs, ring, ring_sem = refs[3 + n_pieces + n_in :]
    groups = counts[part]
    depth = RING // UNROLL

    def fetch(group, slot):
        for j in range(UNROLL):
            at = lists[part * LIST + group * UNROLL + j] & 255
            pltpu.make_async_copy(tiles.at[at], ring.at[slot, j], ring_sem.at[slot, j]).start()

    def landed(slot):
        for j in range(UNROLL):
            pltpu.make_async_copy(tiles.at[0], ring.at[slot, j], ring_sem.at[slot, j]).wait()

    for s in range(depth - 1):

        @pl.when(s < groups)
        def _(s=s):
            fetch(s, s)

    def halve(j, carry):
        for i, piece in enumerate(pieces):
            xs[i * BLOCKS + j] = halves(piece[j])
        return carry

    lax.fori_loop(0, BLOCKS, halve, 0)

    def begin(d, carry):
        acc[d] = refs[3 + n_pieces][d] if n_in else jnp.zeros((TILE, FEAT), f32)
        return carry

    lax.fori_loop(0, DUMMY + 1, begin, 0, unroll=5)

    def step(group, carry):
        slot = group % depth
        ahead = group + depth - 1

        @pl.when(ahead < groups)
        def _():
            fetch(ahead, ahead % depth)

        landed(slot)
        words = [lists[part * LIST + group * UNROLL + j] for j in range(UNROLL)]
        results = [
            product(ring[slot, j], xs[((words[j] >> 8) & 255) - base]) for j in range(UNROLL)
        ]
        for j in range(UNROLL):
            acc[words[j] >> 16] += results[j]
        return carry

    lax.fori_loop(0, groups, step, 0)
    if n_parts:

        def hand_out(j, carry):
            for i, out in enumerate(parts):
                out[j] = acc[i * BLOCKS + j]
            return carry

        lax.fori_loop(0, BLOCKS, hand_out, 0)


def tile_products(part, base, lists, counts, tiles, pieces, acc_in, n_parts):
    n_in = 0 if acc_in is None else 1
    smem = pl.BlockSpec(memory_space=pltpu.SMEM)
    vmem = pl.BlockSpec(memory_space=pltpu.VMEM)
    hbm = pl.BlockSpec(memory_space=pltpu.HBM)
    return pl.pallas_call(
        functools.partial(tile_kernel, part, base, len(pieces), n_in, n_parts),
        out_shape=[jax.ShapeDtypeStruct((BLOCKS, TILE, FEAT), f32)] * n_parts
        or [jax.ShapeDtypeStruct((DUMMY + 1, TILE, FEAT), f32)],
        in_specs=[smem, smem, hbm] + [vmem] * (len(pieces) + n_in),
        out_specs=[vmem] * max(1, n_parts),
        scratch_shapes=[pltpu.VMEM((DUMMY + 1, TILE, FEAT), f32)] * (n_parts > 0)
        + [
            pltpu.VMEM((len(pieces) * BLOCKS, TILE, 2 * FEAT), bf16),
            pltpu.VMEM((RING // UNROLL, UNROLL, TILE, TILE), f32),
            pltpu.SemaphoreType.DMA((RING // UNROLL, UNROLL)),
        ],
        compiler_params=pltpu.CompilerParams(vmem_limit_bytes=40 * 2**20),
        cost_estimate=pl.CostEstimate(
            flops=2 * TILE * TILE * FEAT * 4 * 60, bytes_accessed=8 * 2**20, transcendentals=0
        ),
    )(lists, counts, tiles, *pieces, *([] if acc_in is None else [acc_in]))


def finish_kernel(a, b, c, d, weight, bias, out):
    total = a[...] + b[...] + c[...] + d[...]
    hidden = product(total.reshape(BLOCKS * TILE, FEAT), halves(weight[...]))
    out[...] = jnp.maximum(hidden + bias[...], 0.0)


def after(value, *others):
    return lax.optimization_barrier((value, *others))[0]


def body(features, new_slot, tile_values, tile_dest, tile_source, weight, bias_vector):
    move = lax.ppermute
    own = features.reshape(BLOCKS, TILE, FEAT)
    prim = move(own, ("y", "core"), AHEAD)
    sec = move(own, ("y", "core"), BACK)
    far = move(own, "z_hi", SWAP)
    other = move(own, "core", SWAP)

    slots = jnp.concatenate([new_slot, move(new_slot, "core", SWAP)])
    slots = jnp.concatenate([slots, move(slots, "z_hi", SWAP)])
    slots_prim = move(slots, ("y", "core"), AHEAD)
    slots_sec = move(slots, ("y", "core"), BACK)
    slots_two = move(slots_prim, ("y", "core"), AHEAD)

    z_lo, x, core = (lax.axis_index(a) for a in ("z_lo", "x", "core"))
    bucket = lax.broadcasted_iota(jnp.int32, (BUCKETS, SLOTS), 0)
    slot = lax.broadcasted_iota(jnp.int32, (BUCKETS, SLOTS), 1)
    dest = tile_dest.reshape(BUCKETS, SLOTS)
    group = dest >> 3
    turned = (((group >> 2) ^ z_lo) * 4 + (((group & 3) - x) * (1 - 2 * core) & 3)) * BLOCKS + (dest & 7)
    position = bucket * BLOCKS + tile_source.reshape(BUCKETS, SLOTS)
    packed = jnp.where(dest >= 0, (bucket * SLOTS + slot) + position * 256 + turned * 65536, -1)

    smem = pl.BlockSpec(memory_space=pltpu.SMEM)
    lists, counts = pl.pallas_call(
        plan_kernel,
        out_shape=[
            jax.ShapeDtypeStruct((3 * LIST,), jnp.int32),
            jax.ShapeDtypeStruct((3,), jnp.int32),
        ],
        in_specs=[smem] * 5,
        out_specs=[smem] * 2,
        scratch_shapes=[pltpu.SMEM((128,), jnp.int32)],
        cost_estimate=pl.CostEstimate(flops=10**7, bytes_accessed=10**4, transcendentals=0),
    )(slots, slots_prim, slots_two, slots_sec, packed.reshape(TILES))

    prim = after(prim, slots_two)
    two = move(prim, ("y", "core"), AHEAD)
    prim_other, sec_other, far_other = [move(p, "core", SWAP) for p in (prim, sec, far)]
    far = after(far, two, lists)
    far_prim = move(far, ("y", "core"), AHEAD)
    far_sec = move(far, ("y", "core"), BACK)
    far_two = move(two, "z_hi", SWAP)
    two_other = move(two, "core", SWAP)
    second = [far_prim, far_two, far_sec]
    third = [move(p, "core", SWAP) for p in second]

    tiles = tile_values.reshape(TILES, TILE, TILE)
    first = [own, other, prim, prim_other, two, two_other, sec, sec_other, far, far_other]
    [acc] = tile_products(0, 0, lists, counts, tiles, first, None, 0)
    [acc] = tile_products(1, FIRST, lists, counts, tiles, second, acc, 0)
    mine, prim, two, sec, z_mine, z_prim, z_two, z_sec = tile_products(
        2, FIRST + SECOND, lists, counts, tiles, third, acc, 8
    )

    got_two = move(z_two, "z_lo", SWAP)
    got_prim = move(z_prim, ("x", "core"), AHEAD)
    got_sec = move(z_sec, ("x", "core"), BACK)
    got = move(two + got_two, ("x", "core"), AHEAD)
    end_sec = move(sec, ("x", "core"), BACK)
    end_z = move(z_mine + got_prim + got_sec, "z_lo", SWAP)
    end_prim = move(prim + got, ("x", "core"), AHEAD)

    return pl.pallas_call(
        finish_kernel,
        out_shape=jax.ShapeDtypeStruct((BLOCKS * TILE, FEAT), f32),
        compiler_params=pltpu.CompilerParams(vmem_limit_bytes=24 * 2**20),
    )(mine, end_prim, end_sec, end_z, weight, bias_vector.reshape(1, FEAT))


def solution(mesh):
    fine = Mesh(mesh.devices.reshape(2, 4, 2, 4, 2), AXES)
    grp, blk = AXES[:2], AXES[2:]
    return jax.shard_map(
        body,
        mesh=fine,
        in_specs=(
            P(AXES, None),
            P(AXES),
            P(grp, blk, None, None, None, None),
            P(grp, blk, None, None),
            P(grp, blk, None, None),
            P(),
            P(),
        ),
        out_specs=P(AXES, None),
        check_vma=False,
    )
```

time: 144 us -> 121 us (0.84); the launches traced: 141 us -> 120 us
  blocking collectives: 20.9 us -> 0 us
  waiting for transfers between devices: 48.6 us -> 63.4 us
  Pallas kernels: 34.1 us -> 22.1 us
  local copies, waits for them, and re-layouts: 10.7 us -> 3.55 us
  other arithmetic: 0.95 us -> 3.77 us
    all_gather x1 -> x0, blocking collectives: 20.9 us -> none  [body(): lax.all_gather(wide, ('z_hi', 'y', 'core'), axis=0, tiled=True)[:, 0]]
    ppermute x0 -> x5, waiting for transfers between devices: none -> 18.9 us  [the longest x1 8.26 us: body(): slots = jnp.concatenate([slots, move(slots, 'z_hi', SWAP)])]
    ppermute x1, waiting for transfers between devices: 9.69 us -> 0.25 us  [body(): two = move(prim, ('y', 'core'), AHEAD)]
    pallas_call x4 -> x3, Pallas kernels: 26.1 us -> 17.5 us  [tile_products(): pl.pallas_call(functools.partial(tile_kernel, part, base, len(pieces), n_...]
    ppermute x1, waiting for transfers between devices: 0.01 us -> 7.21 us  [body(): far_sec = move(far, ('y', 'core'), BACK)]
    unnamed x26 -> x18, local copies, waits for them, and re-layouts: 6.74 us -> 2.37 us
    ppermute x0 -> x5, starting transfers between devices: none -> 3.77 us  [the longest x1 3.24 us: body(): slots_sec = move(slots, ('y', 'core'), BACK)]
    pallas_call x1, Pallas kernels: 6.83 us -> 3.51 us  [body(): pl.pallas_call(plan_kernel, out_shape=[jax.ShapeDtypeStruct((3 * LIST,),...]
  transfers between devices with their start and end apart: 22 -> 27, of which waited for: 7 -> 13; matrix products, arithmetic and copies ran while one was open for 3% -> 4% of each run, Pallas kernels for 19% -> 14%
where the time goes in v2:
time: 121 us; the launch traced here: 120 us
  waiting for transfers between devices  63.4 us (52%)
  starting transfers between devices  27.1 us (22%)
  Pallas kernels  22.1 us (18%)
  other arithmetic  3.77 us (3%)
  local copies, waits for them, and re-layouts  3.55 us (3%)
    pallas_call x3, Pallas kernels, tile_products(): pl.pallas_call(functools.partial(tile_kernel, part, base, len(pieces), n_...  17.5 us
    ppermute x1, waiting for transfers between devices, body(): got = move(two + got_two, ('x', 'core'), AHEAD)  12 us
    ppermute x1, waiting for transfers between devices, body(): got_two = move(z_two, 'z_lo', SWAP)  10.4 us
    ppermute x1, waiting for transfers between devices, body(): end_prim = move(prim + got, ('x', 'core'), AHEAD)  10.2 us
    ppermute x1, waiting for transfers between devices, body(): slots = jnp.concatenate([slots, move(slots, 'z_hi', SWAP)])  8.26 us
    ppermute x1, waiting for transfers between devices, body(): far_sec = move(far, ('y', 'core'), BACK)  7.21 us
    ppermute x1, waiting for transfers between devices, body(): slots_prim = move(slots, ('y', 'core'), AHEAD)  4.67 us
    ppermute x1, waiting for transfers between devices, body(): slots_two = move(slots_prim, ('y', 'core'), AHEAD)  4.59 us
  transfers between devices with their start and end apart: 27, of which 13 were waited for; matrix products, arithmetic and copies ran while one was open for 4% of the time, Pallas kernels for 14%

profile of v2, /device:TPU:0, one launch (start us, length us, event | category | flops | bytes accessed | tf_op | source)
XLA Modules:
  0.0 120.1 jit_solution(14265244821567158249)
XLA Ops:
  0.0 1.7 %collective-permute-start.6 = (f32[8,128,128]{2,1,0:T(8,128)}, f32[8,128,128]{2,1,0:T(8,128)S(1)}, u32[]{:S(2)}, u32[]{:S(2)}) collective-permute-start(f32[8,128,128]{2,1,0:T(8,128)} %bitcast.9), channel_id=1, source_target_pairs={{0,2},{1,7},{2,4},{3,1},{4,6},{5,3},{6,0},{7,5},{8,10},{9,15},{10,... | collective-permute-start | bytes 1572872 | tf_op jit(solution)/shard_map/ppermute | solution.py:178
  1.7 3.9 %collective-permute-start.5 = (f32[8,128,128]{2,1,0:T(8,128)}, f32[8,128,128]{2,1,0:T(8,128)S(1)}, u32[]{:S(2)}, u32[]{:S(2)}) collective-permute-start(f32[8,128,128]{2,1,0:T(8,128)} %bitcast.10), channel_id=1, source_target_pairs={{0,8},{8,0},{1,9},{9,1},{2,10},{10,2},{3,11},{11,3},{4,12},{12,4},... | collective-permute-start | bytes 1572872 | tf_op jit(solution)/shard_map/ppermute | solution.py:180
  5.5 1.7 %collective-permute-start.17 = (f32[8,128,128]{2,1,0:T(8,128)}, f32[8,128,128]{2,1,0:T(8,128)S(1)}, u32[]{:S(2)}, u32[]{:S(2)}) collective-permute-start(f32[8,128,128]{2,1,0:T(8,128)} %bitcast.11), channel_id=1, source_target_pairs={{2,0},{7,1},{4,2},{1,3},{6,4},{3,5},{0,6},{5,7},{10,8},{15,9},{12,... | collective-permute-start | bytes 1572872 | tf_op jit(solution)/shard_map/ppermute | solution.py:179
  7.2 0.5 collective-permute-start
  7.7 0.7 add_multiply_fusion
  8.4 0.9 collective-permute-done
  9.3 0.7 pad_add_fusion
  10.1 8.3 %collective-permute-done.1 = s32[16]{0:T(128)S(1)} collective-permute-done((s32[16]{0:T(128)S(1)}, s32[16]{0:T(128)S(1)}, u32[]{:S(2)}, u32[]{:S(2)}) %collective-permute-start.1) | collective-permute-done | bytes 96 | tf_op jit(solution)/shard_map/ppermute | solution.py:184
  18.3 0.7 pad_add_fusion.1.own
  19.1 4.7 %collective-permute-done.2.prim = s32[32]{0:T(128)S(1)} collective-permute-done((s32[32]{0:T(128)S(1)}, s32[32]{0:T(128)S(1)}, u32[]{:S(2)}, u32[]{:S(2)}) %collective-permute-start.2) | collective-permute-done | bytes 160 | tf_op jit(solution)/shard_map/ppermute | solution.py:185
  23.8 0.1 reshape.49
  23.9 0.1 add.40
  24.0 4.6 %collective-permute-done.3.two = s32[32]{0:T(128)S(1)} collective-permute-done((s32[32]{0:T(128)S(1)}, s32[32]{0:T(128)S(1)}, u32[]{:S(2)}, u32[]{:S(2)}) %collective-permute-start.3) | collective-permute-done | bytes 160 | tf_op jit(solution)/shard_map/ppermute | solution.py:187
  28.7 0.1 iota.24
  28.7 0.7 broadcast_compare_fusion
  29.4 0.1 ge.12
  29.5 3.2 %collective-permute-start.4 = (s32[32]{0:T(128)S(1)}, s32[32]{0:T(128)S(1)}, u32[]{:S(2)}, u32[]{:S(2)}) collective-permute-start(s32[32]{0:T(128)S(1)} %pad_add_fusion.1.own), channel_id=1, source_target_pairs={{2,0},{7,1},{4,2},{1,3},{6,4},{3,5},{0,6},{5,7},{10,8},{15,9},{12,... | collective-permute-start | bytes 392 | tf_op jit(solution)/shard_map/ppermute | solution.py:186
  32.8 0.8 reshape.38
  33.6 0.5 collective-permute-done.4.sec
  34.1 0.5 collective-permute-start.18
  34.6 0.6 add_select_fusion.packed
  35.2 3.5 %shard_map.73 = (s32[780]{0:T(1024)}, s32[3]{0:T(128)}) custom-call(s32[32]{0:T(128)} %copy-done.5, s32[32]{0:T(128)} %copy-done.6, s32[32]{0:T(128)} %copy-done.7, s32[32]{0:T(128)} %copy-done.8, s32[256]{0:T(256)} %add_select_fusion.packed), custom_call_target="tpu_custom_call" | custom-call | flops 10000000 | bytes 10000 | tf_op jit(solution)/shard_map/pallas_call | solution.py:199
  38.7 0.3 collective-permute-done.7.refs_7_
  39.0 3.3 %collective-permute-start.12 = (f32[8,128,128]{2,1,0:T(8,128)S(1)}, f32[8,128,128]{2,1,0:T(8,128)S(1)}, u32[]{:S(2)}, u32[]{:S(2)}) collective-permute-start(f32[8,128,128]{2,1,0:T(8,128)S(1)} %collective-permute-done.5.refs_11_), channel_id=1, source_target_pairs={{2,0},{7,1},{4,2},{1,3},{6,4},{3,5},{0,6},{5,7},{10,8},{15,9},{12,... | collective-permute-start | bytes 1572872 | tf_op jit(solution)/shard_map/ppermute | solution.py:216
  42.2 3.8 %collective-permute-start.10 = (f32[8,128,128]{2,1,0:T(8,128)S(1)}, f32[8,128,128]{2,1,0:T(8,128)S(1)}, u32[]{:S(2)}, u32[]{:S(2)}) collective-permute-start(f32[8,128,128]{2,1,0:T(8,128)S(1)} %collective-permute-done.7.refs_7_), channel_id=1, source_target_pairs={{0,8},{8,0},{1,9},{9,1},{2,10},{10,2},{3,11},{11,3},{4,12},{12,4},... | collective-permute-start | bytes 1572872 | tf_op jit(solution)/shard_map/ppermute | solution.py:217
  46.0 0.5 collective-permute-start.16
  46.5 7.2 %collective-permute-done.12.refs_5_ = f32[8,128,128]{2,1,0:T(8,128)S(1)} collective-permute-done((f32[8,128,128]{2,1,0:T(8,128)S(1)}, f32[8,128,128]{2,1,0:T(8,128)S(1)}, u32[]{:S(2)}, u32[]{:S(2)}) %collective-permute-start.12) | collective-permute-done | bytes 524320 | tf_op jit(solution)/shard_map/ppermute | solution.py:216
  53.8 0.7 collective-permute-done.8.refs_3_
  54.4 3.6 %collective-permute-done.10.refs_4_ = f32[8,128,128]{2,1,0:T(8,128)S(1)} collective-permute-done((f32[8,128,128]{2,1,0:T(8,128)S(1)}, f32[8,128,128]{2,1,0:T(8,128)S(1)}, u32[]{:S(2)}, u32[]{:S(2)}) %collective-permute-start.10) | collective-permute-done | bytes 524320 | tf_op jit(solution)/shard_map/ppermute | solution.py:217
  58.0 1.0 copy-done
  59.1 0.7 copy-done.2
  59.7 0.6 copy-done.3
  60.4 9.7 %shard_map.74.refs_6_ = f32[65,128,128]{2,1,0:T(8,128)S(1)} custom-call(s32[780]{0:T(1024)S(1)} %copy-done.2, s32[3]{0:T(128)S(1)} %copy-done.3, f32[256,128,128]{2,1,0:T(8,128)} %bitcast.15, f32[8,128,128]{2,1,0:T(8,128)S(1)} %bitcast.13, f32[8,128,128]{2,1,0:T(8,128)S(1)} %collective-permute-done.14.refs_4_, ...), custom_call_target="tpu_custom_call" | custom-call | flops 1006632960 | bytes 8388608 | tf_op jit(solution)/shard_map/pallas_call | solution.py:146
  70.1 4.0 %shard_map.75.refs_6_ = f32[65,128,128]{2,1,0:T(8,128)S(1)} custom-call(s32[780]{0:T(1024)S(1)} %copy-done.2, s32[3]{0:T(128)S(1)} %copy-done.3, f32[256,128,128]{2,1,0:T(8,128)} %bitcast.16, f32[8,128,128]{2,1,0:T(8,128)S(1)} %collective-permute-done.8.refs_3_, f32[8,128,128]{2,1,0:T(8,128)S(1)} %collective-permute-done.10.refs_4_, ...), custom_call_target="tpu_custom_call" | custom-call | flops 1006632960 | bytes 8388608 | tf_op jit(solution)/shard_map/pallas_call | solution.py:146
  74.1 3.7 %shard_map.76 = (f32[8,128,128]{2,1,0:T(8,128)S(1)}, f32[8,128,128]{2,1,0:T(8,128)S(1)}, f32[8,128,128]{2,1,0:T(8,128)S(1)}, f32[8,128,128]{2,1,0:T(8,128)S(1)},...) custom-call(s32[780]{0:T(1024)S(1)} %copy-done.2, ...), custom_call_target="tpu_custom_call" | custom-call | flops 1006632960 | bytes 8388608 | tf_op jit(solution)/shard_map/pallas_call | solution.py:146
  77.9 1.0 collective-permute-start.20
  78.9 0.9 collective-permute-start.24
  79.8 2.4 %collective-permute-start.25 = (f32[8,128,128]{2,1,0:T(8,128)S(1)}, f32[8,128,128]{2,1,0:T(8,128)S(1)}, u32[]{:S(2)}, u32[]{:S(2)}) collective-permute-start(f32[8,128,128]{2,1,0:T(8,128)S(1)} %get-tuple-element.28), channel_id=1, source_target_pairs={{16,0},{49,1},{32,16},{1,17},{48,32},{17,33},{0,48},{33,49},{18,2}... | collective-permute-start | bytes 1572872 | tf_op jit(solution)/shard_map/ppermute | solution.py:232
  82.2 10.4 %collective-permute-done.20 = f32[8,128,128]{2,1,0:T(8,128)S(1)} collective-permute-done((f32[8,128,128]{2,1,0:T(8,128)S(1)}, f32[8,128,128]{2,1,0:T(8,128)S(1)}, u32[]{:S(2)}, u32[]{:S(2)}) %collective-permute-start.20) | collective-permute-done | bytes 524320 | tf_op jit(solution)/shard_map/ppermute | solution.py:230
  92.6 0.1 collective-permute-start.21
  92.7 3.2 %collective-permute-start.23 = (f32[8,128,128]{2,1,0:T(8,128)S(1)}, f32[8,128,128]{2,1,0:T(8,128)S(1)}, u32[]{:S(2)}, u32[]{:S(2)}) collective-permute-start(f32[8,128,128]{2,1,0:T(8,128)S(1)} %get-tuple-element.25), channel_id=1, source_target_pairs={{16,0},{49,1},{32,16},{1,17},{48,32},{17,33},{0,48},{33,49},{18,2}... | collective-permute-start | bytes 1572872 | tf_op jit(solution)/shard_map/ppermute | solution.py:234
  95.9 0.1 add_add_fusion
  96.1 0.4 collective-permute-start.26
  96.4 12.0 %collective-permute-done.21 = f32[8,128,128]{2,1,0:T(8,128)S(1)} collective-permute-done((f32[8,128,128]{2,1,0:T(8,128)S(1)}, f32[8,128,128]{2,1,0:T(8,128)S(1)}, u32[]{:S(2)}, u32[]{:S(2)}) %collective-permute-start.21) | collective-permute-done | bytes 524320 | tf_op jit(solution)/shard_map/ppermute | solution.py:233
  108.5 0.1 collective-permute-start.22
  108.6 0.2 collective-permute-done.26.d
  108.8 10.2 %collective-permute-done.22.b = f32[8,128,128]{2,1,0:T(8,128)S(1)} collective-permute-done((f32[8,128,128]{2,1,0:T(8,128)S(1)}, f32[8,128,128]{2,1,0:T(8,128)S(1)}, u32[]{:S(2)}, u32[]{:S(2)}) %collective-permute-start.22) | collective-permute-done | bytes 524320 | tf_op jit(solution)/shard_map/ppermute | solution.py:236
  119.0 1.1 shard_map.77
  (46 shorter events, 0.4 us)
Async XLA Ops:
  0.0 28.6 %collective-permute-start.6 = (f32[8,128,128]{2,1,0:T(8,128)}, f32[8,128,128]{2,1,0:T(8,128)S(1)}, u32[]{:S(2)}, u32[]{:S(2)}) collective-permute-start(f32[8,128,128]{2,1,0:T(8,128)} %bitcast.9), channel_id=1, source_target_pairs={{0,2},{1,7},{2,4},{3,1},{4,6},{5,3},{6,0},{7,5},{8,10},{9,15},{10,... | collective-permute-start | bytes 1572872 | tf_op jit(solution)/shard_map/ppermute | solution.py:178
  1.7 37.0 %collective-permute-start.5 = (f32[8,128,128]{2,1,0:T(8,128)}, f32[8,128,128]{2,1,0:T(8,128)S(1)}, u32[]{:S(2)}, u32[]{:S(2)}) collective-permute-start(f32[8,128,128]{2,1,0:T(8,128)} %bitcast.10), channel_id=1, source_target_pairs={{0,8},{8,0},{1,9},{9,1},{2,10},{10,2},{3,11},{11,3},{4,12},{12,4},... | collective-permute-start | bytes 1572872 | tf_op jit(solution)/shard_map/ppermute | solution.py:180
  5.5 28.5 %collective-permute-start.17 = (f32[8,128,128]{2,1,0:T(8,128)}, f32[8,128,128]{2,1,0:T(8,128)S(1)}, u32[]{:S(2)}, u32[]{:S(2)}) collective-permute-start(f32[8,128,128]{2,1,0:T(8,128)} %bitcast.11), channel_id=1, source_target_pairs={{2,0},{7,1},{4,2},{1,3},{6,4},{3,5},{0,6},{5,7},{10,8},{15,9},{12,... | collective-permute-start | bytes 1572872 | tf_op jit(solution)/shard_map/ppermute | solution.py:179
  7.2 35.0 %collective-permute-start.14 = (f32[8,128,128]{2,1,0:T(8,128)}, f32[8,128,128]{2,1,0:T(8,128)S(1)}, u32[]{:S(2)}, u32[]{:S(2)}) collective-permute-start(f32[8,128,128]{2,1,0:T(8,128)} %bitcast.12), channel_id=1, source_target_pairs={{0,1},{1,0},{2,3},{3,2},{4,5},{5,4},{6,7},{7,6},{8,9},{9,8},{10,11... | collective-permute-start | bytes 1572872 | tf_op jit(solution)/shard_map/ppermute | solution.py:181
  7.2 2.1 %collective-permute-start = (s32[8]{0:T(128)}, s32[8]{0:T(128)S(1)}, u32[]{:S(2)}, u32[]{:S(2)}) collective-permute-start(s32[8]{0:T(128)} %param.8), channel_id=1, source_target_pairs={{0,1},{1,0},{2,3},{3,2},{4,5},{5,4},{6,7},{7,6},{8,9},{9,8},{10,11... | collective-permute-start | bytes 104 | tf_op jit(solution)/shard_map/ppermute | solution.py:183
  10.0 8.3 %collective-permute-start.1 = (s32[16]{0:T(128)S(1)}, s32[16]{0:T(128)S(1)}, u32[]{:S(2)}, u32[]{:S(2)}) collective-permute-start(s32[16]{0:T(128)S(1)} %pad_add_fusion), channel_id=1, source_target_pairs={{0,8},{8,0},{1,9},{9,1},{2,10},{10,2},{3,11},{11,3},{4,12},{12,4},... | collective-permute-start | bytes 200 | tf_op jit(solution)/shard_map/ppermute | solution.py:184
  19.0 16.1 %copy-start.5 = (s32[32]{0:T(128)}, s32[32]{0:T(128)S(1)}, u32[]{:S(2)}) copy-start(s32[32]{0:T(128)S(1)} %pad_add_fusion.1.own) | copy-start | bytes 388
  19.0 4.8 %collective-permute-start.2 = (s32[32]{0:T(128)S(1)}, s32[32]{0:T(128)S(1)}, u32[]{:S(2)}, u32[]{:S(2)}) collective-permute-start(s32[32]{0:T(128)S(1)} %pad_add_fusion.1.own), channel_id=1, source_target_pairs={{0,2},{1,7},{2,4},{3,1},{4,6},{5,3},{6,0},{7,5},{8,10},{9,15},{10,... | collective-permute-start | bytes 392 | tf_op jit(solution)/shard_map/ppermute | solution.py:185
  23.8 11.4 %copy-start.6 = (s32[32]{0:T(128)}, s32[32]{0:T(128)S(1)}, u32[]{:S(2)}) copy-start(s32[32]{0:T(128)S(1)} %collective-permute-done.2.prim) | copy-start | bytes 388
  23.8 4.8 %collective-permute-start.3 = (s32[32]{0:T(128)S(1)}, s32[32]{0:T(128)S(1)}, u32[]{:S(2)}, u32[]{:S(2)}) collective-permute-start(s32[32]{0:T(128)S(1)} %collective-permute-done.2.prim), channel_id=1, source_target_pairs={{0,2},{1,7},{2,4},{3,1},{4,6},{5,3},{6,0},{7,5},{8,10},{9,15},{10,... | collective-permute-start | bytes 392 | tf_op jit(solution)/shard_map/ppermute | solution.py:187
  28.6 6.6 %copy-start.7 = (s32[32]{0:T(128)}, s32[32]{0:T(128)S(1)}, u32[]{:S(2)}) copy-start(s32[32]{0:T(128)S(1)} %collective-permute-done.3.two) | copy-start | bytes 388
  28.6 10.4 %collective-permute-start.7 = (f32[8,128,128]{2,1,0:T(8,128)S(1)}, f32[8,128,128]{2,1,0:T(8,128)S(1)}, u32[]{:S(2)}, u32[]{:S(2)}) collective-permute-start(f32[8,128,128]{2,1,0:T(8,128)S(1)} %collective-permute-done.6.refs_5_), channel_id=1, source_target_pairs={{0,2},{1,7},{2,4},{3,1},{4,6},{5,3},{6,0},{7,5},{8,10},{9,15},{10,... | collective-permute-start | bytes 1572872 | tf_op jit(solution)/shard_map/ppermute | solution.py:212
  29.5 4.5 %collective-permute-start.4 = (s32[32]{0:T(128)S(1)}, s32[32]{0:T(128)S(1)}, u32[]{:S(2)}, u32[]{:S(2)}) collective-permute-start(s32[32]{0:T(128)S(1)} %pad_add_fusion.1.own), channel_id=1, source_target_pairs={{2,0},{7,1},{4,2},{1,3},{6,4},{3,5},{0,6},{5,7},{10,8},{15,9},{12,... | collective-permute-start | bytes 392 | tf_op jit(solution)/shard_map/ppermute | solution.py:186
  34.1 1.1 copy-start.8
  34.1 12.0 %collective-permute-start.15 = (f32[8,128,128]{2,1,0:T(8,128)S(1)}, f32[8,128,128]{2,1,0:T(8,128)S(1)}, u32[]{:S(2)}, u32[]{:S(2)}) collective-permute-start(f32[8,128,128]{2,1,0:T(8,128)S(1)} %collective-permute-done.6.refs_5_), channel_id=1, source_target_pairs={{0,1},{1,0},{2,3},{3,2},{4,5},{5,4},{6,7},{7,6},{8,9},{9,8},{10,11... | collective-permute-start | bytes 1572872 | tf_op jit(solution)/shard_map/ppermute | solution.py:213
  34.1 12.0 %collective-permute-start.18 = (f32[8,128,128]{2,1,0:T(8,128)S(1)}, f32[8,128,128]{2,1,0:T(8,128)}, u32[]{:S(2)}, u32[]{:S(2)}) collective-permute-start(f32[8,128,128]{2,1,0:T(8,128)S(1)} %collective-permute-done.17.refs_9_), channel_id=1, source_target_pairs={{0,1},{1,0},{2,3},{3,2},{4,5},{5,4},{6,7},{7,6},{8,9},{9,8},{10,11... | collective-permute-start | bytes 1572872 | tf_op jit(solution)/shard_map/ppermute | solution.py:213
  39.0 14.8 %collective-permute-start.12 = (f32[8,128,128]{2,1,0:T(8,128)S(1)}, f32[8,128,128]{2,1,0:T(8,128)S(1)}, u32[]{:S(2)}, u32[]{:S(2)}) collective-permute-start(f32[8,128,128]{2,1,0:T(8,128)S(1)} %collective-permute-done.5.refs_11_), channel_id=1, source_target_pairs={{2,0},{7,1},{4,2},{1,3},{6,4},{3,5},{0,6},{5,7},{10,8},{15,9},{12,... | collective-permute-start | bytes 1572872 | tf_op jit(solution)/shard_map/ppermute | solution.py:216
  42.2 12.2 %collective-permute-start.8 = (f32[8,128,128]{2,1,0:T(8,128)S(1)}, f32[8,128,128]{2,1,0:T(8,128)S(1)}, u32[]{:S(2)}, u32[]{:S(2)}) collective-permute-start(f32[8,128,128]{2,1,0:T(8,128)S(1)} %collective-permute-done.5.refs_11_), channel_id=1, source_target_pairs={{0,2},{1,7},{2,4},{3,1},{4,6},{5,3},{6,0},{7,5},{8,10},{9,15},{10,... | collective-permute-start | bytes 1572872 | tf_op jit(solution)/shard_map/ppermute | solution.py:215
  42.2 15.7 %collective-permute-start.10 = (f32[8,128,128]{2,1,0:T(8,128)S(1)}, f32[8,128,128]{2,1,0:T(8,128)S(1)}, u32[]{:S(2)}, u32[]{:S(2)}) collective-permute-start(f32[8,128,128]{2,1,0:T(8,128)S(1)} %collective-permute-done.7.refs_7_), channel_id=1, source_target_pairs={{0,8},{8,0},{1,9},{9,1},{2,10},{10,2},{3,11},{11,3},{4,12},{12,4},... | collective-permute-start | bytes 1572872 | tf_op jit(solution)/shard_map/ppermute | solution.py:217
  46.0 12.0 %collective-permute-start.19 = (f32[8,128,128]{2,1,0:T(8,128)S(1)}, f32[8,128,128]{2,1,0:T(8,128)S(1)}, u32[]{:S(2)}, u32[]{:S(2)}) collective-permute-start(f32[8,128,128]{2,1,0:T(8,128)S(1)} %collective-permute-done.5.refs_11_), channel_id=1, source_target_pairs={{0,1},{1,0},{2,3},{3,2},{4,5},{5,4},{6,7},{7,6},{8,9},{9,8},{10,11... | collective-permute-start | bytes 1572872 | tf_op jit(solution)/shard_map/ppermute | solution.py:213
  46.0 12.0 %collective-permute-start.16 = (f32[8,128,128]{2,1,0:T(8,128)S(1)}, f32[8,128,128]{2,1,0:T(8,128)S(1)}, u32[]{:S(2)}, u32[]{:S(2)}) collective-permute-start(f32[8,128,128]{2,1,0:T(8,128)S(1)} %collective-permute-done.7.refs_7_), channel_id=1, source_target_pairs={{0,1},{1,0},{2,3},{3,2},{4,5},{5,4},{6,7},{7,6},{8,9},{9,8},{10,11... | collective-permute-start | bytes 1572872 | tf_op jit(solution)/shard_map/ppermute | solution.py:218
  53.8 20.4 %collective-permute-start.13 = (f32[8,128,128]{2,1,0:T(8,128)S(1)}, f32[8,128,128]{2,1,0:T(8,128)S(1)}, u32[]{:S(2)}, u32[]{:S(2)}) collective-permute-start(f32[8,128,128]{2,1,0:T(8,128)S(1)} %collective-permute-done.12.refs_5_), channel_id=1, source_target_pairs={{0,1},{1,0},{2,3},{3,2},{4,5},{5,4},{6,7},{7,6},{8,9},{9,8},{10,11... | collective-permute-start | bytes 1572872 | tf_op jit(solution)/shard_map/ppermute | solution.py:220
  54.4 19.7 %collective-permute-start.9 = (f32[8,128,128]{2,1,0:T(8,128)S(1)}, f32[8,128,128]{2,1,0:T(8,128)S(1)}, u32[]{:S(2)}, u32[]{:S(2)}) collective-permute-start(f32[8,128,128]{2,1,0:T(8,128)S(1)} %collective-permute-done.8.refs_3_), channel_id=1, source_target_pairs={{0,1},{1,0},{2,3},{3,2},{4,5},{5,4},{6,7},{7,6},{8,9},{9,8},{10,11... | collective-permute-start | bytes 1572872 | tf_op jit(solution)/shard_map/ppermute | solution.py:220
  58.0 16.1 %collective-permute-start.11 = (f32[8,128,128]{2,1,0:T(8,128)S(1)}, f32[8,128,128]{2,1,0:T(8,128)S(1)}, u32[]{:S(2)}, u32[]{:S(2)}) collective-permute-start(f32[8,128,128]{2,1,0:T(8,128)S(1)} %collective-permute-done.10.refs_4_), channel_id=1, source_target_pairs={{0,1},{1,0},{2,3},{3,2},{4,5},{5,4},{6,7},{7,6},{8,9},{9,8},{10,11... | collective-permute-start | bytes 1572872 | tf_op jit(solution)/shard_map/ppermute | solution.py:220
  58.0 1.0 copy-start
  59.1 0.7 copy-start.2
  59.7 0.6 copy-start.3
  77.9 41.1 %copy-start.1 = (f32[128,128]{1,0:T(8,128)S(1)}, f32[128,128]{1,0:T(8,128)}, u32[]{:S(2)}) copy-start(f32[128,128]{1,0:T(8,128)} %weight.1) | copy-start | bytes 196612
  77.9 41.1 %copy-start.4 = (f32[128]{0:T(128)S(1)}, f32[128]{0:T(128)}, u32[]{:S(2)}) copy-start(f32[128]{0:T(128)} %param.13) | copy-start | bytes 1540
  77.9 14.7 %collective-permute-start.20 = (f32[8,128,128]{2,1,0:T(8,128)S(1)}, f32[8,128,128]{2,1,0:T(8,128)S(1)}, u32[]{:S(2)}, u32[]{:S(2)}) collective-permute-start(f32[8,128,128]{2,1,0:T(8,128)S(1)} %get-tuple-element.24), channel_id=1, source_target_pairs={{0,64},{64,0},{1,65},{65,1},{2,66},{66,2},{3,67},{67,3},{4,68},{68... | collective-permute-start | bytes 1572872 | tf_op jit(solution)/shard_map/ppermute | solution.py:230
  78.9 17.0 %collective-permute-start.24 = (f32[8,128,128]{2,1,0:T(8,128)S(1)}, f32[8,128,128]{2,1,0:T(8,128)S(1)}, u32[]{:S(2)}, u32[]{:S(2)}) collective-permute-start(f32[8,128,128]{2,1,0:T(8,128)S(1)} %get-tuple-element.27), channel_id=1, source_target_pairs={{0,16},{1,49},{16,32},{17,1},{32,48},{33,17},{48,0},{49,33},{2,18}... | collective-permute-start | bytes 1572872 | tf_op jit(solution)/shard_map/ppermute | solution.py:231
  79.8 16.1 %collective-permute-start.25 = (f32[8,128,128]{2,1,0:T(8,128)S(1)}, f32[8,128,128]{2,1,0:T(8,128)S(1)}, u32[]{:S(2)}, u32[]{:S(2)}) collective-permute-start(f32[8,128,128]{2,1,0:T(8,128)S(1)} %get-tuple-element.28), channel_id=1, source_target_pairs={{16,0},{49,1},{32,16},{1,17},{48,32},{17,33},{0,48},{33,49},{18,2}... | collective-permute-start | bytes 1572872 | tf_op jit(solution)/shard_map/ppermute | solution.py:232
  92.6 15.8 %collective-permute-start.21 = (f32[8,128,128]{2,1,0:T(8,128)S(1)}, f32[8,128,128]{2,1,0:T(8,128)S(1)}, u32[]{:S(2)}, u32[]{:S(2)}) collective-permute-start(f32[8,128,128]{2,1,0:T(8,128)S(1)} %add.46), channel_id=1, source_target_pairs={{0,16},{1,49},{16,32},{17,1},{32,48},{33,17},{48,0},{49,33},{2,18}... | collective-permute-start | bytes 1572872 | tf_op jit(solution)/shard_map/ppermute | solution.py:233
  92.7 15.9 %collective-permute-start.23 = (f32[8,128,128]{2,1,0:T(8,128)S(1)}, f32[8,128,128]{2,1,0:T(8,128)S(1)}, u32[]{:S(2)}, u32[]{:S(2)}) collective-permute-start(f32[8,128,128]{2,1,0:T(8,128)S(1)} %get-tuple-element.25), channel_id=1, source_target_pairs={{16,0},{49,1},{32,16},{1,17},{48,32},{17,33},{0,48},{33,49},{18,2}... | collective-permute-start | bytes 1572872 | tf_op jit(solution)/shard_map/ppermute | solution.py:234
  96.1 12.7 %collective-permute-start.26 = (f32[8,128,128]{2,1,0:T(8,128)S(1)}, f32[8,128,128]{2,1,0:T(8,128)S(1)}, u32[]{:S(2)}, u32[]{:S(2)}) collective-permute-start(f32[8,128,128]{2,1,0:T(8,128)S(1)} %add_add_fusion), channel_id=1, source_target_pairs={{0,64},{64,0},{1,65},{65,1},{2,66},{66,2},{3,67},{67,3},{4,68},{68... | collective-permute-start | bytes 1572872 | tf_op jit(solution)/shard_map/ppermute | solution.py:235
  108.5 10.5 %collective-permute-start.22 = (f32[8,128,128]{2,1,0:T(8,128)S(1)}, f32[8,128,128]{2,1,0:T(8,128)S(1)}, u32[]{:S(2)}, u32[]{:S(2)}) collective-permute-start(f32[8,128,128]{2,1,0:T(8,128)S(1)} %add.47), channel_id=1, source_target_pairs={{0,16},{1,49},{16,32},{17,1},{32,48},{33,17},{48,0},{49,33},{2,18}... | collective-permute-start | bytes 1572872 | tf_op jit(solution)/shard_map/ppermute | solution.py:236

commit v3 on v2

v3 whole, which is shorter than its diff:
```python
import functools

import jax
import jax.numpy as jnp
from jax import lax
from jax.experimental import pallas as pl
from jax.experimental.pallas import tpu as pltpu
from jax.sharding import Mesh, PartitionSpec as P

TILE = 128
FEAT = 128
BLOCKS = 8
SLOTS = 16
BUCKETS = 16
TILES = BUCKETS * SLOTS
UNROLL = 4
RING = 16
DUMMY = 64

AXES = ("z_lo", "x", "z_hi", "y", "core")
AHEAD = [(2 * i + c, 2 * ((i + 1 - 2 * c) % 4) + c) for i in range(4) for c in range(2)]
BACK = [(b, a) for a, b in AHEAD]
SWAP = [(0, 1), (1, 0)]

f32, bf16 = jnp.float32, jnp.bfloat16


def live_kernel(packed, words, count):
    def bucket(k, n):
        for t in range(SLOTS):
            word = packed[k * SLOTS + t]
            words[n] = word
            n = n + (word >= 0).astype(jnp.int32)
        return n

    count[0] = lax.fori_loop(0, BUCKETS, bucket, 0)


def split(v):
    hi = v.astype(bf16)
    return hi, (v - hi.astype(f32)).astype(bf16)


def halves(v):
    return jnp.concatenate(split(v), axis=1)


def product(a, right):
    both = jnp.dot(halves(a), jnp.concatenate([right, right], axis=0), preferred_element_type=f32)
    return both[:, :FEAT] + both[:, FEAT:]


def tile_kernel(n_pieces, first, last, *refs):
    words, count, tiles = refs[:3]
    pieces = refs[3 : 3 + n_pieces]
    so_far = None if first else refs[3 + n_pieces]
    outs = refs[4 + n_pieces - first :]
    if last:
        parts, (acc, rest, left) = outs[:BLOCKS], outs[BLOCKS : BLOCKS + 3]
        scratch = outs[BLOCKS + 3 :]
    else:
        acc, rest, left = outs[:3]
        scratch = outs[3:]
    xs, ring, slots, table, mine, ring_sem, slot_sem = scratch
    depth = RING // UNROLL

    reads = [
        pltpu.make_async_copy(piece.at[pl.ds(BLOCKS * TILE, 8)], slots.at[i], slot_sem.at[i])
        for i, piece in enumerate(pieces)
    ]
    for read in reads:
        read.start()
    for p in range(BUCKETS * BLOCKS):
        table[p] = -1
    for read in reads:
        read.wait()
    for i in range(n_pieces):
        for j in range(BLOCKS):
            table[slots[i, 0, j].astype(jnp.int32) & 127] = i * BLOCKS + j

    def sort(at, n):
        here, there = n
        word = words[at]
        s = table[(word >> 8) & 127]
        known = (s >= 0).astype(jnp.int32)
        mine[here] = (word & 0xFF00FF) | (s << 8)
        rest[there] = word
        return here + known, there + 1 - known

    def sort4(group, n):
        for j in range(4):
            n = sort(group * 4 + j, n)
        return n

    total = count[0]
    n = lax.fori_loop(0, total // 4, sort4, (0, 0))
    here, there = lax.fori_loop(total // 4 * 4, total, sort, n)
    left[0] = there
    for j in range(UNROLL):
        mine[here + j] = DUMMY * 65536
    groups = (here + UNROLL - 1) // UNROLL

    def fetch(group, slot):
        for j in range(UNROLL):
            at = mine[group * UNROLL + j] & 255
            pltpu.make_async_copy(tiles.at[at], ring.at[slot, j], ring_sem.at[slot, j]).start()

    def landed(slot):
        for j in range(UNROLL):
            pltpu.make_async_copy(tiles.at[0], ring.at[slot, j], ring_sem.at[slot, j]).wait()

    for s in range(depth - 1):

        @pl.when(s < groups)
        def _(s=s):
            fetch(s, s)

    def halve(j, carry):
        for i, piece in enumerate(pieces):
            xs[i * BLOCKS + j] = halves(piece[pl.ds(pl.multiple_of(j * TILE, TILE), TILE), :])
        return carry

    lax.fori_loop(0, BLOCKS, halve, 0)

    def begin(d, carry):
        acc[d] = jnp.zeros((TILE, FEAT), f32) if first else so_far[d]
        return carry

    lax.fori_loop(0, DUMMY + 1, begin, 0, unroll=5)

    def step(group, carry):
        slot = group % depth
        ahead = group + depth - 1

        @pl.when(ahead < groups)
        def _():
            fetch(ahead, ahead % depth)

        landed(slot)
        own = [mine[group * UNROLL + j] for j in range(UNROLL)]
        results = [product(ring[slot, j], xs[(own[j] >> 8) & 127]) for j in range(UNROLL)]
        for j in range(UNROLL):
            acc[own[j] >> 16] += results[j]
        return carry

    lax.fori_loop(0, groups, step, 0)
    if last:

        def hand_out(j, carry):
            for i, out in enumerate(parts):
                out[j] = acc[i * BLOCKS + j]
            return carry

        lax.fori_loop(0, BLOCKS, hand_out, 0)


def tile_products(words, count, tiles, pieces, so_far=None, last=False):
    first = so_far is None
    smem = pl.BlockSpec(memory_space=pltpu.SMEM)
    vmem = pl.BlockSpec(memory_space=pltpu.VMEM)
    hbm = pl.BlockSpec(memory_space=pltpu.HBM)
    sums = pltpu.VMEM((DUMMY + 1, TILE, FEAT), f32)
    going_on = [pltpu.SMEM((TILES + 8,), jnp.int32), pltpu.SMEM((1,), jnp.int32)]
    part = jax.ShapeDtypeStruct((BLOCKS, TILE, FEAT), f32)
    return pl.pallas_call(
        functools.partial(tile_kernel, len(pieces), first, last),
        out_shape=[part] * BLOCKS
        if last
        else [jax.ShapeDtypeStruct(r.shape, r.dtype) for r in (sums, *going_on)],
        in_specs=[smem, smem, hbm] + [vmem] * (len(pieces) + (not first)),
        out_specs=[vmem] * BLOCKS if last else [vmem, smem, smem],
        scratch_shapes=([sums, *going_on] if last else [])
        + [
            pltpu.VMEM((len(pieces) * BLOCKS, TILE, 2 * FEAT), bf16),
            pltpu.VMEM((RING // UNROLL, UNROLL, TILE, TILE), f32),
            pltpu.SMEM((len(pieces), 8, 128), f32),
            pltpu.SMEM((BUCKETS * BLOCKS,), jnp.int32),
            pltpu.SMEM((TILES + 8,), jnp.int32),
            pltpu.SemaphoreType.DMA((RING // UNROLL, UNROLL)),
            pltpu.SemaphoreType.DMA((len(pieces),)),
        ],
        compiler_params=pltpu.CompilerParams(vmem_limit_bytes=40 * 2**20),
        cost_estimate=pl.CostEstimate(
            flops=2 * TILE * TILE * FEAT * 4 * 60, bytes_accessed=8 * 2**20, transcendentals=0
        ),
    )(words, count, tiles, *pieces, *([] if first else [so_far]))


def finish_kernel(a, b, c, d, weight, bias, out):
    total = a[...] + b[...] + c[...] + d[...]
    hidden = product(total.reshape(BLOCKS * TILE, FEAT), halves(weight[...]))
    out[...] = jnp.maximum(hidden + bias[...], 0.0)


def after(value, *others):
    return lax.optimization_barrier((value, *others))[0]


def body(features, new_slot, tile_values, tile_dest, tile_source, weight, bias_vector):
    move = lax.ppermute
    row = jnp.pad(new_slot.astype(f32)[None, :], ((0, 7), (0, FEAT - BLOCKS)))
    own = jnp.concatenate([features, row])
    prim = move(own, ("y", "core"), AHEAD)
    sec = move(own, ("y", "core"), BACK)
    far = move(own, "z_hi", SWAP)
    other = move(own, "core", SWAP)

    z_lo, x, core = (lax.axis_index(a) for a in ("z_lo", "x", "core"))
    bucket = lax.broadcasted_iota(jnp.int32, (BUCKETS, SLOTS), 0)
    slot = lax.broadcasted_iota(jnp.int32, (BUCKETS, SLOTS), 1)
    dest = tile_dest.reshape(BUCKETS, SLOTS)
    group = dest >> 3
    turned = (((group >> 2) ^ z_lo) * 4 + (((group & 3) - x) * (1 - 2 * core) & 3)) * BLOCKS + (dest & 7)
    position = bucket * BLOCKS + tile_source.reshape(BUCKETS, SLOTS)
    packed = jnp.where(dest >= 0, (bucket * SLOTS + slot) + position * 256 + turned * 65536, -1)

    smem = pl.BlockSpec(memory_space=pltpu.SMEM)
    words, count = pl.pallas_call(
        live_kernel,
        out_shape=[
            jax.ShapeDtypeStruct((TILES + 8,), jnp.int32),
            jax.ShapeDtypeStruct((1,), jnp.int32),
        ],
        in_specs=[smem],
        out_specs=[smem] * 2,
        cost_estimate=pl.CostEstimate(flops=10**7, bytes_accessed=10**4, transcendentals=0),
    )(packed.reshape(TILES))

    prim = after(prim, words)
    two = move(prim, ("y", "core"), AHEAD)
    prim_other, sec_other, far_other = [move(p, "core", SWAP) for p in (prim, sec, far)]
    far_now = after(far, two)
    far_prim = move(far_now, ("y", "core"), AHEAD)
    far_sec = move(far_now, ("y", "core"), BACK)
    far_two = move(two, "z_hi", SWAP)
    two_other = move(two, "core", SWAP)

    tiles = tile_values.reshape(TILES, TILE, TILE)
    near = [own, other, prim, prim_other, two, two_other, sec, sec_other, far, far_other]
    sums, words, count = tile_products(words, count, tiles, near)
    second = [after(p, sums) for p in (far_prim, far_sec, far_two)]
    third = [move(p, "core", SWAP) for p in second]
    sums, words, count = tile_products(words, count, tiles, second, sums)
    mine, prim, two, sec, z_mine, z_prim, z_two, z_sec = tile_products(
        words, count, tiles, third, sums, last=True
    )

    got_two = move(z_two, "z_lo", SWAP)
    got_prim = move(z_prim, ("x", "core"), AHEAD)
    got_sec = move(z_sec, ("x", "core"), BACK)
    got = move(two + got_two, ("x", "core"), AHEAD)
    end_sec = move(after(sec, got), ("x", "core"), BACK)
    end_z = move(z_mine + got_prim + got_sec, "z_lo", SWAP)
    end_prim = move(prim + got, ("x", "core"), AHEAD)

    return pl.pallas_call(
        finish_kernel,
        out_shape=jax.ShapeDtypeStruct((BLOCKS * TILE, FEAT), f32),
        compiler_params=pltpu.CompilerParams(vmem_limit_bytes=24 * 2**20),
    )(mine, end_prim, end_sec, end_z, weight, bias_vector.reshape(1, FEAT))


def solution(mesh):
    fine = Mesh(mesh.devices.reshape(2, 4, 2, 4, 2), AXES)
    grp, blk = AXES[:2], AXES[2:]
    return jax.shard_map(
        body,
        mesh=fine,
        in_specs=(
            P(AXES, None),
            P(AXES),
            P(grp, blk, None, None, None, None),
            P(grp, blk, None, None),
            P(grp, blk, None, None),
            P(),
            P(),
        ),
        out_specs=P(AXES, None),
        check_vma=False,
    )
```

time: 121 us -> 101 us (0.83)
  waiting for transfers between devices: 63.4 us -> 34.4 us
  starting transfers between devices: 27.1 us -> 34 us
  Pallas kernels: 22.1 us -> 25.6 us
  local copies, waits for them, and re-layouts: 3.55 us -> 1.88 us
    ppermute x8 -> x3, waiting for transfers between devices: 26.8 us -> 8.31 us  [the longest x1 7.87 us: body(): end_sec = move(after(sec, got), ('x', 'core'), BACK)]
    ppermute x1, waiting for transfers between devices: 10.2 us -> 0.01 us  [body(): end_prim = move(prim + got, ('x', 'core'), AHEAD)]
    ppermute x8 -> x3, starting transfers between devices: 10.3 us -> 4.05 us  [the longest x1 2.02 us: body(): end_sec = move(after(sec, got), ('x', 'core'), BACK)]
    ppermute x1, waiting for transfers between devices: 12 us -> 5.97 us  [body(): got = move(two + got_two, ('x', 'core'), AHEAD)]
    ppermute x1, starting transfers between devices: 0.07 us -> 4.94 us  [body(): got = move(two + got_two, ('x', 'core'), AHEAD)]
    ppermute x1, waiting for transfers between devices: 0.25 us -> 4.26 us  [body(): two = move(prim, ('y', 'core'), AHEAD)]
    ppermute x1, waiting for transfers between devices: 0.01 us -> 3.93 us  [body(): far = move(own, 'z_hi', SWAP)]
    ppermute x1, waiting for transfers between devices: 0.21 us -> 4.09 us  [body(): end_z = move(z_mine + got_prim + got_sec, 'z_lo', SWAP)]
  transfers between devices with their start and end apart: 27 -> 22, of which waited for: 13 -> 7; matrix products, arithmetic and copies ran while one was open for 4% -> 3% of each run, Pallas kernels for 14% -> 19%
where the time goes in v3:
time: 101 us; the launch traced here: 100 us
  waiting for transfers between devices  34.4 us (34%)
  starting transfers between devices  34 us (34%)
  Pallas kernels  25.6 us (25%)
  other arithmetic  4.04 us (4%)
  local copies, waits for them, and re-layouts  1.88 us (2%)
    pallas_call x3, Pallas kernels, tile_products(): pl.pallas_call(functools.partial(tile_kernel, len(pieces), first, last),...  22.6 us
    ppermute x1, waiting for transfers between devices, body(): end_sec = move(after(sec, got), ('x', 'core'), BACK)  7.87 us
    ppermute x1, waiting for transfers between devices, body(): got_two = move(z_two, 'z_lo', SWAP)  7.79 us
    ppermute x1, waiting for transfers between devices, body(): got = move(two + got_two, ('x', 'core'), AHEAD)  5.97 us
    ppermute x1, starting transfers between devices, body(): far_two = move(two, 'z_hi', SWAP)  5.95 us
    ppermute x1, starting transfers between devices, body(): got = move(two + got_two, ('x', 'core'), AHEAD)  4.94 us
    ppermute x1, waiting for transfers between devices, body(): two = move(prim, ('y', 'core'), AHEAD)  4.26 us
    ppermute x1, waiting for transfers between devices, body(): end_z = move(z_mine + got_prim + got_sec, 'z_lo', SWAP)  4.09 us
  transfers between devices with their start and end apart: 22, of which 7 were waited for; matrix products, arithmetic and copies ran while one was open for 3% of the time, Pallas kernels for 19%

profile of v3, /device:TPU:0, one launch (start us, length us, event | category | flops | bytes accessed | tf_op | source)
XLA Modules:
  0.0 100.0 jit_solution(543871077893696166)
XLA Ops:
  0.0 0.7 convert_bitcast_fusion
  0.7 1.1 %select_maximum_fusion.refs_3_ = f32[1032,128]{1,0:T(8,128)S(1)} fusion(f32[1,8]{1,0:T(1,128)S(1)} %convert_bitcast_fusion, f32[1024,128]{1,0:T(8,128)} %param.7), kind=kLoop, calls=%fused_computation | loop fusion | flops 396288 | bytes 1052704 | tf_op jit(solution)/shard_map/concatenate | solution.py:202
  1.7 1.7 %collective-permute-start.1 = (f32[1032,128]{1,0:T(8,128)S(1)}, f32[1032,128]{1,0:T(8,128)S(1)}, u32[]{:S(2)}, u32[]{:S(2)}) collective-permute-start(f32[1032,128]{1,0:T(8,128)S(1)} %select_maximum_fusion.refs_3_), channel_id=1, source_target_pairs={{0,2},{1,7},{2,4},{3,1},{4,6},{5,3},{6,0},{7,5},{8,10},{9,15},{10,... | collective-permute-start | bytes 1585160 | tf_op jit(solution)/shard_map/ppermute | solution.py:203
  3.5 3.9 %collective-permute-start.7 = (f32[1032,128]{1,0:T(8,128)S(1)}, f32[1032,128]{1,0:T(8,128)S(1)}, u32[]{:S(2)}, u32[]{:S(2)}) collective-permute-start(f32[1032,128]{1,0:T(8,128)S(1)} %select_maximum_fusion.refs_3_), channel_id=1, source_target_pairs={{0,8},{8,0},{1,9},{9,1},{2,10},{10,2},{3,11},{11,3},{4,12},{12,4},... | collective-permute-start | bytes 1585160 | tf_op jit(solution)/shard_map/ppermute | solution.py:205
  7.3 1.7 %collective-permute-start.5 = (f32[1032,128]{1,0:T(8,128)S(1)}, f32[1032,128]{1,0:T(8,128)S(1)}, u32[]{:S(2)}, u32[]{:S(2)}) collective-permute-start(f32[1032,128]{1,0:T(8,128)S(1)} %select_maximum_fusion.refs_3_), channel_id=1, source_target_pairs={{2,0},{7,1},{4,2},{1,3},{6,4},{3,5},{0,6},{5,7},{10,8},{15,9},{12,... | collective-permute-start | bytes 1585160 | tf_op jit(solution)/shard_map/ppermute | solution.py:204
  9.0 0.7 add_multiply_fusion
  9.7 0.1 reshape.45
  9.8 0.1 iota_add_fusion
  9.9 0.1 add.42
  10.0 0.1 iota.23
  10.0 0.1 iota.24
  10.1 0.7 broadcast_compare_fusion
  10.8 0.1 ge.12
  10.9 0.8 reshape.35
  11.7 0.6 add_select_fusion.packed
  12.3 1.9 %shard_map.73 = (s32[264]{0:T(512)}, s32[1]{0:T(128)}) custom-call(s32[256]{0:T(256)} %add_select_fusion.packed), custom_call_target="tpu_custom_call" | custom-call | flops 10000000 | bytes 10000 | tf_op jit(solution)/shard_map/pallas_call | solution.py:218
  14.2 0.6 collective-permute-start.3
  14.7 1.2 %collective-permute-start = (f32[1032,128]{1,0:T(8,128)S(1)}, f32[1032,128]{1,0:T(8,128)S(1)}, u32[]{:S(2)}, u32[]{:S(2)}) collective-permute-start(f32[1032,128]{1,0:T(8,128)S(1)} %select_maximum_fusion.refs_3_), channel_id=1, source_target_pairs={{0,1},{1,0},{2,3},{3,2},{4,5},{5,4},{6,7},{7,6},{8,9},{9,8},{10,11... | collective-permute-start | bytes 1585160 | tf_op jit(solution)/shard_map/ppermute | solution.py:206
  16.0 3.9 %collective-permute-done.7.refs_11_ = f32[1032,128]{1,0:T(8,128)S(1)} collective-permute-done((f32[1032,128]{1,0:T(8,128)S(1)}, f32[1032,128]{1,0:T(8,128)S(1)}, u32[]{:S(2)}, u32[]{:S(2)}) %collective-permute-start.7) | collective-permute-done | bytes 528416 | tf_op jit(solution)/shard_map/ppermute | solution.py:205
  19.9 0.1 collective-permute-start.8
  20.0 0.4 collective-permute-start.6
  20.4 4.3 %collective-permute-done.3.refs_7_ = f32[1032,128]{1,0:T(8,128)S(1)} collective-permute-done((f32[1032,128]{1,0:T(8,128)S(1)}, f32[1032,128]{1,0:T(8,128)S(1)}, u32[]{:S(2)}, u32[]{:S(2)}) %collective-permute-start.3) | collective-permute-done | bytes 528416 | tf_op jit(solution)/shard_map/ppermute | solution.py:230
  24.7 6.0 %collective-permute-start.11 = (f32[1032,128]{1,0:T(8,128)S(1)}, f32[1032,128]{1,0:T(8,128)S(1)}, u32[]{:S(2)}, u32[]{:S(2)}) collective-permute-start(f32[1032,128]{1,0:T(8,128)S(1)} %collective-permute-done.3.refs_7_), channel_id=1, source_target_pairs={{0,8},{8,0},{1,9},{9,1},{2,10},{10,2},{3,11},{11,3},{4,12},{12,4},... | collective-permute-start | bytes 1585160 | tf_op jit(solution)/shard_map/ppermute | solution.py:235
  30.6 1.6 %collective-permute-start.10 = (f32[1032,128]{1,0:T(8,128)S(1)}, f32[1032,128]{1,0:T(8,128)S(1)}, u32[]{:S(2)}, u32[]{:S(2)}) collective-permute-start(f32[1032,128]{1,0:T(8,128)S(1)} %collective-permute-done.7.refs_11_), channel_id=1, source_target_pairs={{2,0},{7,1},{4,2},{1,3},{6,4},{3,5},{0,6},{5,7},{10,8},{15,9},{12,... | collective-permute-start | bytes 1585160 | tf_op jit(solution)/shard_map/ppermute | solution.py:234
  32.2 0.4 collective-permute-start.9
  32.7 0.7 copy-done.1
  33.4 12.2 %shard_map.74 = (f32[65,128,128]{2,1,0:T(8,128)S(1)}, s32[264]{0:T(512)S(1)}, s32[1]{0:T(128)}) custom-call(s32[264]{0:T(512)S(1)} %copy-done.1, s32[1]{0:T(128)} %get-tuple-element.28.refs_1_, f32[256,128,128]{2,1,0:T(8,128)} %bitcast.11, f32[1032,128]{1,0:T(8,128)S(1)} %select_maximum_fusion.refs_3_, f32[1032,128]{1,0:T(8,128)S(1)} %collective-permute-done.refs_4_, ...), custom_call_target="tpu_custom_call" | custom-call | flops 1006632960 | bytes 8388608 | tf_op jit(solution)/shard_map/pallas_call | solution.py:165
  45.6 0.4 collective-permute-done.9.refs_3_
  46.0 0.5 collective-permute-start.13
  46.5 0.0 collective-permute-start.12
  46.5 5.1 %shard_map.75 = (f32[65,128,128]{2,1,0:T(8,128)S(1)}, s32[264]{0:T(512)S(1)}, s32[1]{0:T(128)}) custom-call(s32[264]{0:T(512)S(1)} %get-tuple-element.30.refs_0_, s32[1]{0:T(128)} %get-tuple-element.31.refs_1_, f32[256,128,128]{2,1,0:T(8,128)} %bitcast.12, f32[1032,128]{1,0:T(8,128)S(1)} %collective-permute-done.9.refs_3_, ...), custom_call_target="tpu_custom_call" | custom-call | flops 1006632960 | bytes 8388608 | tf_op jit(solution)/shard_map/pallas_call | solution.py:165
  51.6 5.3 %shard_map.76 = (f32[8,128,128]{2,1,0:T(8,128)S(1)}, f32[8,128,128]{2,1,0:T(8,128)S(1)}, f32[8,128,128]{2,1,0:T(8,128)S(1)}, f32[8,128,128]{2,1,0:T(8,128)S(1)},...) custom-call(s32[264]{0:T(512)S(1)} %get-tuple-element.37.refs_0_, ...), custom_call_target="tpu_custom_call" | custom-call | flops 1006632960 | bytes 8388608 | tf_op jit(solution)/shard_map/pallas_call | solution.py:165
  56.9 0.0 copy-start
  57.0 0.0 copy-start.2
  57.0 3.4 %collective-permute-start.15 = (f32[8,128,128]{2,1,0:T(8,128)S(1)}, f32[8,128,128]{2,1,0:T(8,128)S(1)}, u32[]{:S(2)}, u32[]{:S(2)}) collective-permute-start(f32[8,128,128]{2,1,0:T(8,128)S(1)} %get-tuple-element.43), channel_id=1, source_target_pairs={{0,64},{64,0},{1,65},{65,1},{2,66},{66,2},{3,67},{67,3},{4,68},{68... | collective-permute-start | bytes 1572872 | tf_op jit(solution)/shard_map/ppermute | solution.py:248
  60.3 3.5 %collective-permute-start.19 = (f32[8,128,128]{2,1,0:T(8,128)S(1)}, f32[8,128,128]{2,1,0:T(8,128)S(1)}, u32[]{:S(2)}, u32[]{:S(2)}) collective-permute-start(f32[8,128,128]{2,1,0:T(8,128)S(1)} %get-tuple-element.47), channel_id=1, source_target_pairs={{0,16},{1,49},{16,32},{17,1},{32,48},{33,17},{48,0},{49,33},{2,18}... | collective-permute-start | bytes 1572872 | tf_op jit(solution)/shard_map/ppermute | solution.py:249
  63.9 7.8 %collective-permute-done.15 = f32[8,128,128]{2,1,0:T(8,128)S(1)} collective-permute-done((f32[8,128,128]{2,1,0:T(8,128)S(1)}, f32[8,128,128]{2,1,0:T(8,128)S(1)}, u32[]{:S(2)}, u32[]{:S(2)}) %collective-permute-start.15) | collective-permute-done | bytes 524320 | tf_op jit(solution)/shard_map/ppermute | solution.py:248
  71.6 0.1 add.48
  71.7 4.9 %collective-permute-start.16 = (f32[8,128,128]{2,1,0:T(8,128)S(1)}, f32[8,128,128]{2,1,0:T(8,128)S(1)}, u32[]{:S(2)}, u32[]{:S(2)}) collective-permute-start(f32[8,128,128]{2,1,0:T(8,128)S(1)} %add.48), channel_id=1, source_target_pairs={{0,16},{1,49},{16,32},{17,1},{32,48},{33,17},{48,0},{49,33},{2,18}... | collective-permute-start | bytes 1572872 | tf_op jit(solution)/shard_map/ppermute | solution.py:251
  76.7 0.1 add_add_fusion
  76.8 2.0 %collective-permute-start.21 = (f32[8,128,128]{2,1,0:T(8,128)S(1)}, f32[8,128,128]{2,1,0:T(8,128)S(1)}, u32[]{:S(2)}, u32[]{:S(2)}) collective-permute-start(f32[8,128,128]{2,1,0:T(8,128)S(1)} %add_add_fusion), channel_id=1, source_target_pairs={{0,64},{64,0},{1,65},{65,1},{2,66},{66,2},{3,67},{67,3},{4,68},{68... | collective-permute-start | bytes 1572872 | tf_op jit(solution)/shard_map/ppermute | solution.py:253
  78.8 6.0 %collective-permute-done.16 = f32[8,128,128]{2,1,0:T(8,128)S(1)} collective-permute-done((f32[8,128,128]{2,1,0:T(8,128)S(1)}, f32[8,128,128]{2,1,0:T(8,128)S(1)}, u32[]{:S(2)}, u32[]{:S(2)}) %collective-permute-start.16) | collective-permute-done | bytes 524320 | tf_op jit(solution)/shard_map/ppermute | solution.py:251
  84.8 2.0 %collective-permute-start.18 = (f32[8,128,128]{2,1,0:T(8,128)S(1)}, f32[8,128,128]{2,1,0:T(8,128)S(1)}, u32[]{:S(2)}, u32[]{:S(2)}) collective-permute-start(f32[8,128,128]{2,1,0:T(8,128)S(1)} %get-tuple-element.45), channel_id=1, source_target_pairs={{16,0},{49,1},{32,16},{1,17},{48,32},{17,33},{0,48},{33,49},{18,2}... | collective-permute-start | bytes 1572872 | tf_op jit(solution)/shard_map/ppermute | solution.py:252
  86.8 0.1 add.49
  86.8 0.1 collective-permute-start.17
  86.9 4.1 %collective-permute-done.21.d = f32[8,128,128]{2,1,0:T(8,128)S(1)} collective-permute-done((f32[8,128,128]{2,1,0:T(8,128)S(1)}, f32[8,128,128]{2,1,0:T(8,128)S(1)}, u32[]{:S(2)}, u32[]{:S(2)}) %collective-permute-start.21) | collective-permute-done | bytes 524320 | tf_op jit(solution)/shard_map/ppermute | solution.py:253
  91.0 7.9 %collective-permute-done.18.c = f32[8,128,128]{2,1,0:T(8,128)S(1)} collective-permute-done((f32[8,128,128]{2,1,0:T(8,128)S(1)}, f32[8,128,128]{2,1,0:T(8,128)S(1)}, u32[]{:S(2)}, u32[]{:S(2)}) %collective-permute-start.18) | collective-permute-done | bytes 524320 | tf_op jit(solution)/shard_map/ppermute | solution.py:252
  98.9 1.1 %shard_map.77 = f32[1024,128]{1,0:T(8,128)} custom-call(f32[8,128,128]{2,1,0:T(8,128)S(1)} %get-tuple-element.40.a, f32[8,128,128]{2,1,0:T(8,128)S(1)} %collective-permute-done.17.b, f32[8,128,128]{2,1,0:T(8,128)S(1)} %collective-permute-done.18.c, f32[8,128,128]{2,1,0:T(8,128)S(1)} %collective-permute-done.21.d, f32[128,128]{1,0:T(8,128)S(1)} %copy-done, ...), custom_call_target="tpu_custom_call" | custom-call | tf_op jit(solution)/shard_map/pallas_call | solution.py:256
  (24 shorter events, 0.1 us)
Async XLA Ops:
  1.7 12.4 %collective-permute-start.1 = (f32[1032,128]{1,0:T(8,128)S(1)}, f32[1032,128]{1,0:T(8,128)S(1)}, u32[]{:S(2)}, u32[]{:S(2)}) collective-permute-start(f32[1032,128]{1,0:T(8,128)S(1)} %select_maximum_fusion.refs_3_), channel_id=1, source_target_pairs={{0,2},{1,7},{2,4},{3,1},{4,6},{5,3},{6,0},{7,5},{8,10},{9,15},{10,... | collective-permute-start | bytes 1585160 | tf_op jit(solution)/shard_map/ppermute | solution.py:203
  3.5 16.4 %collective-permute-start.7 = (f32[1032,128]{1,0:T(8,128)S(1)}, f32[1032,128]{1,0:T(8,128)S(1)}, u32[]{:S(2)}, u32[]{:S(2)}) collective-permute-start(f32[1032,128]{1,0:T(8,128)S(1)} %select_maximum_fusion.refs_3_), channel_id=1, source_target_pairs={{0,8},{8,0},{1,9},{9,1},{2,10},{10,2},{3,11},{11,3},{4,12},{12,4},... | collective-permute-start | bytes 1585160 | tf_op jit(solution)/shard_map/ppermute | solution.py:205
  7.3 12.7 %collective-permute-start.5 = (f32[1032,128]{1,0:T(8,128)S(1)}, f32[1032,128]{1,0:T(8,128)S(1)}, u32[]{:S(2)}, u32[]{:S(2)}) collective-permute-start(f32[1032,128]{1,0:T(8,128)S(1)} %select_maximum_fusion.refs_3_), channel_id=1, source_target_pairs={{2,0},{7,1},{4,2},{1,3},{6,4},{3,5},{0,6},{5,7},{10,8},{15,9},{12,... | collective-permute-start | bytes 1585160 | tf_op jit(solution)/shard_map/ppermute | solution.py:204
  14.2 10.5 %collective-permute-start.3 = (f32[1032,128]{1,0:T(8,128)S(1)}, f32[1032,128]{1,0:T(8,128)S(1)}, u32[]{:S(2)}, u32[]{:S(2)}) collective-permute-start(f32[1032,128]{1,0:T(8,128)S(1)} %collective-permute-done.1.refs_5_), channel_id=1, source_target_pairs={{0,2},{1,7},{2,4},{3,1},{4,6},{5,3},{6,0},{7,5},{8,10},{9,15},{10,... | collective-permute-start | bytes 1585160 | tf_op jit(solution)/shard_map/ppermute | solution.py:230
  14.7 9.9 %collective-permute-start = (f32[1032,128]{1,0:T(8,128)S(1)}, f32[1032,128]{1,0:T(8,128)S(1)}, u32[]{:S(2)}, u32[]{:S(2)}) collective-permute-start(f32[1032,128]{1,0:T(8,128)S(1)} %select_maximum_fusion.refs_3_), channel_id=1, source_target_pairs={{0,1},{1,0},{2,3},{3,2},{4,5},{5,4},{6,7},{7,6},{8,9},{9,8},{10,11... | collective-permute-start | bytes 1585160 | tf_op jit(solution)/shard_map/ppermute | solution.py:206
  16.0 14.7 %collective-permute-start.2 = (f32[1032,128]{1,0:T(8,128)S(1)}, f32[1032,128]{1,0:T(8,128)S(1)}, u32[]{:S(2)}, u32[]{:S(2)}) collective-permute-start(f32[1032,128]{1,0:T(8,128)S(1)} %collective-permute-done.1.refs_5_), channel_id=1, source_target_pairs={{0,1},{1,0},{2,3},{3,2},{4,5},{5,4},{6,7},{7,6},{8,9},{9,8},{10,11... | collective-permute-start | bytes 1585160 | tf_op jit(solution)/shard_map/ppermute | solution.py:231
  19.9 12.3 %collective-permute-start.8 = (f32[1032,128]{1,0:T(8,128)S(1)}, f32[1032,128]{1,0:T(8,128)S(1)}, u32[]{:S(2)}, u32[]{:S(2)}) collective-permute-start(f32[1032,128]{1,0:T(8,128)S(1)} %collective-permute-done.7.refs_11_), channel_id=1, source_target_pairs={{0,1},{1,0},{2,3},{3,2},{4,5},{5,4},{6,7},{7,6},{8,9},{9,8},{10,11... | collective-permute-start | bytes 1585160 | tf_op jit(solution)/shard_map/ppermute | solution.py:231
  20.0 12.6 %collective-permute-start.6 = (f32[1032,128]{1,0:T(8,128)S(1)}, f32[1032,128]{1,0:T(8,128)S(1)}, u32[]{:S(2)}, u32[]{:S(2)}) collective-permute-start(f32[1032,128]{1,0:T(8,128)S(1)} %collective-permute-done.5.refs_9_), channel_id=1, source_target_pairs={{0,1},{1,0},{2,3},{3,2},{4,5},{5,4},{6,7},{7,6},{8,9},{9,8},{10,11... | collective-permute-start | bytes 1585160 | tf_op jit(solution)/shard_map/ppermute | solution.py:231
  24.7 8.0 %collective-permute-start.4 = (f32[1032,128]{1,0:T(8,128)S(1)}, f32[1032,128]{1,0:T(8,128)S(1)}, u32[]{:S(2)}, u32[]{:S(2)}) collective-permute-start(f32[1032,128]{1,0:T(8,128)S(1)} %collective-permute-done.3.refs_7_), channel_id=1, source_target_pairs={{0,1},{1,0},{2,3},{3,2},{4,5},{5,4},{6,7},{7,6},{8,9},{9,8},{10,11... | collective-permute-start | bytes 1585160 | tf_op jit(solution)/shard_map/ppermute | solution.py:236
  24.7 20.9 %collective-permute-start.11 = (f32[1032,128]{1,0:T(8,128)S(1)}, f32[1032,128]{1,0:T(8,128)S(1)}, u32[]{:S(2)}, u32[]{:S(2)}) collective-permute-start(f32[1032,128]{1,0:T(8,128)S(1)} %collective-permute-done.3.refs_7_), channel_id=1, source_target_pairs={{0,8},{8,0},{1,9},{9,1},{2,10},{10,2},{3,11},{11,3},{4,12},{12,4},... | collective-permute-start | bytes 1585160 | tf_op jit(solution)/shard_map/ppermute | solution.py:235
  30.6 14.9 %collective-permute-start.10 = (f32[1032,128]{1,0:T(8,128)S(1)}, f32[1032,128]{1,0:T(8,128)S(1)}, u32[]{:S(2)}, u32[]{:S(2)}) collective-permute-start(f32[1032,128]{1,0:T(8,128)S(1)} %collective-permute-done.7.refs_11_), channel_id=1, source_target_pairs={{2,0},{7,1},{4,2},{1,3},{6,4},{3,5},{0,6},{5,7},{10,8},{15,9},{12,... | collective-permute-start | bytes 1585160 | tf_op jit(solution)/shard_map/ppermute | solution.py:234
  32.2 13.8 %collective-permute-start.9 = (f32[1032,128]{1,0:T(8,128)S(1)}, f32[1032,128]{1,0:T(8,128)S(1)}, u32[]{:S(2)}, u32[]{:S(2)}) collective-permute-start(f32[1032,128]{1,0:T(8,128)S(1)} %collective-permute-done.7.refs_11_), channel_id=1, source_target_pairs={{0,2},{1,7},{2,4},{3,1},{4,6},{5,3},{6,0},{7,5},{8,10},{9,15},{10,... | collective-permute-start | bytes 1585160 | tf_op jit(solution)/shard_map/ppermute | solution.py:233
  32.7 0.7 copy-start.1
  46.0 5.6 %collective-permute-start.14 = (f32[1032,128]{1,0:T(8,128)S(1)}, f32[1032,128]{1,0:T(8,128)S(1)}, u32[]{:S(2)}, u32[]{:S(2)}) collective-permute-start(f32[1032,128]{1,0:T(8,128)S(1)} %collective-permute-done.11.refs_5_), channel_id=1, source_target_pairs={{0,1},{1,0},{2,3},{3,2},{4,5},{5,4},{6,7},{7,6},{8,9},{9,8},{10,11... | collective-permute-start | bytes 1585160 | tf_op jit(solution)/shard_map/ppermute | solution.py:242
  46.0 5.6 %collective-permute-start.13 = (f32[1032,128]{1,0:T(8,128)S(1)}, f32[1032,128]{1,0:T(8,128)S(1)}, u32[]{:S(2)}, u32[]{:S(2)}) collective-permute-start(f32[1032,128]{1,0:T(8,128)S(1)} %collective-permute-done.10.refs_4_), channel_id=1, source_target_pairs={{0,1},{1,0},{2,3},{3,2},{4,5},{5,4},{6,7},{7,6},{8,9},{9,8},{10,11... | collective-permute-start | bytes 1585160 | tf_op jit(solution)/shard_map/ppermute | solution.py:242
  46.5 5.1 %collective-permute-start.12 = (f32[1032,128]{1,0:T(8,128)S(1)}, f32[1032,128]{1,0:T(8,128)S(1)}, u32[]{:S(2)}, u32[]{:S(2)}) collective-permute-start(f32[1032,128]{1,0:T(8,128)S(1)} %collective-permute-done.9.refs_3_), channel_id=1, source_target_pairs={{0,1},{1,0},{2,3},{3,2},{4,5},{5,4},{6,7},{7,6},{8,9},{9,8},{10,11... | collective-permute-start | bytes 1585160 | tf_op jit(solution)/shard_map/ppermute | solution.py:242
  56.9 42.0 %copy-start = (f32[128,128]{1,0:T(8,128)S(1)}, f32[128,128]{1,0:T(8,128)}, u32[]{:S(2)}) copy-start(f32[128,128]{1,0:T(8,128)} %weight.1) | copy-start | bytes 196612
  57.0 41.9 %copy-start.2 = (f32[128]{0:T(128)S(1)}, f32[128]{0:T(128)}, u32[]{:S(2)}) copy-start(f32[128]{0:T(128)} %param.13) | copy-start | bytes 1540
  57.0 14.7 %collective-permute-start.15 = (f32[8,128,128]{2,1,0:T(8,128)S(1)}, f32[8,128,128]{2,1,0:T(8,128)S(1)}, u32[]{:S(2)}, u32[]{:S(2)}) collective-permute-start(f32[8,128,128]{2,1,0:T(8,128)S(1)} %get-tuple-element.43), channel_id=1, source_target_pairs={{0,64},{64,0},{1,65},{65,1},{2,66},{66,2},{3,67},{67,3},{4,68},{68... | collective-permute-start | bytes 1572872 | tf_op jit(solution)/shard_map/ppermute | solution.py:248
  60.3 16.3 %collective-permute-start.19 = (f32[8,128,128]{2,1,0:T(8,128)S(1)}, f32[8,128,128]{2,1,0:T(8,128)S(1)}, u32[]{:S(2)}, u32[]{:S(2)}) collective-permute-start(f32[8,128,128]{2,1,0:T(8,128)S(1)} %get-tuple-element.47), channel_id=1, source_target_pairs={{0,16},{1,49},{16,32},{17,1},{32,48},{33,17},{48,0},{49,33},{2,18}... | collective-permute-start | bytes 1572872 | tf_op jit(solution)/shard_map/ppermute | solution.py:249
  63.9 12.8 %collective-permute-start.20 = (f32[8,128,128]{2,1,0:T(8,128)S(1)}, f32[8,128,128]{2,1,0:T(8,128)S(1)}, u32[]{:S(2)}, u32[]{:S(2)}) collective-permute-start(f32[8,128,128]{2,1,0:T(8,128)S(1)} %get-tuple-element.48), channel_id=1, source_target_pairs={{16,0},{49,1},{32,16},{1,17},{48,32},{17,33},{0,48},{33,49},{18,2}... | collective-permute-start | bytes 1572872 | tf_op jit(solution)/shard_map/ppermute | solution.py:250
  71.7 13.1 %collective-permute-start.16 = (f32[8,128,128]{2,1,0:T(8,128)S(1)}, f32[8,128,128]{2,1,0:T(8,128)S(1)}, u32[]{:S(2)}, u32[]{:S(2)}) collective-permute-start(f32[8,128,128]{2,1,0:T(8,128)S(1)} %add.48), channel_id=1, source_target_pairs={{0,16},{1,49},{16,32},{17,1},{32,48},{33,17},{48,0},{49,33},{2,18}... | collective-permute-start | bytes 1572872 | tf_op jit(solution)/shard_map/ppermute | solution.py:251
  76.8 14.3 %collective-permute-start.21 = (f32[8,128,128]{2,1,0:T(8,128)S(1)}, f32[8,128,128]{2,1,0:T(8,128)S(1)}, u32[]{:S(2)}, u32[]{:S(2)}) collective-permute-start(f32[8,128,128]{2,1,0:T(8,128)S(1)} %add_add_fusion), channel_id=1, source_target_pairs={{0,64},{64,0},{1,65},{65,1},{2,66},{66,2},{3,67},{67,3},{4,68},{68... | collective-permute-start | bytes 1572872 | tf_op jit(solution)/shard_map/ppermute | solution.py:253
  84.8 14.1 %collective-permute-start.18 = (f32[8,128,128]{2,1,0:T(8,128)S(1)}, f32[8,128,128]{2,1,0:T(8,128)S(1)}, u32[]{:S(2)}, u32[]{:S(2)}) collective-permute-start(f32[8,128,128]{2,1,0:T(8,128)S(1)} %get-tuple-element.45), channel_id=1, source_target_pairs={{16,0},{49,1},{32,16},{1,17},{48,32},{17,33},{0,48},{33,49},{18,2}... | collective-permute-start | bytes 1572872 | tf_op jit(solution)/shard_map/ppermute | solution.py:252
  86.8 12.0 %collective-permute-start.17 = (f32[8,128,128]{2,1,0:T(8,128)S(1)}, f32[8,128,128]{2,1,0:T(8,128)S(1)}, u32[]{:S(2)}, u32[]{:S(2)}) collective-permute-start(f32[8,128,128]{2,1,0:T(8,128)S(1)} %add.49), channel_id=1, source_target_pairs={{0,16},{1,49},{16,32},{17,1},{32,48},{33,17},{48,0},{49,33},{2,18}... | collective-permute-start | bytes 1572872 | tf_op jit(solution)/shard_map/ppermute | solution.py:254

commit v4 on v3

v4 whole, which is shorter than its diff:
```python
import functools

import jax
import jax.numpy as jnp
from jax import lax
from jax.experimental import pallas as pl
from jax.experimental.pallas import tpu as pltpu
from jax.sharding import Mesh, PartitionSpec as P

TILE = 128
FEAT = 128
BLOCKS = 8
SLOTS = 16
BUCKETS = 16
TILES = BUCKETS * SLOTS
UNROLL = 8
AHEAD_BY = 8
GROUP = 4
DUMMY = 64

AXES = ("z_lo", "x", "z_hi", "y", "core")
UP = [(i, (i + 1) % 4) for i in range(4)]
DOWN = [(i, (i - 1) % 4) for i in range(4)]
SWAP = [(0, 1), (1, 0)]

f32, bf16 = jnp.float32, jnp.bfloat16


def split(v):
    hi = v.astype(bf16)
    return hi, (v - hi.astype(f32)).astype(bf16)


def halves(v):
    return jnp.concatenate(split(v), axis=1)


def product(left, right):
    both = jnp.dot(left, jnp.concatenate([right, right], axis=0), preferred_element_type=f32)
    return both[:, :FEAT] + both[:, FEAT:]


def live_kernel(packed, tiles, words, count, split_tiles, at, ring, sem):
    def bucket(k, n):
        loaded = [packed[k * SLOTS + t] for t in range(SLOTS)]
        for t, word in enumerate(loaded):
            at[n] = word & 255
            words[n] = (word & 0xFFFF00) | n
            n = n + (word >= 0).astype(jnp.int32)
        return n

    total = lax.fori_loop(0, BUCKETS, bucket, 0)
    count[0] = total
    for j in range(UNROLL):
        words[total + j] = -1
        at[total + j] = 0
    groups = (total + GROUP - 1) // GROUP

    def fetch(group, slot):
        for j in range(GROUP):
            pltpu.make_async_copy(tiles.at[at[group * GROUP + j]], ring.at[slot, j], sem.at[slot, j]).start()

    for s in range(AHEAD_BY - 1):

        @pl.when(s < groups)
        def _(s=s):
            fetch(s, s)

    def step(group, carry):
        slot = group % AHEAD_BY
        ahead = group + AHEAD_BY - 1

        @pl.when(ahead < groups)
        def _():
            fetch(ahead, ahead % AHEAD_BY)

        for j in range(GROUP):
            pltpu.make_async_copy(tiles.at[0], ring.at[slot, j], sem.at[slot, j]).wait()
        for j in range(GROUP):
            split_tiles[group * GROUP + j] = halves(ring[slot, j])
        return carry

    lax.fori_loop(0, groups, step, 0)


def tile_kernel(n_pieces, first, last, *refs):
    words, count, tiles = refs[:3]
    pieces = refs[3 : 3 + n_pieces]
    so_far = None if first else refs[3 + n_pieces]
    outs = refs[4 + n_pieces - first :]
    if last:
        parts, (acc, rest, left) = outs[:BLOCKS], outs[BLOCKS : BLOCKS + 3]
        scratch = outs[BLOCKS + 3 :]
    else:
        acc, rest, left = outs[:3]
        scratch = outs[3:]
    xs, slots, table, mine, slot_sem = scratch

    reads = [
        pltpu.make_async_copy(piece.at[pl.ds(BLOCKS * TILE, 8)], slots.at[i], slot_sem.at[i])
        for i, piece in enumerate(pieces)
    ]
    for read in reads:
        read.start()
    for p in range(BUCKETS * BLOCKS):
        table[p] = -1
    for read in reads:
        read.wait()
    for i in range(n_pieces):
        for j in range(BLOCKS):
            table[slots[i, 0, j].astype(jnp.int32) & 127] = i * BLOCKS + j

    def sort(group, n):
        here, there = n
        loaded = [words[group * UNROLL + j] for j in range(UNROLL)]
        found = [table[(word >> 8) & 127] for word in loaded]
        for word, s in zip(loaded, found):
            live = (word >= 0).astype(jnp.int32)
            known = jnp.where(s >= 0, live, 0)
            mine[here] = (word & 0xFF00FF) | (s << 8)
            rest[there] = word
            here, there = here + known, there + live - known
        return here, there

    here, there = lax.fori_loop(0, (count[0] + UNROLL - 1) // UNROLL, sort, (0, 0))
    left[0] = there
    for j in range(UNROLL):
        mine[here + j] = DUMMY * 65536
        rest[there + j] = -1

    def halve(j, carry):
        for i, piece in enumerate(pieces):
            xs[i * BLOCKS + j] = halves(piece[pl.ds(pl.multiple_of(j * TILE, TILE), TILE), :])
        return carry

    lax.fori_loop(0, BLOCKS, halve, 0)

    def begin(d, carry):
        acc[d] = jnp.zeros((TILE, FEAT), f32) if first else so_far[d]
        return carry

    lax.fori_loop(0, DUMMY + 1, begin, 0, unroll=5)

    def step(group, carry):
        own = [mine[group * UNROLL + j] for j in range(UNROLL)]
        results = [product(tiles[w & 255], xs[(w >> 8) & 127]) for w in own]
        for w, result in zip(own, results):
            acc[w >> 16] += result
        return carry

    lax.fori_loop(0, (here + UNROLL - 1) // UNROLL, step, 0)
    if last:

        def hand_out(j, carry):
            for i, out in enumerate(parts):
                out[j] = acc[i * BLOCKS + j]
            return carry

        lax.fori_loop(0, BLOCKS, hand_out, 0)


def tile_products(words, count, tiles, pieces, so_far=None, last=False):
    first = so_far is None
    smem = pl.BlockSpec(memory_space=pltpu.SMEM)
    vmem = pl.BlockSpec(memory_space=pltpu.VMEM)
    sums = pltpu.VMEM((DUMMY + 1, TILE, FEAT), f32)
    going_on = [pltpu.SMEM((TILES + 2 * UNROLL,), jnp.int32), pltpu.SMEM((1,), jnp.int32)]
    part = jax.ShapeDtypeStruct((BLOCKS, TILE, FEAT), f32)
    return pl.pallas_call(
        functools.partial(tile_kernel, len(pieces), first, last),
        out_shape=[part] * BLOCKS
        if last
        else [jax.ShapeDtypeStruct(r.shape, r.dtype) for r in (sums, *going_on)],
        in_specs=[smem, smem] + [vmem] * (1 + len(pieces) + (not first)),
        out_specs=[vmem] * BLOCKS if last else [vmem, smem, smem],
        scratch_shapes=([sums, *going_on] if last else [])
        + [
            pltpu.VMEM((len(pieces) * BLOCKS, TILE, 2 * FEAT), bf16),
            pltpu.SMEM((len(pieces), 8, 128), f32),
            pltpu.SMEM((BUCKETS * BLOCKS,), jnp.int32),
            pltpu.SMEM((TILES + 2 * UNROLL,), jnp.int32),
            pltpu.SemaphoreType.DMA((len(pieces),)),
        ],
        compiler_params=pltpu.CompilerParams(vmem_limit_bytes=16 * 2**20),
        cost_estimate=pl.CostEstimate(
            flops=2 * TILE * TILE * FEAT * 4 * 60, bytes_accessed=8 * 2**20, transcendentals=0
        ),
    )(words, count, tiles, *pieces, *([] if first else [so_far]))


def finish_kernel(a, b, c, d, weight, bias, out):
    total = a[...] + b[...] + c[...] + d[...]
    hidden = product(halves(total.reshape(BLOCKS * TILE, FEAT)), halves(weight[...]))
    out[...] = jnp.maximum(hidden + bias[...], 0.0)


def after(value, *others):
    return lax.optimization_barrier((value, *others))[0]


def body(features, new_slot, tile_values, tile_dest, tile_source, weight, bias_vector):
    move = lax.ppermute
    row = jnp.pad(new_slot.astype(f32)[None, :], ((0, 7), (0, FEAT - BLOCKS)))
    own = jnp.concatenate([features, row])
    below = move(own, "y", UP)
    above = move(own, "y", DOWN)
    far = move(own, "z_hi", SWAP)
    other = move(own, "core", SWAP)

    z_lo, x = lax.axis_index("z_lo"), lax.axis_index("x")
    bucket = lax.broadcasted_iota(jnp.int32, (BUCKETS, SLOTS), 0)
    slot = lax.broadcasted_iota(jnp.int32, (BUCKETS, SLOTS), 1)
    dest = tile_dest.reshape(BUCKETS, SLOTS)
    group = dest >> 3
    turned = (((group >> 2) ^ z_lo) * 4 + ((group & 3) - x & 3)) * BLOCKS + (dest & 7)
    position = bucket * BLOCKS + tile_source.reshape(BUCKETS, SLOTS)
    packed = jnp.where(dest >= 0, (bucket * SLOTS + slot) + position * 256 + turned * 65536, -1)

    smem = pl.BlockSpec(memory_space=pltpu.SMEM)
    words, count, tiles = pl.pallas_call(
        live_kernel,
        out_shape=[
            jax.ShapeDtypeStruct((TILES + 2 * UNROLL,), jnp.int32),
            jax.ShapeDtypeStruct((1,), jnp.int32),
            jax.ShapeDtypeStruct((TILES + GROUP, TILE, 2 * TILE), bf16),
        ],
        in_specs=[smem, pl.BlockSpec(memory_space=pltpu.HBM)],
        out_specs=[smem, smem, pl.BlockSpec(memory_space=pltpu.VMEM)],
        scratch_shapes=[
            pltpu.SMEM((TILES + 2 * UNROLL,), jnp.int32),
            pltpu.VMEM((AHEAD_BY, GROUP, TILE, TILE), f32),
            pltpu.SemaphoreType.DMA((AHEAD_BY, GROUP)),
        ],
        compiler_params=pltpu.CompilerParams(vmem_limit_bytes=20 * 2**20),
        cost_estimate=pl.CostEstimate(flops=10**7, bytes_accessed=16 * 2**20, transcendentals=0),
    )(packed.reshape(TILES), tile_values.reshape(TILES, TILE, TILE))

    below = after(below, words)
    two = move(below, "y", UP)
    far_above = move(far, "y", DOWN)
    far_below = move(below, "z_hi", SWAP)
    swapped = [move(p, "core", SWAP) for p in (below, above, far)]
    sums, words, count = tile_products(words, count, tiles, [own, other, below, above, far, *swapped])

    two = after(two, sums)
    far_two = move(two, "z_hi", SWAP)
    late = [two, far_above, far_below]
    swapped = [move(p, "core", SWAP) for p in late]
    sums, words, count = tile_products(words, count, tiles, [*late, *swapped], sums)

    far_two = after(far_two, sums)
    mine, up, two, down, z_mine, z_up, z_two, z_down = tile_products(
        words, count, tiles, [far_two, move(far_two, "core", SWAP)], sums, last=True
    )

    got_two = move(z_two, "z_lo", SWAP)
    got_down = move(z_down, "x", DOWN)
    end_down = move(down, "x", DOWN)
    got_up = move(after(z_up, got_two), "z_lo", SWAP)
    got = move(two + got_two, "x", UP)
    end_z = move(z_mine + got_down, "z_lo", SWAP)
    end_up = move(up + got + got_up, "x", UP)

    return pl.pallas_call(
        finish_kernel,
        out_shape=jax.ShapeDtypeStruct((BLOCKS * TILE, FEAT), f32),
        compiler_params=pltpu.CompilerParams(vmem_limit_bytes=24 * 2**20),
    )(mine, end_up, end_down, end_z, weight, bias_vector.reshape(1, FEAT))


def solution(mesh):
    fine = Mesh(mesh.devices.reshape(2, 4, 2, 4, 2), AXES)
    grp, blk = AXES[:2], AXES[2:]
    return jax.shard_map(
        body,
        mesh=fine,
        in_specs=(
            P(AXES, None),
            P(AXES),
            P(grp, blk, None, None, None, None),
            P(grp, blk, None, None),
            P(grp, blk, None, None),
            P(),
            P(),
        ),
        out_specs=P(AXES, None),
        check_vma=False,
    )
```

time: 101 us -> 120 us (1.19)
  Pallas kernels: 25.6 us -> 39.9 us
  waiting for transfers between devices: 34.4 us -> 45.1 us
  starting transfers between devices: 34 us -> 23.3 us
  local copies, waits for them, and re-layouts: 1.88 us -> 6.96 us
    pallas_call x1, Pallas kernels: 1.85 us -> 19.2 us  [body(): pl.pallas_call(live_kernel, out_shape=[jax.ShapeDtypeStruct((TILES + 2 *...]
    ppermute x18, waiting for transfers between devices: 22.7 us -> 29.7 us  [the longest x1 8.82 us: body(): end_z = move(z_mine + got_down, 'z_lo', SWAP)]
    ppermute x1, waiting for transfers between devices: 0.01 us -> 5.72 us  [body(): far_two = move(two, 'z_hi', SWAP)]
    unnamed x6, local copies, waits for them, and re-layouts: 0.69 us -> 5.78 us
    ppermute x1, starting transfers between devices: 5.95 us -> 1.7 us  [body(): far_two = move(two, 'z_hi', SWAP)]
    ppermute x1, waiting for transfers between devices: 3.93 us -> 0.01 us  [body(): far = move(own, 'z_hi', SWAP)]
    pallas_call x3, Pallas kernels: 22.6 us -> 19.6 us  [tile_products(): pl.pallas_call(functools.partial(tile_kernel, len(pieces), first, last),...]
    ppermute x18, starting transfers between devices: 19.6 us -> 16.6 us  [the longest x1 3.27 us: body(): got_down = move(z_down, 'x', DOWN)]
  transfers between devices with their start and end apart: 22 -> 22, of which waited for: 7 -> 12; matrix products, arithmetic and copies ran while one was open for 3% -> 2% of each run, Pallas kernels for 19% -> 29%
where the time goes in v4:
time: 120 us; the launch traced here: 119 us
  waiting for transfers between devices  45.1 us (38%)
  Pallas kernels  39.9 us (33%)
  starting transfers between devices  23.3 us (19%)
  local copies, waits for them, and re-layouts  6.96 us (6%)
  other arithmetic  3.48 us (3%)
    pallas_call x3, Pallas kernels, tile_products(): pl.pallas_call(functools.partial(tile_kernel, len(pieces), first, last),...  19.6 us
    pallas_call x1, Pallas kernels, body(): pl.pallas_call(live_kernel, out_shape=[jax.ShapeDtypeStruct((TILES + 2 *...  19.2 us
    ppermute x1, waiting for transfers between devices, body(): got_two = move(z_two, 'z_lo', SWAP)  9.66 us
    ppermute x1, waiting for transfers between devices, body(): end_z = move(z_mine + got_down, 'z_lo', SWAP)  8.82 us
    ppermute x1, waiting for transfers between devices, body(): got = move(two + got_two, 'x', UP)  8.68 us
    unnamed x6, local copies, waits for them, and re-layouts  5.78 us
    ppermute x1, waiting for transfers between devices, body(): far_two = move(two, 'z_hi', SWAP)  5.72 us
    ppermute x1, starting transfers between devices, body(): far = move(own, 'z_hi', SWAP)  3.88 us
  transfers between devices with their start and end apart: 22, of which 12 were waited for; matrix products, arithmetic and copies ran while one was open for 2% of the time, Pallas kernels for 29%

profile of v4, /device:TPU:0, one launch (start us, length us, event | category | flops | bytes accessed | tf_op | source)
XLA Modules:
  0.0 118.9 jit_solution(16098509544484374569)
XLA Ops:
  0.0 0.7 convert_bitcast_fusion
  0.7 1.1 select_maximum_fusion.refs_3_
  1.7 1.7 %collective-permute-start.1 = (f32[1032,128]{1,0:T(8,128)S(1)}, f32[1032,128]{1,0:T(8,128)S(1)}, u32[]{:S(2)}, u32[]{:S(2)}) collective-permute-start(f32[1032,128]{1,0:T(8,128)S(1)} %select_maximum_fusion.refs_3_), channel_id=1, source_target_pairs={{0,2},{2,4},{4,6},{6,0},{1,3},{3,5},{5,7},{7,1},{8,10},{10,12},{12... | collective-permute-start | bytes 1585160 | tf_op jit(solution)/shard_map/ppermute | solution.py:205
  3.5 3.9 %collective-permute-start.3 = (f32[1032,128]{1,0:T(8,128)S(1)}, f32[1032,128]{1,0:T(8,128)S(1)}, u32[]{:S(2)}, u32[]{:S(2)}) collective-permute-start(f32[1032,128]{1,0:T(8,128)S(1)} %select_maximum_fusion.refs_3_), channel_id=1, source_target_pairs={{0,8},{8,0},{1,9},{9,1},{2,10},{10,2},{3,11},{11,3},{4,12},{12,4},... | collective-permute-start | bytes 1585160 | tf_op jit(solution)/shard_map/ppermute | solution.py:207
  7.3 1.7 %collective-permute-start.2 = (f32[1032,128]{1,0:T(8,128)S(1)}, f32[1032,128]{1,0:T(8,128)S(1)}, u32[]{:S(2)}, u32[]{:S(2)}) collective-permute-start(f32[1032,128]{1,0:T(8,128)S(1)} %select_maximum_fusion.refs_3_), channel_id=1, source_target_pairs={{0,6},{2,0},{4,2},{6,4},{1,7},{3,1},{5,3},{7,5},{8,14},{10,8},{12,... | collective-permute-start | bytes 1585160 | tf_op jit(solution)/shard_map/ppermute | solution.py:206
  9.0 0.7 add_multiply_fusion
  9.7 0.1 reshape.43
  9.8 0.1 iota_add_fusion
  9.9 0.1 add.42
  10.0 0.1 iota.23
  10.0 0.1 iota.24
  10.1 0.7 broadcast_compare_fusion
  10.8 0.1 ge.12
  10.9 0.8 reshape.35
  11.7 5.8 %copy-done = f32[1,1,16,16,128,128]{5,4,3,2,1,0:T(8,128)S(1)} copy-done((f32[1,1,16,16,128,128]{5,4,3,2,1,0:T(8,128)S(1)}, f32[1,1,16,16,128,128]{5,4,3,2,1,0:T(8,128)}, u32[]{:S(2)}) %copy-start) | copy-done | bytes 16777240
  17.5 19.2 %shard_map.73 = (s32[272]{0:T(512)S(1)}, s32[1]{0:T(128)}, bf16[260,128,256]{2,1,0:T(8,128)(2,1)S(1)}) custom-call(s32[256]{0:T(256)S(1)} %add_select_fusion.packed, f32[256,128,128]{2,1,0:T(8,128)S(1)} %bitcast.10), custom_call_target="tpu_custom_call" | custom-call | flops 10000000 | bytes 16777216 | tf_op jit(solution)/shard_map/pallas_call | solution.py:220
  36.7 0.1 collective-permute-start.4
  36.8 0.5 collective-permute-start.6
  37.3 0.1 collective-permute-start.5
  37.4 1.3 %collective-permute-done.4.refs_8_ = f32[1032,128]{1,0:T(8,128)S(1)} collective-permute-done((f32[1032,128]{1,0:T(8,128)S(1)}, f32[1032,128]{1,0:T(8,128)S(1)}, u32[]{:S(2)}, u32[]{:S(2)}) %collective-permute-start.4) | collective-permute-done | bytes 528416 | tf_op jit(solution)/shard_map/ppermute | solution.py:242
  38.7 2.0 %collective-permute-start.8 = (f32[1032,128]{1,0:T(8,128)S(1)}, f32[1032,128]{1,0:T(8,128)S(1)}, u32[]{:S(2)}, u32[]{:S(2)}) collective-permute-start(f32[1032,128]{1,0:T(8,128)S(1)} %collective-permute-done.3.refs_7_), channel_id=1, source_target_pairs={{0,6},{2,0},{4,2},{6,4},{1,7},{3,1},{5,3},{7,5},{8,14},{10,8},{12,... | collective-permute-start | bytes 1585160 | tf_op jit(solution)/shard_map/ppermute | solution.py:240
  40.7 8.4 %shard_map.74 = (f32[65,128,128]{2,1,0:T(8,128)S(1)}, s32[272]{0:T(512)S(1)}, s32[1]{0:T(128)}) custom-call(s32[272]{0:T(512)S(1)} %get-tuple-element.26.refs_0_, s32[1]{0:T(128)} %get-tuple-element.27.refs_1_, bf16[260,128,256]{2,1,0:T(8,128)(2,1)S(1)} %get-tuple-element.28.refs_2_, f32[1032,128]{1,0:T(8,128)S(1)} %select_maximum_fusion.refs_3_, ...), custom_call_target="tpu_custom_call" | custom-call | flops 1006632960 | bytes 8388608 | tf_op jit(solution)/shard_map/pallas_call | solution.py:169
  49.1 3.8 %collective-permute-done.7.refs_3_ = f32[1032,128]{1,0:T(8,128)S(1)} collective-permute-done((f32[1032,128]{1,0:T(8,128)S(1)}, f32[1032,128]{1,0:T(8,128)S(1)}, u32[]{:S(2)}, u32[]{:S(2)}) %collective-permute-start.7) | collective-permute-done | bytes 528416 | tf_op jit(solution)/shard_map/ppermute | solution.py:239
  53.0 0.3 collective-permute-done.9.refs_5_
  53.3 0.2 collective-permute-start.12
  53.5 0.3 collective-permute-start.11
  53.8 1.7 %collective-permute-start.13 = (f32[1032,128]{1,0:T(8,128)S(1)}, f32[1032,128]{1,0:T(8,128)S(1)}, u32[]{:S(2)}, u32[]{:S(2)}) collective-permute-start(f32[1032,128]{1,0:T(8,128)S(1)} %collective-permute-done.7.refs_3_), channel_id=1, source_target_pairs={{0,8},{8,0},{1,9},{9,1},{2,10},{10,2},{3,11},{11,3},{4,12},{12,4},... | collective-permute-start | bytes 1585160 | tf_op jit(solution)/shard_map/ppermute | solution.py:246
  55.5 0.1 collective-permute-done.12.refs_8_
  55.6 0.8 collective-permute-done.11.refs_7_
  56.4 7.3 %shard_map.75 = (f32[65,128,128]{2,1,0:T(8,128)S(1)}, s32[272]{0:T(512)S(1)}, s32[1]{0:T(128)}) custom-call(s32[272]{0:T(512)S(1)} %get-tuple-element.30.refs_0_, s32[1]{0:T(128)} %get-tuple-element.31.refs_1_, bf16[260,128,256]{2,1,0:T(8,128)(2,1)S(1)} %get-tuple-element.28.refs_2_, f32[1032,128]{1,0:T(8,128)S(1)} %collective-permute-done.7.refs_3_, ...), custom_call_target="tpu_custom_call" | custom-call | flops 1006632960 | bytes 8388608 | tf_op jit(solution)/shard_map/pallas_call | solution.py:169
  63.7 5.7 %collective-permute-done.13.refs_3_ = f32[1032,128]{1,0:T(8,128)S(1)} collective-permute-done((f32[1032,128]{1,0:T(8,128)S(1)}, f32[1032,128]{1,0:T(8,128)S(1)}, u32[]{:S(2)}, u32[]{:S(2)}) %collective-permute-start.13) | collective-permute-done | bytes 528416 | tf_op jit(solution)/shard_map/ppermute | solution.py:246
  69.4 1.9 %collective-permute-done.14.refs_4_ = f32[1032,128]{1,0:T(8,128)S(1)} collective-permute-done((f32[1032,128]{1,0:T(8,128)S(1)}, f32[1032,128]{1,0:T(8,128)S(1)}, u32[]{:S(2)}, u32[]{:S(2)}) %collective-permute-start.14) | collective-permute-done | bytes 528416 | tf_op jit(solution)/shard_map/ppermute | solution.py:253
  71.3 3.9 %shard_map.76 = (f32[8,128,128]{2,1,0:T(8,128)S(1)}, f32[8,128,128]{2,1,0:T(8,128)S(1)}, f32[8,128,128]{2,1,0:T(8,128)S(1)}, f32[8,128,128]{2,1,0:T(8,128)S(1)},...) custom-call(s32[272]{0:T(512)S(1)} %get-tuple-element.34.refs_0_, ...), custom_call_target="tpu_custom_call" | custom-call | flops 1006632960 | bytes 8388608 | tf_op jit(solution)/shard_map/pallas_call | solution.py:169
  75.2 1.1 collective-permute-start.15
  76.3 3.3 %collective-permute-start.20 = (f32[8,128,128]{2,1,0:T(8,128)S(1)}, f32[8,128,128]{2,1,0:T(8,128)S(1)}, u32[]{:S(2)}, u32[]{:S(2)}) collective-permute-start(f32[8,128,128]{2,1,0:T(8,128)S(1)} %get-tuple-element.46), channel_id=1, source_target_pairs={{0,48},{16,0},{32,16},{48,32},{1,49},{17,1},{33,17},{49,33},{2,50}... | collective-permute-start | bytes 1572872 | tf_op jit(solution)/shard_map/ppermute | solution.py:257
  79.6 9.7 %collective-permute-done.15 = f32[8,128,128]{2,1,0:T(8,128)S(1)} collective-permute-done((f32[8,128,128]{2,1,0:T(8,128)S(1)}, f32[8,128,128]{2,1,0:T(8,128)S(1)}, u32[]{:S(2)}, u32[]{:S(2)}) %collective-permute-start.15) | collective-permute-done | bytes 524320 | tf_op jit(solution)/shard_map/ppermute | solution.py:256
  89.3 1.6 %collective-permute-start.16 = (f32[8,128,128]{2,1,0:T(8,128)S(1)}, f32[8,128,128]{2,1,0:T(8,128)S(1)}, u32[]{:S(2)}, u32[]{:S(2)}) collective-permute-start(f32[8,128,128]{2,1,0:T(8,128)S(1)} %add.48), channel_id=1, source_target_pairs={{0,16},{16,32},{32,48},{48,0},{1,17},{17,33},{33,49},{49,1},{2,18}... | collective-permute-start | bytes 1572872 | tf_op jit(solution)/shard_map/ppermute | solution.py:260
  91.0 1.7 %collective-permute-start.17 = (f32[8,128,128]{2,1,0:T(8,128)S(1)}, f32[8,128,128]{2,1,0:T(8,128)S(1)}, u32[]{:S(2)}, u32[]{:S(2)}) collective-permute-start(f32[8,128,128]{2,1,0:T(8,128)S(1)} %get-tuple-element.43), channel_id=1, source_target_pairs={{0,64},{64,0},{1,65},{65,1},{2,66},{66,2},{3,67},{67,3},{4,68},{68... | collective-permute-start | bytes 1572872 | tf_op jit(solution)/shard_map/ppermute | solution.py:259
  92.7 1.0 collective-permute-start.19
  93.7 0.1 add.51
  93.8 1.8 %collective-permute-start.21 = (f32[8,128,128]{2,1,0:T(8,128)S(1)}, f32[8,128,128]{2,1,0:T(8,128)S(1)}, u32[]{:S(2)}, u32[]{:S(2)}) collective-permute-start(f32[8,128,128]{2,1,0:T(8,128)S(1)} %add.51), channel_id=1, source_target_pairs={{0,64},{64,0},{1,65},{65,1},{2,66},{66,2},{3,67},{67,3},{4,68},{68... | collective-permute-start | bytes 1572872 | tf_op jit(solution)/shard_map/ppermute | solution.py:261
  95.5 8.7 %collective-permute-done.16 = f32[8,128,128]{2,1,0:T(8,128)S(1)} collective-permute-done((f32[8,128,128]{2,1,0:T(8,128)S(1)}, f32[8,128,128]{2,1,0:T(8,128)S(1)}, u32[]{:S(2)}, u32[]{:S(2)}) %collective-permute-start.16) | collective-permute-done | bytes 524320 | tf_op jit(solution)/shard_map/ppermute | solution.py:260
  104.2 1.6 %collective-permute-done.17 = f32[8,128,128]{2,1,0:T(8,128)S(1)} collective-permute-done((f32[8,128,128]{2,1,0:T(8,128)S(1)}, f32[8,128,128]{2,1,0:T(8,128)S(1)}, u32[]{:S(2)}, u32[]{:S(2)}) %collective-permute-start.17) | collective-permute-done | bytes 524320 | tf_op jit(solution)/shard_map/ppermute | solution.py:259
  105.8 0.1 add_add_fusion
  105.9 0.6 collective-permute-start.18
  106.6 8.8 %collective-permute-done.21.d = f32[8,128,128]{2,1,0:T(8,128)S(1)} collective-permute-done((f32[8,128,128]{2,1,0:T(8,128)S(1)}, f32[8,128,128]{2,1,0:T(8,128)S(1)}, u32[]{:S(2)}, u32[]{:S(2)}) %collective-permute-start.21) | collective-permute-done | bytes 524320 | tf_op jit(solution)/shard_map/ppermute | solution.py:261
  115.4 2.4 %collective-permute-done.18.b = f32[8,128,128]{2,1,0:T(8,128)S(1)} collective-permute-done((f32[8,128,128]{2,1,0:T(8,128)S(1)}, f32[8,128,128]{2,1,0:T(8,128)S(1)}, u32[]{:S(2)}, u32[]{:S(2)}) %collective-permute-start.18) | collective-permute-done | bytes 524320 | tf_op jit(solution)/shard_map/ppermute | solution.py:262
  117.8 1.1 shard_map.77
  (24 shorter events, 0.1 us)
Async XLA Ops:
  1.7 35.0 %collective-permute-start.1 = (f32[1032,128]{1,0:T(8,128)S(1)}, f32[1032,128]{1,0:T(8,128)S(1)}, u32[]{:S(2)}, u32[]{:S(2)}) collective-permute-start(f32[1032,128]{1,0:T(8,128)S(1)} %select_maximum_fusion.refs_3_), channel_id=1, source_target_pairs={{0,2},{2,4},{4,6},{6,0},{1,3},{3,5},{5,7},{7,1},{8,10},{10,12},{12... | collective-permute-start | bytes 1585160 | tf_op jit(solution)/shard_map/ppermute | solution.py:205
  3.5 33.3 %collective-permute-start.3 = (f32[1032,128]{1,0:T(8,128)S(1)}, f32[1032,128]{1,0:T(8,128)S(1)}, u32[]{:S(2)}, u32[]{:S(2)}) collective-permute-start(f32[1032,128]{1,0:T(8,128)S(1)} %select_maximum_fusion.refs_3_), channel_id=1, source_target_pairs={{0,8},{8,0},{1,9},{9,1},{2,10},{10,2},{3,11},{11,3},{4,12},{12,4},... | collective-permute-start | bytes 1585160 | tf_op jit(solution)/shard_map/ppermute | solution.py:207
  7.3 30.0 %collective-permute-start.2 = (f32[1032,128]{1,0:T(8,128)S(1)}, f32[1032,128]{1,0:T(8,128)S(1)}, u32[]{:S(2)}, u32[]{:S(2)}) collective-permute-start(f32[1032,128]{1,0:T(8,128)S(1)} %select_maximum_fusion.refs_3_), channel_id=1, source_target_pairs={{0,6},{2,0},{4,2},{6,4},{1,7},{3,1},{5,3},{7,5},{8,14},{10,8},{12,... | collective-permute-start | bytes 1585160 | tf_op jit(solution)/shard_map/ppermute | solution.py:206
  9.0 28.4 %collective-permute-start = (f32[1032,128]{1,0:T(8,128)S(1)}, f32[1032,128]{1,0:T(8,128)S(1)}, u32[]{:S(2)}, u32[]{:S(2)}) collective-permute-start(f32[1032,128]{1,0:T(8,128)S(1)} %select_maximum_fusion.refs_3_), channel_id=1, source_target_pairs={{0,1},{1,0},{2,3},{3,2},{4,5},{5,4},{6,7},{7,6},{8,9},{9,8},{10,11... | collective-permute-start | bytes 1585160 | tf_op jit(solution)/shard_map/ppermute | solution.py:208
  11.7 5.8 %copy-start = (f32[1,1,16,16,128,128]{5,4,3,2,1,0:T(8,128)S(1)}, f32[1,1,16,16,128,128]{5,4,3,2,1,0:T(8,128)}, u32[]{:S(2)}) copy-start(f32[1,1,16,16,128,128]{5,4,3,2,1,0:T(8,128)} %param.9) | copy-start | bytes 50331652
  36.7 2.0 %collective-permute-start.4 = (f32[1032,128]{1,0:T(8,128)S(1)}, f32[1032,128]{1,0:T(8,128)S(1)}, u32[]{:S(2)}, u32[]{:S(2)}) collective-permute-start(f32[1032,128]{1,0:T(8,128)S(1)} %collective-permute-done.1.refs_5_), channel_id=1, source_target_pairs={{0,1},{1,0},{2,3},{3,2},{4,5},{5,4},{6,7},{7,6},{8,9},{9,8},{10,11... | collective-permute-start | bytes 1585160 | tf_op jit(solution)/shard_map/ppermute | solution.py:242
  36.8 3.9 %collective-permute-start.6 = (f32[1032,128]{1,0:T(8,128)S(1)}, f32[1032,128]{1,0:T(8,128)S(1)}, u32[]{:S(2)}, u32[]{:S(2)}) collective-permute-start(f32[1032,128]{1,0:T(8,128)S(1)} %collective-permute-done.3.refs_7_), channel_id=1, source_target_pairs={{0,1},{1,0},{2,3},{3,2},{4,5},{5,4},{6,7},{7,6},{8,9},{9,8},{10,11... | collective-permute-start | bytes 1585160 | tf_op jit(solution)/shard_map/ppermute | solution.py:242
  37.3 3.4 %collective-permute-start.5 = (f32[1032,128]{1,0:T(8,128)S(1)}, f32[1032,128]{1,0:T(8,128)S(1)}, u32[]{:S(2)}, u32[]{:S(2)}) collective-permute-start(f32[1032,128]{1,0:T(8,128)S(1)} %collective-permute-done.2.refs_6_), channel_id=1, source_target_pairs={{0,1},{1,0},{2,3},{3,2},{4,5},{5,4},{6,7},{7,6},{8,9},{9,8},{10,11... | collective-permute-start | bytes 1585160 | tf_op jit(solution)/shard_map/ppermute | solution.py:242
  37.4 15.6 %collective-permute-start.7 = (f32[1032,128]{1,0:T(8,128)S(1)}, f32[1032,128]{1,0:T(8,128)S(1)}, u32[]{:S(2)}, u32[]{:S(2)}) collective-permute-start(f32[1032,128]{1,0:T(8,128)S(1)} %collective-permute-done.1.refs_5_), channel_id=1, source_target_pairs={{0,2},{2,4},{4,6},{6,0},{1,3},{3,5},{5,7},{7,1},{8,10},{10,12},{12... | collective-permute-start | bytes 1585160 | tf_op jit(solution)/shard_map/ppermute | solution.py:239
  37.4 15.9 %collective-permute-start.9 = (f32[1032,128]{1,0:T(8,128)S(1)}, f32[1032,128]{1,0:T(8,128)S(1)}, u32[]{:S(2)}, u32[]{:S(2)}) collective-permute-start(f32[1032,128]{1,0:T(8,128)S(1)} %collective-permute-done.1.refs_5_), channel_id=1, source_target_pairs={{0,8},{8,0},{1,9},{9,1},{2,10},{10,2},{3,11},{11,3},{4,12},{12,4},... | collective-permute-start | bytes 1585160 | tf_op jit(solution)/shard_map/ppermute | solution.py:241
  38.7 14.8 %collective-permute-start.8 = (f32[1032,128]{1,0:T(8,128)S(1)}, f32[1032,128]{1,0:T(8,128)S(1)}, u32[]{:S(2)}, u32[]{:S(2)}) collective-permute-start(f32[1032,128]{1,0:T(8,128)S(1)} %collective-permute-done.3.refs_7_), channel_id=1, source_target_pairs={{0,6},{2,0},{4,2},{6,4},{1,7},{3,1},{5,3},{7,5},{8,14},{10,8},{12,... | collective-permute-start | bytes 1585160 | tf_op jit(solution)/shard_map/ppermute | solution.py:240
  53.0 2.5 %collective-permute-start.10 = (f32[1032,128]{1,0:T(8,128)S(1)}, f32[1032,128]{1,0:T(8,128)S(1)}, u32[]{:S(2)}, u32[]{:S(2)}) collective-permute-start(f32[1032,128]{1,0:T(8,128)S(1)} %collective-permute-done.7.refs_3_), channel_id=1, source_target_pairs={{0,1},{1,0},{2,3},{3,2},{4,5},{5,4},{6,7},{7,6},{8,9},{9,8},{10,11... | collective-permute-start | bytes 1585160 | tf_op jit(solution)/shard_map/ppermute | solution.py:248
  53.3 2.4 %collective-permute-start.12 = (f32[1032,128]{1,0:T(8,128)S(1)}, f32[1032,128]{1,0:T(8,128)S(1)}, u32[]{:S(2)}, u32[]{:S(2)}) collective-permute-start(f32[1032,128]{1,0:T(8,128)S(1)} %collective-permute-done.9.refs_5_), channel_id=1, source_target_pairs={{0,1},{1,0},{2,3},{3,2},{4,5},{5,4},{6,7},{7,6},{8,9},{9,8},{10,11... | collective-permute-start | bytes 1585160 | tf_op jit(solution)/shard_map/ppermute | solution.py:248
  53.5 2.9 %collective-permute-start.11 = (f32[1032,128]{1,0:T(8,128)S(1)}, f32[1032,128]{1,0:T(8,128)S(1)}, u32[]{:S(2)}, u32[]{:S(2)}) collective-permute-start(f32[1032,128]{1,0:T(8,128)S(1)} %collective-permute-done.8.refs_4_), channel_id=1, source_target_pairs={{0,1},{1,0},{2,3},{3,2},{4,5},{5,4},{6,7},{7,6},{8,9},{9,8},{10,11... | collective-permute-start | bytes 1585160 | tf_op jit(solution)/shard_map/ppermute | solution.py:248
  53.8 15.6 %collective-permute-start.13 = (f32[1032,128]{1,0:T(8,128)S(1)}, f32[1032,128]{1,0:T(8,128)S(1)}, u32[]{:S(2)}, u32[]{:S(2)}) collective-permute-start(f32[1032,128]{1,0:T(8,128)S(1)} %collective-permute-done.7.refs_3_), channel_id=1, source_target_pairs={{0,8},{8,0},{1,9},{9,1},{2,10},{10,2},{3,11},{11,3},{4,12},{12,4},... | collective-permute-start | bytes 1585160 | tf_op jit(solution)/shard_map/ppermute | solution.py:246
  63.7 54.1 %copy-start.1 = (f32[128,128]{1,0:T(8,128)S(1)}, f32[128,128]{1,0:T(8,128)}, u32[]{:S(2)}) copy-start(f32[128,128]{1,0:T(8,128)} %weight.1) | copy-start | bytes 196612
  63.7 54.1 %copy-start.2 = (f32[128]{0:T(128)S(1)}, f32[128]{0:T(128)}, u32[]{:S(2)}) copy-start(f32[128]{0:T(128)} %param.13) | copy-start | bytes 1540
  69.4 1.9 %collective-permute-start.14 = (f32[1032,128]{1,0:T(8,128)S(1)}, f32[1032,128]{1,0:T(8,128)S(1)}, u32[]{:S(2)}, u32[]{:S(2)}) collective-permute-start(f32[1032,128]{1,0:T(8,128)S(1)} %collective-permute-done.13.refs_3_), channel_id=1, source_target_pairs={{0,1},{1,0},{2,3},{3,2},{4,5},{5,4},{6,7},{7,6},{8,9},{9,8},{10,11... | collective-permute-start | bytes 1585160 | tf_op jit(solution)/shard_map/ppermute | solution.py:253
  75.2 14.1 %collective-permute-start.15 = (f32[8,128,128]{2,1,0:T(8,128)S(1)}, f32[8,128,128]{2,1,0:T(8,128)S(1)}, u32[]{:S(2)}, u32[]{:S(2)}) collective-permute-start(f32[8,128,128]{2,1,0:T(8,128)S(1)} %get-tuple-element.41), channel_id=1, source_target_pairs={{0,64},{64,0},{1,65},{65,1},{2,66},{66,2},{3,67},{67,3},{4,68},{68... | collective-permute-start | bytes 1572872 | tf_op jit(solution)/shard_map/ppermute | solution.py:256
  76.3 17.3 %collective-permute-start.20 = (f32[8,128,128]{2,1,0:T(8,128)S(1)}, f32[8,128,128]{2,1,0:T(8,128)S(1)}, u32[]{:S(2)}, u32[]{:S(2)}) collective-permute-start(f32[8,128,128]{2,1,0:T(8,128)S(1)} %get-tuple-element.46), channel_id=1, source_target_pairs={{0,48},{16,0},{32,16},{48,32},{1,49},{17,1},{33,17},{49,33},{2,50}... | collective-permute-start | bytes 1572872 | tf_op jit(solution)/shard_map/ppermute | solution.py:257
  89.3 14.9 %collective-permute-start.16 = (f32[8,128,128]{2,1,0:T(8,128)S(1)}, f32[8,128,128]{2,1,0:T(8,128)S(1)}, u32[]{:S(2)}, u32[]{:S(2)}) collective-permute-start(f32[8,128,128]{2,1,0:T(8,128)S(1)} %add.48), channel_id=1, source_target_pairs={{0,16},{16,32},{32,48},{48,0},{1,17},{17,33},{33,49},{49,1},{2,18}... | collective-permute-start | bytes 1572872 | tf_op jit(solution)/shard_map/ppermute | solution.py:260
  91.0 14.9 %collective-permute-start.17 = (f32[8,128,128]{2,1,0:T(8,128)S(1)}, f32[8,128,128]{2,1,0:T(8,128)S(1)}, u32[]{:S(2)}, u32[]{:S(2)}) collective-permute-start(f32[8,128,128]{2,1,0:T(8,128)S(1)} %get-tuple-element.43), channel_id=1, source_target_pairs={{0,64},{64,0},{1,65},{65,1},{2,66},{66,2},{3,67},{67,3},{4,68},{68... | collective-permute-start | bytes 1572872 | tf_op jit(solution)/shard_map/ppermute | solution.py:259
  92.7 13.8 %collective-permute-start.19 = (f32[8,128,128]{2,1,0:T(8,128)S(1)}, f32[8,128,128]{2,1,0:T(8,128)S(1)}, u32[]{:S(2)}, u32[]{:S(2)}) collective-permute-start(f32[8,128,128]{2,1,0:T(8,128)S(1)} %get-tuple-element.44), channel_id=1, source_target_pairs={{0,48},{16,0},{32,16},{48,32},{1,49},{17,1},{33,17},{49,33},{2,50}... | collective-permute-start | bytes 1572872 | tf_op jit(solution)/shard_map/ppermute | solution.py:258
  93.8 21.6 %collective-permute-start.21 = (f32[8,128,128]{2,1,0:T(8,128)S(1)}, f32[8,128,128]{2,1,0:T(8,128)S(1)}, u32[]{:S(2)}, u32[]{:S(2)}) collective-permute-start(f32[8,128,128]{2,1,0:T(8,128)S(1)} %add.51), channel_id=1, source_target_pairs={{0,64},{64,0},{1,65},{65,1},{2,66},{66,2},{3,67},{67,3},{4,68},{68... | collective-permute-start | bytes 1572872 | tf_op jit(solution)/shard_map/ppermute | solution.py:261
  105.9 11.8 %collective-permute-start.18 = (f32[8,128,128]{2,1,0:T(8,128)S(1)}, f32[8,128,128]{2,1,0:T(8,128)S(1)}, u32[]{:S(2)}, u32[]{:S(2)}) collective-permute-start(f32[8,128,128]{2,1,0:T(8,128)S(1)} %add_add_fusion), channel_id=1, source_target_pairs={{0,16},{16,32},{32,48},{48,0},{1,17},{17,33},{33,49},{49,1},{2,18}... | collective-permute-start | bytes 1572872 | tf_op jit(solution)/shard_map/ppermute | solution.py:262

commit v5 on v4

v5 whole, which is shorter than its diff:
```python
import functools

import jax
import jax.numpy as jnp
from jax import lax
from jax.experimental import pallas as pl
from jax.experimental.pallas import tpu as pltpu
from jax.sharding import Mesh, PartitionSpec as P

TILE = 128
FEAT = 128
BLOCKS = 8
SLOTS = 16
BUCKETS = 16
TILES = BUCKETS * SLOTS
UNROLL = 8
DEPTH = 6
DUMMY = 64

AXES = ("z_lo", "x", "z_hi", "y", "core")
UP = [(i, (i + 1) % 4) for i in range(4)]
DOWN = [(i, (i - 1) % 4) for i in range(4)]
SWAP = [(0, 1), (1, 0)]

f32, bf16 = jnp.float32, jnp.bfloat16


def split(v):
    hi = v.astype(bf16)
    return hi, (v - hi.astype(f32)).astype(bf16)


def halves(v):
    return jnp.concatenate(split(v), axis=1)


def product(left, right):
    both = jnp.dot(left, jnp.concatenate([right, right], axis=0), preferred_element_type=f32)
    return both[:, :FEAT] + both[:, FEAT:]


def live_kernel(dest, source, words, count):
    def bucket(k, n):
        loaded = [(dest[k, t], source[k, t]) for t in range(SLOTS)]
        for t, (d, s) in enumerate(loaded):
            words[n] = (k * SLOTS + t) + (k * BLOCKS + s) * 256 + d * 65536
            n = n + (d >= 0).astype(jnp.int32)
        return n

    total = lax.fori_loop(0, BUCKETS, bucket, 0)
    count[0] = total
    for j in range(UNROLL):
        words[total + j] = -1


def tile_kernel(n_pieces, first, last, *refs):
    place, words, count, tiles = refs[:4]
    refs = refs[1:]
    pieces = refs[3 : 3 + n_pieces]
    so_far = None if first else refs[3 + n_pieces]
    outs = refs[4 + n_pieces - first :]
    if last:
        parts, (acc, rest, left) = outs[:BLOCKS], outs[BLOCKS : BLOCKS + 3]
        scratch = outs[BLOCKS + 3 :]
    else:
        acc, rest, left = outs[:3]
        scratch = outs[3:]
    xs, ring, slots, table, mine, ring_sem, slot_sem = scratch

    reads = [
        pltpu.make_async_copy(piece.at[pl.ds(BLOCKS * TILE, 8)], slots.at[i], slot_sem.at[i])
        for i, piece in enumerate(pieces)
    ]
    for read in reads:
        read.start()
    for p in range(BUCKETS * BLOCKS):
        table[p] = -1
    for read in reads:
        read.wait()
    for i in range(n_pieces):
        for j in range(BLOCKS):
            table[slots[i, 0, j].astype(jnp.int32) & 127] = i * BLOCKS + j

    def sort(group, n):
        here, there = n
        loaded = [words[group * UNROLL + j] for j in range(UNROLL)]
        found = [table[(word >> 8) & 127] for word in loaded]
        for word, s in zip(loaded, found):
            live = (word >= 0).astype(jnp.int32)
            known = jnp.where(s >= 0, live, 0)
            mine[here] = (word & 0xFF00FF) | (s << 8)
            rest[there] = word
            here, there = here + known, there + live - known
        return here, there

    here, there = lax.fori_loop(0, (count[0] + UNROLL - 1) // UNROLL, sort, (0, 0))
    left[0] = there
    for j in range(UNROLL):
        mine[here + j] = DUMMY * 65536
        rest[there + j] = -1
    groups = (here + UNROLL - 1) // UNROLL

    def fetch(group):
        slot = group % DEPTH
        for j in range(UNROLL):
            at = mine[group * UNROLL + j] & 255
            pltpu.make_async_copy(tiles.at[at], ring.at[slot, j], ring_sem.at[slot, j]).start()

    for group in range(DEPTH - 1):

        @pl.when(group < groups)
        def _(group=group):
            fetch(group)

    def halve(j, carry):
        for i, piece in enumerate(pieces):
            xs[i * BLOCKS + j] = halves(piece[pl.ds(pl.multiple_of(j * TILE, TILE), TILE), :])
        return carry

    lax.fori_loop(0, BLOCKS, halve, 0)

    def begin(d, carry):
        acc[d] = jnp.zeros((TILE, FEAT), f32) if first else so_far[d]
        return carry

    lax.fori_loop(0, DUMMY + 1, begin, 0, unroll=5)

    def step(group, carry):
        @pl.when(group + DEPTH - 1 < groups)
        def _():
            fetch(group + DEPTH - 1)

        slot = group % DEPTH
        own = [mine[group * UNROLL + j] for j in range(UNROLL)]
        for j in range(UNROLL):
            pltpu.make_async_copy(tiles.at[0], ring.at[slot, j], ring_sem.at[slot, j]).wait()
        results = [product(halves(ring[slot, j]), xs[(own[j] >> 8) & 127]) for j in range(UNROLL)]
        for w, result in zip(own, results):
            acc[w >> 16] += result
        return carry

    lax.fori_loop(0, groups, step, 0)
    if last:

        def hand_out(j, carry):
            for i, out in enumerate(parts):
                owner = ((i // 4) ^ place[0]) * 4 + (i % 4 + place[1] & 3)
                out[j] = acc[owner * BLOCKS + j]
            return carry

        lax.fori_loop(0, BLOCKS, hand_out, 0)


def tile_products(place, words, count, tiles, pieces, so_far=None, last=False):
    first = so_far is None
    smem = pl.BlockSpec(memory_space=pltpu.SMEM)
    vmem = pl.BlockSpec(memory_space=pltpu.VMEM)
    hbm = pl.BlockSpec(memory_space=pltpu.HBM)
    sums = pltpu.VMEM((DUMMY + 1, TILE, FEAT), f32)
    going_on = [pltpu.SMEM((TILES + 2 * UNROLL,), jnp.int32), pltpu.SMEM((1,), jnp.int32)]
    part = jax.ShapeDtypeStruct((BLOCKS, TILE, FEAT), f32)
    return pl.pallas_call(
        functools.partial(tile_kernel, len(pieces), first, last),
        out_shape=[part] * BLOCKS
        if last
        else [jax.ShapeDtypeStruct(r.shape, r.dtype) for r in (sums, *going_on)],
        in_specs=[smem, smem, smem, hbm] + [vmem] * (len(pieces) + (not first)),
        out_specs=[vmem] * BLOCKS if last else [vmem, smem, smem],
        scratch_shapes=([sums, *going_on] if last else [])
        + [
            pltpu.VMEM((len(pieces) * BLOCKS, TILE, 2 * FEAT), bf16),
            pltpu.VMEM((DEPTH, UNROLL, TILE, TILE), f32),
            pltpu.SMEM((len(pieces), 8, 128), f32),
            pltpu.SMEM((BUCKETS * BLOCKS,), jnp.int32),
            pltpu.SMEM((TILES + 2 * UNROLL,), jnp.int32),
            pltpu.SemaphoreType.DMA((DEPTH, UNROLL)),
            pltpu.SemaphoreType.DMA((len(pieces),)),
        ],
        compiler_params=pltpu.CompilerParams(vmem_limit_bytes=40 * 2**20),
        cost_estimate=pl.CostEstimate(flops=10**5, bytes_accessed=10**4, transcendentals=0),
    )(place, words, count, tiles, *pieces, *([] if first else [so_far]))


def finish_kernel(a, b, c, d, weight, bias, out):
    total = a[...] + b[...] + c[...] + d[...]
    hidden = product(halves(total.reshape(BLOCKS * TILE, FEAT)), halves(weight[...]))
    out[...] = jnp.maximum(hidden + bias[...], 0.0)


def after(value, *others):
    return lax.optimization_barrier((value, *others))[0]


def body(features, new_slot, tile_values, tile_dest, tile_source, weight, bias_vector):
    move = lax.ppermute
    row = jnp.pad(new_slot.astype(f32)[None, :], ((0, 7), (0, FEAT - BLOCKS)))
    own = jnp.concatenate([features, row])
    below = move(own, "y", UP)
    above = move(own, "y", DOWN)
    far = move(own, "z_hi", SWAP)
    other = move(own, "core", SWAP)

    place = jnp.stack([lax.axis_index("z_lo"), lax.axis_index("x")]).astype(jnp.int32)
    tiles = tile_values.reshape(TILES, TILE, TILE)
    smem = pl.BlockSpec(memory_space=pltpu.SMEM)
    words, count = pl.pallas_call(
        live_kernel,
        out_shape=[
            jax.ShapeDtypeStruct((TILES + 2 * UNROLL,), jnp.int32),
            jax.ShapeDtypeStruct((1,), jnp.int32),
        ],
        in_specs=[smem, smem],
        out_specs=[smem, smem],
        cost_estimate=pl.CostEstimate(flops=10**5, bytes_accessed=10**4, transcendentals=0),
    )(tile_dest.reshape(BUCKETS, SLOTS), tile_source.reshape(BUCKETS, SLOTS))

    below = after(below, words)
    two = move(below, "y", UP)
    far_above = move(far, "y", DOWN)
    far_below = move(below, "z_hi", SWAP)
    swapped = [move(p, "core", SWAP) for p in (below, above, far)]
    sums, words, count = tile_products(place, words, count, tiles, [own, other, below, above, far, *swapped])

    two = after(two, sums)
    far_two = move(two, "z_hi", SWAP)
    late = [two, far_above, far_below]
    swapped = [move(p, "core", SWAP) for p in late]
    sums, words, count = tile_products(place, words, count, tiles, late, sums)

    far_two = after(far_two, sums)
    mine, up, two, down, z_mine, z_up, z_two, z_down = tile_products(
        place, words, count, tiles, [*swapped, far_two, move(far_two, "core", SWAP)], sums, last=True
    )

    half = BLOCKS // 2
    got_two = move(z_two, "z_lo", SWAP)
    got_up = move(z_up, "x", UP)
    got_down = move(z_down, "x", DOWN)
    two_up = move(two[:half] + got_two[:half], "x", UP)
    two_down = move(two[half:] + got_two[half:], "x", DOWN)
    end_z = move(z_mine + got_up + got_down, "z_lo", SWAP)
    end_up = move(jnp.concatenate([up[:half] + two_up, up[half:]]), "x", UP)
    end_down = move(jnp.concatenate([down[:half], down[half:] + two_down]), "x", DOWN)

    return pl.pallas_call(
        finish_kernel,
        out_shape=jax.ShapeDtypeStruct((BLOCKS * TILE, FEAT), f32),
        compiler_params=pltpu.CompilerParams(vmem_limit_bytes=24 * 2**20),
    )(mine, end_up, end_down, end_z, weight, bias_vector.reshape(1, FEAT))


def solution(mesh):
    fine = Mesh(mesh.devices.reshape(2, 4, 2, 4, 2), AXES)
    grp, blk = AXES[:2], AXES[2:]
    return jax.shard_map(
        body,
        mesh=fine,
        in_specs=(
            P(AXES, None),
            P(AXES),
            P(grp, blk, None, None, None, None),
            P(grp, blk, None, None),
            P(grp, blk, None, None),
            P(),
            P(),
        ),
        out_specs=P(AXES, None),
        check_vma=False,
    )
```

time: 120 us -> 104 us (0.87)
  Pallas kernels: 39.9 us -> 26.2 us
  local copies, waits for them, and re-layouts: 6.96 us -> 0.69 us
  starting transfers between devices: 23.3 us -> 27.7 us
  other arithmetic: 3.48 us -> 2.18 us
    pallas_call x1, Pallas kernels: 19.2 us -> 2.86 us  [body(): pl.pallas_call(live_kernel, out_shape=[jax.ShapeDtypeStruct((TILES + 2 *...]
    unnamed x6, local copies, waits for them, and re-layouts: 5.78 us -> 0.69 us
    ppermute x1, waiting for transfers between devices: 0.01 us -> 5.04 us  [body(): below = move(own, 'y', UP)]
    ppermute x1, waiting for transfers between devices: 3.84 us -> 0.01 us  [body(): two = move(below, 'y', UP)]
    ppermute x5 -> x6, starting transfers between devices: 6.72 us -> 10.2 us  [the longest x1 3.76 us: body(): move(jnp.concatenate([down[:half], down[half:] + two_down]), 'x', DOWN)]
    ppermute x5 -> x6, waiting for transfers between devices: 21.5 us -> 18.3 us  [the longest x1 6.51 us: body(): move(jnp.concatenate([down[:half], down[half:] + two_down]), 'x', DOWN)]
    pallas_call x3, Pallas kernels: 19.6 us -> 22.2 us  [tile_products(): pl.pallas_call(functools.partial(tile_kernel, len(pieces), first, last),...]
    ppermute x1, starting transfers between devices: 0.02 us -> 2.31 us  [body(): far_below = move(below, 'z_hi', SWAP)]
  transfers between devices with their start and end apart: 22 -> 23, of which waited for: 12 -> 10; matrix products, arithmetic and copies ran while one was open for 2% -> 0% of each run, Pallas kernels for 29% -> 18%
where the time goes in v5:
time: 104 us; the launch traced here: 103 us
  waiting for transfers between devices  45.9 us (44%)
  starting transfers between devices  27.7 us (27%)
  Pallas kernels  26.2 us (25%)
  other arithmetic  2.18 us (2%)
    pallas_call x3, Pallas kernels, tile_products(): pl.pallas_call(functools.partial(tile_kernel, len(pieces), first, last),...  22.2 us
    ppermute x1, waiting for transfers between devices, body(): got_two = move(z_two, 'z_lo', SWAP)  9.61 us
    ppermute x1, waiting for transfers between devices, body(): far_two = move(two, 'z_hi', SWAP)  7.34 us
    ppermute x1, waiting for transfers between devices, body(): move(jnp.concatenate([down[:half], down[half:] + two_down]), 'x', DOWN)  6.51 us
    ppermute x1, waiting for transfers between devices, body(): below = move(own, 'y', UP)  5.04 us
    ppermute x1, waiting for transfers between devices, body(): two_down = move(two[half:] + got_two[half:], 'x', DOWN)  4.29 us
    ppermute x1, waiting for transfers between devices, body(): end_z = move(z_mine + got_up + got_down, 'z_lo', SWAP)  3.95 us
    ppermute x1, starting transfers between devices, body(): far = move(own, 'z_hi', SWAP)  3.88 us
  transfers between devices with their start and end apart: 23, of which 10 were waited for; matrix products, arithmetic and copies ran while one was open for 0% of the time, Pallas kernels for 18%

profile of v5, /device:TPU:0, one launch (start us, length us, event | category | flops | bytes accessed | tf_op | source)
XLA Modules:
  0.0 102.8 jit_solution(8816243372826611626)
XLA Ops:
  0.0 0.7 convert_bitcast_fusion
  0.7 1.1 %select_maximum_fusion.refs_4_ = f32[1032,128]{1,0:T(8,128)S(1)} fusion(f32[1,8]{1,0:T(1,128)S(1)} %convert_bitcast_fusion, f32[1024,128]{1,0:T(8,128)} %param.7), kind=kLoop, calls=%fused_computation | loop fusion | flops 396288 | bytes 1052704 | tf_op jit(solution)/shard_map/concatenate | solution.py:197
  1.7 1.7 %collective-permute-start.1 = (f32[1032,128]{1,0:T(8,128)S(1)}, f32[1032,128]{1,0:T(8,128)S(1)}, u32[]{:S(2)}, u32[]{:S(2)}) collective-permute-start(f32[1032,128]{1,0:T(8,128)S(1)} %select_maximum_fusion.refs_4_), channel_id=1, source_target_pairs={{0,2},{2,4},{4,6},{6,0},{1,3},{3,5},{5,7},{7,1},{8,10},{10,12},{12... | collective-permute-start | bytes 1585160 | tf_op jit(solution)/shard_map/ppermute | solution.py:198
  3.5 3.9 %collective-permute-start.3 = (f32[1032,128]{1,0:T(8,128)S(1)}, f32[1032,128]{1,0:T(8,128)S(1)}, u32[]{:S(2)}, u32[]{:S(2)}) collective-permute-start(f32[1032,128]{1,0:T(8,128)S(1)} %select_maximum_fusion.refs_4_), channel_id=1, source_target_pairs={{0,8},{8,0},{1,9},{9,1},{2,10},{10,2},{3,11},{11,3},{4,12},{12,4},... | collective-permute-start | bytes 1585160 | tf_op jit(solution)/shard_map/ppermute | solution.py:200
  7.3 1.7 %collective-permute-start.2 = (f32[1032,128]{1,0:T(8,128)S(1)}, f32[1032,128]{1,0:T(8,128)S(1)}, u32[]{:S(2)}, u32[]{:S(2)}) collective-permute-start(f32[1032,128]{1,0:T(8,128)S(1)} %select_maximum_fusion.refs_4_), channel_id=1, source_target_pairs={{0,6},{2,0},{4,2},{6,4},{1,7},{3,1},{5,3},{7,5},{8,14},{10,8},{12,... | collective-permute-start | bytes 1585160 | tf_op jit(solution)/shard_map/ppermute | solution.py:199
  9.0 0.0 collective-permute-start
  9.0 2.9 %shard_map.73 = (s32[272]{0:T(512)}, s32[1]{0:T(128)}) custom-call(s32[16,16]{1,0:T(8,128)} %bitcast.12, s32[16,16]{1,0:T(8,128)} %bitcast.13), custom_call_target="tpu_custom_call" | custom-call | flops 100000 | bytes 10000 | tf_op jit(solution)/shard_map/pallas_call | solution.py:206
  11.9 5.0 %collective-permute-done.1.refs_6_ = f32[1032,128]{1,0:T(8,128)S(1)} collective-permute-done((f32[1032,128]{1,0:T(8,128)S(1)}, f32[1032,128]{1,0:T(8,128)S(1)}, u32[]{:S(2)}, u32[]{:S(2)}) %collective-permute-start.1) | collective-permute-done | bytes 528416 | tf_op jit(solution)/shard_map/ppermute | solution.py:198
  16.9 0.0 collective-permute-start.4
  16.9 2.2 %collective-permute-done.3.refs_8_ = f32[1032,128]{1,0:T(8,128)S(1)} collective-permute-done((f32[1032,128]{1,0:T(8,128)S(1)}, f32[1032,128]{1,0:T(8,128)S(1)}, u32[]{:S(2)}, u32[]{:S(2)}) %collective-permute-start.3) | collective-permute-done | bytes 528416 | tf_op jit(solution)/shard_map/ppermute | solution.py:200
  19.1 1.5 %collective-permute-done.2.refs_7_ = f32[1032,128]{1,0:T(8,128)S(1)} collective-permute-done((f32[1032,128]{1,0:T(8,128)S(1)}, f32[1032,128]{1,0:T(8,128)S(1)}, u32[]{:S(2)}, u32[]{:S(2)}) %collective-permute-start.2) | collective-permute-done | bytes 528416 | tf_op jit(solution)/shard_map/ppermute | solution.py:199
  20.5 0.0 collective-permute-start.5
  20.5 1.6 %collective-permute-start.7 = (f32[1032,128]{1,0:T(8,128)S(1)}, f32[1032,128]{1,0:T(8,128)S(1)}, u32[]{:S(2)}, u32[]{:S(2)}) collective-permute-start(f32[1032,128]{1,0:T(8,128)S(1)} %collective-permute-done.1.refs_6_), channel_id=1, source_target_pairs={{0,2},{2,4},{4,6},{6,0},{1,3},{3,5},{5,7},{7,1},{8,10},{10,12},{12... | collective-permute-start | bytes 1585160 | tf_op jit(solution)/shard_map/ppermute | solution.py:218
  22.1 0.1 pad_add_fusion.refs_0_
  22.2 0.0 collective-permute-done.refs_5_
  22.2 2.3 %collective-permute-start.9 = (f32[1032,128]{1,0:T(8,128)S(1)}, f32[1032,128]{1,0:T(8,128)S(1)}, u32[]{:S(2)}, u32[]{:S(2)}) collective-permute-start(f32[1032,128]{1,0:T(8,128)S(1)} %collective-permute-done.1.refs_6_), channel_id=1, source_target_pairs={{0,8},{8,0},{1,9},{9,1},{2,10},{10,2},{3,11},{11,3},{4,12},{12,4},... | collective-permute-start | bytes 1585160 | tf_op jit(solution)/shard_map/ppermute | solution.py:220
  24.5 0.0 collective-permute-done.4.refs_9_
  24.5 1.7 %collective-permute-start.8 = (f32[1032,128]{1,0:T(8,128)S(1)}, f32[1032,128]{1,0:T(8,128)S(1)}, u32[]{:S(2)}, u32[]{:S(2)}) collective-permute-start(f32[1032,128]{1,0:T(8,128)S(1)} %collective-permute-done.3.refs_8_), channel_id=1, source_target_pairs={{0,6},{2,0},{4,2},{6,4},{1,7},{3,1},{5,3},{7,5},{8,14},{10,8},{12,... | collective-permute-start | bytes 1585160 | tf_op jit(solution)/shard_map/ppermute | solution.py:219
  26.2 0.0 collective-permute-done.6.refs_11_
  26.2 0.7 copy-done.1
  26.9 9.6 %shard_map.74 = (f32[65,128,128]{2,1,0:T(8,128)S(1)}, s32[272]{0:T(512)S(1)}, s32[1]{0:T(128)}) custom-call(s32[2]{0:T(128)S(1)} %pad_add_fusion.refs_0_, s32[272]{0:T(512)S(1)} %copy-done.1, s32[1]{0:T(128)} %get-tuple-element.25.refs_2_, f32[256,128,128]{2,1,0:T(8,128)} %bitcast.9, f32[1032,128]{1,0:T(8,128)S(1)} %select_maximum_fusion.refs_4_, ...), custom_call_target="tpu_custom_call" | custom-call | flops 100000 | bytes 10000 | tf_op jit(solution)/shard_map/pallas_call | solution.py:162
  36.5 1.8 %collective-permute-start.13 = (f32[1032,128]{1,0:T(8,128)S(1)}, f32[1032,128]{1,0:T(8,128)S(1)}, u32[]{:S(2)}, u32[]{:S(2)}) collective-permute-start(f32[1032,128]{1,0:T(8,128)S(1)} %collective-permute-done.7.refs_4_), channel_id=1, source_target_pairs={{0,8},{8,0},{1,9},{9,1},{2,10},{10,2},{3,11},{11,3},{4,12},{12,4},... | collective-permute-start | bytes 1585160 | tf_op jit(solution)/shard_map/ppermute | solution.py:225
  38.3 0.5 collective-permute-start.12
  38.8 0.1 collective-permute-start.11
  38.9 5.7 %shard_map.75 = (f32[65,128,128]{2,1,0:T(8,128)S(1)}, s32[272]{0:T(512)S(1)}, s32[1]{0:T(128)}) custom-call(s32[2]{0:T(128)S(1)} %pad_add_fusion.refs_0_, s32[272]{0:T(512)S(1)} %get-tuple-element.27.refs_1_, s32[1]{0:T(128)} %get-tuple-element.28.refs_2_, f32[256,128,128]{2,1,0:T(8,128)} %bitcast.10, f32[1032,128]{1,0:T(8,128)S(1)} %collective-permute-done.7.refs_4_, ...), custom_call_target="tpu_custom_call" | custom-call | flops 100000 | bytes 10000 | tf_op jit(solution)/shard_map/pallas_call | solution.py:162
  44.6 7.3 %collective-permute-done.13.refs_7_ = f32[1032,128]{1,0:T(8,128)S(1)} collective-permute-done((f32[1032,128]{1,0:T(8,128)S(1)}, f32[1032,128]{1,0:T(8,128)S(1)}, u32[]{:S(2)}, u32[]{:S(2)}) %collective-permute-start.13) | collective-permute-done | bytes 528416 | tf_op jit(solution)/shard_map/ppermute | solution.py:225
  51.9 1.9 %collective-permute-done.14.refs_8_ = f32[1032,128]{1,0:T(8,128)S(1)} collective-permute-done((f32[1032,128]{1,0:T(8,128)S(1)}, f32[1032,128]{1,0:T(8,128)S(1)}, u32[]{:S(2)}, u32[]{:S(2)}) %collective-permute-start.14) | collective-permute-done | bytes 528416 | tf_op jit(solution)/shard_map/ppermute | solution.py:232
  53.8 6.9 %shard_map.76 = (f32[8,128,128]{2,1,0:T(8,128)S(1)}, f32[8,128,128]{2,1,0:T(8,128)S(1)}, f32[8,128,128]{2,1,0:T(8,128)S(1)}, f32[8,128,128]{2,1,0:T(8,128)S(1)},...) custom-call(s32[2]{0:T(128)S(1)} %pad_add_fusion.refs_0_, ...), custom_call_target="tpu_custom_call" | custom-call | flops 100000 | bytes 10000 | tf_op jit(solution)/shard_map/pallas_call | solution.py:162
  60.7 0.0 copy-start
  60.8 0.0 copy-start.2
  60.8 0.4 collective-permute-start.15
  61.1 1.3 %collective-permute-start.20 = (f32[8,128,128]{2,1,0:T(8,128)S(1)}, f32[8,128,128]{2,1,0:T(8,128)S(1)}, u32[]{:S(2)}, u32[]{:S(2)}) collective-permute-start(f32[8,128,128]{2,1,0:T(8,128)S(1)} %get-tuple-element.41), channel_id=1, source_target_pairs={{0,16},{16,32},{32,48},{48,0},{1,17},{17,33},{33,49},{49,1},{2,18}... | collective-permute-start | bytes 1572872 | tf_op jit(solution)/shard_map/ppermute | solution.py:237
  62.5 1.9 %collective-permute-start.21 = (f32[8,128,128]{2,1,0:T(8,128)S(1)}, f32[8,128,128]{2,1,0:T(8,128)S(1)}, u32[]{:S(2)}, u32[]{:S(2)}) collective-permute-start(f32[8,128,128]{2,1,0:T(8,128)S(1)} %get-tuple-element.42), channel_id=1, source_target_pairs={{0,48},{16,0},{32,16},{48,32},{1,49},{17,1},{33,17},{49,33},{2,50}... | collective-permute-start | bytes 1572872 | tf_op jit(solution)/shard_map/ppermute | solution.py:238
  64.4 9.6 %collective-permute-done.15 = f32[8,128,128]{2,1,0:T(8,128)S(1)} collective-permute-done((f32[8,128,128]{2,1,0:T(8,128)S(1)}, f32[8,128,128]{2,1,0:T(8,128)S(1)}, u32[]{:S(2)}, u32[]{:S(2)}) %collective-permute-start.15) | collective-permute-done | bytes 524320 | tf_op jit(solution)/shard_map/ppermute | solution.py:236
  74.0 0.1 slice_add_fusion
  74.1 3.6 %collective-permute-start.18 = (f32[4,128,128]{2,1,0:T(8,128)S(1)}, f32[4,128,128]{2,1,0:T(8,128)S(1)}, u32[]{:S(2)}, u32[]{:S(2)}) collective-permute-start(f32[4,128,128]{2,1,0:T(8,128)S(1)} %get-tuple-element.43), channel_id=1, source_target_pairs={{0,48},{16,0},{32,16},{48,32},{1,49},{17,1},{33,17},{49,33},{2,50}... | collective-permute-start | bytes 786440 | tf_op jit(solution)/shard_map/ppermute | solution.py:240
  77.7 0.1 add_add_fusion
  77.8 0.7 collective-permute-start.22
  78.5 0.8 collective-permute-start.16
  79.2 4.3 %collective-permute-done.18 = f32[4,128,128]{2,1,0:T(8,128)S(1)} collective-permute-done((f32[4,128,128]{2,1,0:T(8,128)S(1)}, f32[4,128,128]{2,1,0:T(8,128)S(1)}, u32[]{:S(2)}, u32[]{:S(2)}) %collective-permute-start.18) | collective-permute-done | bytes 262176 | tf_op jit(solution)/shard_map/ppermute | solution.py:240
  83.5 0.1 fusion
  83.6 3.8 %collective-permute-start.19 = (f32[8,128,128]{2,1,0:T(8,128)S(1)}, f32[8,128,128]{2,1,0:T(8,128)S(1)}, u32[]{:S(2)}, u32[]{:S(2)}) collective-permute-start(f32[8,128,128]{2,1,0:T(8,128)S(1)} %pad_maximum_fusion.1), channel_id=1, source_target_pairs={{0,48},{16,0},{32,16},{48,32},{1,49},{17,1},{33,17},{49,33},{2,50}... | collective-permute-start | bytes 1572872 | tf_op jit(solution)/shard_map/ppermute | solution.py:243
  87.4 0.1 slice_add_fusion.3
  87.5 0.1 collective-permute-start.17
  87.6 4.0 %collective-permute-done.22.d = f32[8,128,128]{2,1,0:T(8,128)S(1)} collective-permute-done((f32[8,128,128]{2,1,0:T(8,128)S(1)}, f32[8,128,128]{2,1,0:T(8,128)S(1)}, u32[]{:S(2)}, u32[]{:S(2)}) %collective-permute-start.22) | collective-permute-done | bytes 524320 | tf_op jit(solution)/shard_map/ppermute | solution.py:241
  91.5 6.5 %collective-permute-done.19.c = f32[8,128,128]{2,1,0:T(8,128)S(1)} collective-permute-done((f32[8,128,128]{2,1,0:T(8,128)S(1)}, f32[8,128,128]{2,1,0:T(8,128)S(1)}, u32[]{:S(2)}, u32[]{:S(2)}) %collective-permute-start.19) | collective-permute-done | bytes 524320 | tf_op jit(solution)/shard_map/ppermute | solution.py:243
  98.0 3.6 %collective-permute-done.17.b = f32[8,128,128]{2,1,0:T(8,128)S(1)} collective-permute-done((f32[8,128,128]{2,1,0:T(8,128)S(1)}, f32[8,128,128]{2,1,0:T(8,128)S(1)}, u32[]{:S(2)}, u32[]{:S(2)}) %collective-permute-start.17) | collective-permute-done | bytes 524320 | tf_op jit(solution)/shard_map/ppermute | solution.py:242
  101.6 1.1 %shard_map.77 = f32[1024,128]{1,0:T(8,128)} custom-call(f32[8,128,128]{2,1,0:T(8,128)S(1)} %get-tuple-element.35.a, f32[8,128,128]{2,1,0:T(8,128)S(1)} %collective-permute-done.17.b, f32[8,128,128]{2,1,0:T(8,128)S(1)} %collective-permute-done.19.c, f32[8,128,128]{2,1,0:T(8,128)S(1)} %collective-permute-done.22.d, f32[128,128]{1,0:T(8,128)S(1)} %copy-done, ...), custom_call_target="tpu_custom_call" | custom-call | tf_op jit(solution)/shard_map/pallas_call | solution.py:245
  (18 shorter events, 0.1 us)
Async XLA Ops:
  1.7 15.2 %collective-permute-start.1 = (f32[1032,128]{1,0:T(8,128)S(1)}, f32[1032,128]{1,0:T(8,128)S(1)}, u32[]{:S(2)}, u32[]{:S(2)}) collective-permute-start(f32[1032,128]{1,0:T(8,128)S(1)} %select_maximum_fusion.refs_4_), channel_id=1, source_target_pairs={{0,2},{2,4},{4,6},{6,0},{1,3},{3,5},{5,7},{7,1},{8,10},{10,12},{12... | collective-permute-start | bytes 1585160 | tf_op jit(solution)/shard_map/ppermute | solution.py:198
  3.5 15.6 %collective-permute-start.3 = (f32[1032,128]{1,0:T(8,128)S(1)}, f32[1032,128]{1,0:T(8,128)S(1)}, u32[]{:S(2)}, u32[]{:S(2)}) collective-permute-start(f32[1032,128]{1,0:T(8,128)S(1)} %select_maximum_fusion.refs_4_), channel_id=1, source_target_pairs={{0,8},{8,0},{1,9},{9,1},{2,10},{10,2},{3,11},{11,3},{4,12},{12,4},... | collective-permute-start | bytes 1585160 | tf_op jit(solution)/shard_map/ppermute | solution.py:200
  7.3 13.2 %collective-permute-start.2 = (f32[1032,128]{1,0:T(8,128)S(1)}, f32[1032,128]{1,0:T(8,128)S(1)}, u32[]{:S(2)}, u32[]{:S(2)}) collective-permute-start(f32[1032,128]{1,0:T(8,128)S(1)} %select_maximum_fusion.refs_4_), channel_id=1, source_target_pairs={{0,6},{2,0},{4,2},{6,4},{1,7},{3,1},{5,3},{7,5},{8,14},{10,8},{12,... | collective-permute-start | bytes 1585160 | tf_op jit(solution)/shard_map/ppermute | solution.py:199
  9.0 13.2 %collective-permute-start = (f32[1032,128]{1,0:T(8,128)S(1)}, f32[1032,128]{1,0:T(8,128)S(1)}, u32[]{:S(2)}, u32[]{:S(2)}) collective-permute-start(f32[1032,128]{1,0:T(8,128)S(1)} %select_maximum_fusion.refs_4_), channel_id=1, source_target_pairs={{0,1},{1,0},{2,3},{3,2},{4,5},{5,4},{6,7},{7,6},{8,9},{9,8},{10,11... | collective-permute-start | bytes 1585160 | tf_op jit(solution)/shard_map/ppermute | solution.py:201
  16.9 7.6 %collective-permute-start.4 = (f32[1032,128]{1,0:T(8,128)S(1)}, f32[1032,128]{1,0:T(8,128)}, u32[]{:S(2)}, u32[]{:S(2)}) collective-permute-start(f32[1032,128]{1,0:T(8,128)S(1)} %collective-permute-done.1.refs_6_), channel_id=1, source_target_pairs={{0,1},{1,0},{2,3},{3,2},{4,5},{5,4},{6,7},{7,6},{8,9},{9,8},{10,11... | collective-permute-start | bytes 1585160 | tf_op jit(solution)/shard_map/ppermute | solution.py:221
  19.1 7.1 %collective-permute-start.6 = (f32[1032,128]{1,0:T(8,128)S(1)}, f32[1032,128]{1,0:T(8,128)}, u32[]{:S(2)}, u32[]{:S(2)}) collective-permute-start(f32[1032,128]{1,0:T(8,128)S(1)} %collective-permute-done.3.refs_8_), channel_id=1, source_target_pairs={{0,1},{1,0},{2,3},{3,2},{4,5},{5,4},{6,7},{7,6},{8,9},{9,8},{10,11... | collective-permute-start | bytes 1585160 | tf_op jit(solution)/shard_map/ppermute | solution.py:221
  20.5 5.6 %collective-permute-start.5 = (f32[1032,128]{1,0:T(8,128)S(1)}, f32[1032,128]{1,0:T(8,128)}, u32[]{:S(2)}, u32[]{:S(2)}) collective-permute-start(f32[1032,128]{1,0:T(8,128)S(1)} %collective-permute-done.2.refs_7_), channel_id=1, source_target_pairs={{0,1},{1,0},{2,3},{3,2},{4,5},{5,4},{6,7},{7,6},{8,9},{9,8},{10,11... | collective-permute-start | bytes 1585160 | tf_op jit(solution)/shard_map/ppermute | solution.py:221
  20.5 15.9 %collective-permute-start.7 = (f32[1032,128]{1,0:T(8,128)S(1)}, f32[1032,128]{1,0:T(8,128)S(1)}, u32[]{:S(2)}, u32[]{:S(2)}) collective-permute-start(f32[1032,128]{1,0:T(8,128)S(1)} %collective-permute-done.1.refs_6_), channel_id=1, source_target_pairs={{0,2},{2,4},{4,6},{6,0},{1,3},{3,5},{5,7},{7,1},{8,10},{10,12},{12... | collective-permute-start | bytes 1585160 | tf_op jit(solution)/shard_map/ppermute | solution.py:218
  22.2 16.1 %collective-permute-start.9 = (f32[1032,128]{1,0:T(8,128)S(1)}, f32[1032,128]{1,0:T(8,128)S(1)}, u32[]{:S(2)}, u32[]{:S(2)}) collective-permute-start(f32[1032,128]{1,0:T(8,128)S(1)} %collective-permute-done.1.refs_6_), channel_id=1, source_target_pairs={{0,8},{8,0},{1,9},{9,1},{2,10},{10,2},{3,11},{11,3},{4,12},{12,4},... | collective-permute-start | bytes 1585160 | tf_op jit(solution)/shard_map/ppermute | solution.py:220
  24.5 14.3 %collective-permute-start.8 = (f32[1032,128]{1,0:T(8,128)S(1)}, f32[1032,128]{1,0:T(8,128)S(1)}, u32[]{:S(2)}, u32[]{:S(2)}) collective-permute-start(f32[1032,128]{1,0:T(8,128)S(1)} %collective-permute-done.3.refs_8_), channel_id=1, source_target_pairs={{0,6},{2,0},{4,2},{6,4},{1,7},{3,1},{5,3},{7,5},{8,14},{10,8},{12,... | collective-permute-start | bytes 1585160 | tf_op jit(solution)/shard_map/ppermute | solution.py:219
  26.2 0.7 copy-start.1
  36.5 15.4 %collective-permute-start.13 = (f32[1032,128]{1,0:T(8,128)S(1)}, f32[1032,128]{1,0:T(8,128)S(1)}, u32[]{:S(2)}, u32[]{:S(2)}) collective-permute-start(f32[1032,128]{1,0:T(8,128)S(1)} %collective-permute-done.7.refs_4_), channel_id=1, source_target_pairs={{0,8},{8,0},{1,9},{9,1},{2,10},{10,2},{3,11},{11,3},{4,12},{12,4},... | collective-permute-start | bytes 1585160 | tf_op jit(solution)/shard_map/ppermute | solution.py:225
  38.3 13.6 %collective-permute-start.10 = (f32[1032,128]{1,0:T(8,128)S(1)}, f32[1032,128]{1,0:T(8,128)S(1)}, u32[]{:S(2)}, u32[]{:S(2)}) collective-permute-start(f32[1032,128]{1,0:T(8,128)S(1)} %collective-permute-done.7.refs_4_), channel_id=1, source_target_pairs={{0,1},{1,0},{2,3},{3,2},{4,5},{5,4},{6,7},{7,6},{8,9},{9,8},{10,11... | collective-permute-start | bytes 1585160 | tf_op jit(solution)/shard_map/ppermute | solution.py:227
  38.3 13.6 %collective-permute-start.12 = (f32[1032,128]{1,0:T(8,128)S(1)}, f32[1032,128]{1,0:T(8,128)S(1)}, u32[]{:S(2)}, u32[]{:S(2)}) collective-permute-start(f32[1032,128]{1,0:T(8,128)S(1)} %collective-permute-done.9.refs_6_), channel_id=1, source_target_pairs={{0,1},{1,0},{2,3},{3,2},{4,5},{5,4},{6,7},{7,6},{8,9},{9,8},{10,11... | collective-permute-start | bytes 1585160 | tf_op jit(solution)/shard_map/ppermute | solution.py:227
  38.8 13.1 %collective-permute-start.11 = (f32[1032,128]{1,0:T(8,128)S(1)}, f32[1032,128]{1,0:T(8,128)S(1)}, u32[]{:S(2)}, u32[]{:S(2)}) collective-permute-start(f32[1032,128]{1,0:T(8,128)S(1)} %collective-permute-done.8.refs_5_), channel_id=1, source_target_pairs={{0,1},{1,0},{2,3},{3,2},{4,5},{5,4},{6,7},{7,6},{8,9},{9,8},{10,11... | collective-permute-start | bytes 1585160 | tf_op jit(solution)/shard_map/ppermute | solution.py:227
  51.9 1.9 %collective-permute-start.14 = (f32[1032,128]{1,0:T(8,128)S(1)}, f32[1032,128]{1,0:T(8,128)S(1)}, u32[]{:S(2)}, u32[]{:S(2)}) collective-permute-start(f32[1032,128]{1,0:T(8,128)S(1)} %collective-permute-done.13.refs_7_), channel_id=1, source_target_pairs={{0,1},{1,0},{2,3},{3,2},{4,5},{5,4},{6,7},{7,6},{8,9},{9,8},{10,11... | collective-permute-start | bytes 1585160 | tf_op jit(solution)/shard_map/ppermute | solution.py:232
  60.7 40.9 %copy-start = (f32[128,128]{1,0:T(8,128)S(1)}, f32[128,128]{1,0:T(8,128)}, u32[]{:S(2)}) copy-start(f32[128,128]{1,0:T(8,128)} %weight.1) | copy-start | bytes 196612
  60.8 40.9 %copy-start.2 = (f32[128]{0:T(128)S(1)}, f32[128]{0:T(128)}, u32[]{:S(2)}) copy-start(f32[128]{0:T(128)} %param.13) | copy-start | bytes 1540
  60.8 13.2 %collective-permute-start.15 = (f32[8,128,128]{2,1,0:T(8,128)S(1)}, f32[8,128,128]{2,1,0:T(8,128)S(1)}, u32[]{:S(2)}, u32[]{:S(2)}) collective-permute-start(f32[8,128,128]{2,1,0:T(8,128)S(1)} %get-tuple-element.38), channel_id=1, source_target_pairs={{0,64},{64,0},{1,65},{65,1},{2,66},{66,2},{3,67},{67,3},{4,68},{68... | collective-permute-start | bytes 1572872 | tf_op jit(solution)/shard_map/ppermute | solution.py:236
  61.1 16.5 %collective-permute-start.20 = (f32[8,128,128]{2,1,0:T(8,128)S(1)}, f32[8,128,128]{2,1,0:T(8,128)S(1)}, u32[]{:S(2)}, u32[]{:S(2)}) collective-permute-start(f32[8,128,128]{2,1,0:T(8,128)S(1)} %get-tuple-element.41), channel_id=1, source_target_pairs={{0,16},{16,32},{32,48},{48,0},{1,17},{17,33},{33,49},{49,1},{2,18}... | collective-permute-start | bytes 1572872 | tf_op jit(solution)/shard_map/ppermute | solution.py:237
  62.5 15.2 %collective-permute-start.21 = (f32[8,128,128]{2,1,0:T(8,128)S(1)}, f32[8,128,128]{2,1,0:T(8,128)S(1)}, u32[]{:S(2)}, u32[]{:S(2)}) collective-permute-start(f32[8,128,128]{2,1,0:T(8,128)S(1)} %get-tuple-element.42), channel_id=1, source_target_pairs={{0,48},{16,0},{32,16},{48,32},{1,49},{17,1},{33,17},{49,33},{2,50}... | collective-permute-start | bytes 1572872 | tf_op jit(solution)/shard_map/ppermute | solution.py:238
  74.1 9.5 %collective-permute-start.18 = (f32[4,128,128]{2,1,0:T(8,128)S(1)}, f32[4,128,128]{2,1,0:T(8,128)S(1)}, u32[]{:S(2)}, u32[]{:S(2)}) collective-permute-start(f32[4,128,128]{2,1,0:T(8,128)S(1)} %get-tuple-element.43), channel_id=1, source_target_pairs={{0,48},{16,0},{32,16},{48,32},{1,49},{17,1},{33,17},{49,33},{2,50}... | collective-permute-start | bytes 786440 | tf_op jit(solution)/shard_map/ppermute | solution.py:240
  77.8 13.8 %collective-permute-start.22 = (f32[8,128,128]{2,1,0:T(8,128)S(1)}, f32[8,128,128]{2,1,0:T(8,128)S(1)}, u32[]{:S(2)}, u32[]{:S(2)}) collective-permute-start(f32[8,128,128]{2,1,0:T(8,128)S(1)} %add_add_fusion), channel_id=1, source_target_pairs={{0,64},{64,0},{1,65},{65,1},{2,66},{66,2},{3,67},{67,3},{4,68},{68... | collective-permute-start | bytes 1572872 | tf_op jit(solution)/shard_map/ppermute | solution.py:241
  78.5 8.9 %collective-permute-start.16 = (f32[4,128,128]{2,1,0:T(8,128)S(1)}, f32[4,128,128]{2,1,0:T(8,128)S(1)}, u32[]{:S(2)}, u32[]{:S(2)}) collective-permute-start(f32[4,128,128]{2,1,0:T(8,128)S(1)} %get-tuple-element.44), channel_id=1, source_target_pairs={{0,16},{16,32},{32,48},{48,0},{1,17},{17,33},{33,49},{49,1},{2,18}... | collective-permute-start | bytes 786440 | tf_op jit(solution)/shard_map/ppermute | solution.py:239
  83.6 14.4 %collective-permute-start.19 = (f32[8,128,128]{2,1,0:T(8,128)S(1)}, f32[8,128,128]{2,1,0:T(8,128)S(1)}, u32[]{:S(2)}, u32[]{:S(2)}) collective-permute-start(f32[8,128,128]{2,1,0:T(8,128)S(1)} %pad_maximum_fusion.1), channel_id=1, source_target_pairs={{0,48},{16,0},{32,16},{48,32},{1,49},{17,1},{33,17},{49,33},{2,50}... | collective-permute-start | bytes 1572872 | tf_op jit(solution)/shard_map/ppermute | solution.py:243
  87.5 14.1 %collective-permute-start.17 = (f32[8,128,128]{2,1,0:T(8,128)S(1)}, f32[8,128,128]{2,1,0:T(8,128)S(1)}, u32[]{:S(2)}, u32[]{:S(2)}) collective-permute-start(f32[8,128,128]{2,1,0:T(8,128)S(1)} %pad_maximum_fusion), channel_id=1, source_target_pairs={{0,16},{16,32},{32,48},{48,0},{1,17},{17,33},{33,49},{49,1},{2,18}... | collective-permute-start | bytes 1572872 | tf_op jit(solution)/shard_map/ppermute | solution.py:242

commit v6 on v5

--- a/solution.py
+++ b/solution.py
@@ -13,8 +13,9 @@
 SLOTS = 16
 BUCKETS = 16
 TILES = BUCKETS * SLOTS
-UNROLL = 8
-DEPTH = 6
+STEP = 16
+LAST_STEP = 8
+RING = 48
 DUMMY = 64
 
 AXES = ("z_lo", "x", "z_hi", "y", "core")
@@ -49,7 +50,7 @@
 
     total = lax.fori_loop(0, BUCKETS, bucket, 0)
     count[0] = total
-    for j in range(UNROLL):
+    for j in range(STEP):
         words[total + j] = -1
 
 
@@ -60,12 +61,12 @@
     so_far = None if first else refs[3 + n_pieces]
     outs = refs[4 + n_pieces - first :]
     if last:
-        parts, (acc, rest, left) = outs[:BLOCKS], outs[BLOCKS : BLOCKS + 3]
-        scratch = outs[BLOCKS + 3 :]
+        parts, (acc, *scratch) = outs[:BLOCKS], outs[BLOCKS:]
     else:
-        acc, rest, left = outs[:3]
-        scratch = outs[3:]
-    xs, ring, slots, table, mine, ring_sem, slot_sem = scratch
+        acc, rest, left, mine, *scratch = outs
+    xs, ring, slots, table, ring_sem, slot_sem = scratch
+    size = LAST_STEP if last else STEP
+    depth = RING // size
 
     reads = [
         pltpu.make_async_copy(piece.at[pl.ds(BLOCKS * TILE, 8)], slots.at[i], slot_sem.at[i])
@@ -73,8 +74,34 @@
     ]
     for read in reads:
         read.start()
-    for p in range(BUCKETS * BLOCKS):
-        table[p] = -1
+
+    def fetch(group):
+        slot = group % depth
+        for j in range(size):
+            pltpu.make_async_copy(
+                tiles.at[todo[group * size + j] & 255], ring.at[slot, j], ring_sem.at[slot, j]
+            ).start()
+
+    def fetch_first():
+        for group in range(depth - 1):
+
+            @pl.when(group < groups)
+            def _(group=group):
+                fetch(group)
+
+    if last:
+        todo, here = words, count[0]
+        groups = (here + size - 1) // size
+        fetch_first()
+    else:
+        for p in range(BUCKETS * BLOCKS):
+            table[p] = -1
+
+    def begin(d, carry):
+        acc[d] = jnp.zeros((TILE, FEAT), f32) if first else so_far[d]
+        return carry
+
+    lax.fori_loop(0, DUMMY + 1, begin, 0, unroll=5)
     for read in reads:
         read.wait()
     for i in range(n_pieces):
@@ -83,34 +110,24 @@
 
     def sort(group, n):
         here, there = n
-        loaded = [words[group * UNROLL + j] for j in range(UNROLL)]
+        loaded = [words[group * 8 + j] for j in range(8)]
         found = [table[(word >> 8) & 127] for word in loaded]
         for word, s in zip(loaded, found):
             live = (word >= 0).astype(jnp.int32)
             known = jnp.where(s >= 0, live, 0)
-            mine[here] = (word & 0xFF00FF) | (s << 8)
+            mine[here] = word
             rest[there] = word
             here, there = here + known, there + live - known
         return here, there
 
-    here, there = lax.fori_loop(0, (count[0] + UNROLL - 1) // UNROLL, sort, (0, 0))
-    left[0] = there
-    for j in range(UNROLL):
-        mine[here + j] = DUMMY * 65536
-        rest[there + j] = -1
-    groups = (here + UNROLL - 1) // UNROLL
-
-    def fetch(group):
-        slot = group % DEPTH
-        for j in range(UNROLL):
-            at = mine[group * UNROLL + j] & 255
-            pltpu.make_async_copy(tiles.at[at], ring.at[slot, j], ring_sem.at[slot, j]).start()
-
-    for group in range(DEPTH - 1):
-
-        @pl.when(group < groups)
-        def _(group=group):
-            fetch(group)
+    if not last:
+        here, there = lax.fori_loop(0, (count[0] + 7) // 8, sort, (0, 0))
+        left[0] = there
+        for j in range(STEP):
+            mine[here + j] = -1
+            rest[there + j] = -1
+        todo, groups = mine, (here + size - 1) // size
+        fetch_first()
 
     def halve(j, carry):
         for i, piece in enumerate(pieces):
@@ -119,24 +136,21 @@
 
     lax.fori_loop(0, BLOCKS, halve, 0)
 
-    def begin(d, carry):
-        acc[d] = jnp.zeros((TILE, FEAT), f32) if first else so_far[d]
-        return carry
-
-    lax.fori_loop(0, DUMMY + 1, begin, 0, unroll=5)
-
     def step(group, carry):
-        @pl.when(group + DEPTH - 1 < groups)
+        @pl.when(group + depth - 1 < groups)
         def _():
-            fetch(group + DEPTH - 1)
-
-        slot = group % DEPTH
-        own = [mine[group * UNROLL + j] for j in range(UNROLL)]
-        for j in range(UNROLL):
+            fetch(group + depth - 1)
+
+        slot = group % depth
+        own = [todo[group * size + j] for j in range(size)]
+        live = [w >= 0 for w in own]
+        source = [jnp.where(l, table[(w >> 8) & 127], 0) for w, l in zip(own, live)]
+        target = [jnp.where(l, w >> 16, DUMMY) for w, l in zip(own, live)]
+        for j in range(size):
             pltpu.make_async_copy(tiles.at[0], ring.at[slot, j], ring_sem.at[slot, j]).wait()
-        results = [product(halves(ring[slot, j]), xs[(own[j] >> 8) & 127]) for j in range(UNROLL)]
-        for w, result in zip(own, results):
-            acc[w >> 16] += result
+        results = [product(halves(ring[slot, j]), xs[source[j]]) for j in range(size)]
+        for d, result in zip(target, results):
+            acc[d] += result
         return carry
 
     lax.fori_loop(0, groups, step, 0)
@@ -153,11 +167,12 @@
 
 def tile_products(place, words, count, tiles, pieces, so_far=None, last=False):
     first = so_far is None
+    size = LAST_STEP if last else STEP
     smem = pl.BlockSpec(memory_space=pltpu.SMEM)
     vmem = pl.BlockSpec(memory_space=pltpu.VMEM)
     hbm = pl.BlockSpec(memory_space=pltpu.HBM)
     sums = pltpu.VMEM((DUMMY + 1, TILE, FEAT), f32)
-    going_on = [pltpu.SMEM((TILES + 2 * UNROLL,), jnp.int32), pltpu.SMEM((1,), jnp.int32)]
+    going_on = [pltpu.SMEM((TILES + 2 * STEP,), jnp.int32), pltpu.SMEM((1,), jnp.int32)]
     part = jax.ShapeDtypeStruct((BLOCKS, TILE, FEAT), f32)
     return pl.pallas_call(
         functools.partial(tile_kernel, len(pieces), first, last),
@@ -166,14 +181,13 @@
         else [jax.ShapeDtypeStruct(r.shape, r.dtype) for r in (sums, *going_on)],
         in_specs=[smem, smem, smem, hbm] + [vmem] * (len(pieces) + (not first)),
         out_specs=[vmem] * BLOCKS if last else [vmem, smem, smem],
-        scratch_shapes=([sums, *going_on] if last else [])
+        scratch_shapes=[sums if last else going_on[0]]
         + [
             pltpu.VMEM((len(pieces) * BLOCKS, TILE, 2 * FEAT), bf16),
-            pltpu.VMEM((DEPTH, UNROLL, TILE, TILE), f32),
+            pltpu.VMEM((RING // size, size, TILE, TILE), f32),
             pltpu.SMEM((len(pieces), 8, 128), f32),
             pltpu.SMEM((BUCKETS * BLOCKS,), jnp.int32),
-            pltpu.SMEM((TILES + 2 * UNROLL,), jnp.int32),
-            pltpu.SemaphoreType.DMA((DEPTH, UNROLL)),
+            pltpu.SemaphoreType.DMA((RING // size, size)),
             pltpu.SemaphoreType.DMA((len(pieces),)),
         ],
         compiler_params=pltpu.CompilerParams(vmem_limit_bytes=40 * 2**20),
@@ -206,7 +220,7 @@
     words, count = pl.pallas_call(
         live_kernel,
         out_shape=[
-            jax.ShapeDtypeStruct((TILES + 2 * UNROLL,), jnp.int32),
+            jax.ShapeDtypeStruct((TILES + 2 * STEP,), jnp.int32),
             jax.ShapeDtypeStruct((1,), jnp.int32),
         ],
         in_specs=[smem, smem],
@@ -219,17 +233,14 @@
     far_above = move(far, "y", DOWN)
     far_below = move(below, "z_hi", SWAP)
     swapped = [move(p, "core", SWAP) for p in (below, above, far)]
-    sums, words, count = tile_products(place, words, count, tiles, [own, other, below, above, far, *swapped])
-
-    two = after(two, sums)
     far_two = move(two, "z_hi", SWAP)
     late = [two, far_above, far_below]
-    swapped = [move(p, "core", SWAP) for p in late]
-    sums, words, count = tile_products(place, words, count, tiles, late, sums)
-
+    late_swapped = [move(p, "core", SWAP) for p in late]
+    early = [own, other, below, above, far, *swapped, *late]
+    sums, words, count = tile_products(place, words, count, tiles, early)
     far_two = after(far_two, sums)
     mine, up, two, down, z_mine, z_up, z_two, z_down = tile_products(
-        place, words, count, tiles, [*swapped, far_two, move(far_two, "core", SWAP)], sums, last=True
+        place, words, count, tiles, [*late_swapped, far_two, move(far_two, "core", SWAP)], sums, last=True
     )
 
     half = BLOCKS // 2

time: 104 us -> 99.4 us (0.956)
  starting transfers between devices: 27.7 us -> 33.2 us
  Pallas kernels: 26.2 us -> 21.1 us
  waiting for transfers between devices: 45.9 us -> 41.3 us
    ppermute x1, waiting for transfers between devices: 7.34 us -> 0.01 us  [body(): far_two = move(two, 'z_hi', SWAP)]
    ppermute x1, waiting for transfers between devices: 0.01 us -> 6.9 us  [body(): two = move(below, 'y', UP)]
    pallas_call x3 -> x2, Pallas kernels: 22.2 us -> 17.1 us  [tile_products(): pl.pallas_call(functools.partial(tile_kernel, len(pieces), first, last),...]
    ppermute x1, waiting for transfers between devices: 2.15 us -> 0.01 us  [body(): far = move(own, 'z_hi', SWAP)]
    ppermute x1, starting transfers between devices: 2.31 us -> 3.88 us  [body(): far_below = move(below, 'z_hi', SWAP)]
    ppermute x1, waiting for transfers between devices: 1.46 us -> 0.01 us  [body(): above = move(own, 'y', DOWN)]
    ppermute x1, starting transfers between devices: 1.82 us -> 3.25 us  [body(): far_two = move(two, 'z_hi', SWAP)]
    ppermute x1, starting transfers between devices: 1.66 us -> 3 us  [body(): far_above = move(far, 'y', DOWN)]
  transfers between devices with their start and end apart: 23 -> 23, of which waited for: 10 -> 10; matrix products, arithmetic and copies ran while one was open for 0% -> 0% of each run, Pallas kernels for 18% -> 14%
where the time goes in v6:
time: 99.4 us; the launch traced here: 98.5 us
  waiting for transfers between devices  41.3 us (42%)
  starting transfers between devices  33.2 us (33%)
  Pallas kernels  21.1 us (21%)
  other arithmetic  2.18 us (2%)
    pallas_call x2, Pallas kernels, tile_products(): pl.pallas_call(functools.partial(tile_kernel, len(pieces), first, last),...  17.1 us
    ppermute x1, waiting for transfers between devices, body(): got_two = move(z_two, 'z_lo', SWAP)  9.86 us
    ppermute x1, waiting for transfers between devices, body(): two = move(below, 'y', UP)  6.9 us
    ppermute x1, waiting for transfers between devices, body(): move(jnp.concatenate([down[:half], down[half:] + two_down]), 'x', DOWN)  6.25 us
    ppermute x1, waiting for transfers between devices, body(): below = move(own, 'y', UP)  5.03 us
    ppermute x1, starting transfers between devices, body(): far_below = move(below, 'z_hi', SWAP)  3.88 us
    ppermute x1, starting transfers between devices, body(): far = move(own, 'z_hi', SWAP)  3.88 us
    ppermute x1, starting transfers between devices, body(): move(jnp.concatenate([down[:half], down[half:] + two_down]), 'x', DOWN)  3.76 us
  transfers between devices with their start and end apart: 23, of which 10 were waited for; matrix products, arithmetic and copies ran while one was open for 0% of the time, Pallas kernels for 14%

profile of v6, /device:TPU:0, one launch (start us, length us, event | category | flops | bytes accessed | tf_op | source)
XLA Modules:
  0.0 98.5 jit_solution(3343225844874237413)
XLA Ops:
  0.0 0.7 convert_bitcast_fusion
  0.7 1.1 %select_maximum_fusion.refs_4_ = f32[1032,128]{1,0:T(8,128)S(1)} fusion(f32[1,8]{1,0:T(1,128)S(1)} %convert_bitcast_fusion, f32[1024,128]{1,0:T(8,128)} %param.7), kind=kLoop, calls=%fused_computation | loop fusion | flops 396288 | bytes 1052704 | tf_op jit(solution)/shard_map/concatenate | solution.py:211
  1.7 1.7 %collective-permute-start.1 = (f32[1032,128]{1,0:T(8,128)S(1)}, f32[1032,128]{1,0:T(8,128)S(1)}, u32[]{:S(2)}, u32[]{:S(2)}) collective-permute-start(f32[1032,128]{1,0:T(8,128)S(1)} %select_maximum_fusion.refs_4_), channel_id=1, source_target_pairs={{0,2},{2,4},{4,6},{6,0},{1,3},{3,5},{5,7},{7,1},{8,10},{10,12},{12... | collective-permute-start | bytes 1585160 | tf_op jit(solution)/shard_map/ppermute | solution.py:212
  3.5 3.9 %collective-permute-start.3 = (f32[1032,128]{1,0:T(8,128)S(1)}, f32[1032,128]{1,0:T(8,128)S(1)}, u32[]{:S(2)}, u32[]{:S(2)}) collective-permute-start(f32[1032,128]{1,0:T(8,128)S(1)} %select_maximum_fusion.refs_4_), channel_id=1, source_target_pairs={{0,8},{8,0},{1,9},{9,1},{2,10},{10,2},{3,11},{11,3},{4,12},{12,4},... | collective-permute-start | bytes 1585160 | tf_op jit(solution)/shard_map/ppermute | solution.py:214
  7.3 1.7 %collective-permute-start.2 = (f32[1032,128]{1,0:T(8,128)S(1)}, f32[1032,128]{1,0:T(8,128)S(1)}, u32[]{:S(2)}, u32[]{:S(2)}) collective-permute-start(f32[1032,128]{1,0:T(8,128)S(1)} %select_maximum_fusion.refs_4_), channel_id=1, source_target_pairs={{0,6},{2,0},{4,2},{6,4},{1,7},{3,1},{5,3},{7,5},{8,14},{10,8},{12,... | collective-permute-start | bytes 1585160 | tf_op jit(solution)/shard_map/ppermute | solution.py:213
  9.0 2.9 %shard_map.73 = (s32[288]{0:T(512)}, s32[1]{0:T(128)}) custom-call(s32[16,16]{1,0:T(8,128)} %bitcast.11, s32[16,16]{1,0:T(8,128)} %bitcast.12), custom_call_target="tpu_custom_call" | custom-call | flops 100000 | bytes 10000 | tf_op jit(solution)/shard_map/pallas_call | solution.py:220
  11.9 5.0 %collective-permute-done.1.refs_6_ = f32[1032,128]{1,0:T(8,128)S(1)} collective-permute-done((f32[1032,128]{1,0:T(8,128)S(1)}, f32[1032,128]{1,0:T(8,128)S(1)}, u32[]{:S(2)}, u32[]{:S(2)}) %collective-permute-start.1) | collective-permute-done | bytes 528416 | tf_op jit(solution)/shard_map/ppermute | solution.py:212
  16.9 0.3 collective-permute-start.7
  17.2 3.9 %collective-permute-start.9 = (f32[1032,128]{1,0:T(8,128)S(1)}, f32[1032,128]{1,0:T(8,128)S(1)}, u32[]{:S(2)}, u32[]{:S(2)}) collective-permute-start(f32[1032,128]{1,0:T(8,128)S(1)} %collective-permute-done.1.refs_6_), channel_id=1, source_target_pairs={{0,8},{8,0},{1,9},{9,1},{2,10},{10,2},{3,11},{11,3},{4,12},{12,4},... | collective-permute-start | bytes 1585160 | tf_op jit(solution)/shard_map/ppermute | solution.py:234
  21.1 3.0 %collective-permute-start.8 = (f32[1032,128]{1,0:T(8,128)S(1)}, f32[1032,128]{1,0:T(8,128)}, u32[]{:S(2)}, u32[]{:S(2)}) collective-permute-start(f32[1032,128]{1,0:T(8,128)S(1)} %collective-permute-done.3.refs_8_), channel_id=1, source_target_pairs={{0,6},{2,0},{4,2},{6,4},{1,7},{3,1},{5,3},{7,5},{8,14},{10,8},{12,... | collective-permute-start | bytes 1585160 | tf_op jit(solution)/shard_map/ppermute | solution.py:233
  24.1 0.0 collective-permute-done.refs_5_
  24.1 0.2 collective-permute-start.6
  24.3 6.9 %collective-permute-done.7.refs_12_ = f32[1032,128]{1,0:T(8,128)S(1)} collective-permute-done((f32[1032,128]{1,0:T(8,128)S(1)}, f32[1032,128]{1,0:T(8,128)S(1)}, u32[]{:S(2)}, u32[]{:S(2)}) %collective-permute-start.7) | collective-permute-done | bytes 528416 | tf_op jit(solution)/shard_map/ppermute | solution.py:232
  31.2 0.0 collective-permute-start.5
  31.2 0.8 collective-permute-done.9.refs_14_
  32.0 3.2 %collective-permute-start.13 = (f32[1032,128]{1,0:T(8,128)S(1)}, f32[1032,128]{1,0:T(8,128)}, u32[]{:S(2)}, u32[]{:S(2)}) collective-permute-start(f32[1032,128]{1,0:T(8,128)S(1)} %collective-permute-done.7.refs_12_), channel_id=1, source_target_pairs={{0,8},{8,0},{1,9},{9,1},{2,10},{10,2},{3,11},{11,3},{4,12},{12,4},... | collective-permute-start | bytes 1585160 | tf_op jit(solution)/shard_map/ppermute | solution.py:236
  35.3 0.1 pad_add_fusion.refs_0_
  35.3 0.0 collective-permute-start.10
  35.4 0.6 collective-permute-done.8.refs_13_
  36.0 0.0 collective-permute-done.6.refs_11_
  36.0 0.5 collective-permute-start.11
  36.5 0.0 collective-permute-done.5.refs_10_
  36.5 0.7 copy-done.1
  37.2 10.9 %shard_map.74 = (f32[65,128,128]{2,1,0:T(8,128)S(1)}, s32[288]{0:T(512)S(1)}, s32[1]{0:T(128)}) custom-call(s32[2]{0:T(128)S(1)} %pad_add_fusion.refs_0_, s32[288]{0:T(512)S(1)} %copy-done.1, s32[1]{0:T(128)} %get-tuple-element.21.refs_2_, f32[256,128,128]{2,1,0:T(8,128)} %bitcast.9, f32[1032,128]{1,0:T(8,128)S(1)} %select_maximum_fusion.refs_4_, ...), custom_call_target="tpu_custom_call" | custom-call | flops 100000 | bytes 10000 | tf_op jit(solution)/shard_map/pallas_call | solution.py:177
  48.1 0.0 copy-start
  48.1 0.0 copy-start.2
  48.1 0.0 collective-permute-done.13.refs_7_
  48.1 0.6 collective-permute-start.14
  48.7 0.0 collective-permute-done.11.refs_5_
  48.7 1.7 %collective-permute-done.14.refs_8_ = f32[1032,128]{1,0:T(8,128)S(1)} collective-permute-done((f32[1032,128]{1,0:T(8,128)}, f32[1032,128]{1,0:T(8,128)S(1)}, u32[]{:S(2)}, u32[]{:S(2)}) %collective-permute-start.14) | collective-permute-done | bytes 528416 | tf_op jit(solution)/shard_map/ppermute | solution.py:243
  50.4 6.2 %shard_map.75 = (f32[8,128,128]{2,1,0:T(8,128)S(1)}, f32[8,128,128]{2,1,0:T(8,128)S(1)}, f32[8,128,128]{2,1,0:T(8,128)S(1)}, f32[8,128,128]{2,1,0:T(8,128)S(1)},...) custom-call(s32[2]{0:T(128)S(1)} %pad_add_fusion.refs_0_, ...), custom_call_target="tpu_custom_call" | custom-call | flops 100000 | bytes 10000 | tf_op jit(solution)/shard_map/pallas_call | solution.py:177
  56.6 0.8 collective-permute-start.15
  57.4 1.5 %collective-permute-start.20 = (f32[8,128,128]{2,1,0:T(8,128)S(1)}, f32[8,128,128]{2,1,0:T(8,128)S(1)}, u32[]{:S(2)}, u32[]{:S(2)}) collective-permute-start(f32[8,128,128]{2,1,0:T(8,128)S(1)} %get-tuple-element.33), channel_id=1, source_target_pairs={{0,16},{16,32},{32,48},{48,0},{1,17},{17,33},{33,49},{49,1},{2,18}... | collective-permute-start | bytes 1572872 | tf_op jit(solution)/shard_map/ppermute | solution.py:248
  58.9 1.7 %collective-permute-start.21 = (f32[8,128,128]{2,1,0:T(8,128)S(1)}, f32[8,128,128]{2,1,0:T(8,128)S(1)}, u32[]{:S(2)}, u32[]{:S(2)}) collective-permute-start(f32[8,128,128]{2,1,0:T(8,128)S(1)} %get-tuple-element.34), channel_id=1, source_target_pairs={{0,48},{16,0},{32,16},{48,32},{1,49},{17,1},{33,17},{49,33},{2,50}... | collective-permute-start | bytes 1572872 | tf_op jit(solution)/shard_map/ppermute | solution.py:249
  60.7 9.9 %collective-permute-done.15 = f32[8,128,128]{2,1,0:T(8,128)S(1)} collective-permute-done((f32[8,128,128]{2,1,0:T(8,128)S(1)}, f32[8,128,128]{2,1,0:T(8,128)S(1)}, u32[]{:S(2)}, u32[]{:S(2)}) %collective-permute-start.15) | collective-permute-done | bytes 524320 | tf_op jit(solution)/shard_map/ppermute | solution.py:247
  70.5 0.1 slice_add_fusion
  70.6 3.3 %collective-permute-start.18 = (f32[4,128,128]{2,1,0:T(8,128)S(1)}, f32[4,128,128]{2,1,0:T(8,128)S(1)}, u32[]{:S(2)}, u32[]{:S(2)}) collective-permute-start(f32[4,128,128]{2,1,0:T(8,128)S(1)} %get-tuple-element.35), channel_id=1, source_target_pairs={{0,48},{16,0},{32,16},{48,32},{1,49},{17,1},{33,17},{49,33},{2,50}... | collective-permute-start | bytes 786440 | tf_op jit(solution)/shard_map/ppermute | solution.py:251
  73.9 0.1 add_add_fusion
  74.0 1.0 %collective-permute-start.22 = (f32[8,128,128]{2,1,0:T(8,128)S(1)}, f32[8,128,128]{2,1,0:T(8,128)S(1)}, u32[]{:S(2)}, u32[]{:S(2)}) collective-permute-start(f32[8,128,128]{2,1,0:T(8,128)S(1)} %add_add_fusion), channel_id=1, source_target_pairs={{0,64},{64,0},{1,65},{65,1},{2,66},{66,2},{3,67},{67,3},{4,68},{68... | collective-permute-start | bytes 1572872 | tf_op jit(solution)/shard_map/ppermute | solution.py:252
  75.0 1.2 %collective-permute-start.16 = (f32[4,128,128]{2,1,0:T(8,128)S(1)}, f32[4,128,128]{2,1,0:T(8,128)S(1)}, u32[]{:S(2)}, u32[]{:S(2)}) collective-permute-start(f32[4,128,128]{2,1,0:T(8,128)S(1)} %get-tuple-element.36), channel_id=1, source_target_pairs={{0,16},{16,32},{32,48},{48,0},{1,17},{17,33},{33,49},{49,1},{2,18}... | collective-permute-start | bytes 786440 | tf_op jit(solution)/shard_map/ppermute | solution.py:250
  76.2 3.3 %collective-permute-done.18 = f32[4,128,128]{2,1,0:T(8,128)S(1)} collective-permute-done((f32[4,128,128]{2,1,0:T(8,128)S(1)}, f32[4,128,128]{2,1,0:T(8,128)S(1)}, u32[]{:S(2)}, u32[]{:S(2)}) %collective-permute-start.18) | collective-permute-done | bytes 262176 | tf_op jit(solution)/shard_map/ppermute | solution.py:251
  79.6 3.8 %collective-permute-start.19 = (f32[8,128,128]{2,1,0:T(8,128)S(1)}, f32[8,128,128]{2,1,0:T(8,128)S(1)}, u32[]{:S(2)}, u32[]{:S(2)}) collective-permute-start(f32[8,128,128]{2,1,0:T(8,128)S(1)} %pad_maximum_fusion.1), channel_id=1, source_target_pairs={{0,48},{16,0},{32,16},{48,32},{1,49},{17,1},{33,17},{49,33},{2,50}... | collective-permute-start | bytes 1572872 | tf_op jit(solution)/shard_map/ppermute | solution.py:254
  83.4 0.1 slice_add_fusion.3
  83.5 0.9 collective-permute-start.17
  84.4 3.1 %collective-permute-done.22.d = f32[8,128,128]{2,1,0:T(8,128)S(1)} collective-permute-done((f32[8,128,128]{2,1,0:T(8,128)S(1)}, f32[8,128,128]{2,1,0:T(8,128)S(1)}, u32[]{:S(2)}, u32[]{:S(2)}) %collective-permute-start.22) | collective-permute-done | bytes 524320 | tf_op jit(solution)/shard_map/ppermute | solution.py:252
  87.6 6.3 %collective-permute-done.19.c = f32[8,128,128]{2,1,0:T(8,128)S(1)} collective-permute-done((f32[8,128,128]{2,1,0:T(8,128)S(1)}, f32[8,128,128]{2,1,0:T(8,128)S(1)}, u32[]{:S(2)}, u32[]{:S(2)}) %collective-permute-start.19) | collective-permute-done | bytes 524320 | tf_op jit(solution)/shard_map/ppermute | solution.py:254
  93.8 3.6 %collective-permute-done.17.b = f32[8,128,128]{2,1,0:T(8,128)S(1)} collective-permute-done((f32[8,128,128]{2,1,0:T(8,128)S(1)}, f32[8,128,128]{2,1,0:T(8,128)S(1)}, u32[]{:S(2)}, u32[]{:S(2)}) %collective-permute-start.17) | collective-permute-done | bytes 524320 | tf_op jit(solution)/shard_map/ppermute | solution.py:253
  97.4 1.1 %shard_map.76 = f32[1024,128]{1,0:T(8,128)} custom-call(f32[8,128,128]{2,1,0:T(8,128)S(1)} %get-tuple-element.27.a, f32[8,128,128]{2,1,0:T(8,128)S(1)} %collective-permute-done.17.b, f32[8,128,128]{2,1,0:T(8,128)S(1)} %collective-permute-done.19.c, f32[8,128,128]{2,1,0:T(8,128)S(1)} %collective-permute-done.22.d, f32[128,128]{1,0:T(8,128)S(1)} %copy-done, ...), custom_call_target="tpu_custom_call" | custom-call | tf_op jit(solution)/shard_map/pallas_call | solution.py:256
  (17 shorter events, 0.2 us)
Async XLA Ops:
  1.7 15.2 %collective-permute-start.1 = (f32[1032,128]{1,0:T(8,128)S(1)}, f32[1032,128]{1,0:T(8,128)S(1)}, u32[]{:S(2)}, u32[]{:S(2)}) collective-permute-start(f32[1032,128]{1,0:T(8,128)S(1)} %select_maximum_fusion.refs_4_), channel_id=1, source_target_pairs={{0,2},{2,4},{4,6},{6,0},{1,3},{3,5},{5,7},{7,1},{8,10},{10,12},{12... | collective-permute-start | bytes 1585160 | tf_op jit(solution)/shard_map/ppermute | solution.py:212
  3.5 17.6 %collective-permute-start.3 = (f32[1032,128]{1,0:T(8,128)S(1)}, f32[1032,128]{1,0:T(8,128)S(1)}, u32[]{:S(2)}, u32[]{:S(2)}) collective-permute-start(f32[1032,128]{1,0:T(8,128)S(1)} %select_maximum_fusion.refs_4_), channel_id=1, source_target_pairs={{0,8},{8,0},{1,9},{9,1},{2,10},{10,2},{3,11},{11,3},{4,12},{12,4},... | collective-permute-start | bytes 1585160 | tf_op jit(solution)/shard_map/ppermute | solution.py:214
  7.3 13.8 %collective-permute-start.2 = (f32[1032,128]{1,0:T(8,128)S(1)}, f32[1032,128]{1,0:T(8,128)S(1)}, u32[]{:S(2)}, u32[]{:S(2)}) collective-permute-start(f32[1032,128]{1,0:T(8,128)S(1)} %select_maximum_fusion.refs_4_), channel_id=1, source_target_pairs={{0,6},{2,0},{4,2},{6,4},{1,7},{3,1},{5,3},{7,5},{8,14},{10,8},{12,... | collective-permute-start | bytes 1585160 | tf_op jit(solution)/shard_map/ppermute | solution.py:213
  9.0 15.1 %collective-permute-start = (f32[1032,128]{1,0:T(8,128)S(1)}, f32[1032,128]{1,0:T(8,128)}, u32[]{:S(2)}, u32[]{:S(2)}) collective-permute-start(f32[1032,128]{1,0:T(8,128)S(1)} %select_maximum_fusion.refs_4_), channel_id=1, source_target_pairs={{0,1},{1,0},{2,3},{3,2},{4,5},{5,4},{6,7},{7,6},{8,9},{9,8},{10,11... | collective-permute-start | bytes 1585160 | tf_op jit(solution)/shard_map/ppermute | solution.py:215
  16.9 14.3 %collective-permute-start.7 = (f32[1032,128]{1,0:T(8,128)S(1)}, f32[1032,128]{1,0:T(8,128)S(1)}, u32[]{:S(2)}, u32[]{:S(2)}) collective-permute-start(f32[1032,128]{1,0:T(8,128)S(1)} %collective-permute-done.1.refs_6_), channel_id=1, source_target_pairs={{0,2},{2,4},{4,6},{6,0},{1,3},{3,5},{5,7},{7,1},{8,10},{10,12},{12... | collective-permute-start | bytes 1585160 | tf_op jit(solution)/shard_map/ppermute | solution.py:232
  17.2 14.8 %collective-permute-start.9 = (f32[1032,128]{1,0:T(8,128)S(1)}, f32[1032,128]{1,0:T(8,128)S(1)}, u32[]{:S(2)}, u32[]{:S(2)}) collective-permute-start(f32[1032,128]{1,0:T(8,128)S(1)} %collective-permute-done.1.refs_6_), channel_id=1, source_target_pairs={{0,8},{8,0},{1,9},{9,1},{2,10},{10,2},{3,11},{11,3},{4,12},{12,4},... | collective-permute-start | bytes 1585160 | tf_op jit(solution)/shard_map/ppermute | solution.py:234
  21.1 14.2 %collective-permute-start.4 = (f32[1032,128]{1,0:T(8,128)S(1)}, f32[1032,128]{1,0:T(8,128)}, u32[]{:S(2)}, u32[]{:S(2)}) collective-permute-start(f32[1032,128]{1,0:T(8,128)S(1)} %collective-permute-done.1.refs_6_), channel_id=1, source_target_pairs={{0,1},{1,0},{2,3},{3,2},{4,5},{5,4},{6,7},{7,6},{8,9},{9,8},{10,11... | collective-permute-start | bytes 1585160 | tf_op jit(solution)/shard_map/ppermute | solution.py:235
  21.1 14.9 %collective-permute-start.8 = (f32[1032,128]{1,0:T(8,128)S(1)}, f32[1032,128]{1,0:T(8,128)}, u32[]{:S(2)}, u32[]{:S(2)}) collective-permute-start(f32[1032,128]{1,0:T(8,128)S(1)} %collective-permute-done.3.refs_8_), channel_id=1, source_target_pairs={{0,6},{2,0},{4,2},{6,4},{1,7},{3,1},{5,3},{7,5},{8,14},{10,8},{12,... | collective-permute-start | bytes 1585160 | tf_op jit(solution)/shard_map/ppermute | solution.py:233
  24.1 11.9 %collective-permute-start.6 = (f32[1032,128]{1,0:T(8,128)S(1)}, f32[1032,128]{1,0:T(8,128)}, u32[]{:S(2)}, u32[]{:S(2)}) collective-permute-start(f32[1032,128]{1,0:T(8,128)S(1)} %collective-permute-done.3.refs_8_), channel_id=1, source_target_pairs={{0,1},{1,0},{2,3},{3,2},{4,5},{5,4},{6,7},{7,6},{8,9},{9,8},{10,11... | collective-permute-start | bytes 1585160 | tf_op jit(solution)/shard_map/ppermute | solution.py:235
  31.2 5.3 %collective-permute-start.5 = (f32[1032,128]{1,0:T(8,128)S(1)}, f32[1032,128]{1,0:T(8,128)}, u32[]{:S(2)}, u32[]{:S(2)}) collective-permute-start(f32[1032,128]{1,0:T(8,128)S(1)} %collective-permute-done.2.refs_7_), channel_id=1, source_target_pairs={{0,1},{1,0},{2,3},{3,2},{4,5},{5,4},{6,7},{7,6},{8,9},{9,8},{10,11... | collective-permute-start | bytes 1585160 | tf_op jit(solution)/shard_map/ppermute | solution.py:235
  32.0 16.1 %collective-permute-start.13 = (f32[1032,128]{1,0:T(8,128)S(1)}, f32[1032,128]{1,0:T(8,128)}, u32[]{:S(2)}, u32[]{:S(2)}) collective-permute-start(f32[1032,128]{1,0:T(8,128)S(1)} %collective-permute-done.7.refs_12_), channel_id=1, source_target_pairs={{0,8},{8,0},{1,9},{9,1},{2,10},{10,2},{3,11},{11,3},{4,12},{12,4},... | collective-permute-start | bytes 1585160 | tf_op jit(solution)/shard_map/ppermute | solution.py:236
  35.3 13.4 %collective-permute-start.10 = (f32[1032,128]{1,0:T(8,128)S(1)}, f32[1032,128]{1,0:T(8,128)S(1)}, u32[]{:S(2)}, u32[]{:S(2)}) collective-permute-start(f32[1032,128]{1,0:T(8,128)S(1)} %collective-permute-done.7.refs_12_), channel_id=1, source_target_pairs={{0,1},{1,0},{2,3},{3,2},{4,5},{5,4},{6,7},{7,6},{8,9},{9,8},{10,11... | collective-permute-start | bytes 1585160 | tf_op jit(solution)/shard_map/ppermute | solution.py:238
  36.0 12.7 %collective-permute-start.12 = (f32[1032,128]{1,0:T(8,128)S(1)}, f32[1032,128]{1,0:T(8,128)S(1)}, u32[]{:S(2)}, u32[]{:S(2)}) collective-permute-start(f32[1032,128]{1,0:T(8,128)S(1)} %collective-permute-done.9.refs_14_), channel_id=1, source_target_pairs={{0,1},{1,0},{2,3},{3,2},{4,5},{5,4},{6,7},{7,6},{8,9},{9,8},{10,11... | collective-permute-start | bytes 1585160 | tf_op jit(solution)/shard_map/ppermute | solution.py:238
  36.0 12.7 %collective-permute-start.11 = (f32[1032,128]{1,0:T(8,128)}, f32[1032,128]{1,0:T(8,128)S(1)}, u32[]{:S(2)}, u32[]{:S(2)}) collective-permute-start(f32[1032,128]{1,0:T(8,128)} %collective-permute-done.8.refs_13_), channel_id=1, source_target_pairs={{0,1},{1,0},{2,3},{3,2},{4,5},{5,4},{6,7},{7,6},{8,9},{9,8},{10,11... | collective-permute-start | bytes 1585160 | tf_op jit(solution)/shard_map/ppermute | solution.py:238
  36.5 0.7 copy-start.1
  48.1 49.3 %copy-start = (f32[128,128]{1,0:T(8,128)S(1)}, f32[128,128]{1,0:T(8,128)}, u32[]{:S(2)}) copy-start(f32[128,128]{1,0:T(8,128)} %weight.1) | copy-start | bytes 196612
  48.1 49.3 %copy-start.2 = (f32[128]{0:T(128)S(1)}, f32[128]{0:T(128)}, u32[]{:S(2)}) copy-start(f32[128]{0:T(128)} %param.13) | copy-start | bytes 1540
  48.1 2.3 %collective-permute-start.14 = (f32[1032,128]{1,0:T(8,128)}, f32[1032,128]{1,0:T(8,128)S(1)}, u32[]{:S(2)}, u32[]{:S(2)}) collective-permute-start(f32[1032,128]{1,0:T(8,128)} %collective-permute-done.13.refs_7_), channel_id=1, source_target_pairs={{0,1},{1,0},{2,3},{3,2},{4,5},{5,4},{6,7},{7,6},{8,9},{9,8},{10,11... | collective-permute-start | bytes 1585160 | tf_op jit(solution)/shard_map/ppermute | solution.py:243
  56.6 13.9 %collective-permute-start.15 = (f32[8,128,128]{2,1,0:T(8,128)S(1)}, f32[8,128,128]{2,1,0:T(8,128)S(1)}, u32[]{:S(2)}, u32[]{:S(2)}) collective-permute-start(f32[8,128,128]{2,1,0:T(8,128)S(1)} %get-tuple-element.30), channel_id=1, source_target_pairs={{0,64},{64,0},{1,65},{65,1},{2,66},{66,2},{3,67},{67,3},{4,68},{68... | collective-permute-start | bytes 1572872 | tf_op jit(solution)/shard_map/ppermute | solution.py:247
  57.4 16.5 %collective-permute-start.20 = (f32[8,128,128]{2,1,0:T(8,128)S(1)}, f32[8,128,128]{2,1,0:T(8,128)S(1)}, u32[]{:S(2)}, u32[]{:S(2)}) collective-permute-start(f32[8,128,128]{2,1,0:T(8,128)S(1)} %get-tuple-element.33), channel_id=1, source_target_pairs={{0,16},{16,32},{32,48},{48,0},{1,17},{17,33},{33,49},{49,1},{2,18}... | collective-permute-start | bytes 1572872 | tf_op jit(solution)/shard_map/ppermute | solution.py:248
  58.9 15.0 %collective-permute-start.21 = (f32[8,128,128]{2,1,0:T(8,128)S(1)}, f32[8,128,128]{2,1,0:T(8,128)S(1)}, u32[]{:S(2)}, u32[]{:S(2)}) collective-permute-start(f32[8,128,128]{2,1,0:T(8,128)S(1)} %get-tuple-element.34), channel_id=1, source_target_pairs={{0,48},{16,0},{32,16},{48,32},{1,49},{17,1},{33,17},{49,33},{2,50}... | collective-permute-start | bytes 1572872 | tf_op jit(solution)/shard_map/ppermute | solution.py:249
  70.6 8.9 %collective-permute-start.18 = (f32[4,128,128]{2,1,0:T(8,128)S(1)}, f32[4,128,128]{2,1,0:T(8,128)S(1)}, u32[]{:S(2)}, u32[]{:S(2)}) collective-permute-start(f32[4,128,128]{2,1,0:T(8,128)S(1)} %get-tuple-element.35), channel_id=1, source_target_pairs={{0,48},{16,0},{32,16},{48,32},{1,49},{17,1},{33,17},{49,33},{2,50}... | collective-permute-start | bytes 786440 | tf_op jit(solution)/shard_map/ppermute | solution.py:251
  74.0 13.6 %collective-permute-start.22 = (f32[8,128,128]{2,1,0:T(8,128)S(1)}, f32[8,128,128]{2,1,0:T(8,128)S(1)}, u32[]{:S(2)}, u32[]{:S(2)}) collective-permute-start(f32[8,128,128]{2,1,0:T(8,128)S(1)} %add_add_fusion), channel_id=1, source_target_pairs={{0,64},{64,0},{1,65},{65,1},{2,66},{66,2},{3,67},{67,3},{4,68},{68... | collective-permute-start | bytes 1572872 | tf_op jit(solution)/shard_map/ppermute | solution.py:252
  75.0 8.4 %collective-permute-start.16 = (f32[4,128,128]{2,1,0:T(8,128)S(1)}, f32[4,128,128]{2,1,0:T(8,128)S(1)}, u32[]{:S(2)}, u32[]{:S(2)}) collective-permute-start(f32[4,128,128]{2,1,0:T(8,128)S(1)} %get-tuple-element.36), channel_id=1, source_target_pairs={{0,16},{16,32},{32,48},{48,0},{1,17},{17,33},{33,49},{49,1},{2,18}... | collective-permute-start | bytes 786440 | tf_op jit(solution)/shard_map/ppermute | solution.py:250
  79.6 14.2 %collective-permute-start.19 = (f32[8,128,128]{2,1,0:T(8,128)S(1)}, f32[8,128,128]{2,1,0:T(8,128)S(1)}, u32[]{:S(2)}, u32[]{:S(2)}) collective-permute-start(f32[8,128,128]{2,1,0:T(8,128)S(1)} %pad_maximum_fusion.1), channel_id=1, source_target_pairs={{0,48},{16,0},{32,16},{48,32},{1,49},{17,1},{33,17},{49,33},{2,50}... | collective-permute-start | bytes 1572872 | tf_op jit(solution)/shard_map/ppermute | solution.py:254
  83.5 13.9 %collective-permute-start.17 = (f32[8,128,128]{2,1,0:T(8,128)S(1)}, f32[8,128,128]{2,1,0:T(8,128)S(1)}, u32[]{:S(2)}, u32[]{:S(2)}) collective-permute-start(f32[8,128,128]{2,1,0:T(8,128)S(1)} %pad_maximum_fusion), channel_id=1, source_target_pairs={{0,16},{16,32},{32,48},{48,0},{1,17},{17,33},{33,49},{49,1},{2,18}... | collective-permute-start | bytes 1572872 | tf_op jit(solution)/shard_map/ppermute | solution.py:253

commit v7 on v6

--- a/solution.py
+++ b/solution.py
@@ -54,18 +54,20 @@
         words[total + j] = -1
 
 
-def tile_kernel(n_pieces, first, last, *refs):
+def tile_kernel(n_pieces, first, split_rest, owners, *refs):
     place, words, count, tiles = refs[:4]
-    refs = refs[1:]
-    pieces = refs[3 : 3 + n_pieces]
-    so_far = None if first else refs[3 + n_pieces]
-    outs = refs[4 + n_pieces - first :]
-    if last:
-        parts, (acc, *scratch) = outs[:BLOCKS], outs[BLOCKS:]
+    refs = refs[4:]
+    pieces, refs = refs[:n_pieces], refs[n_pieces:]
+    so_far = None if first else refs[0]
+    outs = refs[1 - first :]
+    if owners:
+        parts, (acc, *scratch) = outs[: len(owners)], outs[len(owners) :]
+        dummy, size = len(owners) * BLOCKS, LAST_STEP
     else:
-        acc, rest, left, mine, *scratch = outs
+        acc, *outs = outs
+        rests, (mine, *scratch) = outs[: 2 + 2 * split_rest], outs[2 + 2 * split_rest :]
+        dummy, size = DUMMY, STEP
     xs, ring, slots, table, ring_sem, slot_sem = scratch
-    size = LAST_STEP if last else STEP
     depth = RING // size
 
     reads = [
@@ -89,19 +91,26 @@
             def _(group=group):
                 fetch(group)
 
-    if last:
-        todo, here = words, count[0]
-        groups = (here + size - 1) // size
+    if owners:
+        todo, groups = words, (count[0] + size - 1) // size
         fetch_first()
+
+        def begin(j, carry):
+            for i, owner in enumerate(owners):
+                at = ((owner // 4) ^ place[0]) * 4 + (owner % 4 + place[1] & 3)
+                acc[i * BLOCKS + j] = so_far[at * BLOCKS + j]
+            return carry
+
+        lax.fori_loop(0, BLOCKS, begin, 0)
     else:
         for p in range(BUCKETS * BLOCKS):
             table[p] = -1
 
-    def begin(d, carry):
-        acc[d] = jnp.zeros((TILE, FEAT), f32) if first else so_far[d]
-        return carry
-
-    lax.fori_loop(0, DUMMY + 1, begin, 0, unroll=5)
+        def begin(d, carry):
+            acc[d] = jnp.zeros((TILE, FEAT), f32) if first else so_far[d]
+            return carry
+
+        lax.fori_loop(0, DUMMY + 1, begin, 0, unroll=5)
     for read in reads:
         read.wait()
     for i in range(n_pieces):
@@ -109,23 +118,32 @@
             table[slots[i, 0, j].astype(jnp.int32) & 127] = i * BLOCKS + j
 
     def sort(group, n):
-        here, there = n
+        here, *others = n
         loaded = [words[group * 8 + j] for j in range(8)]
         found = [table[(word >> 8) & 127] for word in loaded]
         for word, s in zip(loaded, found):
             live = (word >= 0).astype(jnp.int32)
             known = jnp.where(s >= 0, live, 0)
             mine[here] = word
-            rest[there] = word
-            here, there = here + known, there + live - known
-        return here, there
-
-    if not last:
-        here, there = lax.fori_loop(0, (count[0] + 7) // 8, sort, (0, 0))
-        left[0] = there
+            here = here + known
+            left = [live - known]
+            if split_rest:
+                g = word >> 19
+                soon = jnp.where((g & 3) != place[1], (g >> 2) ^ place[0], 0) * left[0]
+                left = [soon, left[0] - soon]
+            for i, more in enumerate(left):
+                rests[2 * i][others[i]] = word
+                others[i] = others[i] + more
+        return (here, *others)
+
+    if not owners:
+        here, *others = lax.fori_loop(0, (count[0] + 7) // 8, sort, (0,) * (2 + split_rest))
         for j in range(STEP):
             mine[here + j] = -1
-            rest[there + j] = -1
+        for i, n in enumerate(others):
+            rests[2 * i + 1][0] = n
+            for j in range(STEP):
+                rests[2 * i][n + j] = -1
         todo, groups = mine, (here + size - 1) // size
         fetch_first()
 
@@ -136,6 +154,13 @@
 
     lax.fori_loop(0, BLOCKS, halve, 0)
 
+    def goal(word):
+        if not owners:
+            return word >> 16
+        g = word >> 19
+        distance = ((g >> 2) ^ place[0]) * 4 + ((g & 3) - place[1] & 3)
+        return (distance - owners[0]) * BLOCKS + ((word >> 16) & 7)
+
     def step(group, carry):
         @pl.when(group + depth - 1 < groups)
         def _():
@@ -145,7 +170,7 @@
         own = [todo[group * size + j] for j in range(size)]
         live = [w >= 0 for w in own]
         source = [jnp.where(l, table[(w >> 8) & 127], 0) for w, l in zip(own, live)]
-        target = [jnp.where(l, w >> 16, DUMMY) for w, l in zip(own, live)]
+        target = [jnp.where(l, goal(w), dummy) for w, l in zip(own, live)]
         for j in range(size):
             pltpu.make_async_copy(tiles.at[0], ring.at[slot, j], ring_sem.at[slot, j]).wait()
         results = [product(halves(ring[slot, j]), xs[source[j]]) for j in range(size)]
@@ -154,34 +179,33 @@
         return carry
 
     lax.fori_loop(0, groups, step, 0)
-    if last:
+    if owners:
 
         def hand_out(j, carry):
             for i, out in enumerate(parts):
-                owner = ((i // 4) ^ place[0]) * 4 + (i % 4 + place[1] & 3)
-                out[j] = acc[owner * BLOCKS + j]
+                out[j] = acc[i * BLOCKS + j]
             return carry
 
         lax.fori_loop(0, BLOCKS, hand_out, 0)
 
 
-def tile_products(place, words, count, tiles, pieces, so_far=None, last=False):
+def tile_products(place, words, count, tiles, pieces, so_far=None, split_rest=False, owners=()):
     first = so_far is None
-    size = LAST_STEP if last else STEP
+    size = LAST_STEP if owners else STEP
     smem = pl.BlockSpec(memory_space=pltpu.SMEM)
     vmem = pl.BlockSpec(memory_space=pltpu.VMEM)
     hbm = pl.BlockSpec(memory_space=pltpu.HBM)
-    sums = pltpu.VMEM((DUMMY + 1, TILE, FEAT), f32)
-    going_on = [pltpu.SMEM((TILES + 2 * STEP,), jnp.int32), pltpu.SMEM((1,), jnp.int32)]
+    listed = [pltpu.SMEM((TILES + 2 * STEP,), jnp.int32), pltpu.SMEM((1,), jnp.int32)]
+    rests = listed * (1 + split_rest)
     part = jax.ShapeDtypeStruct((BLOCKS, TILE, FEAT), f32)
+    sums = pltpu.VMEM(((len(owners) * BLOCKS or DUMMY) + 1, TILE, FEAT), f32)
     return pl.pallas_call(
-        functools.partial(tile_kernel, len(pieces), first, last),
-        out_shape=[part] * BLOCKS
-        if last
-        else [jax.ShapeDtypeStruct(r.shape, r.dtype) for r in (sums, *going_on)],
+        functools.partial(tile_kernel, len(pieces), first, split_rest, owners),
+        out_shape=[part] * len(owners)
+        or [jax.ShapeDtypeStruct(r.shape, r.dtype) for r in (sums, *rests)],
         in_specs=[smem, smem, smem, hbm] + [vmem] * (len(pieces) + (not first)),
-        out_specs=[vmem] * BLOCKS if last else [vmem, smem, smem],
-        scratch_shapes=[sums if last else going_on[0]]
+        out_specs=[vmem] * len(owners) or [vmem] + [smem] * len(rests),
+        scratch_shapes=[sums if owners else listed[0]]
         + [
             pltpu.VMEM((len(pieces) * BLOCKS, TILE, 2 * FEAT), bf16),
             pltpu.VMEM((RING // size, size, TILE, TILE), f32),
@@ -233,14 +257,21 @@
     far_above = move(far, "y", DOWN)
     far_below = move(below, "z_hi", SWAP)
     swapped = [move(p, "core", SWAP) for p in (below, above, far)]
+    sums, words, count = tile_products(place, words, count, tiles, [own, other, below, above, far])
+
+    two = after(two, sums)
     far_two = move(two, "z_hi", SWAP)
     late = [two, far_above, far_below]
     late_swapped = [move(p, "core", SWAP) for p in late]
-    early = [own, other, below, above, far, *swapped, *late]
-    sums, words, count = tile_products(place, words, count, tiles, early)
+    sums, soon, n_soon, words, count = tile_products(
+        place, words, count, tiles, [*swapped, *late], sums, split_rest=True
+    )
+
     far_two = after(far_two, sums)
-    mine, up, two, down, z_mine, z_up, z_two, z_down = tile_products(
-        place, words, count, tiles, [*late_swapped, far_two, move(far_two, "core", SWAP)], sums, last=True
+    last = [*late_swapped, far_two, move(far_two, "core", SWAP)]
+    z_up, z_two, z_down = tile_products(place, soon, n_soon, tiles, last, sums, owners=(5, 6, 7))
+    mine, up, two, down, z_mine = tile_products(
+        place, words, count, tiles, last, after(sums, z_two), owners=(0, 1, 2, 3, 4)
     )
 
     half = BLOCKS // 2

time: 99.4 us -> 96.5 us (0.971)
  Pallas kernels: 21.1 us -> 29.6 us
  waiting for transfers between devices: 41.3 us -> 33.4 us
  starting transfers between devices: 33.2 us -> 29.8 us
    pallas_call x2 -> x4, Pallas kernels: 17.1 us -> 25.6 us  [tile_products(): pl.pallas_call(functools.partial(tile_kernel, len(pieces), first, split_r...]
    ppermute x1, waiting for transfers between devices: 6.9 us -> 0.01 us  [body(): two = move(below, 'y', UP)]
    ppermute x1, waiting for transfers between devices: 9.86 us -> 4.24 us  [body(): got_two = move(z_two, 'z_lo', SWAP)]
    ppermute x1, waiting for transfers between devices: 0.01 us -> 3.94 us  [body(): far_two = move(two, 'z_hi', SWAP)]
    ppermute x1, starting transfers between devices: 1.22 us -> 0.01 us  [body(): two_up = move(two[:half] + got_two[:half], 'x', UP)]
  transfers between devices with their start and end apart: 23 -> 23, of which waited for: 10 -> 10; matrix products, arithmetic and copies ran while one was open for 0% -> 0% of each run, Pallas kernels for 14% -> 25%
where the time goes in v7:
time: 96.5 us; the launch traced here: 95.8 us
  waiting for transfers between devices  33.4 us (35%)
  starting transfers between devices  29.8 us (31%)
  Pallas kernels  29.6 us (31%)
  other arithmetic  2.16 us (2%)
    pallas_call x4, Pallas kernels, tile_products(): pl.pallas_call(functools.partial(tile_kernel, len(pieces), first, split_r...  25.6 us
    ppermute x1, waiting for transfers between devices, body(): move(jnp.concatenate([down[:half], down[half:] + two_down]), 'x', DOWN)  5.95 us
    ppermute x1, waiting for transfers between devices, body(): below = move(own, 'y', UP)  5.03 us
    ppermute x1, waiting for transfers between devices, body(): got_two = move(z_two, 'z_lo', SWAP)  4.24 us
    ppermute x1, waiting for transfers between devices, body(): far_two = move(two, 'z_hi', SWAP)  3.94 us
    ppermute x1, starting transfers between devices, body(): far = move(own, 'z_hi', SWAP)  3.88 us
    ppermute x1, starting transfers between devices, body(): far_below = move(below, 'z_hi', SWAP)  3.88 us
    ppermute x1, waiting for transfers between devices, body(): end_up = move(jnp.concatenate([up[:half] + two_up, up[half:]]), 'x', UP)  3.82 us
  transfers between devices with their start and end apart: 23, of which 10 were waited for; matrix products, arithmetic and copies ran while one was open for 0% of the time, Pallas kernels for 25%

profile of v7, /device:TPU:0, one launch (start us, length us, event | category | flops | bytes accessed | tf_op | source)
XLA Modules:
  0.0 95.8 jit_solution(15440643313842971753)
XLA Ops:
  0.0 0.7 convert_bitcast_fusion
  0.7 1.1 %select_maximum_fusion.refs_4_ = f32[1032,128]{1,0:T(8,128)S(1)} fusion(f32[1,8]{1,0:T(1,128)S(1)} %convert_bitcast_fusion, f32[1024,128]{1,0:T(8,128)} %param.7), kind=kLoop, calls=%fused_computation | loop fusion | flops 396288 | bytes 1052704 | tf_op jit(solution)/shard_map/concatenate | solution.py:235
  1.7 1.7 %collective-permute-start.1 = (f32[1032,128]{1,0:T(8,128)S(1)}, f32[1032,128]{1,0:T(8,128)S(1)}, u32[]{:S(2)}, u32[]{:S(2)}) collective-permute-start(f32[1032,128]{1,0:T(8,128)S(1)} %select_maximum_fusion.refs_4_), channel_id=1, source_target_pairs={{0,2},{2,4},{4,6},{6,0},{1,3},{3,5},{5,7},{7,1},{8,10},{10,12},{12... | collective-permute-start | bytes 1585160 | tf_op jit(solution)/shard_map/ppermute | solution.py:236
  3.5 3.9 %collective-permute-start.3 = (f32[1032,128]{1,0:T(8,128)S(1)}, f32[1032,128]{1,0:T(8,128)S(1)}, u32[]{:S(2)}, u32[]{:S(2)}) collective-permute-start(f32[1032,128]{1,0:T(8,128)S(1)} %select_maximum_fusion.refs_4_), channel_id=1, source_target_pairs={{0,8},{8,0},{1,9},{9,1},{2,10},{10,2},{3,11},{11,3},{4,12},{12,4},... | collective-permute-start | bytes 1585160 | tf_op jit(solution)/shard_map/ppermute | solution.py:238
  7.3 1.7 %collective-permute-start.2 = (f32[1032,128]{1,0:T(8,128)S(1)}, f32[1032,128]{1,0:T(8,128)S(1)}, u32[]{:S(2)}, u32[]{:S(2)}) collective-permute-start(f32[1032,128]{1,0:T(8,128)S(1)} %select_maximum_fusion.refs_4_), channel_id=1, source_target_pairs={{0,6},{2,0},{4,2},{6,4},{1,7},{3,1},{5,3},{7,5},{8,14},{10,8},{12,... | collective-permute-start | bytes 1585160 | tf_op jit(solution)/shard_map/ppermute | solution.py:237
  9.0 0.0 collective-permute-start
  9.0 2.9 %shard_map.73 = (s32[288]{0:T(512)}, s32[1]{0:T(128)}) custom-call(s32[16,16]{1,0:T(8,128)} %bitcast.13, s32[16,16]{1,0:T(8,128)} %bitcast.14), custom_call_target="tpu_custom_call" | custom-call | flops 100000 | bytes 10000 | tf_op jit(solution)/shard_map/pallas_call | solution.py:244
  11.9 5.0 %collective-permute-done.1.refs_6_ = f32[1032,128]{1,0:T(8,128)S(1)} collective-permute-done((f32[1032,128]{1,0:T(8,128)S(1)}, f32[1032,128]{1,0:T(8,128)S(1)}, u32[]{:S(2)}, u32[]{:S(2)}) %collective-permute-start.1) | collective-permute-done | bytes 528416 | tf_op jit(solution)/shard_map/ppermute | solution.py:236
  16.9 0.3 collective-permute-start.7
  17.2 3.9 %collective-permute-start.9 = (f32[1032,128]{1,0:T(8,128)S(1)}, f32[1032,128]{1,0:T(8,128)}, u32[]{:S(2)}, u32[]{:S(2)}) collective-permute-start(f32[1032,128]{1,0:T(8,128)S(1)} %collective-permute-done.1.refs_6_), channel_id=1, source_target_pairs={{0,8},{8,0},{1,9},{9,1},{2,10},{10,2},{3,11},{11,3},{4,12},{12,4},... | collective-permute-start | bytes 1585160 | tf_op jit(solution)/shard_map/ppermute | solution.py:258
  21.1 0.1 pad_add_fusion.refs_0_
  21.2 0.0 collective-permute-done.3.refs_8_
  21.2 0.0 collective-permute-start.4
  21.2 0.0 collective-permute-done.2.refs_7_
  21.2 3.0 %collective-permute-start.8 = (f32[1032,128]{1,0:T(8,128)S(1)}, f32[1032,128]{1,0:T(8,128)S(1)}, u32[]{:S(2)}, u32[]{:S(2)}) collective-permute-start(f32[1032,128]{1,0:T(8,128)S(1)} %collective-permute-done.3.refs_8_), channel_id=1, source_target_pairs={{0,6},{2,0},{4,2},{6,4},{1,7},{3,1},{5,3},{7,5},{8,14},{10,8},{12,... | collective-permute-start | bytes 1585160 | tf_op jit(solution)/shard_map/ppermute | solution.py:257
  24.2 0.0 collective-permute-done.refs_5_
  24.2 0.2 collective-permute-start.6
  24.4 0.7 copy-done.1
  25.1 7.9 %shard_map.74 = (f32[65,128,128]{2,1,0:T(8,128)S(1)}, s32[288]{0:T(512)S(1)}, s32[1]{0:T(128)}) custom-call(s32[2]{0:T(128)S(1)} %pad_add_fusion.refs_0_, s32[288]{0:T(512)S(1)} %copy-done.1, s32[1]{0:T(128)} %get-tuple-element.28.refs_2_, f32[256,128,128]{2,1,0:T(8,128)} %bitcast.9, f32[1032,128]{1,0:T(8,128)S(1)} %select_maximum_fusion.refs_4_, ...), custom_call_target="tpu_custom_call" | custom-call | flops 100000 | bytes 10000 | tf_op jit(solution)/shard_map/pallas_call | solution.py:202
  33.0 0.1 collective-permute-start.5
  33.1 2.3 %collective-permute-start.13 = (f32[1032,128]{1,0:T(8,128)S(1)}, f32[1032,128]{1,0:T(8,128)S(1)}, u32[]{:S(2)}, u32[]{:S(2)}) collective-permute-start(f32[1032,128]{1,0:T(8,128)S(1)} %collective-permute-done.7.refs_7_), channel_id=1, source_target_pairs={{0,8},{8,0},{1,9},{9,1},{2,10},{10,2},{3,11},{11,3},{4,12},{12,4},... | collective-permute-start | bytes 1585160 | tf_op jit(solution)/shard_map/ppermute | solution.py:263
  35.4 0.7 collective-permute-done.8.refs_8_
  36.1 0.5 collective-permute-start.11
  36.6 8.5 %shard_map.75 = (f32[65,128,128]{2,1,0:T(8,128)S(1)}, s32[288]{0:T(512)S(1)}, s32[1]{0:T(128)}, s32[288]{0:T(512)S(1)}, s32[1]{0:T(128)}) custom-call(s32[2]{0:T(128)S(1)} %pad_add_fusion.refs_0_, s32[288]{0:T(512)S(1)} %get-tuple-element.30.refs_1_, s32[1]{0:T(128)} %get-tuple-element.31.refs_2_, f32[256,128,128]{2,1,0:T(8,128)} %bitcast.10, ...), custom_call_target="tpu_custom_call" | custom-call | flops 100000 | bytes 10000 | tf_op jit(solution)/shard_map/pallas_call | solution.py:202
  45.1 3.9 %collective-permute-done.13.refs_7_ = f32[1032,128]{1,0:T(8,128)S(1)} collective-permute-done((f32[1032,128]{1,0:T(8,128)S(1)}, f32[1032,128]{1,0:T(8,128)S(1)}, u32[]{:S(2)}, u32[]{:S(2)}) %collective-permute-start.13) | collective-permute-done | bytes 528416 | tf_op jit(solution)/shard_map/ppermute | solution.py:263
  49.0 1.9 %collective-permute-done.14.refs_8_ = f32[1032,128]{1,0:T(8,128)S(1)} collective-permute-done((f32[1032,128]{1,0:T(8,128)S(1)}, f32[1032,128]{1,0:T(8,128)S(1)}, u32[]{:S(2)}, u32[]{:S(2)}) %collective-permute-start.14) | collective-permute-done | bytes 528416 | tf_op jit(solution)/shard_map/ppermute | solution.py:271
  50.9 4.4 %shard_map.76 = (f32[8,128,128]{2,1,0:T(8,128)S(1)}, f32[8,128,128]{2,1,0:T(8,128)S(1)}, f32[8,128,128]{2,1,0:T(8,128)S(1)}) custom-call(s32[2]{0:T(128)S(1)} %pad_add_fusion.refs_0_, s32[288]{0:T(512)S(1)} %get-tuple-element.38.refs_1_, s32[1]{0:T(128)} %get-tuple-element.39.refs_2_, f32[256,128,128]{2,1,0:T(8,128)} %bitcast.11, ...), custom_call_target="tpu_custom_call" | custom-call | flops 100000 | bytes 10000 | tf_op jit(solution)/shard_map/pallas_call | solution.py:202
  55.4 1.3 %collective-permute-start.15 = (f32[8,128,128]{2,1,0:T(8,128)S(1)}, f32[8,128,128]{2,1,0:T(8,128)S(1)}, u32[]{:S(2)}, u32[]{:S(2)}) collective-permute-start(f32[8,128,128]{2,1,0:T(8,128)S(1)} %get-tuple-element.40), channel_id=1, source_target_pairs={{0,64},{64,0},{1,65},{65,1},{2,66},{66,2},{3,67},{67,3},{4,68},{68... | collective-permute-start | bytes 1572872 | tf_op jit(solution)/shard_map/ppermute | solution.py:278
  56.6 1.2 %collective-permute-start.20 = (f32[8,128,128]{2,1,0:T(8,128)S(1)}, f32[8,128,128]{2,1,0:T(8,128)S(1)}, u32[]{:S(2)}, u32[]{:S(2)}) collective-permute-start(f32[8,128,128]{2,1,0:T(8,128)S(1)} %get-tuple-element.47), channel_id=1, source_target_pairs={{0,16},{16,32},{32,48},{48,0},{1,17},{17,33},{33,49},{49,1},{2,18}... | collective-permute-start | bytes 1572872 | tf_op jit(solution)/shard_map/ppermute | solution.py:279
  57.8 2.1 %collective-permute-start.21 = (f32[8,128,128]{2,1,0:T(8,128)S(1)}, f32[8,128,128]{2,1,0:T(8,128)S(1)}, u32[]{:S(2)}, u32[]{:S(2)}) collective-permute-start(f32[8,128,128]{2,1,0:T(8,128)S(1)} %get-tuple-element.48), channel_id=1, source_target_pairs={{0,48},{16,0},{32,16},{48,32},{1,49},{17,1},{33,17},{49,33},{2,50}... | collective-permute-start | bytes 1572872 | tf_op jit(solution)/shard_map/ppermute | solution.py:280
  59.9 4.8 %shard_map.77 = (f32[8,128,128]{2,1,0:T(8,128)S(1)}, f32[8,128,128]{2,1,0:T(8,128)S(1)}, f32[8,128,128]{2,1,0:T(8,128)S(1)}, f32[8,128,128]{2,1,0:T(8,128)S(1)}, f32[8,128,128]{2,1,0:T(8,128)S(1)}) custom-call(s32[2]{0:T(128)S(1)} %pad_add_fusion.refs_0_, s32[288]{0:T(512)S(1)} %get-tuple-element.34.refs_1_, s32[1]{0:T(128)} %get-tuple-element.35.refs_2_, ...), custom_call_target="tpu_custom_call" | custom-call | flops 100000 | bytes 10000 | tf_op jit(solution)/shard_map/pallas_call | solution.py:202
  64.7 0.0 copy-start
  64.7 0.0 copy-start.2
  64.8 4.2 %collective-permute-done.15 = f32[8,128,128]{2,1,0:T(8,128)S(1)} collective-permute-done((f32[8,128,128]{2,1,0:T(8,128)S(1)}, f32[8,128,128]{2,1,0:T(8,128)S(1)}, u32[]{:S(2)}, u32[]{:S(2)}) %collective-permute-start.15) | collective-permute-done | bytes 524320 | tf_op jit(solution)/shard_map/ppermute | solution.py:278
  69.0 0.1 slice_add_fusion
  69.1 2.5 %collective-permute-start.18 = (f32[4,128,128]{2,1,0:T(8,128)S(1)}, f32[4,128,128]{2,1,0:T(8,128)S(1)}, u32[]{:S(2)}, u32[]{:S(2)}) collective-permute-start(f32[4,128,128]{2,1,0:T(8,128)S(1)} %get-tuple-element.49), channel_id=1, source_target_pairs={{0,48},{16,0},{32,16},{48,32},{1,49},{17,1},{33,17},{49,33},{2,50}... | collective-permute-start | bytes 786440 | tf_op jit(solution)/shard_map/ppermute | solution.py:282
  71.6 0.1 add_add_fusion
  71.7 1.8 %collective-permute-start.22 = (f32[8,128,128]{2,1,0:T(8,128)S(1)}, f32[8,128,128]{2,1,0:T(8,128)S(1)}, u32[]{:S(2)}, u32[]{:S(2)}) collective-permute-start(f32[8,128,128]{2,1,0:T(8,128)S(1)} %add_add_fusion), channel_id=1, source_target_pairs={{0,64},{64,0},{1,65},{65,1},{2,66},{66,2},{3,67},{67,3},{4,68},{68... | collective-permute-start | bytes 1572872 | tf_op jit(solution)/shard_map/ppermute | solution.py:283
  73.5 3.8 %collective-permute-done.18 = f32[4,128,128]{2,1,0:T(8,128)S(1)} collective-permute-done((f32[4,128,128]{2,1,0:T(8,128)S(1)}, f32[4,128,128]{2,1,0:T(8,128)S(1)}, u32[]{:S(2)}, u32[]{:S(2)}) %collective-permute-start.18) | collective-permute-done | bytes 262176 | tf_op jit(solution)/shard_map/ppermute | solution.py:282
  77.3 0.1 fusion
  77.4 3.4 %collective-permute-start.19 = (f32[8,128,128]{2,1,0:T(8,128)S(1)}, f32[8,128,128]{2,1,0:T(8,128)S(1)}, u32[]{:S(2)}, u32[]{:S(2)}) collective-permute-start(f32[8,128,128]{2,1,0:T(8,128)S(1)} %pad_maximum_fusion.1), channel_id=1, source_target_pairs={{0,48},{16,0},{32,16},{48,32},{1,49},{17,1},{33,17},{49,33},{2,50}... | collective-permute-start | bytes 1572872 | tf_op jit(solution)/shard_map/ppermute | solution.py:285
  80.8 0.9 collective-permute-done.16
  81.7 0.1 slice_add_fusion.3
  81.8 0.1 collective-permute-start.17
  81.9 3.1 %collective-permute-done.22.d = f32[8,128,128]{2,1,0:T(8,128)S(1)} collective-permute-done((f32[8,128,128]{2,1,0:T(8,128)S(1)}, f32[8,128,128]{2,1,0:T(8,128)S(1)}, u32[]{:S(2)}, u32[]{:S(2)}) %collective-permute-start.22) | collective-permute-done | bytes 524320 | tf_op jit(solution)/shard_map/ppermute | solution.py:283
  84.9 6.0 %collective-permute-done.19.c = f32[8,128,128]{2,1,0:T(8,128)S(1)} collective-permute-done((f32[8,128,128]{2,1,0:T(8,128)S(1)}, f32[8,128,128]{2,1,0:T(8,128)S(1)}, u32[]{:S(2)}, u32[]{:S(2)}) %collective-permute-start.19) | collective-permute-done | bytes 524320 | tf_op jit(solution)/shard_map/ppermute | solution.py:285
  90.9 3.8 %collective-permute-done.17.b = f32[8,128,128]{2,1,0:T(8,128)S(1)} collective-permute-done((f32[8,128,128]{2,1,0:T(8,128)S(1)}, f32[8,128,128]{2,1,0:T(8,128)S(1)}, u32[]{:S(2)}, u32[]{:S(2)}) %collective-permute-start.17) | collective-permute-done | bytes 524320 | tf_op jit(solution)/shard_map/ppermute | solution.py:284
  94.7 1.1 %shard_map.78 = f32[1024,128]{1,0:T(8,128)} custom-call(f32[8,128,128]{2,1,0:T(8,128)S(1)} %get-tuple-element.42.a, f32[8,128,128]{2,1,0:T(8,128)S(1)} %collective-permute-done.17.b, f32[8,128,128]{2,1,0:T(8,128)S(1)} %collective-permute-done.19.c, f32[8,128,128]{2,1,0:T(8,128)S(1)} %collective-permute-done.22.d, f32[128,128]{1,0:T(8,128)S(1)} %copy-done, ...), custom_call_target="tpu_custom_call" | custom-call | tf_op jit(solution)/shard_map/pallas_call | solution.py:287
  (19 shorter events, 0.1 us)
Async XLA Ops:
  1.7 15.2 %collective-permute-start.1 = (f32[1032,128]{1,0:T(8,128)S(1)}, f32[1032,128]{1,0:T(8,128)S(1)}, u32[]{:S(2)}, u32[]{:S(2)}) collective-permute-start(f32[1032,128]{1,0:T(8,128)S(1)} %select_maximum_fusion.refs_4_), channel_id=1, source_target_pairs={{0,2},{2,4},{4,6},{6,0},{1,3},{3,5},{5,7},{7,1},{8,10},{10,12},{12... | collective-permute-start | bytes 1585160 | tf_op jit(solution)/shard_map/ppermute | solution.py:236
  3.5 17.7 %collective-permute-start.3 = (f32[1032,128]{1,0:T(8,128)S(1)}, f32[1032,128]{1,0:T(8,128)S(1)}, u32[]{:S(2)}, u32[]{:S(2)}) collective-permute-start(f32[1032,128]{1,0:T(8,128)S(1)} %select_maximum_fusion.refs_4_), channel_id=1, source_target_pairs={{0,8},{8,0},{1,9},{9,1},{2,10},{10,2},{3,11},{11,3},{4,12},{12,4},... | collective-permute-start | bytes 1585160 | tf_op jit(solution)/shard_map/ppermute | solution.py:238
  7.3 13.9 %collective-permute-start.2 = (f32[1032,128]{1,0:T(8,128)S(1)}, f32[1032,128]{1,0:T(8,128)S(1)}, u32[]{:S(2)}, u32[]{:S(2)}) collective-permute-start(f32[1032,128]{1,0:T(8,128)S(1)} %select_maximum_fusion.refs_4_), channel_id=1, source_target_pairs={{0,6},{2,0},{4,2},{6,4},{1,7},{3,1},{5,3},{7,5},{8,14},{10,8},{12,... | collective-permute-start | bytes 1585160 | tf_op jit(solution)/shard_map/ppermute | solution.py:237
  9.0 15.2 %collective-permute-start = (f32[1032,128]{1,0:T(8,128)S(1)}, f32[1032,128]{1,0:T(8,128)S(1)}, u32[]{:S(2)}, u32[]{:S(2)}) collective-permute-start(f32[1032,128]{1,0:T(8,128)S(1)} %select_maximum_fusion.refs_4_), channel_id=1, source_target_pairs={{0,1},{1,0},{2,3},{3,2},{4,5},{5,4},{6,7},{7,6},{8,9},{9,8},{10,11... | collective-permute-start | bytes 1585160 | tf_op jit(solution)/shard_map/ppermute | solution.py:239
  16.9 16.1 %collective-permute-start.7 = (f32[1032,128]{1,0:T(8,128)S(1)}, f32[1032,128]{1,0:T(8,128)S(1)}, u32[]{:S(2)}, u32[]{:S(2)}) collective-permute-start(f32[1032,128]{1,0:T(8,128)S(1)} %collective-permute-done.1.refs_6_), channel_id=1, source_target_pairs={{0,2},{2,4},{4,6},{6,0},{1,3},{3,5},{5,7},{7,1},{8,10},{10,12},{12... | collective-permute-start | bytes 1585160 | tf_op jit(solution)/shard_map/ppermute | solution.py:256
  17.2 15.9 %collective-permute-start.9 = (f32[1032,128]{1,0:T(8,128)S(1)}, f32[1032,128]{1,0:T(8,128)}, u32[]{:S(2)}, u32[]{:S(2)}) collective-permute-start(f32[1032,128]{1,0:T(8,128)S(1)} %collective-permute-done.1.refs_6_), channel_id=1, source_target_pairs={{0,8},{8,0},{1,9},{9,1},{2,10},{10,2},{3,11},{11,3},{4,12},{12,4},... | collective-permute-start | bytes 1585160 | tf_op jit(solution)/shard_map/ppermute | solution.py:258
  21.2 14.2 %collective-permute-start.4 = (f32[1032,128]{1,0:T(8,128)S(1)}, f32[1032,128]{1,0:T(8,128)S(1)}, u32[]{:S(2)}, u32[]{:S(2)}) collective-permute-start(f32[1032,128]{1,0:T(8,128)S(1)} %collective-permute-done.1.refs_6_), channel_id=1, source_target_pairs={{0,1},{1,0},{2,3},{3,2},{4,5},{5,4},{6,7},{7,6},{8,9},{9,8},{10,11... | collective-permute-start | bytes 1585160 | tf_op jit(solution)/shard_map/ppermute | solution.py:259
  21.2 14.9 %collective-permute-start.8 = (f32[1032,128]{1,0:T(8,128)S(1)}, f32[1032,128]{1,0:T(8,128)S(1)}, u32[]{:S(2)}, u32[]{:S(2)}) collective-permute-start(f32[1032,128]{1,0:T(8,128)S(1)} %collective-permute-done.3.refs_8_), channel_id=1, source_target_pairs={{0,6},{2,0},{4,2},{6,4},{1,7},{3,1},{5,3},{7,5},{8,14},{10,8},{12,... | collective-permute-start | bytes 1585160 | tf_op jit(solution)/shard_map/ppermute | solution.py:257
  24.2 11.9 %collective-permute-start.6 = (f32[1032,128]{1,0:T(8,128)S(1)}, f32[1032,128]{1,0:T(8,128)S(1)}, u32[]{:S(2)}, u32[]{:S(2)}) collective-permute-start(f32[1032,128]{1,0:T(8,128)S(1)} %collective-permute-done.3.refs_8_), channel_id=1, source_target_pairs={{0,1},{1,0},{2,3},{3,2},{4,5},{5,4},{6,7},{7,6},{8,9},{9,8},{10,11... | collective-permute-start | bytes 1585160 | tf_op jit(solution)/shard_map/ppermute | solution.py:259
  24.4 0.7 copy-start.1
  33.0 3.6 %collective-permute-start.5 = (f32[1032,128]{1,0:T(8,128)S(1)}, f32[1032,128]{1,0:T(8,128)S(1)}, u32[]{:S(2)}, u32[]{:S(2)}) collective-permute-start(f32[1032,128]{1,0:T(8,128)S(1)} %collective-permute-done.2.refs_7_), channel_id=1, source_target_pairs={{0,1},{1,0},{2,3},{3,2},{4,5},{5,4},{6,7},{7,6},{8,9},{9,8},{10,11... | collective-permute-start | bytes 1585160 | tf_op jit(solution)/shard_map/ppermute | solution.py:259
  33.1 15.9 %collective-permute-start.13 = (f32[1032,128]{1,0:T(8,128)S(1)}, f32[1032,128]{1,0:T(8,128)S(1)}, u32[]{:S(2)}, u32[]{:S(2)}) collective-permute-start(f32[1032,128]{1,0:T(8,128)S(1)} %collective-permute-done.7.refs_7_), channel_id=1, source_target_pairs={{0,8},{8,0},{1,9},{9,1},{2,10},{10,2},{3,11},{11,3},{4,12},{12,4},... | collective-permute-start | bytes 1585160 | tf_op jit(solution)/shard_map/ppermute | solution.py:263
  35.4 13.7 %collective-permute-start.10 = (f32[1032,128]{1,0:T(8,128)S(1)}, f32[1032,128]{1,0:T(8,128)S(1)}, u32[]{:S(2)}, u32[]{:S(2)}) collective-permute-start(f32[1032,128]{1,0:T(8,128)S(1)} %collective-permute-done.7.refs_7_), channel_id=1, source_target_pairs={{0,1},{1,0},{2,3},{3,2},{4,5},{5,4},{6,7},{7,6},{8,9},{9,8},{10,11... | collective-permute-start | bytes 1585160 | tf_op jit(solution)/shard_map/ppermute | solution.py:265
  36.1 12.9 %collective-permute-start.12 = (f32[1032,128]{1,0:T(8,128)}, f32[1032,128]{1,0:T(8,128)S(1)}, u32[]{:S(2)}, u32[]{:S(2)}) collective-permute-start(f32[1032,128]{1,0:T(8,128)} %collective-permute-done.9.refs_9_), channel_id=1, source_target_pairs={{0,1},{1,0},{2,3},{3,2},{4,5},{5,4},{6,7},{7,6},{8,9},{9,8},{10,11... | collective-permute-start | bytes 1585160 | tf_op jit(solution)/shard_map/ppermute | solution.py:265
  36.1 12.9 %collective-permute-start.11 = (f32[1032,128]{1,0:T(8,128)S(1)}, f32[1032,128]{1,0:T(8,128)S(1)}, u32[]{:S(2)}, u32[]{:S(2)}) collective-permute-start(f32[1032,128]{1,0:T(8,128)S(1)} %collective-permute-done.8.refs_8_), channel_id=1, source_target_pairs={{0,1},{1,0},{2,3},{3,2},{4,5},{5,4},{6,7},{7,6},{8,9},{9,8},{10,11... | collective-permute-start | bytes 1585160 | tf_op jit(solution)/shard_map/ppermute | solution.py:265
  49.0 1.9 %collective-permute-start.14 = (f32[1032,128]{1,0:T(8,128)S(1)}, f32[1032,128]{1,0:T(8,128)S(1)}, u32[]{:S(2)}, u32[]{:S(2)}) collective-permute-start(f32[1032,128]{1,0:T(8,128)S(1)} %collective-permute-done.13.refs_7_), channel_id=1, source_target_pairs={{0,1},{1,0},{2,3},{3,2},{4,5},{5,4},{6,7},{7,6},{8,9},{9,8},{10,11... | collective-permute-start | bytes 1585160 | tf_op jit(solution)/shard_map/ppermute | solution.py:271
  55.4 13.6 %collective-permute-start.15 = (f32[8,128,128]{2,1,0:T(8,128)S(1)}, f32[8,128,128]{2,1,0:T(8,128)S(1)}, u32[]{:S(2)}, u32[]{:S(2)}) collective-permute-start(f32[8,128,128]{2,1,0:T(8,128)S(1)} %get-tuple-element.40), channel_id=1, source_target_pairs={{0,64},{64,0},{1,65},{65,1},{2,66},{66,2},{3,67},{67,3},{4,68},{68... | collective-permute-start | bytes 1572872 | tf_op jit(solution)/shard_map/ppermute | solution.py:278
  56.6 15.0 %collective-permute-start.20 = (f32[8,128,128]{2,1,0:T(8,128)S(1)}, f32[8,128,128]{2,1,0:T(8,128)S(1)}, u32[]{:S(2)}, u32[]{:S(2)}) collective-permute-start(f32[8,128,128]{2,1,0:T(8,128)S(1)} %get-tuple-element.47), channel_id=1, source_target_pairs={{0,16},{16,32},{32,48},{48,0},{1,17},{17,33},{33,49},{49,1},{2,18}... | collective-permute-start | bytes 1572872 | tf_op jit(solution)/shard_map/ppermute | solution.py:279
  57.8 13.8 %collective-permute-start.21 = (f32[8,128,128]{2,1,0:T(8,128)S(1)}, f32[8,128,128]{2,1,0:T(8,128)S(1)}, u32[]{:S(2)}, u32[]{:S(2)}) collective-permute-start(f32[8,128,128]{2,1,0:T(8,128)S(1)} %get-tuple-element.48), channel_id=1, source_target_pairs={{0,48},{16,0},{32,16},{48,32},{1,49},{17,1},{33,17},{49,33},{2,50}... | collective-permute-start | bytes 1572872 | tf_op jit(solution)/shard_map/ppermute | solution.py:280
  64.7 30.0 %copy-start = (f32[128,128]{1,0:T(8,128)S(1)}, f32[128,128]{1,0:T(8,128)}, u32[]{:S(2)}) copy-start(f32[128,128]{1,0:T(8,128)} %weight.1) | copy-start | bytes 196612
  64.7 30.0 %copy-start.2 = (f32[128]{0:T(128)S(1)}, f32[128]{0:T(128)}, u32[]{:S(2)}) copy-start(f32[128]{0:T(128)} %param.13) | copy-start | bytes 1540
  69.1 8.2 %collective-permute-start.18 = (f32[4,128,128]{2,1,0:T(8,128)S(1)}, f32[4,128,128]{2,1,0:T(8,128)S(1)}, u32[]{:S(2)}, u32[]{:S(2)}) collective-permute-start(f32[4,128,128]{2,1,0:T(8,128)S(1)} %get-tuple-element.49), channel_id=1, source_target_pairs={{0,48},{16,0},{32,16},{48,32},{1,49},{17,1},{33,17},{49,33},{2,50}... | collective-permute-start | bytes 786440 | tf_op jit(solution)/shard_map/ppermute | solution.py:282
  71.7 13.3 %collective-permute-start.22 = (f32[8,128,128]{2,1,0:T(8,128)S(1)}, f32[8,128,128]{2,1,0:T(8,128)S(1)}, u32[]{:S(2)}, u32[]{:S(2)}) collective-permute-start(f32[8,128,128]{2,1,0:T(8,128)S(1)} %add_add_fusion), channel_id=1, source_target_pairs={{0,64},{64,0},{1,65},{65,1},{2,66},{66,2},{3,67},{67,3},{4,68},{68... | collective-permute-start | bytes 1572872 | tf_op jit(solution)/shard_map/ppermute | solution.py:283
  73.5 8.2 %collective-permute-start.16 = (f32[4,128,128]{2,1,0:T(8,128)S(1)}, f32[4,128,128]{2,1,0:T(8,128)S(1)}, u32[]{:S(2)}, u32[]{:S(2)}) collective-permute-start(f32[4,128,128]{2,1,0:T(8,128)S(1)} %get-tuple-element.50), channel_id=1, source_target_pairs={{0,16},{16,32},{32,48},{48,0},{1,17},{17,33},{33,49},{49,1},{2,18}... | collective-permute-start | bytes 786440 | tf_op jit(solution)/shard_map/ppermute | solution.py:281
  77.4 13.5 %collective-permute-start.19 = (f32[8,128,128]{2,1,0:T(8,128)S(1)}, f32[8,128,128]{2,1,0:T(8,128)S(1)}, u32[]{:S(2)}, u32[]{:S(2)}) collective-permute-start(f32[8,128,128]{2,1,0:T(8,128)S(1)} %pad_maximum_fusion.1), channel_id=1, source_target_pairs={{0,48},{16,0},{32,16},{48,32},{1,49},{17,1},{33,17},{49,33},{2,50}... | collective-permute-start | bytes 1572872 | tf_op jit(solution)/shard_map/ppermute | solution.py:285
  81.8 12.9 %collective-permute-start.17 = (f32[8,128,128]{2,1,0:T(8,128)S(1)}, f32[8,128,128]{2,1,0:T(8,128)S(1)}, u32[]{:S(2)}, u32[]{:S(2)}) collective-permute-start(f32[8,128,128]{2,1,0:T(8,128)S(1)} %pad_maximum_fusion), channel_id=1, source_target_pairs={{0,16},{16,32},{32,48},{48,0},{1,17},{17,33},{33,49},{49,1},{2,18}... | collective-permute-start | bytes 1572872 | tf_op jit(solution)/shard_map/ppermute | solution.py:284

commit v8 on v7

--- a/solution.py
+++ b/solution.py
@@ -10,6 +10,7 @@
 TILE = 128
 FEAT = 128
 BLOCKS = 8
+HALF = 4
 SLOTS = 16
 BUCKETS = 16
 TILES = BUCKETS * SLOTS
@@ -54,14 +55,15 @@
         words[total + j] = -1
 
 
-def tile_kernel(n_pieces, first, split_rest, owners, *refs):
+def tile_kernel(n_pieces, first, split_rest, owners, halved, *refs):
     place, words, count, tiles = refs[:4]
     refs = refs[4:]
     pieces, refs = refs[:n_pieces], refs[n_pieces:]
     so_far = None if first else refs[0]
     outs = refs[1 - first :]
     if owners:
-        parts, (acc, *scratch) = outs[: len(owners)], outs[len(owners) :]
+        n_parts = len(owners) + len(halved)
+        parts, (acc, *scratch) = outs[:n_parts], outs[n_parts:]
         dummy, size = len(owners) * BLOCKS, LAST_STEP
     else:
         acc, *outs = outs
@@ -182,14 +184,17 @@
     if owners:
 
         def hand_out(j, carry):
-            for i, out in enumerate(parts):
-                out[j] = acc[i * BLOCKS + j]
+            at = 0
+            for out in parts:
+                for part in range(out.shape[0] // HALF):
+                    out[part * HALF + j] = acc[at + j]
+                    at += HALF
             return carry
 
-        lax.fori_loop(0, BLOCKS, hand_out, 0)
-
-
-def tile_products(place, words, count, tiles, pieces, so_far=None, split_rest=False, owners=()):
+        lax.fori_loop(0, HALF, hand_out, 0)
+
+
+def tile_products(place, words, count, tiles, pieces, so_far=None, split_rest=False, owners=(), halved=()):
     first = so_far is None
     size = LAST_STEP if owners else STEP
     smem = pl.BlockSpec(memory_space=pltpu.SMEM)
@@ -197,14 +202,15 @@
     hbm = pl.BlockSpec(memory_space=pltpu.HBM)
     listed = [pltpu.SMEM((TILES + 2 * STEP,), jnp.int32), pltpu.SMEM((1,), jnp.int32)]
     rests = listed * (1 + split_rest)
-    part = jax.ShapeDtypeStruct((BLOCKS, TILE, FEAT), f32)
+    sizes = [n for o in owners for n in ([HALF, HALF] if o in halved else [BLOCKS])]
+    parts = [jax.ShapeDtypeStruct((n, TILE, FEAT), f32) for n in sizes]
     sums = pltpu.VMEM(((len(owners) * BLOCKS or DUMMY) + 1, TILE, FEAT), f32)
     return pl.pallas_call(
-        functools.partial(tile_kernel, len(pieces), first, split_rest, owners),
-        out_shape=[part] * len(owners)
+        functools.partial(tile_kernel, len(pieces), first, split_rest, owners, halved),
+        out_shape=parts
         or [jax.ShapeDtypeStruct(r.shape, r.dtype) for r in (sums, *rests)],
         in_specs=[smem, smem, smem, hbm] + [vmem] * (len(pieces) + (not first)),
-        out_specs=[vmem] * len(owners) or [vmem] + [smem] * len(rests),
+        out_specs=[vmem] * len(parts) or [vmem] + [smem] * len(rests),
         scratch_shapes=[sums if owners else listed[0]]
         + [
             pltpu.VMEM((len(pieces) * BLOCKS, TILE, 2 * FEAT), bf16),
@@ -219,10 +225,12 @@
     )(place, words, count, tiles, *pieces, *([] if first else [so_far]))
 
 
-def finish_kernel(a, b, c, d, weight, bias, out):
-    total = a[...] + b[...] + c[...] + d[...]
-    hidden = product(halves(total.reshape(BLOCKS * TILE, FEAT)), halves(weight[...]))
-    out[...] = jnp.maximum(hidden + bias[...], 0.0)
+def finish_kernel(own, far, up_a, up_b, down_a, down_b, weight, bias, out):
+    for half, (up, down) in enumerate(((up_a, down_a), (up_b, down_b))):
+        rows = pl.ds(half * HALF, HALF)
+        total = (own[rows] + far[rows] + up[...] + down[...]).reshape(HALF * TILE, FEAT)
+        hidden = product(halves(total), halves(weight[...]))
+        out[pl.ds(half * HALF * TILE, HALF * TILE), :] = jnp.maximum(hidden + bias[...], 0.0)
 
 
 def after(value, *others):
@@ -259,36 +267,36 @@
     swapped = [move(p, "core", SWAP) for p in (below, above, far)]
     sums, words, count = tile_products(place, words, count, tiles, [own, other, below, above, far])
 
-    two = after(two, sums)
+    two = after(two, sums, far_above, far_below)
     far_two = move(two, "z_hi", SWAP)
-    late = [two, far_above, far_below]
-    late_swapped = [move(p, "core", SWAP) for p in late]
+    late_swapped = [move(p, "core", SWAP) for p in (two, far_above, far_below)]
     sums, soon, n_soon, words, count = tile_products(
-        place, words, count, tiles, [*swapped, *late], sums, split_rest=True
+        place, words, count, tiles, [*swapped, two], sums, split_rest=True
     )
 
     far_two = after(far_two, sums)
-    last = [*late_swapped, far_two, move(far_two, "core", SWAP)]
+    last = [far_above, far_below, *late_swapped, far_two, move(far_two, "core", SWAP)]
     z_up, z_two, z_down = tile_products(place, soon, n_soon, tiles, last, sums, owners=(5, 6, 7))
-    mine, up, two, down, z_mine = tile_products(
-        place, words, count, tiles, last, after(sums, z_two), owners=(0, 1, 2, 3, 4)
+    mine, up_a, up_b, two_a, two_b, down_a, down_b, z_mine = tile_products(
+        place, words, count, tiles, last, after(sums, z_two), owners=(0, 1, 2, 3, 4), halved=(1, 2, 3)
     )
 
-    half = BLOCKS // 2
     got_two = move(z_two, "z_lo", SWAP)
     got_up = move(z_up, "x", UP)
     got_down = move(z_down, "x", DOWN)
-    two_up = move(two[:half] + got_two[:half], "x", UP)
-    two_down = move(two[half:] + got_two[half:], "x", DOWN)
-    end_z = move(z_mine + got_up + got_down, "z_lo", SWAP)
-    end_up = move(jnp.concatenate([up[:half] + two_up, up[half:]]), "x", UP)
-    end_down = move(jnp.concatenate([down[:half], down[half:] + two_down]), "x", DOWN)
+    end_up_b = move(up_b, "x", UP)
+    end_down_a = move(down_a, "x", DOWN)
+    two_a = move(two_a + got_two[:HALF], "x", UP)
+    two_b = move(two_b + got_two[HALF:], "x", DOWN)
+    end_z = move(after(z_mine + got_up + got_down, end_up_b, end_down_a), "z_lo", SWAP)
+    end_up_a = move(up_a + two_a, "x", UP)
+    end_down_b = move(down_b + two_b, "x", DOWN)
 
     return pl.pallas_call(
         finish_kernel,
         out_shape=jax.ShapeDtypeStruct((BLOCKS * TILE, FEAT), f32),
         compiler_params=pltpu.CompilerParams(vmem_limit_bytes=24 * 2**20),
-    )(mine, end_up, end_down, end_z, weight, bias_vector.reshape(1, FEAT))
+    )(mine, end_z, end_up_a, end_up_b, end_down_a, end_down_b, weight, bias_vector.reshape(1, FEAT))
 
 
 def solution(mesh):

time: 96.5 us -> 96.7 us (level)
  starting transfers between devices: 29.8 us -> 30.9 us
  waiting for transfers between devices: 33.4 us -> 32.4 us
    ppermute x1, waiting for transfers between devices: 4.24 us -> 0.01 us  [body(): got_two = move(z_two, 'z_lo', SWAP)]
    ppermute x1, waiting for transfers between devices: 0.01 us -> 2.06 us  [body(): two = move(below, 'y', UP)]
    ppermute x9 -> x11, starting transfers between devices: 8.35 us -> 10.3 us  [the longest x1 3.22 us: body(): end_down_a = move(down_a, 'x', DOWN)]
    ppermute x1, waiting for transfers between devices: 3.94 us -> 5.84 us  [body(): far_two = move(two, 'z_hi', SWAP)]
    ppermute x1, starting transfers between devices: 2.28 us -> 0.56 us  [body(): far_two = move(two, 'z_hi', SWAP)]
    ppermute x1, waiting for transfers between devices: 0.01 us -> 1.07 us  [body(): got_up = move(z_up, 'x', UP)]
    ppermute x9 -> x11, waiting for transfers between devices: 19.4 us -> 18.4 us  [the longest x1 5.5 us: body(): end_up_b = move(up_b, 'x', UP)]
  transfers between devices with their start and end apart: 23 -> 25, of which waited for: 10 -> 9; matrix products, arithmetic and copies ran while one was open for 0% -> 0% of each run, Pallas kernels for 25% -> 25%
where the time goes in v8:
time: 96.7 us; the launch traced here: 95.7 us
  waiting for transfers between devices  32.4 us (34%)
  starting transfers between devices  30.9 us (32%)
  Pallas kernels  29.4 us (30%)
  other arithmetic  2.07 us (2%)
    pallas_call x4, Pallas kernels, tile_products(): pl.pallas_call(functools.partial(tile_kernel, len(pieces), first, split_r...  25.4 us
    ppermute x1, waiting for transfers between devices, body(): far_two = move(two, 'z_hi', SWAP)  5.84 us
    ppermute x1, waiting for transfers between devices, body(): end_up_b = move(up_b, 'x', UP)  5.5 us
    ppermute x1, waiting for transfers between devices, body(): below = move(own, 'y', UP)  5.03 us
    ppermute x1, waiting for transfers between devices, body(): end_down_b = move(down_b + two_b, 'x', DOWN)  4.26 us
    ppermute x1, starting transfers between devices, body(): far = move(own, 'z_hi', SWAP)  3.88 us
    ppermute x1, starting transfers between devices, body(): far_below = move(below, 'z_hi', SWAP)  3.88 us
    ppermute x1, waiting for transfers between devices, body(): end_up_a = move(up_a + two_a, 'x', UP)  3.52 us
  transfers between devices with their start and end apart: 25, of which 9 were waited for; matrix products, arithmetic and copies ran while one was open for 0% of the time, Pallas kernels for 25%

profile of v8, /device:TPU:0, one launch (start us, length us, event | category | flops | bytes accessed | tf_op | source)
XLA Modules:
  0.0 95.7 jit_solution(17580527431893149063)
XLA Ops:
  0.0 0.7 convert_bitcast_fusion
  0.7 1.1 %select_maximum_fusion.refs_4_ = f32[1032,128]{1,0:T(8,128)S(1)} fusion(f32[1,8]{1,0:T(1,128)S(1)} %convert_bitcast_fusion, f32[1024,128]{1,0:T(8,128)} %param.7), kind=kLoop, calls=%fused_computation | loop fusion | flops 396288 | bytes 1052704 | tf_op jit(solution)/shard_map/concatenate | solution.py:243
  1.7 1.7 %collective-permute-start.1 = (f32[1032,128]{1,0:T(8,128)S(1)}, f32[1032,128]{1,0:T(8,128)S(1)}, u32[]{:S(2)}, u32[]{:S(2)}) collective-permute-start(f32[1032,128]{1,0:T(8,128)S(1)} %select_maximum_fusion.refs_4_), channel_id=1, source_target_pairs={{0,2},{2,4},{4,6},{6,0},{1,3},{3,5},{5,7},{7,1},{8,10},{10,12},{12... | collective-permute-start | bytes 1585160 | tf_op jit(solution)/shard_map/ppermute | solution.py:244
  3.5 3.9 %collective-permute-start.3 = (f32[1032,128]{1,0:T(8,128)S(1)}, f32[1032,128]{1,0:T(8,128)S(1)}, u32[]{:S(2)}, u32[]{:S(2)}) collective-permute-start(f32[1032,128]{1,0:T(8,128)S(1)} %select_maximum_fusion.refs_4_), channel_id=1, source_target_pairs={{0,8},{8,0},{1,9},{9,1},{2,10},{10,2},{3,11},{11,3},{4,12},{12,4},... | collective-permute-start | bytes 1585160 | tf_op jit(solution)/shard_map/ppermute | solution.py:246
  7.3 1.7 %collective-permute-start.2 = (f32[1032,128]{1,0:T(8,128)S(1)}, f32[1032,128]{1,0:T(8,128)S(1)}, u32[]{:S(2)}, u32[]{:S(2)}) collective-permute-start(f32[1032,128]{1,0:T(8,128)S(1)} %select_maximum_fusion.refs_4_), channel_id=1, source_target_pairs={{0,6},{2,0},{4,2},{6,4},{1,7},{3,1},{5,3},{7,5},{8,14},{10,8},{12,... | collective-permute-start | bytes 1585160 | tf_op jit(solution)/shard_map/ppermute | solution.py:245
  9.0 2.9 %shard_map.73 = (s32[288]{0:T(512)}, s32[1]{0:T(128)}) custom-call(s32[16,16]{1,0:T(8,128)} %bitcast.13, s32[16,16]{1,0:T(8,128)} %bitcast.14), custom_call_target="tpu_custom_call" | custom-call | flops 100000 | bytes 10000 | tf_op jit(solution)/shard_map/pallas_call | solution.py:252
  11.9 5.0 %collective-permute-done.1.refs_6_ = f32[1032,128]{1,0:T(8,128)S(1)} collective-permute-done((f32[1032,128]{1,0:T(8,128)S(1)}, f32[1032,128]{1,0:T(8,128)S(1)}, u32[]{:S(2)}, u32[]{:S(2)}) %collective-permute-start.1) | collective-permute-done | bytes 528416 | tf_op jit(solution)/shard_map/ppermute | solution.py:244
  16.9 3.9 %collective-permute-start.9 = (f32[1032,128]{1,0:T(8,128)S(1)}, f32[1032,128]{1,0:T(8,128)S(1)}, u32[]{:S(2)}, u32[]{:S(2)}) collective-permute-start(f32[1032,128]{1,0:T(8,128)S(1)} %collective-permute-done.1.refs_6_), channel_id=1, source_target_pairs={{0,8},{8,0},{1,9},{9,1},{2,10},{10,2},{3,11},{11,3},{4,12},{12,4},... | collective-permute-start | bytes 1585160 | tf_op jit(solution)/shard_map/ppermute | solution.py:266
  20.8 0.3 collective-permute-start.7
  21.1 2.9 %collective-permute-start.8 = (f32[1032,128]{1,0:T(8,128)S(1)}, f32[1032,128]{1,0:T(8,128)S(1)}, u32[]{:S(2)}, u32[]{:S(2)}) collective-permute-start(f32[1032,128]{1,0:T(8,128)S(1)} %collective-permute-done.3.refs_8_), channel_id=1, source_target_pairs={{0,6},{2,0},{4,2},{6,4},{1,7},{3,1},{5,3},{7,5},{8,14},{10,8},{12,... | collective-permute-start | bytes 1585160 | tf_op jit(solution)/shard_map/ppermute | solution.py:265
  24.0 0.1 pad_add_fusion.refs_0_
  24.1 0.0 collective-permute-done.2.refs_7_
  24.1 0.0 collective-permute-start.4
  24.1 0.0 collective-permute-done.refs_5_
  24.2 0.5 collective-permute-start.6
  24.6 0.7 copy-done.1
  25.3 7.3 %shard_map.74 = (f32[65,128,128]{2,1,0:T(8,128)S(1)}, s32[288]{0:T(512)S(1)}, s32[1]{0:T(128)}) custom-call(s32[2]{0:T(128)S(1)} %pad_add_fusion.refs_0_, s32[288]{0:T(512)S(1)} %copy-done.1, s32[1]{0:T(128)} %get-tuple-element.32.refs_2_, f32[256,128,128]{2,1,0:T(8,128)} %bitcast.9, f32[1032,128]{1,0:T(8,128)S(1)} %select_maximum_fusion.refs_4_, ...), custom_call_target="tpu_custom_call" | custom-call | flops 100000 | bytes 10000 | tf_op jit(solution)/shard_map/pallas_call | solution.py:208
  32.6 0.0 collective-permute-done.9.refs_5_
  32.6 0.1 collective-permute-start.5
  32.7 2.1 %collective-permute-done.7.refs_7_ = f32[1032,128]{1,0:T(8,128)} collective-permute-done((f32[1032,128]{1,0:T(8,128)S(1)}, f32[1032,128]{1,0:T(8,128)}, u32[]{:S(2)}, u32[]{:S(2)}) %collective-permute-start.7) | collective-permute-done | bytes 528416 | tf_op jit(solution)/shard_map/ppermute | solution.py:264
  34.8 0.6 collective-permute-start.13
  35.3 0.2 collective-permute-start.10
  35.5 0.3 collective-permute-start.12
  35.9 0.2 collective-permute-start.11
  36.0 7.0 %shard_map.75 = (f32[65,128,128]{2,1,0:T(8,128)S(1)}, s32[288]{0:T(512)S(1)}, s32[1]{0:T(128)}, s32[288]{0:T(512)S(1)}, s32[1]{0:T(128)}) custom-call(s32[2]{0:T(128)S(1)} %pad_add_fusion.refs_0_, s32[288]{0:T(512)S(1)} %get-tuple-element.34.refs_1_, s32[1]{0:T(128)} %get-tuple-element.35.refs_2_, f32[256,128,128]{2,1,0:T(8,128)} %bitcast.10, ...), custom_call_target="tpu_custom_call" | custom-call | flops 100000 | bytes 10000 | tf_op jit(solution)/shard_map/pallas_call | solution.py:208
  43.0 5.8 %collective-permute-done.13.refs_9_ = f32[1032,128]{1,0:T(8,128)S(1)} collective-permute-done((f32[1032,128]{1,0:T(8,128)}, f32[1032,128]{1,0:T(8,128)S(1)}, u32[]{:S(2)}, u32[]{:S(2)}) %collective-permute-start.13) | collective-permute-done | bytes 528416 | tf_op jit(solution)/shard_map/ppermute | solution.py:271
  48.9 1.9 %collective-permute-done.14.refs_10_ = f32[1032,128]{1,0:T(8,128)S(1)} collective-permute-done((f32[1032,128]{1,0:T(8,128)S(1)}, f32[1032,128]{1,0:T(8,128)S(1)}, u32[]{:S(2)}, u32[]{:S(2)}) %collective-permute-start.14) | collective-permute-done | bytes 528416 | tf_op jit(solution)/shard_map/ppermute | solution.py:278
  50.8 4.7 %shard_map.76 = (f32[8,128,128]{2,1,0:T(8,128)S(1)}, f32[8,128,128]{2,1,0:T(8,128)S(1)}, f32[8,128,128]{2,1,0:T(8,128)S(1)}) custom-call(s32[2]{0:T(128)S(1)} %pad_add_fusion.refs_0_, s32[288]{0:T(512)S(1)} %get-tuple-element.42.refs_1_, s32[1]{0:T(128)} %get-tuple-element.43.refs_2_, f32[256,128,128]{2,1,0:T(8,128)} %bitcast.11, ...), custom_call_target="tpu_custom_call" | custom-call | flops 100000 | bytes 10000 | tf_op jit(solution)/shard_map/pallas_call | solution.py:208
  55.5 1.9 %collective-permute-start.20 = (f32[8,128,128]{2,1,0:T(8,128)S(1)}, f32[8,128,128]{2,1,0:T(8,128)S(1)}, u32[]{:S(2)}, u32[]{:S(2)}) collective-permute-start(f32[8,128,128]{2,1,0:T(8,128)S(1)} %get-tuple-element.44), channel_id=1, source_target_pairs={{0,64},{64,0},{1,65},{65,1},{2,66},{66,2},{3,67},{67,3},{4,68},{68... | collective-permute-start | bytes 1572872 | tf_op jit(solution)/shard_map/ppermute | solution.py:284
  57.4 0.7 collective-permute-start.15
  58.1 2.6 %collective-permute-start.16 = (f32[8,128,128]{2,1,0:T(8,128)S(1)}, f32[8,128,128]{2,1,0:T(8,128)S(1)}, u32[]{:S(2)}, u32[]{:S(2)}) collective-permute-start(f32[8,128,128]{2,1,0:T(8,128)S(1)} %get-tuple-element.49), channel_id=1, source_target_pairs={{0,48},{16,0},{32,16},{48,32},{1,49},{17,1},{33,17},{49,33},{2,50}... | collective-permute-start | bytes 1572872 | tf_op jit(solution)/shard_map/ppermute | solution.py:286
  60.6 6.4 %shard_map.77 = (f32[8,128,128]{2,1,0:T(8,128)S(1)}, f32[4,128,128]{2,1,0:T(8,128)S(1)}, f32[4,128,128]{2,1,0:T(8,128)S(1)}, f32[4,128,128]{2,1,0:T(8,128)S(1)},...) custom-call(s32[2]{0:T(128)S(1)} %pad_add_fusion.refs_0_, ...), custom_call_target="tpu_custom_call" | custom-call | flops 100000 | bytes 10000 | tf_op jit(solution)/shard_map/pallas_call | solution.py:208
  67.0 0.0 copy-start
  67.1 0.0 copy-start.2
  67.1 0.1 collective-permute-start.17
  67.2 3.2 %collective-permute-start.18 = (f32[4,128,128]{2,1,0:T(8,128)S(1)}, f32[4,128,128]{2,1,0:T(8,128)S(1)}, u32[]{:S(2)}, u32[]{:S(2)}) collective-permute-start(f32[4,128,128]{2,1,0:T(8,128)S(1)} %get-tuple-element.51), channel_id=1, source_target_pairs={{0,48},{16,0},{32,16},{48,32},{1,49},{17,1},{33,17},{49,33},{2,50}... | collective-permute-start | bytes 786440 | tf_op jit(solution)/shard_map/ppermute | solution.py:288
  70.4 0.1 slice_add_fusion
  70.5 1.9 %collective-permute-start.23 = (f32[4,128,128]{2,1,0:T(8,128)S(1)}, f32[4,128,128]{2,1,0:T(8,128)S(1)}, u32[]{:S(2)}, u32[]{:S(2)}) collective-permute-start(f32[4,128,128]{2,1,0:T(8,128)S(1)} %get-tuple-element.57), channel_id=1, source_target_pairs={{0,48},{16,0},{32,16},{48,32},{1,49},{17,1},{33,17},{49,33},{2,50}... | collective-permute-start | bytes 786440 | tf_op jit(solution)/shard_map/ppermute | solution.py:290
  72.4 1.1 %collective-permute-done.15 = f32[8,128,128]{2,1,0:T(8,128)S(1)} collective-permute-done((f32[8,128,128]{2,1,0:T(8,128)S(1)}, f32[8,128,128]{2,1,0:T(8,128)S(1)}, u32[]{:S(2)}, u32[]{:S(2)}) %collective-permute-start.15) | collective-permute-done | bytes 524320 | tf_op jit(solution)/shard_map/ppermute | solution.py:285
  73.4 0.1 add_add_fusion
  73.5 5.5 %collective-permute-done.17.up_b = f32[4,128,128]{2,1,0:T(8,128)S(1)} collective-permute-done((f32[4,128,128]{2,1,0:T(8,128)S(1)}, f32[4,128,128]{2,1,0:T(8,128)S(1)}, u32[]{:S(2)}, u32[]{:S(2)}) %collective-permute-start.17) | collective-permute-done | bytes 262176 | tf_op jit(solution)/shard_map/ppermute | solution.py:287
  79.1 1.1 %collective-permute-start.19 = (f32[8,128,128]{2,1,0:T(8,128)S(1)}, f32[8,128,128]{2,1,0:T(8,128)S(1)}, u32[]{:S(2)}, u32[]{:S(2)}) collective-permute-start(f32[8,128,128]{2,1,0:T(8,128)S(1)} %add_add_fusion), channel_id=1, source_target_pairs={{0,64},{64,0},{1,65},{65,1},{2,66},{66,2},{3,67},{67,3},{4,68},{68... | collective-permute-start | bytes 1572872 | tf_op jit(solution)/shard_map/ppermute | solution.py:291
  80.2 3.2 %collective-permute-done.23 = f32[4,128,128]{2,1,0:T(8,128)S(1)} collective-permute-done((f32[4,128,128]{2,1,0:T(8,128)S(1)}, f32[4,128,128]{2,1,0:T(8,128)S(1)}, u32[]{:S(2)}, u32[]{:S(2)}) %collective-permute-start.23) | collective-permute-done | bytes 262176 | tf_op jit(solution)/shard_map/ppermute | solution.py:290
  83.4 3.2 %collective-permute-start.24 = (f32[4,128,128]{2,1,0:T(8,128)S(1)}, f32[4,128,128]{2,1,0:T(8,128)S(1)}, u32[]{:S(2)}, u32[]{:S(2)}) collective-permute-start(f32[4,128,128]{2,1,0:T(8,128)S(1)} %add.25), channel_id=1, source_target_pairs={{0,48},{16,0},{32,16},{48,32},{1,49},{17,1},{33,17},{49,33},{2,50}... | collective-permute-start | bytes 786440 | tf_op jit(solution)/shard_map/ppermute | solution.py:293
  86.6 0.1 collective-permute-start.22
  86.7 4.3 %collective-permute-done.24.down_b = f32[4,128,128]{2,1,0:T(8,128)S(1)} collective-permute-done((f32[4,128,128]{2,1,0:T(8,128)S(1)}, f32[4,128,128]{2,1,0:T(8,128)S(1)}, u32[]{:S(2)}, u32[]{:S(2)}) %collective-permute-start.24) | collective-permute-done | bytes 262176 | tf_op jit(solution)/shard_map/ppermute | solution.py:293
  91.0 3.5 %collective-permute-done.22.up_a = f32[4,128,128]{2,1,0:T(8,128)S(1)} collective-permute-done((f32[4,128,128]{2,1,0:T(8,128)S(1)}, f32[4,128,128]{2,1,0:T(8,128)S(1)}, u32[]{:S(2)}, u32[]{:S(2)}) %collective-permute-start.22) | collective-permute-done | bytes 262176 | tf_op jit(solution)/shard_map/ppermute | solution.py:292
  94.5 1.1 %shard_map.78 = f32[1024,128]{1,0:T(8,128)} custom-call(f32[8,128,128]{2,1,0:T(8,128)S(1)} %get-tuple-element.46.own, f32[8,128,128]{2,1,0:T(8,128)S(1)} %collective-permute-done.19.far, f32[4,128,128]{2,1,0:T(8,128)S(1)} %collective-permute-done.22.up_a, f32[4,128,128]{2,1,0:T(8,128)S(1)} %collective-permute-done.17.up_b, ...), custom_call_target="tpu_custom_call" | custom-call | tf_op jit(solution)/shard_map/pallas_call | solution.py:295
  (21 shorter events, 0.1 us)
Async XLA Ops:
  1.7 15.2 %collective-permute-start.1 = (f32[1032,128]{1,0:T(8,128)S(1)}, f32[1032,128]{1,0:T(8,128)S(1)}, u32[]{:S(2)}, u32[]{:S(2)}) collective-permute-start(f32[1032,128]{1,0:T(8,128)S(1)} %select_maximum_fusion.refs_4_), channel_id=1, source_target_pairs={{0,2},{2,4},{4,6},{6,0},{1,3},{3,5},{5,7},{7,1},{8,10},{10,12},{12... | collective-permute-start | bytes 1585160 | tf_op jit(solution)/shard_map/ppermute | solution.py:244
  3.5 17.6 %collective-permute-start.3 = (f32[1032,128]{1,0:T(8,128)S(1)}, f32[1032,128]{1,0:T(8,128)S(1)}, u32[]{:S(2)}, u32[]{:S(2)}) collective-permute-start(f32[1032,128]{1,0:T(8,128)S(1)} %select_maximum_fusion.refs_4_), channel_id=1, source_target_pairs={{0,8},{8,0},{1,9},{9,1},{2,10},{10,2},{3,11},{11,3},{4,12},{12,4},... | collective-permute-start | bytes 1585160 | tf_op jit(solution)/shard_map/ppermute | solution.py:246
  7.3 16.8 %collective-permute-start.2 = (f32[1032,128]{1,0:T(8,128)S(1)}, f32[1032,128]{1,0:T(8,128)S(1)}, u32[]{:S(2)}, u32[]{:S(2)}) collective-permute-start(f32[1032,128]{1,0:T(8,128)S(1)} %select_maximum_fusion.refs_4_), channel_id=1, source_target_pairs={{0,6},{2,0},{4,2},{6,4},{1,7},{3,1},{5,3},{7,5},{8,14},{10,8},{12,... | collective-permute-start | bytes 1585160 | tf_op jit(solution)/shard_map/ppermute | solution.py:245
  9.0 15.1 %collective-permute-start = (f32[1032,128]{1,0:T(8,128)S(1)}, f32[1032,128]{1,0:T(8,128)}, u32[]{:S(2)}, u32[]{:S(2)}) collective-permute-start(f32[1032,128]{1,0:T(8,128)S(1)} %select_maximum_fusion.refs_4_), channel_id=1, source_target_pairs={{0,1},{1,0},{2,3},{3,2},{4,5},{5,4},{6,7},{7,6},{8,9},{9,8},{10,11... | collective-permute-start | bytes 1585160 | tf_op jit(solution)/shard_map/ppermute | solution.py:247
  16.9 15.7 %collective-permute-start.9 = (f32[1032,128]{1,0:T(8,128)S(1)}, f32[1032,128]{1,0:T(8,128)S(1)}, u32[]{:S(2)}, u32[]{:S(2)}) collective-permute-start(f32[1032,128]{1,0:T(8,128)S(1)} %collective-permute-done.1.refs_6_), channel_id=1, source_target_pairs={{0,8},{8,0},{1,9},{9,1},{2,10},{10,2},{3,11},{11,3},{4,12},{12,4},... | collective-permute-start | bytes 1585160 | tf_op jit(solution)/shard_map/ppermute | solution.py:266
  20.8 14.0 %collective-permute-start.7 = (f32[1032,128]{1,0:T(8,128)S(1)}, f32[1032,128]{1,0:T(8,128)}, u32[]{:S(2)}, u32[]{:S(2)}) collective-permute-start(f32[1032,128]{1,0:T(8,128)S(1)} %collective-permute-done.1.refs_6_), channel_id=1, source_target_pairs={{0,2},{2,4},{4,6},{6,0},{1,3},{3,5},{5,7},{7,1},{8,10},{10,12},{12... | collective-permute-start | bytes 1585160 | tf_op jit(solution)/shard_map/ppermute | solution.py:264
  21.1 13.7 %collective-permute-start.8 = (f32[1032,128]{1,0:T(8,128)S(1)}, f32[1032,128]{1,0:T(8,128)S(1)}, u32[]{:S(2)}, u32[]{:S(2)}) collective-permute-start(f32[1032,128]{1,0:T(8,128)S(1)} %collective-permute-done.3.refs_8_), channel_id=1, source_target_pairs={{0,6},{2,0},{4,2},{6,4},{1,7},{3,1},{5,3},{7,5},{8,14},{10,8},{12,... | collective-permute-start | bytes 1585160 | tf_op jit(solution)/shard_map/ppermute | solution.py:265
  24.1 11.4 %collective-permute-start.4 = (f32[1032,128]{1,0:T(8,128)S(1)}, f32[1032,128]{1,0:T(8,128)S(1)}, u32[]{:S(2)}, u32[]{:S(2)}) collective-permute-start(f32[1032,128]{1,0:T(8,128)S(1)} %collective-permute-done.1.refs_6_), channel_id=1, source_target_pairs={{0,1},{1,0},{2,3},{3,2},{4,5},{5,4},{6,7},{7,6},{8,9},{9,8},{10,11... | collective-permute-start | bytes 1585160 | tf_op jit(solution)/shard_map/ppermute | solution.py:267
  24.2 11.7 %collective-permute-start.6 = (f32[1032,128]{1,0:T(8,128)S(1)}, f32[1032,128]{1,0:T(8,128)S(1)}, u32[]{:S(2)}, u32[]{:S(2)}) collective-permute-start(f32[1032,128]{1,0:T(8,128)S(1)} %collective-permute-done.3.refs_8_), channel_id=1, source_target_pairs={{0,1},{1,0},{2,3},{3,2},{4,5},{5,4},{6,7},{7,6},{8,9},{9,8},{10,11... | collective-permute-start | bytes 1585160 | tf_op jit(solution)/shard_map/ppermute | solution.py:267
  24.6 0.7 copy-start.1
  32.6 3.4 %collective-permute-start.5 = (f32[1032,128]{1,0:T(8,128)S(1)}, f32[1032,128]{1,0:T(8,128)S(1)}, u32[]{:S(2)}, u32[]{:S(2)}) collective-permute-start(f32[1032,128]{1,0:T(8,128)S(1)} %collective-permute-done.2.refs_7_), channel_id=1, source_target_pairs={{0,1},{1,0},{2,3},{3,2},{4,5},{5,4},{6,7},{7,6},{8,9},{9,8},{10,11... | collective-permute-start | bytes 1585160 | tf_op jit(solution)/shard_map/ppermute | solution.py:267
  34.8 14.1 %collective-permute-start.13 = (f32[1032,128]{1,0:T(8,128)}, f32[1032,128]{1,0:T(8,128)S(1)}, u32[]{:S(2)}, u32[]{:S(2)}) collective-permute-start(f32[1032,128]{1,0:T(8,128)} %collective-permute-done.7.refs_7_), channel_id=1, source_target_pairs={{0,8},{8,0},{1,9},{9,1},{2,10},{10,2},{3,11},{11,3},{4,12},{12,4},... | collective-permute-start | bytes 1585160 | tf_op jit(solution)/shard_map/ppermute | solution.py:271
  35.3 13.5 %collective-permute-start.10 = (f32[1032,128]{1,0:T(8,128)}, f32[1032,128]{1,0:T(8,128)S(1)}, u32[]{:S(2)}, u32[]{:S(2)}) collective-permute-start(f32[1032,128]{1,0:T(8,128)} %collective-permute-done.7.refs_7_), channel_id=1, source_target_pairs={{0,1},{1,0},{2,3},{3,2},{4,5},{5,4},{6,7},{7,6},{8,9},{9,8},{10,11... | collective-permute-start | bytes 1585160 | tf_op jit(solution)/shard_map/ppermute | solution.py:272
  35.5 13.4 %collective-permute-start.12 = (f32[1032,128]{1,0:T(8,128)S(1)}, f32[1032,128]{1,0:T(8,128)S(1)}, u32[]{:S(2)}, u32[]{:S(2)}) collective-permute-start(f32[1032,128]{1,0:T(8,128)S(1)} %collective-permute-done.9.refs_5_), channel_id=1, source_target_pairs={{0,1},{1,0},{2,3},{3,2},{4,5},{5,4},{6,7},{7,6},{8,9},{9,8},{10,11... | collective-permute-start | bytes 1585160 | tf_op jit(solution)/shard_map/ppermute | solution.py:272
  35.9 13.0 %collective-permute-start.11 = (f32[1032,128]{1,0:T(8,128)S(1)}, f32[1032,128]{1,0:T(8,128)S(1)}, u32[]{:S(2)}, u32[]{:S(2)}) collective-permute-start(f32[1032,128]{1,0:T(8,128)S(1)} %collective-permute-done.8.refs_4_), channel_id=1, source_target_pairs={{0,1},{1,0},{2,3},{3,2},{4,5},{5,4},{6,7},{7,6},{8,9},{9,8},{10,11... | collective-permute-start | bytes 1585160 | tf_op jit(solution)/shard_map/ppermute | solution.py:272
  48.9 1.9 %collective-permute-start.14 = (f32[1032,128]{1,0:T(8,128)S(1)}, f32[1032,128]{1,0:T(8,128)S(1)}, u32[]{:S(2)}, u32[]{:S(2)}) collective-permute-start(f32[1032,128]{1,0:T(8,128)S(1)} %collective-permute-done.13.refs_9_), channel_id=1, source_target_pairs={{0,1},{1,0},{2,3},{3,2},{4,5},{5,4},{6,7},{7,6},{8,9},{9,8},{10,11... | collective-permute-start | bytes 1585160 | tf_op jit(solution)/shard_map/ppermute | solution.py:278
  55.5 14.9 %collective-permute-start.20 = (f32[8,128,128]{2,1,0:T(8,128)S(1)}, f32[8,128,128]{2,1,0:T(8,128)S(1)}, u32[]{:S(2)}, u32[]{:S(2)}) collective-permute-start(f32[8,128,128]{2,1,0:T(8,128)S(1)} %get-tuple-element.44), channel_id=1, source_target_pairs={{0,64},{64,0},{1,65},{65,1},{2,66},{66,2},{3,67},{67,3},{4,68},{68... | collective-permute-start | bytes 1572872 | tf_op jit(solution)/shard_map/ppermute | solution.py:284
  57.4 16.0 %collective-permute-start.15 = (f32[8,128,128]{2,1,0:T(8,128)S(1)}, f32[8,128,128]{2,1,0:T(8,128)S(1)}, u32[]{:S(2)}, u32[]{:S(2)}) collective-permute-start(f32[8,128,128]{2,1,0:T(8,128)S(1)} %get-tuple-element.48), channel_id=1, source_target_pairs={{0,16},{16,32},{32,48},{48,0},{1,17},{17,33},{33,49},{49,1},{2,18}... | collective-permute-start | bytes 1572872 | tf_op jit(solution)/shard_map/ppermute | solution.py:285
  58.1 15.4 %collective-permute-start.16 = (f32[8,128,128]{2,1,0:T(8,128)S(1)}, f32[8,128,128]{2,1,0:T(8,128)S(1)}, u32[]{:S(2)}, u32[]{:S(2)}) collective-permute-start(f32[8,128,128]{2,1,0:T(8,128)S(1)} %get-tuple-element.49), channel_id=1, source_target_pairs={{0,48},{16,0},{32,16},{48,32},{1,49},{17,1},{33,17},{49,33},{2,50}... | collective-permute-start | bytes 1572872 | tf_op jit(solution)/shard_map/ppermute | solution.py:286
  67.0 27.5 %copy-start = (f32[128,128]{1,0:T(8,128)S(1)}, f32[128,128]{1,0:T(8,128)}, u32[]{:S(2)}) copy-start(f32[128,128]{1,0:T(8,128)} %weight.1) | copy-start | bytes 196612
  67.1 27.5 %copy-start.2 = (f32[128]{0:T(128)S(1)}, f32[128]{0:T(128)}, u32[]{:S(2)}) copy-start(f32[128]{0:T(128)} %param.13) | copy-start | bytes 1540
  67.1 12.0 %collective-permute-start.17 = (f32[4,128,128]{2,1,0:T(8,128)S(1)}, f32[4,128,128]{2,1,0:T(8,128)S(1)}, u32[]{:S(2)}, u32[]{:S(2)}) collective-permute-start(f32[4,128,128]{2,1,0:T(8,128)S(1)} %get-tuple-element.50), channel_id=1, source_target_pairs={{0,16},{16,32},{32,48},{48,0},{1,17},{17,33},{33,49},{49,1},{2,18}... | collective-permute-start | bytes 786440 | tf_op jit(solution)/shard_map/ppermute | solution.py:287
  67.2 11.9 %collective-permute-start.18 = (f32[4,128,128]{2,1,0:T(8,128)S(1)}, f32[4,128,128]{2,1,0:T(8,128)S(1)}, u32[]{:S(2)}, u32[]{:S(2)}) collective-permute-start(f32[4,128,128]{2,1,0:T(8,128)S(1)} %get-tuple-element.51), channel_id=1, source_target_pairs={{0,48},{16,0},{32,16},{48,32},{1,49},{17,1},{33,17},{49,33},{2,50}... | collective-permute-start | bytes 786440 | tf_op jit(solution)/shard_map/ppermute | solution.py:288
  70.5 12.9 %collective-permute-start.23 = (f32[4,128,128]{2,1,0:T(8,128)S(1)}, f32[4,128,128]{2,1,0:T(8,128)S(1)}, u32[]{:S(2)}, u32[]{:S(2)}) collective-permute-start(f32[4,128,128]{2,1,0:T(8,128)S(1)} %get-tuple-element.57), channel_id=1, source_target_pairs={{0,48},{16,0},{32,16},{48,32},{1,49},{17,1},{33,17},{49,33},{2,50}... | collective-permute-start | bytes 786440 | tf_op jit(solution)/shard_map/ppermute | solution.py:290
  73.4 13.2 %collective-permute-start.21 = (f32[4,128,128]{2,1,0:T(8,128)S(1)}, f32[4,128,128]{2,1,0:T(8,128)S(1)}, u32[]{:S(2)}, u32[]{:S(2)}) collective-permute-start(f32[4,128,128]{2,1,0:T(8,128)S(1)} %get-tuple-element.58), channel_id=1, source_target_pairs={{0,16},{16,32},{32,48},{48,0},{1,17},{17,33},{33,49},{49,1},{2,18}... | collective-permute-start | bytes 786440 | tf_op jit(solution)/shard_map/ppermute | solution.py:289
  79.1 15.5 %collective-permute-start.19 = (f32[8,128,128]{2,1,0:T(8,128)S(1)}, f32[8,128,128]{2,1,0:T(8,128)S(1)}, u32[]{:S(2)}, u32[]{:S(2)}) collective-permute-start(f32[8,128,128]{2,1,0:T(8,128)S(1)} %add_add_fusion), channel_id=1, source_target_pairs={{0,64},{64,0},{1,65},{65,1},{2,66},{66,2},{3,67},{67,3},{4,68},{68... | collective-permute-start | bytes 1572872 | tf_op jit(solution)/shard_map/ppermute | solution.py:291
  83.4 7.6 %collective-permute-start.24 = (f32[4,128,128]{2,1,0:T(8,128)S(1)}, f32[4,128,128]{2,1,0:T(8,128)S(1)}, u32[]{:S(2)}, u32[]{:S(2)}) collective-permute-start(f32[4,128,128]{2,1,0:T(8,128)S(1)} %add.25), channel_id=1, source_target_pairs={{0,48},{16,0},{32,16},{48,32},{1,49},{17,1},{33,17},{49,33},{2,50}... | collective-permute-start | bytes 786440 | tf_op jit(solution)/shard_map/ppermute | solution.py:293
  86.6 7.9 %collective-permute-start.22 = (f32[4,128,128]{2,1,0:T(8,128)S(1)}, f32[4,128,128]{2,1,0:T(8,128)S(1)}, u32[]{:S(2)}, u32[]{:S(2)}) collective-permute-start(f32[4,128,128]{2,1,0:T(8,128)S(1)} %add.23), channel_id=1, source_target_pairs={{0,16},{16,32},{32,48},{48,0},{1,17},{17,33},{33,49},{49,1},{2,18}... | collective-permute-start | bytes 786440 | tf_op jit(solution)/shard_map/ppermute | solution.py:292

commit v9 on v7

--- a/solution.py
+++ b/solution.py
@@ -10,6 +10,7 @@
 TILE = 128
 FEAT = 128
 BLOCKS = 8
+HALF = 4
 SLOTS = 16
 BUCKETS = 16
 TILES = BUCKETS * SLOTS
@@ -70,9 +71,16 @@
     xs, ring, slots, table, ring_sem, slot_sem = scratch
     depth = RING // size
 
+    with_slots, held, n_blocks = [], [], 0
+    for piece in pieces:
+        rows = piece.shape[0]
+        held.append(n_blocks)
+        n_blocks += rows // TILE
+        if rows % TILE:
+            with_slots.append((piece, n_blocks - BLOCKS))
     reads = [
-        pltpu.make_async_copy(piece.at[pl.ds(BLOCKS * TILE, 8)], slots.at[i], slot_sem.at[i])
-        for i, piece in enumerate(pieces)
+        pltpu.make_async_copy(piece.at[pl.ds(piece.shape[0] - 8, 8)], slots.at[i], slot_sem.at[i])
+        for i, (piece, at) in enumerate(with_slots)
     ]
     for read in reads:
         read.start()
@@ -113,9 +121,9 @@
         lax.fori_loop(0, DUMMY + 1, begin, 0, unroll=5)
     for read in reads:
         read.wait()
-    for i in range(n_pieces):
+    for i, (piece, at) in enumerate(with_slots):
         for j in range(BLOCKS):
-            table[slots[i, 0, j].astype(jnp.int32) & 127] = i * BLOCKS + j
+            table[slots[i, 0, j].astype(jnp.int32) & 127] = at + j
 
     def sort(group, n):
         here, *others = n
@@ -148,11 +156,13 @@
         fetch_first()
 
     def halve(j, carry):
-        for i, piece in enumerate(pieces):
-            xs[i * BLOCKS + j] = halves(piece[pl.ds(pl.multiple_of(j * TILE, TILE), TILE), :])
+        for piece, at in zip(pieces, held):
+            for k in range(0, piece.shape[0] // TILE, HALF):
+                rows = pl.ds(pl.multiple_of((k + j) * TILE, TILE), TILE)
+                xs[at + k + j] = halves(piece[rows, :])
         return carry
 
-    lax.fori_loop(0, BLOCKS, halve, 0)
+    lax.fori_loop(0, HALF, halve, 0)
 
     def goal(word):
         if not owners:
@@ -207,7 +217,7 @@
         out_specs=[vmem] * len(owners) or [vmem] + [smem] * len(rests),
         scratch_shapes=[sums if owners else listed[0]]
         + [
-            pltpu.VMEM((len(pieces) * BLOCKS, TILE, 2 * FEAT), bf16),
+            pltpu.VMEM((sum(p.shape[0] // TILE for p in pieces), TILE, 2 * FEAT), bf16),
             pltpu.VMEM((RING // size, size, TILE, TILE), f32),
             pltpu.SMEM((len(pieces), 8, 128), f32),
             pltpu.SMEM((BUCKETS * BLOCKS,), jnp.int32),
@@ -256,19 +266,23 @@
     two = move(below, "y", UP)
     far_above = move(far, "y", DOWN)
     far_below = move(below, "z_hi", SWAP)
-    swapped = [move(p, "core", SWAP) for p in (below, above, far)]
-    sums, words, count = tile_products(place, words, count, tiles, [own, other, below, above, far])
-
-    two = after(two, sums)
-    far_two = move(two, "z_hi", SWAP)
+    swapped = [move(p, "core", SWAP) for p in (above, far)]
+    sums, soon, n_soon, words, count = tile_products(
+        place, words, count, tiles, [own, other, below, above, far], split_rest=True
+    )
+
+    two, far_above, far_below = lax.optimization_barrier((two, far_above, far_below, sums))[:3]
+    cut = HALF * TILE
+    cuts = [far_below[:cut], far_above[cut:]]
+    far_two = [move(cuts[0], "y", UP), move(cuts[1], "y", DOWN)]
     late = [two, far_above, far_below]
-    late_swapped = [move(p, "core", SWAP) for p in late]
-    sums, soon, n_soon, words, count = tile_products(
-        place, words, count, tiles, [*swapped, *late], sums, split_rest=True
-    )
-
-    far_two = after(far_two, sums)
-    last = [*late_swapped, far_two, move(far_two, "core", SWAP)]
+    last = [
+        *swapped,
+        *late,
+        *far_two,
+        *[move(after(p, *cuts), "core", SWAP) for p in (*late, after(below, sums))],
+        *[move(p, "core", SWAP) for p in far_two],
+    ]
     z_up, z_two, z_down = tile_products(place, soon, n_soon, tiles, last, sums, owners=(5, 6, 7))
     mine, up, two, down, z_mine = tile_products(
         place, words, count, tiles, last, after(sums, z_two), owners=(0, 1, 2, 3, 4)

time: 96.5 us -> 98.1 us (1.017)
  waiting for transfers between devices: 33.4 us -> 36.5 us
  local copies, waits for them, and re-layouts: 0.69 us -> 2.56 us
  starting transfers between devices: 29.8 us -> 28 us
  Pallas kernels: 29.6 us -> 28.5 us
    ppermute x8 -> x10, waiting for transfers between devices: 5.85 us -> 11.4 us  [the longest x2 8.71 us: body(): far_two = [move(cuts[0], 'y', UP), move(cuts[1], 'y', DOWN)]]
    ppermute x1, waiting for transfers between devices: 5.95 us -> 1.41 us  [body(): move(jnp.concatenate([down[:half], down[half:] + two_down]), 'x', DOWN)]
    ppermute x1, waiting for transfers between devices: 4.24 us -> 1.53 us  [body(): got_two = move(z_two, 'z_lo', SWAP)]
    ppermute x1, waiting for transfers between devices: 3.78 us -> 1.28 us  [body(): two_down = move(two[half:] + got_two[half:], 'x', DOWN)]
    ppermute x1, waiting for transfers between devices: 3.82 us -> 6.17 us  [body(): end_up = move(jnp.concatenate([up[:half] + two_up, up[half:]]), 'x', UP)]
    ppermute x1, waiting for transfers between devices: 0.01 us -> 2.15 us  [body(): far = move(own, 'z_hi', SWAP)]
    ppermute x1, waiting for transfers between devices: 0.86 us -> 2.77 us  [body(): two_up = move(two[:half] + got_two[:half], 'x', UP)]
    unnamed x6 -> x10, local copies, waits for them, and re-layouts: 0.69 us -> 2.52 us
  transfers between devices with their start and end apart: 23 -> 25, of which waited for: 10 -> 15; matrix products, arithmetic and copies ran while one was open for 0% -> 0% of each run, Pallas kernels for 25% -> 21%
where the time goes in v9:
time: 98.1 us; the launch traced here: 97.9 us
  waiting for transfers between devices  36.5 us (37%)
  Pallas kernels  28.5 us (29%)
  starting transfers between devices  28 us (29%)
  local copies, waits for them, and re-layouts  2.56 us (3%)
  other arithmetic  2.18 us (2%)
    pallas_call x3, Pallas kernels, tile_products(): pl.pallas_call(functools.partial(tile_kernel, len(pieces), first, split_r...  24.5 us
    ppermute x2, waiting for transfers between devices, body(): far_two = [move(cuts[0], 'y', UP), move(cuts[1], 'y', DOWN)]  8.71 us
    ppermute x1, waiting for transfers between devices, body(): end_up = move(jnp.concatenate([up[:half] + two_up, up[half:]]), 'x', UP)  6.17 us
    ppermute x1, waiting for transfers between devices, body(): below = move(own, 'y', UP)  5.14 us
    ppermute x1, starting transfers between devices, body(): far = move(own, 'z_hi', SWAP)  3.88 us
    ppermute x1, starting transfers between devices, body(): far_below = move(below, 'z_hi', SWAP)  3.24 us
    pallas_call x1, Pallas kernels, body(): pl.pallas_call(live_kernel, out_shape=[jax.ShapeDtypeStruct((TILES + 2 *...  2.87 us
    ppermute x1, starting transfers between devices, body(): two_down = move(two[half:] + got_two[half:], 'x', DOWN)  2.86 us
  transfers between devices with their start and end apart: 25, of which 15 were waited for; matrix products, arithmetic and copies ran while one was open for 0% of the time, Pallas kernels for 21%

profile of v9, /device:TPU:0, one launch (start us, length us, event | category | flops | bytes accessed | tf_op | source)
XLA Modules:
  0.0 97.9 jit_solution(6478795338970857480)
XLA Ops:
  0.0 0.7 convert_bitcast_fusion
  0.7 1.1 %select_maximum_fusion.refs_4_ = f32[1032,128]{1,0:T(8,128)S(1)} fusion(f32[1,8]{1,0:T(1,128)S(1)} %convert_bitcast_fusion, f32[1024,128]{1,0:T(8,128)} %param.7), kind=kLoop, calls=%fused_computation | loop fusion | flops 396288 | bytes 1052704 | tf_op jit(solution)/shard_map/concatenate | solution.py:245
  1.7 1.7 %collective-permute-start.1 = (f32[1032,128]{1,0:T(8,128)S(1)}, f32[1032,128]{1,0:T(8,128)}, u32[]{:S(2)}, u32[]{:S(2)}) collective-permute-start(f32[1032,128]{1,0:T(8,128)S(1)} %select_maximum_fusion.refs_4_), channel_id=1, source_target_pairs={{0,2},{2,4},{4,6},{6,0},{1,3},{3,5},{5,7},{7,1},{8,10},{10,12},{12... | collective-permute-start | bytes 1585160 | tf_op jit(solution)/shard_map/ppermute | solution.py:246
  3.5 3.9 %collective-permute-start.3 = (f32[1032,128]{1,0:T(8,128)S(1)}, f32[1032,128]{1,0:T(8,128)}, u32[]{:S(2)}, u32[]{:S(2)}) collective-permute-start(f32[1032,128]{1,0:T(8,128)S(1)} %select_maximum_fusion.refs_4_), channel_id=1, source_target_pairs={{0,8},{8,0},{1,9},{9,1},{2,10},{10,2},{3,11},{11,3},{4,12},{12,4},... | collective-permute-start | bytes 1585160 | tf_op jit(solution)/shard_map/ppermute | solution.py:248
  7.3 1.7 %collective-permute-start.2 = (f32[1032,128]{1,0:T(8,128)S(1)}, f32[1032,128]{1,0:T(8,128)}, u32[]{:S(2)}, u32[]{:S(2)}) collective-permute-start(f32[1032,128]{1,0:T(8,128)S(1)} %select_maximum_fusion.refs_4_), channel_id=1, source_target_pairs={{0,6},{2,0},{4,2},{6,4},{1,7},{3,1},{5,3},{7,5},{8,14},{10,8},{12,... | collective-permute-start | bytes 1585160 | tf_op jit(solution)/shard_map/ppermute | solution.py:247
  9.0 2.9 %shard_map.73 = (s32[288]{0:T(512)}, s32[1]{0:T(128)}) custom-call(s32[16,16]{1,0:T(8,128)} %bitcast.12, s32[16,16]{1,0:T(8,128)} %bitcast.13), custom_call_target="tpu_custom_call" | custom-call | flops 100000 | bytes 10000 | tf_op jit(solution)/shard_map/pallas_call | solution.py:254
  11.9 5.1 %collective-permute-done.1.refs_6_ = f32[1032,128]{1,0:T(8,128)} collective-permute-done((f32[1032,128]{1,0:T(8,128)S(1)}, f32[1032,128]{1,0:T(8,128)}, u32[]{:S(2)}, u32[]{:S(2)}) %collective-permute-start.1) | collective-permute-done | bytes 528416 | tf_op jit(solution)/shard_map/ppermute | solution.py:246
  17.0 2.2 %collective-permute-done.3.refs_8_ = f32[1032,128]{1,0:T(8,128)} collective-permute-done((f32[1032,128]{1,0:T(8,128)S(1)}, f32[1032,128]{1,0:T(8,128)}, u32[]{:S(2)}, u32[]{:S(2)}) %collective-permute-start.3) | collective-permute-done | bytes 528416 | tf_op jit(solution)/shard_map/ppermute | solution.py:248
  19.2 1.8 %collective-permute-start.7 = (f32[1032,128]{1,0:T(8,128)}, f32[1032,128]{1,0:T(8,128)S(1)}, u32[]{:S(2)}, u32[]{:S(2)}) collective-permute-start(f32[1032,128]{1,0:T(8,128)} %collective-permute-done.3.refs_8_), channel_id=1, source_target_pairs={{0,6},{2,0},{4,2},{6,4},{1,7},{3,1},{5,3},{7,5},{8,14},{10,8},{12,... | collective-permute-start | bytes 1585160 | tf_op jit(solution)/shard_map/ppermute | solution.py:267
  21.0 3.2 %collective-permute-start.8 = (f32[1032,128]{1,0:T(8,128)}, f32[1032,128]{1,0:T(8,128)S(1)}, u32[]{:S(2)}, u32[]{:S(2)}) collective-permute-start(f32[1032,128]{1,0:T(8,128)} %collective-permute-done.1.refs_6_), channel_id=1, source_target_pairs={{0,8},{8,0},{1,9},{9,1},{2,10},{10,2},{3,11},{11,3},{4,12},{12,4},... | collective-permute-start | bytes 1585160 | tf_op jit(solution)/shard_map/ppermute | solution.py:268
  24.2 0.2 collective-permute-start.6
  24.5 0.8 copy-done
  25.3 0.5 collective-permute-start.4
  25.8 1.0 %copy-done.1 = f32[1032,128]{1,0:T(8,128)S(1)} copy-done((f32[1032,128]{1,0:T(8,128)S(1)}, f32[1032,128]{1,0:T(8,128)}, u32[]{:S(2)}) %copy-start.1) | copy-done | bytes 528408
  26.9 0.7 copy-done.3
  27.6 9.4 %shard_map.74 = (f32[65,128,128]{2,1,0:T(8,128)S(1)}, s32[288]{0:T(512)S(1)}, s32[1]{0:T(128)}, s32[288]{0:T(512)S(1)}, s32[1]{0:T(128)}) custom-call(s32[2]{0:T(128)S(1)} %pad_add_fusion.refs_0_, s32[288]{0:T(512)S(1)} %copy-done.3, s32[1]{0:T(128)} %get-tuple-element.31.refs_2_, f32[256,128,128]{2,1,0:T(8,128)} %bitcast.9, ...), custom_call_target="tpu_custom_call" | custom-call | flops 100000 | bytes 10000 | tf_op jit(solution)/shard_map/pallas_call | solution.py:212
  37.0 0.8 collective-permute-done.6.refs_6_
  37.9 1.2 %collective-permute-start.10 = (f32[520,128]{1,0:T(8,128)S(1)}, f32[520,128]{1,0:T(8,128)S(1)}, u32[]{:S(2)}, u32[]{:S(2)}) collective-permute-start(f32[520,128]{1,0:T(8,128)S(1)} %slice.31), channel_id=1, source_target_pairs={{0,6},{2,0},{4,2},{6,4},{1,7},{3,1},{5,3},{7,5},{8,14},{10,8},{12,... | collective-permute-start | bytes 798728 | tf_op jit(solution)/shard_map/ppermute | solution.py:277
  39.0 1.0 %collective-permute-start.9 = (f32[512,128]{1,0:T(8,128)S(1)}, f32[512,128]{1,0:T(8,128)S(1)}, u32[]{:S(2)}, u32[]{:S(2)}) collective-permute-start(f32[512,128]{1,0:T(8,128)S(1)} %slice.30), channel_id=1, source_target_pairs={{0,2},{2,4},{4,6},{6,0},{1,3},{3,5},{5,7},{7,1},{8,10},{10,12},{12... | collective-permute-start | bytes 786440 | tf_op jit(solution)/shard_map/ppermute | solution.py:277
  40.0 0.5 collective-permute-start.12
  40.6 0.1 collective-permute-start.13
  40.6 8.7 %collective-permute-done.9.refs_9_ = f32[512,128]{1,0:T(8,128)S(1)} collective-permute-done((f32[512,128]{1,0:T(8,128)S(1)}, f32[512,128]{1,0:T(8,128)S(1)}, u32[]{:S(2)}, u32[]{:S(2)}) %collective-permute-start.9) | collective-permute-done | bytes 262176 | tf_op jit(solution)/shard_map/ppermute | solution.py:277
  49.4 0.5 collective-permute-start.15
  49.9 1.5 %collective-permute-done.15.refs_15_ = f32[512,128]{1,0:T(8,128)S(1)} collective-permute-done((f32[512,128]{1,0:T(8,128)S(1)}, f32[512,128]{1,0:T(8,128)S(1)}, u32[]{:S(2)}, u32[]{:S(2)}) %collective-permute-start.15) | collective-permute-done | bytes 262176 | tf_op jit(solution)/shard_map/ppermute | solution.py:284
  51.3 0.3 collective-permute-start.16
  51.7 0.2 collective-permute-done.14.refs_14_
  51.9 1.0 %collective-permute-done.16.refs_16_ = f32[520,128]{1,0:T(8,128)S(1)} collective-permute-done((f32[520,128]{1,0:T(8,128)S(1)}, f32[520,128]{1,0:T(8,128)S(1)}, u32[]{:S(2)}, u32[]{:S(2)}) %collective-permute-start.16) | collective-permute-done | bytes 266272 | tf_op jit(solution)/shard_map/ppermute | solution.py:284
  52.9 7.1 %shard_map.75 = (f32[8,128,128]{2,1,0:T(8,128)S(1)}, f32[8,128,128]{2,1,0:T(8,128)S(1)}, f32[8,128,128]{2,1,0:T(8,128)S(1)}) custom-call(s32[2]{0:T(128)S(1)} %pad_add_fusion.refs_0_, s32[288]{0:T(512)S(1)} %get-tuple-element.44.refs_1_, s32[1]{0:T(128)} %get-tuple-element.45.refs_2_, f32[256,128,128]{2,1,0:T(8,128)} %bitcast.10, ...), custom_call_target="tpu_custom_call" | custom-call | flops 100000 | bytes 10000 | tf_op jit(solution)/shard_map/pallas_call | solution.py:212
  60.0 0.1 collective-permute-start.17
  60.1 1.1 %collective-permute-start.22 = (f32[8,128,128]{2,1,0:T(8,128)S(1)}, f32[8,128,128]{2,1,0:T(8,128)S(1)}, u32[]{:S(2)}, u32[]{:S(2)}) collective-permute-start(f32[8,128,128]{2,1,0:T(8,128)S(1)} %get-tuple-element.53), channel_id=1, source_target_pairs={{0,16},{16,32},{32,48},{48,0},{1,17},{17,33},{33,49},{49,1},{2,18}... | collective-permute-start | bytes 1572872 | tf_op jit(solution)/shard_map/ppermute | solution.py:293
  61.1 2.2 %collective-permute-start.23 = (f32[8,128,128]{2,1,0:T(8,128)S(1)}, f32[8,128,128]{2,1,0:T(8,128)S(1)}, u32[]{:S(2)}, u32[]{:S(2)}) collective-permute-start(f32[8,128,128]{2,1,0:T(8,128)S(1)} %get-tuple-element.54), channel_id=1, source_target_pairs={{0,48},{16,0},{32,16},{48,32},{1,49},{17,1},{33,17},{49,33},{2,50}... | collective-permute-start | bytes 1572872 | tf_op jit(solution)/shard_map/ppermute | solution.py:294
  63.4 8.0 %shard_map.76 = (f32[8,128,128]{2,1,0:T(8,128)S(1)}, f32[8,128,128]{2,1,0:T(8,128)S(1)}, f32[8,128,128]{2,1,0:T(8,128)S(1)}, f32[8,128,128]{2,1,0:T(8,128)S(1)}, f32[8,128,128]{2,1,0:T(8,128)S(1)}) custom-call(s32[2]{0:T(128)S(1)} %pad_add_fusion.refs_0_, s32[288]{0:T(512)S(1)} %get-tuple-element.33.refs_1_, s32[1]{0:T(128)} %get-tuple-element.34.refs_2_, ...), custom_call_target="tpu_custom_call" | custom-call | flops 100000 | bytes 10000 | tf_op jit(solution)/shard_map/pallas_call | solution.py:212
  71.4 1.5 %collective-permute-done.17 = f32[8,128,128]{2,1,0:T(8,128)S(1)} collective-permute-done((f32[8,128,128]{2,1,0:T(8,128)S(1)}, f32[8,128,128]{2,1,0:T(8,128)S(1)}, u32[]{:S(2)}, u32[]{:S(2)}) %collective-permute-start.17) | collective-permute-done | bytes 524320 | tf_op jit(solution)/shard_map/ppermute | solution.py:292
  72.9 0.1 slice_add_fusion
  73.0 1.1 %collective-permute-start.18 = (f32[4,128,128]{2,1,0:T(8,128)S(1)}, f32[4,128,128]{2,1,0:T(8,128)S(1)}, u32[]{:S(2)}, u32[]{:S(2)}) collective-permute-start(f32[4,128,128]{2,1,0:T(8,128)S(1)} %get-tuple-element.56), channel_id=1, source_target_pairs={{0,16},{16,32},{32,48},{48,0},{1,17},{17,33},{33,49},{49,1},{2,18}... | collective-permute-start | bytes 786440 | tf_op jit(solution)/shard_map/ppermute | solution.py:295
  74.1 0.4 collective-permute-done.22
  74.5 1.0 %collective-permute-done.23 = f32[8,128,128]{2,1,0:T(8,128)S(1)} collective-permute-done((f32[8,128,128]{2,1,0:T(8,128)S(1)}, f32[8,128,128]{2,1,0:T(8,128)S(1)}, u32[]{:S(2)}, u32[]{:S(2)}) %collective-permute-start.23) | collective-permute-done | bytes 524320 | tf_op jit(solution)/shard_map/ppermute | solution.py:294
  75.5 0.1 add_add_fusion
  75.6 0.6 collective-permute-start.24
  76.2 2.9 %collective-permute-start.20 = (f32[4,128,128]{2,1,0:T(8,128)S(1)}, f32[4,128,128]{2,1,0:T(8,128)S(1)}, u32[]{:S(2)}, u32[]{:S(2)}) collective-permute-start(f32[4,128,128]{2,1,0:T(8,128)S(1)} %get-tuple-element.55), channel_id=1, source_target_pairs={{0,48},{16,0},{32,16},{48,32},{1,49},{17,1},{33,17},{49,33},{2,50}... | collective-permute-start | bytes 786440 | tf_op jit(solution)/shard_map/ppermute | solution.py:296
  79.1 2.8 %collective-permute-done.18 = f32[4,128,128]{2,1,0:T(8,128)S(1)} collective-permute-done((f32[4,128,128]{2,1,0:T(8,128)S(1)}, f32[4,128,128]{2,1,0:T(8,128)S(1)}, u32[]{:S(2)}, u32[]{:S(2)}) %collective-permute-start.18) | collective-permute-done | bytes 262176 | tf_op jit(solution)/shard_map/ppermute | solution.py:295
  81.9 0.9 collective-permute-start.19
  82.8 1.3 %collective-permute-done.20 = f32[4,128,128]{2,1,0:T(8,128)S(1)} collective-permute-done((f32[4,128,128]{2,1,0:T(8,128)S(1)}, f32[4,128,128]{2,1,0:T(8,128)S(1)}, u32[]{:S(2)}, u32[]{:S(2)}) %collective-permute-start.20) | collective-permute-done | bytes 262176 | tf_op jit(solution)/shard_map/ppermute | solution.py:296
  84.2 2.6 %collective-permute-start.21 = (f32[8,128,128]{2,1,0:T(8,128)S(1)}, f32[8,128,128]{2,1,0:T(8,128)S(1)}, u32[]{:S(2)}, u32[]{:S(2)}) collective-permute-start(f32[8,128,128]{2,1,0:T(8,128)S(1)} %pad_maximum_fusion.1), channel_id=1, source_target_pairs={{0,48},{16,0},{32,16},{48,32},{1,49},{17,1},{33,17},{49,33},{2,50}... | collective-permute-start | bytes 1572872 | tf_op jit(solution)/shard_map/ppermute | solution.py:299
  86.8 2.4 %collective-permute-done.24.d = f32[8,128,128]{2,1,0:T(8,128)S(1)} collective-permute-done((f32[8,128,128]{2,1,0:T(8,128)S(1)}, f32[8,128,128]{2,1,0:T(8,128)S(1)}, u32[]{:S(2)}, u32[]{:S(2)}) %collective-permute-start.24) | collective-permute-done | bytes 524320 | tf_op jit(solution)/shard_map/ppermute | solution.py:297
  89.2 6.2 %collective-permute-done.19.b = f32[8,128,128]{2,1,0:T(8,128)S(1)} collective-permute-done((f32[8,128,128]{2,1,0:T(8,128)S(1)}, f32[8,128,128]{2,1,0:T(8,128)S(1)}, u32[]{:S(2)}, u32[]{:S(2)}) %collective-permute-start.19) | collective-permute-done | bytes 524320 | tf_op jit(solution)/shard_map/ppermute | solution.py:298
  95.4 1.4 %collective-permute-done.21.c = f32[8,128,128]{2,1,0:T(8,128)S(1)} collective-permute-done((f32[8,128,128]{2,1,0:T(8,128)S(1)}, f32[8,128,128]{2,1,0:T(8,128)S(1)}, u32[]{:S(2)}, u32[]{:S(2)}) %collective-permute-start.21) | collective-permute-done | bytes 524320 | tf_op jit(solution)/shard_map/ppermute | solution.py:299
  96.8 1.1 %shard_map.77 = f32[1024,128]{1,0:T(8,128)} custom-call(f32[8,128,128]{2,1,0:T(8,128)S(1)} %get-tuple-element.48.a, f32[8,128,128]{2,1,0:T(8,128)S(1)} %collective-permute-done.19.b, f32[8,128,128]{2,1,0:T(8,128)S(1)} %collective-permute-done.21.c, f32[8,128,128]{2,1,0:T(8,128)S(1)} %collective-permute-done.24.d, f32[128,128]{1,0:T(8,128)S(1)} %copy-done.2, ...), custom_call_target="tpu_custom_call" | custom-call | tf_op jit(solution)/shard_map/pallas_call | solution.py:301
  (28 shorter events, 0.3 us)
Async XLA Ops:
  1.7 15.3 %collective-permute-start.1 = (f32[1032,128]{1,0:T(8,128)S(1)}, f32[1032,128]{1,0:T(8,128)}, u32[]{:S(2)}, u32[]{:S(2)}) collective-permute-start(f32[1032,128]{1,0:T(8,128)S(1)} %select_maximum_fusion.refs_4_), channel_id=1, source_target_pairs={{0,2},{2,4},{4,6},{6,0},{1,3},{3,5},{5,7},{7,1},{8,10},{10,12},{12... | collective-permute-start | bytes 1585160 | tf_op jit(solution)/shard_map/ppermute | solution.py:246
  3.5 15.7 %collective-permute-start.3 = (f32[1032,128]{1,0:T(8,128)S(1)}, f32[1032,128]{1,0:T(8,128)}, u32[]{:S(2)}, u32[]{:S(2)}) collective-permute-start(f32[1032,128]{1,0:T(8,128)S(1)} %select_maximum_fusion.refs_4_), channel_id=1, source_target_pairs={{0,8},{8,0},{1,9},{9,1},{2,10},{10,2},{3,11},{11,3},{4,12},{12,4},... | collective-permute-start | bytes 1585160 | tf_op jit(solution)/shard_map/ppermute | solution.py:248
  7.3 17.1 %collective-permute-start.2 = (f32[1032,128]{1,0:T(8,128)S(1)}, f32[1032,128]{1,0:T(8,128)}, u32[]{:S(2)}, u32[]{:S(2)}) collective-permute-start(f32[1032,128]{1,0:T(8,128)S(1)} %select_maximum_fusion.refs_4_), channel_id=1, source_target_pairs={{0,6},{2,0},{4,2},{6,4},{1,7},{3,1},{5,3},{7,5},{8,14},{10,8},{12,... | collective-permute-start | bytes 1585160 | tf_op jit(solution)/shard_map/ppermute | solution.py:247
  9.0 15.5 %collective-permute-start = (f32[1032,128]{1,0:T(8,128)S(1)}, f32[1032,128]{1,0:T(8,128)S(1)}, u32[]{:S(2)}, u32[]{:S(2)}) collective-permute-start(f32[1032,128]{1,0:T(8,128)S(1)} %select_maximum_fusion.refs_4_), channel_id=1, source_target_pairs={{0,1},{1,0},{2,3},{3,2},{4,5},{5,4},{6,7},{7,6},{8,9},{9,8},{10,11... | collective-permute-start | bytes 1585160 | tf_op jit(solution)/shard_map/ppermute | solution.py:249
  19.2 17.8 %collective-permute-start.7 = (f32[1032,128]{1,0:T(8,128)}, f32[1032,128]{1,0:T(8,128)S(1)}, u32[]{:S(2)}, u32[]{:S(2)}) collective-permute-start(f32[1032,128]{1,0:T(8,128)} %collective-permute-done.3.refs_8_), channel_id=1, source_target_pairs={{0,6},{2,0},{4,2},{6,4},{1,7},{3,1},{5,3},{7,5},{8,14},{10,8},{12,... | collective-permute-start | bytes 1585160 | tf_op jit(solution)/shard_map/ppermute | solution.py:267
  21.0 16.0 %collective-permute-start.8 = (f32[1032,128]{1,0:T(8,128)}, f32[1032,128]{1,0:T(8,128)S(1)}, u32[]{:S(2)}, u32[]{:S(2)}) collective-permute-start(f32[1032,128]{1,0:T(8,128)} %collective-permute-done.1.refs_6_), channel_id=1, source_target_pairs={{0,8},{8,0},{1,9},{9,1},{2,10},{10,2},{3,11},{11,3},{4,12},{12,4},... | collective-permute-start | bytes 1585160 | tf_op jit(solution)/shard_map/ppermute | solution.py:268
  24.2 13.6 %collective-permute-start.6 = (f32[1032,128]{1,0:T(8,128)}, f32[1032,128]{1,0:T(8,128)S(1)}, u32[]{:S(2)}, u32[]{:S(2)}) collective-permute-start(f32[1032,128]{1,0:T(8,128)} %collective-permute-done.1.refs_6_), channel_id=1, source_target_pairs={{0,2},{2,4},{4,6},{6,0},{1,3},{3,5},{5,7},{7,1},{8,10},{10,12},{12... | collective-permute-start | bytes 1585160 | tf_op jit(solution)/shard_map/ppermute | solution.py:266
  24.5 15.6 %collective-permute-start.5 = (f32[1032,128]{1,0:T(8,128)}, f32[1032,128]{1,0:T(8,128)S(1)}, u32[]{:S(2)}, u32[]{:S(2)}) collective-permute-start(f32[1032,128]{1,0:T(8,128)} %collective-permute-done.3.refs_8_), channel_id=1, source_target_pairs={{0,1},{1,0},{2,3},{3,2},{4,5},{5,4},{6,7},{7,6},{8,9},{9,8},{10,11... | collective-permute-start | bytes 1585160 | tf_op jit(solution)/shard_map/ppermute | solution.py:269
  24.5 0.8 copy-start
  25.3 15.3 %collective-permute-start.4 = (f32[1032,128]{1,0:T(8,128)}, f32[1032,128]{1,0:T(8,128)S(1)}, u32[]{:S(2)}, u32[]{:S(2)}) collective-permute-start(f32[1032,128]{1,0:T(8,128)} %collective-permute-done.2.refs_7_), channel_id=1, source_target_pairs={{0,1},{1,0},{2,3},{3,2},{4,5},{5,4},{6,7},{7,6},{8,9},{9,8},{10,11... | collective-permute-start | bytes 1585160 | tf_op jit(solution)/shard_map/ppermute | solution.py:269
  25.8 1.0 %copy-start.1 = (f32[1032,128]{1,0:T(8,128)S(1)}, f32[1032,128]{1,0:T(8,128)}, u32[]{:S(2)}) copy-start(f32[1032,128]{1,0:T(8,128)} %copy-done) | copy-start | bytes 1585156
  26.9 0.7 copy-start.3
  37.9 11.5 %collective-permute-start.10 = (f32[520,128]{1,0:T(8,128)S(1)}, f32[520,128]{1,0:T(8,128)S(1)}, u32[]{:S(2)}, u32[]{:S(2)}) collective-permute-start(f32[520,128]{1,0:T(8,128)S(1)} %slice.31), channel_id=1, source_target_pairs={{0,6},{2,0},{4,2},{6,4},{1,7},{3,1},{5,3},{7,5},{8,14},{10,8},{12,... | collective-permute-start | bytes 798728 | tf_op jit(solution)/shard_map/ppermute | solution.py:277
  39.0 10.3 %collective-permute-start.9 = (f32[512,128]{1,0:T(8,128)S(1)}, f32[512,128]{1,0:T(8,128)S(1)}, u32[]{:S(2)}, u32[]{:S(2)}) collective-permute-start(f32[512,128]{1,0:T(8,128)S(1)} %slice.30), channel_id=1, source_target_pairs={{0,2},{2,4},{4,6},{6,0},{1,3},{3,5},{5,7},{7,1},{8,10},{10,12},{12... | collective-permute-start | bytes 786440 | tf_op jit(solution)/shard_map/ppermute | solution.py:277
  40.0 11.6 %collective-permute-start.11 = (f32[1032,128]{1,0:T(8,128)S(1)}, f32[1032,128]{1,0:T(8,128)S(1)}, u32[]{:S(2)}, u32[]{:S(2)}) collective-permute-start(f32[1032,128]{1,0:T(8,128)S(1)} %collective-permute-done.6.refs_6_), channel_id=1, source_target_pairs={{0,1},{1,0},{2,3},{3,2},{4,5},{5,4},{6,7},{7,6},{8,9},{9,8},{10,11... | collective-permute-start | bytes 1585160 | tf_op jit(solution)/shard_map/ppermute | solution.py:283
  40.0 11.6 %collective-permute-start.12 = (f32[1032,128]{1,0:T(8,128)S(1)}, f32[1032,128]{1,0:T(8,128)S(1)}, u32[]{:S(2)}, u32[]{:S(2)}) collective-permute-start(f32[1032,128]{1,0:T(8,128)S(1)} %collective-permute-done.7.refs_7_), channel_id=1, source_target_pairs={{0,1},{1,0},{2,3},{3,2},{4,5},{5,4},{6,7},{7,6},{8,9},{9,8},{10,11... | collective-permute-start | bytes 1585160 | tf_op jit(solution)/shard_map/ppermute | solution.py:283
  40.6 11.1 %collective-permute-start.13 = (f32[1032,128]{1,0:T(8,128)S(1)}, f32[1032,128]{1,0:T(8,128)S(1)}, u32[]{:S(2)}, u32[]{:S(2)}) collective-permute-start(f32[1032,128]{1,0:T(8,128)S(1)} %collective-permute-done.8.refs_8_), channel_id=1, source_target_pairs={{0,1},{1,0},{2,3},{3,2},{4,5},{5,4},{6,7},{7,6},{8,9},{9,8},{10,11... | collective-permute-start | bytes 1585160 | tf_op jit(solution)/shard_map/ppermute | solution.py:283
  49.4 2.5 %collective-permute-start.14 = (f32[1032,128]{1,0:T(8,128)}, f32[1032,128]{1,0:T(8,128)S(1)}, u32[]{:S(2)}, u32[]{:S(2)}) collective-permute-start(f32[1032,128]{1,0:T(8,128)} %collective-permute-done.1.refs_6_), channel_id=1, source_target_pairs={{0,1},{1,0},{2,3},{3,2},{4,5},{5,4},{6,7},{7,6},{8,9},{9,8},{10,11... | collective-permute-start | bytes 1585160 | tf_op jit(solution)/shard_map/ppermute | solution.py:283
  49.4 2.0 %collective-permute-start.15 = (f32[512,128]{1,0:T(8,128)S(1)}, f32[512,128]{1,0:T(8,128)S(1)}, u32[]{:S(2)}, u32[]{:S(2)}) collective-permute-start(f32[512,128]{1,0:T(8,128)S(1)} %collective-permute-done.9.refs_9_), channel_id=1, source_target_pairs={{0,1},{1,0},{2,3},{3,2},{4,5},{5,4},{6,7},{7,6},{8,9},{9,8},{10,11... | collective-permute-start | bytes 786440 | tf_op jit(solution)/shard_map/ppermute | solution.py:284
  51.3 1.5 %collective-permute-start.16 = (f32[520,128]{1,0:T(8,128)S(1)}, f32[520,128]{1,0:T(8,128)S(1)}, u32[]{:S(2)}, u32[]{:S(2)}) collective-permute-start(f32[520,128]{1,0:T(8,128)S(1)} %collective-permute-done.10.refs_10_), channel_id=1, source_target_pairs={{0,1},{1,0},{2,3},{3,2},{4,5},{5,4},{6,7},{7,6},{8,9},{9,8},{10,11... | collective-permute-start | bytes 798728 | tf_op jit(solution)/shard_map/ppermute | solution.py:284
  60.0 13.0 %collective-permute-start.17 = (f32[8,128,128]{2,1,0:T(8,128)S(1)}, f32[8,128,128]{2,1,0:T(8,128)S(1)}, u32[]{:S(2)}, u32[]{:S(2)}) collective-permute-start(f32[8,128,128]{2,1,0:T(8,128)S(1)} %get-tuple-element.46), channel_id=1, source_target_pairs={{0,64},{64,0},{1,65},{65,1},{2,66},{66,2},{3,67},{67,3},{4,68},{68... | collective-permute-start | bytes 1572872 | tf_op jit(solution)/shard_map/ppermute | solution.py:292
  60.1 14.4 %collective-permute-start.22 = (f32[8,128,128]{2,1,0:T(8,128)S(1)}, f32[8,128,128]{2,1,0:T(8,128)S(1)}, u32[]{:S(2)}, u32[]{:S(2)}) collective-permute-start(f32[8,128,128]{2,1,0:T(8,128)S(1)} %get-tuple-element.53), channel_id=1, source_target_pairs={{0,16},{16,32},{32,48},{48,0},{1,17},{17,33},{33,49},{49,1},{2,18}... | collective-permute-start | bytes 1572872 | tf_op jit(solution)/shard_map/ppermute | solution.py:293
  61.1 14.3 %collective-permute-start.23 = (f32[8,128,128]{2,1,0:T(8,128)S(1)}, f32[8,128,128]{2,1,0:T(8,128)S(1)}, u32[]{:S(2)}, u32[]{:S(2)}) collective-permute-start(f32[8,128,128]{2,1,0:T(8,128)S(1)} %get-tuple-element.54), channel_id=1, source_target_pairs={{0,48},{16,0},{32,16},{48,32},{1,49},{17,1},{33,17},{49,33},{2,50}... | collective-permute-start | bytes 1572872 | tf_op jit(solution)/shard_map/ppermute | solution.py:294
  63.4 33.4 %copy-start.2 = (f32[128,128]{1,0:T(8,128)S(1)}, f32[128,128]{1,0:T(8,128)}, u32[]{:S(2)}) copy-start(f32[128,128]{1,0:T(8,128)} %weight.1) | copy-start | bytes 196612
  63.4 33.4 %copy-start.4 = (f32[128]{0:T(128)S(1)}, f32[128]{0:T(128)}, u32[]{:S(2)}) copy-start(f32[128]{0:T(128)} %param.13) | copy-start | bytes 1540
  73.0 8.8 %collective-permute-start.18 = (f32[4,128,128]{2,1,0:T(8,128)S(1)}, f32[4,128,128]{2,1,0:T(8,128)S(1)}, u32[]{:S(2)}, u32[]{:S(2)}) collective-permute-start(f32[4,128,128]{2,1,0:T(8,128)S(1)} %get-tuple-element.56), channel_id=1, source_target_pairs={{0,16},{16,32},{32,48},{48,0},{1,17},{17,33},{33,49},{49,1},{2,18}... | collective-permute-start | bytes 786440 | tf_op jit(solution)/shard_map/ppermute | solution.py:295
  75.6 13.6 %collective-permute-start.24 = (f32[8,128,128]{2,1,0:T(8,128)S(1)}, f32[8,128,128]{2,1,0:T(8,128)S(1)}, u32[]{:S(2)}, u32[]{:S(2)}) collective-permute-start(f32[8,128,128]{2,1,0:T(8,128)S(1)} %add_add_fusion), channel_id=1, source_target_pairs={{0,64},{64,0},{1,65},{65,1},{2,66},{66,2},{3,67},{67,3},{4,68},{68... | collective-permute-start | bytes 1572872 | tf_op jit(solution)/shard_map/ppermute | solution.py:297
  76.2 7.9 %collective-permute-start.20 = (f32[4,128,128]{2,1,0:T(8,128)S(1)}, f32[4,128,128]{2,1,0:T(8,128)S(1)}, u32[]{:S(2)}, u32[]{:S(2)}) collective-permute-start(f32[4,128,128]{2,1,0:T(8,128)S(1)} %get-tuple-element.55), channel_id=1, source_target_pairs={{0,48},{16,0},{32,16},{48,32},{1,49},{17,1},{33,17},{49,33},{2,50}... | collective-permute-start | bytes 786440 | tf_op jit(solution)/shard_map/ppermute | solution.py:296
  81.9 13.5 %collective-permute-start.19 = (f32[8,128,128]{2,1,0:T(8,128)S(1)}, f32[8,128,128]{2,1,0:T(8,128)S(1)}, u32[]{:S(2)}, u32[]{:S(2)}) collective-permute-start(f32[8,128,128]{2,1,0:T(8,128)S(1)} %pad_maximum_fusion), channel_id=1, source_target_pairs={{0,16},{16,32},{32,48},{48,0},{1,17},{17,33},{33,49},{49,1},{2,18}... | collective-permute-start | bytes 1572872 | tf_op jit(solution)/shard_map/ppermute | solution.py:298
  84.2 12.7 %collective-permute-start.21 = (f32[8,128,128]{2,1,0:T(8,128)S(1)}, f32[8,128,128]{2,1,0:T(8,128)S(1)}, u32[]{:S(2)}, u32[]{:S(2)}) collective-permute-start(f32[8,128,128]{2,1,0:T(8,128)S(1)} %pad_maximum_fusion.1), channel_id=1, source_target_pairs={{0,48},{16,0},{32,16},{48,32},{1,49},{17,1},{33,17},{49,33},{2,50}... | collective-permute-start | bytes 1572872 | tf_op jit(solution)/shard_map/ppermute | solution.py:299

commit v10 on v9

--- a/solution.py
+++ b/solution.py
@@ -53,6 +53,12 @@
     count[0] = total
     for j in range(STEP):
         words[total + j] = -1
+
+
+def cut_up(rows):
+    piece = BLOCKS * TILE + 8
+    step = piece if rows % piece == 0 else rows
+    return [(row, step) for row in range(0, rows, step)]
 
 
 def tile_kernel(n_pieces, first, split_rest, owners, *refs):
@@ -71,16 +77,16 @@
     xs, ring, slots, table, ring_sem, slot_sem = scratch
     depth = RING // size
 
-    with_slots, held, n_blocks = [], [], 0
+    views, with_slots, n_blocks = [], [], 0
     for piece in pieces:
-        rows = piece.shape[0]
-        held.append(n_blocks)
-        n_blocks += rows // TILE
-        if rows % TILE:
-            with_slots.append((piece, n_blocks - BLOCKS))
+        for row, rows in cut_up(piece.shape[0]):
+            views.append((piece, row, rows // TILE, n_blocks))
+            n_blocks += rows // TILE
+            if rows % TILE:
+                with_slots.append((piece, row + rows - 8, n_blocks - BLOCKS))
     reads = [
-        pltpu.make_async_copy(piece.at[pl.ds(piece.shape[0] - 8, 8)], slots.at[i], slot_sem.at[i])
-        for i, (piece, at) in enumerate(with_slots)
+        pltpu.make_async_copy(piece.at[pl.ds(row, 8)], slots.at[i], slot_sem.at[i])
+        for i, (piece, row, at) in enumerate(with_slots)
     ]
     for read in reads:
         read.start()
@@ -121,7 +127,7 @@
         lax.fori_loop(0, DUMMY + 1, begin, 0, unroll=5)
     for read in reads:
         read.wait()
-    for i, (piece, at) in enumerate(with_slots):
+    for i, (piece, row, at) in enumerate(with_slots):
         for j in range(BLOCKS):
             table[slots[i, 0, j].astype(jnp.int32) & 127] = at + j
 
@@ -156,9 +162,9 @@
         fetch_first()
 
     def halve(j, carry):
-        for piece, at in zip(pieces, held):
-            for k in range(0, piece.shape[0] // TILE, HALF):
-                rows = pl.ds(pl.multiple_of((k + j) * TILE, TILE), TILE)
+        for piece, row, blocks, at in views:
+            for k in range(0, blocks, HALF):
+                rows = pl.ds(pl.multiple_of(row + (k + j) * TILE, 8), TILE)
                 xs[at + k + j] = halves(piece[rows, :])
         return carry
 
@@ -201,6 +207,8 @@
 
 def tile_products(place, words, count, tiles, pieces, so_far=None, split_rest=False, owners=()):
     first = so_far is None
+    views = [rows for p in pieces for row, rows in cut_up(p.shape[0])]
+    n_blocks = sum(rows // TILE for rows in views)
     size = LAST_STEP if owners else STEP
     smem = pl.BlockSpec(memory_space=pltpu.SMEM)
     vmem = pl.BlockSpec(memory_space=pltpu.VMEM)
@@ -217,14 +225,14 @@
         out_specs=[vmem] * len(owners) or [vmem] + [smem] * len(rests),
         scratch_shapes=[sums if owners else listed[0]]
         + [
-            pltpu.VMEM((sum(p.shape[0] // TILE for p in pieces), TILE, 2 * FEAT), bf16),
+            pltpu.VMEM((n_blocks, TILE, 2 * FEAT), bf16),
             pltpu.VMEM((RING // size, size, TILE, TILE), f32),
-            pltpu.SMEM((len(pieces), 8, 128), f32),
+            pltpu.SMEM((len(views), 8, 128), f32),
             pltpu.SMEM((BUCKETS * BLOCKS,), jnp.int32),
             pltpu.SemaphoreType.DMA((RING // size, size)),
-            pltpu.SemaphoreType.DMA((len(pieces),)),
+            pltpu.SemaphoreType.DMA((len(views),)),
         ],
-        compiler_params=pltpu.CompilerParams(vmem_limit_bytes=40 * 2**20),
+        compiler_params=pltpu.CompilerParams(vmem_limit_bytes=38 * 2**20),
         cost_estimate=pl.CostEstimate(flops=10**5, bytes_accessed=10**4, transcendentals=0),
     )(place, words, count, tiles, *pieces, *([] if first else [so_far]))
 
@@ -266,7 +274,7 @@
     two = move(below, "y", UP)
     far_above = move(far, "y", DOWN)
     far_below = move(below, "z_hi", SWAP)
-    swapped = [move(p, "core", SWAP) for p in (above, far)]
+    swapped = move(jnp.concatenate([below, above, far]), "core", SWAP)
     sums, soon, n_soon, words, count = tile_products(
         place, words, count, tiles, [own, other, below, above, far], split_rest=True
     )
@@ -277,10 +285,10 @@
     far_two = [move(cuts[0], "y", UP), move(cuts[1], "y", DOWN)]
     late = [two, far_above, far_below]
     last = [
-        *swapped,
+        swapped,
         *late,
         *far_two,
-        *[move(after(p, *cuts), "core", SWAP) for p in (*late, after(below, sums))],
+        move(after(jnp.concatenate(late), *cuts), "core", SWAP),
         *[move(p, "core", SWAP) for p in far_two],
     ]
     z_up, z_two, z_down = tile_products(place, soon, n_soon, tiles, last, sums, owners=(5, 6, 7))

time: 98.1 us -> 95.2 us (0.970)
  Pallas kernels: 28.5 us -> 24.6 us
  starting transfers between devices: 28 us -> 31.7 us
  local copies, waits for them, and re-layouts: 2.56 us -> 0.52 us
  waiting for transfers between devices: 36.5 us -> 35 us
    pallas_call x3, Pallas kernels: 24.5 us -> 20.6 us  [tile_products(): pl.pallas_call(functools.partial(tile_kernel, len(pieces), first, split_r...]
    ppermute x1, waiting for transfers between devices: 2.15 us -> 0.01 us  [body(): far = move(own, 'z_hi', SWAP)]
    unnamed x10 -> x6, local copies, waits for them, and re-layouts: 2.52 us -> 0.48 us
    ppermute x1, waiting for transfers between devices: 0.01 us -> 1.9 us  [body(): far_above = move(far, 'y', DOWN)]
    ppermute x1, waiting for transfers between devices: 6.17 us -> 7.74 us  [body(): end_up = move(jnp.concatenate([up[:half] + two_up, up[half:]]), 'x', UP)]
    ppermute x1, starting transfers between devices: 0.09 us -> 1.51 us  [body(): got_two = move(z_two, 'z_lo', SWAP)]
    ppermute x1, waiting for transfers between devices: 1.41 us -> 0.01 us  [body(): move(jnp.concatenate([down[:half], down[half:] + two_down]), 'x', DOWN)]
    ppermute x1, starting transfers between devices: 1.82 us -> 2.93 us  [body(): far_above = move(far, 'y', DOWN)]
  transfers between devices with their start and end apart: 25 -> 21, of which waited for: 15 -> 12; matrix products, arithmetic and copies ran while one was open for 0% -> 1% of each run, Pallas kernels for 21% -> 18%
where the time goes in v10:
time: 95.2 us; the launch traced here: 94.3 us
  waiting for transfers between devices  35 us (37%)
  starting transfers between devices  31.7 us (33%)
  Pallas kernels  24.6 us (26%)
  other arithmetic  2.38 us (2%)
    pallas_call x3, Pallas kernels, tile_products(): pl.pallas_call(functools.partial(tile_kernel, len(pieces), first, split_r...  20.6 us
    ppermute x2, waiting for transfers between devices, body(): far_two = [move(cuts[0], 'y', UP), move(cuts[1], 'y', DOWN)]  9.58 us
    ppermute x1, waiting for transfers between devices, body(): end_up = move(jnp.concatenate([up[:half] + two_up, up[half:]]), 'x', UP)  7.74 us
    ppermute x1, waiting for transfers between devices, body(): below = move(own, 'y', UP)  5.03 us
    ppermute x1, starting transfers between devices, body(): far = move(own, 'z_hi', SWAP)  3.88 us
    ppermute x1, starting transfers between devices, body(): far_below = move(below, 'z_hi', SWAP)  3.88 us
    ppermute x1, waiting for transfers between devices, body(): two_up = move(two[:half] + got_two[:half], 'x', UP)  3.39 us
    ppermute x2, starting transfers between devices, body(): far_two = [move(cuts[0], 'y', UP), move(cuts[1], 'y', DOWN)]  3.04 us
  transfers between devices with their start and end apart: 21, of which 12 were waited for; matrix products, arithmetic and copies ran while one was open for 1% of the time, Pallas kernels for 18%

profile of v10, /device:TPU:0, one launch (start us, length us, event | category | flops | bytes accessed | tf_op | source)
XLA Modules:
  0.0 94.3 jit_solution(7324974521416481280)
XLA Ops:
  0.0 0.7 convert_bitcast_fusion
  0.7 1.1 %select_maximum_fusion.refs_4_ = f32[1032,128]{1,0:T(8,128)S(1)} fusion(f32[1,8]{1,0:T(1,128)S(1)} %convert_bitcast_fusion, f32[1024,128]{1,0:T(8,128)} %param.7), kind=kLoop, calls=%fused_computation.2 | loop fusion | flops 396288 | bytes 1052704 | tf_op jit(solution)/shard_map/concatenate | solution.py:253
  1.7 1.7 %collective-permute-start.1 = (f32[1032,128]{1,0:T(8,128)S(1)}, f32[1032,128]{1,0:T(8,128)S(1)}, u32[]{:S(2)}, u32[]{:S(2)}) collective-permute-start(f32[1032,128]{1,0:T(8,128)S(1)} %select_maximum_fusion.refs_4_), channel_id=1, source_target_pairs={{0,2},{2,4},{4,6},{6,0},{1,3},{3,5},{5,7},{7,1},{8,10},{10,12},{12... | collective-permute-start | bytes 1585160 | tf_op jit(solution)/shard_map/ppermute | solution.py:254
  3.5 3.9 %collective-permute-start.3 = (f32[1032,128]{1,0:T(8,128)S(1)}, f32[1032,128]{1,0:T(8,128)S(1)}, u32[]{:S(2)}, u32[]{:S(2)}) collective-permute-start(f32[1032,128]{1,0:T(8,128)S(1)} %select_maximum_fusion.refs_4_), channel_id=1, source_target_pairs={{0,8},{8,0},{1,9},{9,1},{2,10},{10,2},{3,11},{11,3},{4,12},{12,4},... | collective-permute-start | bytes 1585160 | tf_op jit(solution)/shard_map/ppermute | solution.py:256
  7.3 1.7 %collective-permute-start.2 = (f32[1032,128]{1,0:T(8,128)S(1)}, f32[1032,128]{1,0:T(8,128)S(1)}, u32[]{:S(2)}, u32[]{:S(2)}) collective-permute-start(f32[1032,128]{1,0:T(8,128)S(1)} %select_maximum_fusion.refs_4_), channel_id=1, source_target_pairs={{0,6},{2,0},{4,2},{6,4},{1,7},{3,1},{5,3},{7,5},{8,14},{10,8},{12,... | collective-permute-start | bytes 1585160 | tf_op jit(solution)/shard_map/ppermute | solution.py:255
  9.0 0.0 collective-permute-start
  9.0 2.9 %shard_map.73 = (s32[288]{0:T(512)}, s32[1]{0:T(128)}) custom-call(s32[16,16]{1,0:T(8,128)} %bitcast.12, s32[16,16]{1,0:T(8,128)} %bitcast.13), custom_call_target="tpu_custom_call" | custom-call | flops 100000 | bytes 10000 | tf_op jit(solution)/shard_map/pallas_call | solution.py:262
  11.9 5.0 %collective-permute-done.1.refs_6_ = f32[1032,128]{1,0:T(8,128)S(1)} collective-permute-done((f32[1032,128]{1,0:T(8,128)S(1)}, f32[1032,128]{1,0:T(8,128)S(1)}, u32[]{:S(2)}, u32[]{:S(2)}) %collective-permute-start.1) | collective-permute-done | bytes 528416 | tf_op jit(solution)/shard_map/ppermute | solution.py:254
  16.9 3.9 %collective-permute-start.7 = (f32[1032,128]{1,0:T(8,128)S(1)}, f32[1032,128]{1,0:T(8,128)S(1)}, u32[]{:S(2)}, u32[]{:S(2)}) collective-permute-start(f32[1032,128]{1,0:T(8,128)S(1)} %collective-permute-done.1.refs_6_), channel_id=1, source_target_pairs={{0,8},{8,0},{1,9},{9,1},{2,10},{10,2},{3,11},{11,3},{4,12},{12,4},... | collective-permute-start | bytes 1585160 | tf_op jit(solution)/shard_map/ppermute | solution.py:276
  20.8 0.3 collective-permute-start.5
  21.1 2.9 %collective-permute-start.6 = (f32[1032,128]{1,0:T(8,128)S(1)}, f32[1032,128]{1,0:T(8,128)S(1)}, u32[]{:S(2)}, u32[]{:S(2)}) collective-permute-start(f32[1032,128]{1,0:T(8,128)S(1)} %collective-permute-done.3.refs_8_), channel_id=1, source_target_pairs={{0,6},{2,0},{4,2},{6,4},{1,7},{3,1},{5,3},{7,5},{8,14},{10,8},{12,... | collective-permute-start | bytes 1585160 | tf_op jit(solution)/shard_map/ppermute | solution.py:275
  24.0 0.1 pad_add_fusion.refs_0_
  24.1 0.1 pad_maximum_fusion
  24.2 0.1 collective-permute-start.4
  24.3 0.5 copy-done.1
  24.8 7.2 %shard_map.74 = (f32[65,128,128]{2,1,0:T(8,128)S(1)}, s32[288]{0:T(512)S(1)}, s32[1]{0:T(128)}, s32[288]{0:T(512)S(1)}, s32[1]{0:T(128)}) custom-call(s32[2]{0:T(128)S(1)} %pad_add_fusion.refs_0_, s32[288]{0:T(512)S(1)} %copy-done.1, s32[1]{0:T(128)} %get-tuple-element.27.refs_2_, f32[256,128,128]{2,1,0:T(8,128)} %bitcast.9, ...), custom_call_target="tpu_custom_call" | custom-call | flops 100000 | bytes 10000 | tf_op jit(solution)/shard_map/pallas_call | solution.py:220
  32.0 1.9 %collective-permute-done.6.refs_6_ = f32[1032,128]{1,0:T(8,128)S(1)} collective-permute-done((f32[1032,128]{1,0:T(8,128)S(1)}, f32[1032,128]{1,0:T(8,128)S(1)}, u32[]{:S(2)}, u32[]{:S(2)}) %collective-permute-start.6) | collective-permute-done | bytes 528416 | tf_op jit(solution)/shard_map/ppermute | solution.py:275
  33.9 0.7 collective-permute-done.5.refs_5_
  34.7 0.1 pad_maximum_fusion.1
  34.8 0.1 collective-permute-start.10
  34.9 3.0 %collective-permute-start.9 = (f32[520,128]{1,0:T(8,128)S(1)}, f32[520,128]{1,0:T(8,128)S(1)}, u32[]{:S(2)}, u32[]{:S(2)}) collective-permute-start(f32[520,128]{1,0:T(8,128)S(1)} %slice.31), channel_id=1, source_target_pairs={{0,6},{2,0},{4,2},{6,4},{1,7},{3,1},{5,3},{7,5},{8,14},{10,8},{12,... | collective-permute-start | bytes 798728 | tf_op jit(solution)/shard_map/ppermute | solution.py:285
  38.0 6.3 %collective-permute-done.9.refs_9_ = f32[520,128]{1,0:T(8,128)S(1)} collective-permute-done((f32[520,128]{1,0:T(8,128)S(1)}, f32[520,128]{1,0:T(8,128)S(1)}, u32[]{:S(2)}, u32[]{:S(2)}) %collective-permute-start.9) | collective-permute-done | bytes 266272 | tf_op jit(solution)/shard_map/ppermute | solution.py:285
  44.2 3.3 %collective-permute-done.8.refs_8_ = f32[512,128]{1,0:T(8,128)S(1)} collective-permute-done((f32[512,128]{1,0:T(8,128)S(1)}, f32[512,128]{1,0:T(8,128)S(1)}, u32[]{:S(2)}, u32[]{:S(2)}) %collective-permute-start.8) | collective-permute-done | bytes 262176 | tf_op jit(solution)/shard_map/ppermute | solution.py:285
  47.6 1.5 %collective-permute-done.11.refs_11_ = f32[512,128]{1,0:T(8,128)S(1)} collective-permute-done((f32[512,128]{1,0:T(8,128)S(1)}, f32[512,128]{1,0:T(8,128)S(1)}, u32[]{:S(2)}, u32[]{:S(2)}) %collective-permute-start.11) | collective-permute-done | bytes 262176 | tf_op jit(solution)/shard_map/ppermute | solution.py:292
  49.1 6.2 %shard_map.75 = (f32[8,128,128]{2,1,0:T(8,128)S(1)}, f32[8,128,128]{2,1,0:T(8,128)S(1)}, f32[8,128,128]{2,1,0:T(8,128)S(1)}) custom-call(s32[2]{0:T(128)S(1)} %pad_add_fusion.refs_0_, s32[288]{0:T(512)S(1)} %get-tuple-element.36.refs_1_, s32[1]{0:T(128)} %get-tuple-element.37.refs_2_, f32[256,128,128]{2,1,0:T(8,128)} %bitcast.10, ...), custom_call_target="tpu_custom_call" | custom-call | flops 100000 | bytes 10000 | tf_op jit(solution)/shard_map/pallas_call | solution.py:220
  55.3 1.5 %collective-permute-start.13 = (f32[8,128,128]{2,1,0:T(8,128)S(1)}, f32[8,128,128]{2,1,0:T(8,128)S(1)}, u32[]{:S(2)}, u32[]{:S(2)}) collective-permute-start(f32[8,128,128]{2,1,0:T(8,128)S(1)} %get-tuple-element.38), channel_id=1, source_target_pairs={{0,64},{64,0},{1,65},{65,1},{2,66},{66,2},{3,67},{67,3},{4,68},{68... | collective-permute-start | bytes 1572872 | tf_op jit(solution)/shard_map/ppermute | solution.py:300
  56.9 0.7 collective-permute-start.18
  57.5 2.6 %collective-permute-start.19 = (f32[8,128,128]{2,1,0:T(8,128)S(1)}, f32[8,128,128]{2,1,0:T(8,128)S(1)}, u32[]{:S(2)}, u32[]{:S(2)}) collective-permute-start(f32[8,128,128]{2,1,0:T(8,128)S(1)} %get-tuple-element.46), channel_id=1, source_target_pairs={{0,48},{16,0},{32,16},{48,32},{1,49},{17,1},{33,17},{49,33},{2,50}... | collective-permute-start | bytes 1572872 | tf_op jit(solution)/shard_map/ppermute | solution.py:302
  60.1 7.1 %shard_map.76 = (f32[8,128,128]{2,1,0:T(8,128)S(1)}, f32[8,128,128]{2,1,0:T(8,128)S(1)}, f32[8,128,128]{2,1,0:T(8,128)S(1)}, f32[8,128,128]{2,1,0:T(8,128)S(1)}, f32[8,128,128]{2,1,0:T(8,128)S(1)}) custom-call(s32[2]{0:T(128)S(1)} %pad_add_fusion.refs_0_, s32[288]{0:T(512)S(1)} %get-tuple-element.29.refs_1_, s32[1]{0:T(128)} %get-tuple-element.30.refs_2_, ...), custom_call_target="tpu_custom_call" | custom-call | flops 100000 | bytes 10000 | tf_op jit(solution)/shard_map/pallas_call | solution.py:220
  67.2 2.2 %collective-permute-done.13 = f32[8,128,128]{2,1,0:T(8,128)S(1)} collective-permute-done((f32[8,128,128]{2,1,0:T(8,128)S(1)}, f32[8,128,128]{2,1,0:T(8,128)S(1)}, u32[]{:S(2)}, u32[]{:S(2)}) %collective-permute-start.13) | collective-permute-done | bytes 524320 | tf_op jit(solution)/shard_map/ppermute | solution.py:300
  69.4 0.1 slice_add_fusion
  69.5 2.0 %collective-permute-start.14 = (f32[4,128,128]{2,1,0:T(8,128)S(1)}, f32[4,128,128]{2,1,0:T(8,128)S(1)}, u32[]{:S(2)}, u32[]{:S(2)}) collective-permute-start(f32[4,128,128]{2,1,0:T(8,128)S(1)} %get-tuple-element.48), channel_id=1, source_target_pairs={{0,16},{16,32},{32,48},{48,0},{1,17},{17,33},{33,49},{49,1},{2,18}... | collective-permute-start | bytes 786440 | tf_op jit(solution)/shard_map/ppermute | solution.py:303
  71.4 0.3 collective-permute-done.18
  71.8 0.0 collective-permute-done.19
  71.8 0.1 add_add_fusion
  71.9 1.1 %collective-permute-start.20 = (f32[8,128,128]{2,1,0:T(8,128)S(1)}, f32[8,128,128]{2,1,0:T(8,128)S(1)}, u32[]{:S(2)}, u32[]{:S(2)}) collective-permute-start(f32[8,128,128]{2,1,0:T(8,128)S(1)} %add_add_fusion), channel_id=1, source_target_pairs={{0,64},{64,0},{1,65},{65,1},{2,66},{66,2},{3,67},{67,3},{4,68},{68... | collective-permute-start | bytes 1572872 | tf_op jit(solution)/shard_map/ppermute | solution.py:305
  73.0 2.5 %collective-permute-start.16 = (f32[4,128,128]{2,1,0:T(8,128)S(1)}, f32[4,128,128]{2,1,0:T(8,128)S(1)}, u32[]{:S(2)}, u32[]{:S(2)}) collective-permute-start(f32[4,128,128]{2,1,0:T(8,128)S(1)} %get-tuple-element.47), channel_id=1, source_target_pairs={{0,48},{16,0},{32,16},{48,32},{1,49},{17,1},{33,17},{49,33},{2,50}... | collective-permute-start | bytes 786440 | tf_op jit(solution)/shard_map/ppermute | solution.py:304
  75.5 3.4 %collective-permute-done.14 = f32[4,128,128]{2,1,0:T(8,128)S(1)} collective-permute-done((f32[4,128,128]{2,1,0:T(8,128)S(1)}, f32[4,128,128]{2,1,0:T(8,128)S(1)}, u32[]{:S(2)}, u32[]{:S(2)}) %collective-permute-start.14) | collective-permute-done | bytes 262176 | tf_op jit(solution)/shard_map/ppermute | solution.py:303
  78.9 0.1 slice_add_fusion.3
  78.9 0.0 copy-start
  79.0 0.0 copy-start.2
  79.0 0.9 collective-permute-start.15
  79.9 0.6 collective-permute-done.16
  80.5 0.1 fusion
  80.6 2.8 %collective-permute-start.17 = (f32[8,128,128]{2,1,0:T(8,128)S(1)}, f32[8,128,128]{2,1,0:T(8,128)S(1)}, u32[]{:S(2)}, u32[]{:S(2)}) collective-permute-start(f32[8,128,128]{2,1,0:T(8,128)S(1)} %pad_maximum_fusion.3), channel_id=1, source_target_pairs={{0,48},{16,0},{32,16},{48,32},{1,49},{17,1},{33,17},{49,33},{2,50}... | collective-permute-start | bytes 1572872 | tf_op jit(solution)/shard_map/ppermute | solution.py:307
  83.5 2.0 %collective-permute-done.20.d = f32[8,128,128]{2,1,0:T(8,128)S(1)} collective-permute-done((f32[8,128,128]{2,1,0:T(8,128)S(1)}, f32[8,128,128]{2,1,0:T(8,128)S(1)}, u32[]{:S(2)}, u32[]{:S(2)}) %collective-permute-start.20) | collective-permute-done | bytes 524320 | tf_op jit(solution)/shard_map/ppermute | solution.py:305
  85.4 7.7 %collective-permute-done.15.b = f32[8,128,128]{2,1,0:T(8,128)S(1)} collective-permute-done((f32[8,128,128]{2,1,0:T(8,128)S(1)}, f32[8,128,128]{2,1,0:T(8,128)S(1)}, u32[]{:S(2)}, u32[]{:S(2)}) %collective-permute-start.15) | collective-permute-done | bytes 524320 | tf_op jit(solution)/shard_map/ppermute | solution.py:306
  93.2 1.1 %shard_map.77 = f32[1024,128]{1,0:T(8,128)} custom-call(f32[8,128,128]{2,1,0:T(8,128)S(1)} %get-tuple-element.40.a, f32[8,128,128]{2,1,0:T(8,128)S(1)} %collective-permute-done.15.b, f32[8,128,128]{2,1,0:T(8,128)S(1)} %collective-permute-done.17.c, f32[8,128,128]{2,1,0:T(8,128)S(1)} %collective-permute-done.20.d, f32[128,128]{1,0:T(8,128)S(1)} %copy-done, ...), custom_call_target="tpu_custom_call" | custom-call | tf_op jit(solution)/shard_map/pallas_call | solution.py:309
  (18 shorter events, 0.1 us)
Async XLA Ops:
  1.7 15.2 %collective-permute-start.1 = (f32[1032,128]{1,0:T(8,128)S(1)}, f32[1032,128]{1,0:T(8,128)S(1)}, u32[]{:S(2)}, u32[]{:S(2)}) collective-permute-start(f32[1032,128]{1,0:T(8,128)S(1)} %select_maximum_fusion.refs_4_), channel_id=1, source_target_pairs={{0,2},{2,4},{4,6},{6,0},{1,3},{3,5},{5,7},{7,1},{8,10},{10,12},{12... | collective-permute-start | bytes 1585160 | tf_op jit(solution)/shard_map/ppermute | solution.py:254
  3.5 17.6 %collective-permute-start.3 = (f32[1032,128]{1,0:T(8,128)S(1)}, f32[1032,128]{1,0:T(8,128)S(1)}, u32[]{:S(2)}, u32[]{:S(2)}) collective-permute-start(f32[1032,128]{1,0:T(8,128)S(1)} %select_maximum_fusion.refs_4_), channel_id=1, source_target_pairs={{0,8},{8,0},{1,9},{9,1},{2,10},{10,2},{3,11},{11,3},{4,12},{12,4},... | collective-permute-start | bytes 1585160 | tf_op jit(solution)/shard_map/ppermute | solution.py:256
  7.3 16.8 %collective-permute-start.2 = (f32[1032,128]{1,0:T(8,128)S(1)}, f32[1032,128]{1,0:T(8,128)S(1)}, u32[]{:S(2)}, u32[]{:S(2)}) collective-permute-start(f32[1032,128]{1,0:T(8,128)S(1)} %select_maximum_fusion.refs_4_), channel_id=1, source_target_pairs={{0,6},{2,0},{4,2},{6,4},{1,7},{3,1},{5,3},{7,5},{8,14},{10,8},{12,... | collective-permute-start | bytes 1585160 | tf_op jit(solution)/shard_map/ppermute | solution.py:255
  9.0 15.3 %collective-permute-start = (f32[1032,128]{1,0:T(8,128)S(1)}, f32[1032,128]{1,0:T(8,128)S(1)}, u32[]{:S(2)}, u32[]{:S(2)}) collective-permute-start(f32[1032,128]{1,0:T(8,128)S(1)} %select_maximum_fusion.refs_4_), channel_id=1, source_target_pairs={{0,1},{1,0},{2,3},{3,2},{4,5},{5,4},{6,7},{7,6},{8,9},{9,8},{10,11... | collective-permute-start | bytes 1585160 | tf_op jit(solution)/shard_map/ppermute | solution.py:257
  16.9 17.0 %collective-permute-start.7 = (f32[1032,128]{1,0:T(8,128)S(1)}, f32[1032,128]{1,0:T(8,128)S(1)}, u32[]{:S(2)}, u32[]{:S(2)}) collective-permute-start(f32[1032,128]{1,0:T(8,128)S(1)} %collective-permute-done.1.refs_6_), channel_id=1, source_target_pairs={{0,8},{8,0},{1,9},{9,1},{2,10},{10,2},{3,11},{11,3},{4,12},{12,4},... | collective-permute-start | bytes 1585160 | tf_op jit(solution)/shard_map/ppermute | solution.py:276
  20.8 13.9 %collective-permute-start.5 = (f32[1032,128]{1,0:T(8,128)S(1)}, f32[1032,128]{1,0:T(8,128)S(1)}, u32[]{:S(2)}, u32[]{:S(2)}) collective-permute-start(f32[1032,128]{1,0:T(8,128)S(1)} %collective-permute-done.1.refs_6_), channel_id=1, source_target_pairs={{0,2},{2,4},{4,6},{6,0},{1,3},{3,5},{5,7},{7,1},{8,10},{10,12},{12... | collective-permute-start | bytes 1585160 | tf_op jit(solution)/shard_map/ppermute | solution.py:274
  21.1 12.8 %collective-permute-start.6 = (f32[1032,128]{1,0:T(8,128)S(1)}, f32[1032,128]{1,0:T(8,128)S(1)}, u32[]{:S(2)}, u32[]{:S(2)}) collective-permute-start(f32[1032,128]{1,0:T(8,128)S(1)} %collective-permute-done.3.refs_8_), channel_id=1, source_target_pairs={{0,6},{2,0},{4,2},{6,4},{1,7},{3,1},{5,3},{7,5},{8,14},{10,8},{12,... | collective-permute-start | bytes 1585160 | tf_op jit(solution)/shard_map/ppermute | solution.py:275
  24.1 0.7 copy-start.1
  24.2 24.9 %collective-permute-start.4 = (f32[3096,128]{1,0:T(8,128)S(1)}, f32[3096,128]{1,0:T(8,128)S(1)}, u32[]{:S(2)}, u32[]{:S(2)}) collective-permute-start(f32[3096,128]{1,0:T(8,128)S(1)} %pad_maximum_fusion), channel_id=1, source_target_pairs={{0,1},{1,0},{2,3},{3,2},{4,5},{5,4},{6,7},{7,6},{8,9},{9,8},{10,11... | collective-permute-start | bytes 4755464 | tf_op jit(solution)/shard_map/ppermute | solution.py:277
  34.8 14.3 %collective-permute-start.10 = (f32[3096,128]{1,0:T(8,128)S(1)}, f32[3096,128]{1,0:T(8,128)S(1)}, u32[]{:S(2)}, u32[]{:S(2)}) collective-permute-start(f32[3096,128]{1,0:T(8,128)S(1)} %pad_maximum_fusion.1), channel_id=1, source_target_pairs={{0,1},{1,0},{2,3},{3,2},{4,5},{5,4},{6,7},{7,6},{8,9},{9,8},{10,11... | collective-permute-start | bytes 4755464 | tf_op jit(solution)/shard_map/ppermute | solution.py:291
  34.9 9.3 %collective-permute-start.9 = (f32[520,128]{1,0:T(8,128)S(1)}, f32[520,128]{1,0:T(8,128)S(1)}, u32[]{:S(2)}, u32[]{:S(2)}) collective-permute-start(f32[520,128]{1,0:T(8,128)S(1)} %slice.31), channel_id=1, source_target_pairs={{0,6},{2,0},{4,2},{6,4},{1,7},{3,1},{5,3},{7,5},{8,14},{10,8},{12,... | collective-permute-start | bytes 798728 | tf_op jit(solution)/shard_map/ppermute | solution.py:285
  38.0 9.6 %collective-permute-start.8 = (f32[512,128]{1,0:T(8,128)S(1)}, f32[512,128]{1,0:T(8,128)S(1)}, u32[]{:S(2)}, u32[]{:S(2)}) collective-permute-start(f32[512,128]{1,0:T(8,128)S(1)} %slice.30), channel_id=1, source_target_pairs={{0,2},{2,4},{4,6},{6,0},{1,3},{3,5},{5,7},{7,1},{8,10},{10,12},{12... | collective-permute-start | bytes 786440 | tf_op jit(solution)/shard_map/ppermute | solution.py:285
  44.2 4.9 %collective-permute-start.12 = (f32[520,128]{1,0:T(8,128)S(1)}, f32[520,128]{1,0:T(8,128)S(1)}, u32[]{:S(2)}, u32[]{:S(2)}) collective-permute-start(f32[520,128]{1,0:T(8,128)S(1)} %collective-permute-done.9.refs_9_), channel_id=1, source_target_pairs={{0,1},{1,0},{2,3},{3,2},{4,5},{5,4},{6,7},{7,6},{8,9},{9,8},{10,11... | collective-permute-start | bytes 798728 | tf_op jit(solution)/shard_map/ppermute | solution.py:292
  47.6 1.5 %collective-permute-start.11 = (f32[512,128]{1,0:T(8,128)S(1)}, f32[512,128]{1,0:T(8,128)S(1)}, u32[]{:S(2)}, u32[]{:S(2)}) collective-permute-start(f32[512,128]{1,0:T(8,128)S(1)} %collective-permute-done.8.refs_8_), channel_id=1, source_target_pairs={{0,1},{1,0},{2,3},{3,2},{4,5},{5,4},{6,7},{7,6},{8,9},{9,8},{10,11... | collective-permute-start | bytes 786440 | tf_op jit(solution)/shard_map/ppermute | solution.py:292
  55.3 14.0 %collective-permute-start.13 = (f32[8,128,128]{2,1,0:T(8,128)S(1)}, f32[8,128,128]{2,1,0:T(8,128)S(1)}, u32[]{:S(2)}, u32[]{:S(2)}) collective-permute-start(f32[8,128,128]{2,1,0:T(8,128)S(1)} %get-tuple-element.38), channel_id=1, source_target_pairs={{0,64},{64,0},{1,65},{65,1},{2,66},{66,2},{3,67},{67,3},{4,68},{68... | collective-permute-start | bytes 1572872 | tf_op jit(solution)/shard_map/ppermute | solution.py:300
  56.9 14.9 %collective-permute-start.18 = (f32[8,128,128]{2,1,0:T(8,128)S(1)}, f32[8,128,128]{2,1,0:T(8,128)S(1)}, u32[]{:S(2)}, u32[]{:S(2)}) collective-permute-start(f32[8,128,128]{2,1,0:T(8,128)S(1)} %get-tuple-element.45), channel_id=1, source_target_pairs={{0,16},{16,32},{32,48},{48,0},{1,17},{17,33},{33,49},{49,1},{2,18}... | collective-permute-start | bytes 1572872 | tf_op jit(solution)/shard_map/ppermute | solution.py:301
  57.5 14.3 %collective-permute-start.19 = (f32[8,128,128]{2,1,0:T(8,128)S(1)}, f32[8,128,128]{2,1,0:T(8,128)S(1)}, u32[]{:S(2)}, u32[]{:S(2)}) collective-permute-start(f32[8,128,128]{2,1,0:T(8,128)S(1)} %get-tuple-element.46), channel_id=1, source_target_pairs={{0,48},{16,0},{32,16},{48,32},{1,49},{17,1},{33,17},{49,33},{2,50}... | collective-permute-start | bytes 1572872 | tf_op jit(solution)/shard_map/ppermute | solution.py:302
  69.5 9.4 %collective-permute-start.14 = (f32[4,128,128]{2,1,0:T(8,128)S(1)}, f32[4,128,128]{2,1,0:T(8,128)S(1)}, u32[]{:S(2)}, u32[]{:S(2)}) collective-permute-start(f32[4,128,128]{2,1,0:T(8,128)S(1)} %get-tuple-element.48), channel_id=1, source_target_pairs={{0,16},{16,32},{32,48},{48,0},{1,17},{17,33},{33,49},{49,1},{2,18}... | collective-permute-start | bytes 786440 | tf_op jit(solution)/shard_map/ppermute | solution.py:303
  71.9 13.5 %collective-permute-start.20 = (f32[8,128,128]{2,1,0:T(8,128)S(1)}, f32[8,128,128]{2,1,0:T(8,128)S(1)}, u32[]{:S(2)}, u32[]{:S(2)}) collective-permute-start(f32[8,128,128]{2,1,0:T(8,128)S(1)} %add_add_fusion), channel_id=1, source_target_pairs={{0,64},{64,0},{1,65},{65,1},{2,66},{66,2},{3,67},{67,3},{4,68},{68... | collective-permute-start | bytes 1572872 | tf_op jit(solution)/shard_map/ppermute | solution.py:305
  73.0 7.6 %collective-permute-start.16 = (f32[4,128,128]{2,1,0:T(8,128)S(1)}, f32[4,128,128]{2,1,0:T(8,128)S(1)}, u32[]{:S(2)}, u32[]{:S(2)}) collective-permute-start(f32[4,128,128]{2,1,0:T(8,128)S(1)} %get-tuple-element.47), channel_id=1, source_target_pairs={{0,48},{16,0},{32,16},{48,32},{1,49},{17,1},{33,17},{49,33},{2,50}... | collective-permute-start | bytes 786440 | tf_op jit(solution)/shard_map/ppermute | solution.py:304
  78.9 14.2 %copy-start = (f32[128,128]{1,0:T(8,128)S(1)}, f32[128,128]{1,0:T(8,128)}, u32[]{:S(2)}) copy-start(f32[128,128]{1,0:T(8,128)} %weight.1) | copy-start | bytes 196612
  79.0 14.2 %copy-start.2 = (f32[128]{0:T(128)S(1)}, f32[128]{0:T(128)}, u32[]{:S(2)}) copy-start(f32[128]{0:T(128)} %param.13) | copy-start | bytes 1540
  79.0 14.2 %collective-permute-start.15 = (f32[8,128,128]{2,1,0:T(8,128)S(1)}, f32[8,128,128]{2,1,0:T(8,128)S(1)}, u32[]{:S(2)}, u32[]{:S(2)}) collective-permute-start(f32[8,128,128]{2,1,0:T(8,128)S(1)} %pad_maximum_fusion.2), channel_id=1, source_target_pairs={{0,16},{16,32},{32,48},{48,0},{1,17},{17,33},{33,49},{49,1},{2,18}... | collective-permute-start | bytes 1572872 | tf_op jit(solution)/shard_map/ppermute | solution.py:306
  80.6 12.5 %collective-permute-start.17 = (f32[8,128,128]{2,1,0:T(8,128)S(1)}, f32[8,128,128]{2,1,0:T(8,128)S(1)}, u32[]{:S(2)}, u32[]{:S(2)}) collective-permute-start(f32[8,128,128]{2,1,0:T(8,128)S(1)} %pad_maximum_fusion.3), channel_id=1, source_target_pairs={{0,48},{16,0},{32,16},{48,32},{1,49},{17,1},{33,17},{49,33},{2,50}... | collective-permute-start | bytes 1572872 | tf_op jit(solution)/shard_map/ppermute | solution.py:307

commit v11 on v10

--- a/solution.py
+++ b/solution.py
@@ -275,18 +275,20 @@
     far_above = move(far, "y", DOWN)
     far_below = move(below, "z_hi", SWAP)
     swapped = move(jnp.concatenate([below, above, far]), "core", SWAP)
-    sums, soon, n_soon, words, count = tile_products(
-        place, words, count, tiles, [own, other, below, above, far], split_rest=True
-    )
+    sums, words, count = tile_products(place, words, count, tiles, [own, other, below, above, far])
 
     two, far_above, far_below = lax.optimization_barrier((two, far_above, far_below, sums))[:3]
     cut = HALF * TILE
     cuts = [far_below[:cut], far_above[cut:]]
     far_two = [move(cuts[0], "y", UP), move(cuts[1], "y", DOWN)]
     late = [two, far_above, far_below]
+    sums, soon, n_soon, words, count = tile_products(
+        place, words, count, tiles, [swapped, two], sums, split_rest=True
+    )
+    far_two = list(lax.optimization_barrier((*far_two, sums))[:2])
     last = [
-        swapped,
-        *late,
+        far_above,
+        far_below,
         *far_two,
         move(after(jnp.concatenate(late), *cuts), "core", SWAP),
         *[move(p, "core", SWAP) for p in far_two],

time: 95.2 us -> 94.7 us (level)
  waiting for transfers between devices: 35 us -> 27.4 us
  Pallas kernels: 24.6 us -> 32.1 us
    ppermute x2, waiting for transfers between devices: 9.58 us -> 1.43 us  [body(): far_two = [move(cuts[0], 'y', UP), move(cuts[1], 'y', DOWN)]]
    pallas_call x3 -> x4, Pallas kernels: 20.6 us -> 28.1 us  [tile_products(): pl.pallas_call(functools.partial(tile_kernel, len(pieces), first, split_r...]
    ppermute x1, waiting for transfers between devices: 2.17 us -> 4.53 us  [body(): got_two = move(z_two, 'z_lo', SWAP)]
    ppermute x1, starting transfers between devices: 1.51 us -> 0.26 us  [body(): got_two = move(z_two, 'z_lo', SWAP)]
    ppermute x1, starting transfers between devices: 2.57 us -> 1.34 us  [body(): got_down = move(z_down, 'x', DOWN)]
    ppermute x1, starting transfers between devices: 0.67 us -> 1.9 us  [body(): got_up = move(z_up, 'x', UP)]
    ppermute x1, waiting for transfers between devices: 0.01 us -> 1.15 us  [body(): move(jnp.concatenate([down[:half], down[half:] + two_down]), 'x', DOWN)]
    ppermute x1, waiting for transfers between devices: 1.9 us -> 0.81 us  [body(): far_above = move(far, 'y', DOWN)]
  transfers between devices with their start and end apart: 21 -> 21, of which waited for: 12 -> 12; matrix products, arithmetic and copies ran while one was open for 1% -> 1% of each run, Pallas kernels for 18% -> 27%
where the time goes in v11:
time: 94.7 us; the launch traced here: 93.9 us
  Pallas kernels  32.1 us (34%)
  starting transfers between devices  31.3 us (33%)
  waiting for transfers between devices  27.4 us (29%)
  other arithmetic  2.39 us (3%)
    pallas_call x4, Pallas kernels, tile_products(): pl.pallas_call(functools.partial(tile_kernel, len(pieces), first, split_r...  28.1 us
    ppermute x1, waiting for transfers between devices, body(): end_up = move(jnp.concatenate([up[:half] + two_up, up[half:]]), 'x', UP)  6.65 us
    ppermute x1, waiting for transfers between devices, body(): below = move(own, 'y', UP)  5.03 us
    ppermute x1, waiting for transfers between devices, body(): got_two = move(z_two, 'z_lo', SWAP)  4.53 us
    ppermute x1, starting transfers between devices, body(): far = move(own, 'z_hi', SWAP)  3.88 us
    ppermute x1, starting transfers between devices, body(): far_below = move(below, 'z_hi', SWAP)  3.88 us
    ppermute x1, starting transfers between devices, body(): move(jnp.concatenate([down[:half], down[half:] + two_down]), 'x', DOWN)  3.76 us
    ppermute x2, starting transfers between devices, body(): far_two = [move(cuts[0], 'y', UP), move(cuts[1], 'y', DOWN)]  3.04 us
  transfers between devices with their start and end apart: 21, of which 12 were waited for; matrix products, arithmetic and copies ran while one was open for 1% of the time, Pallas kernels for 27%

profile of v11, /device:TPU:0, one launch (start us, length us, event | category | flops | bytes accessed | tf_op | source)
XLA Modules:
  0.0 93.9 jit_solution(12804003423292234184)
XLA Ops:
  0.0 0.7 convert_bitcast_fusion
  0.7 1.1 %select_maximum_fusion.refs_4_ = f32[1032,128]{1,0:T(8,128)S(1)} fusion(f32[1,8]{1,0:T(1,128)S(1)} %convert_bitcast_fusion, f32[1024,128]{1,0:T(8,128)} %param.7), kind=kLoop, calls=%fused_computation.2 | loop fusion | flops 396288 | bytes 1052704 | tf_op jit(solution)/shard_map/concatenate | solution.py:253
  1.7 1.7 %collective-permute-start.1 = (f32[1032,128]{1,0:T(8,128)S(1)}, f32[1032,128]{1,0:T(8,128)S(1)}, u32[]{:S(2)}, u32[]{:S(2)}) collective-permute-start(f32[1032,128]{1,0:T(8,128)S(1)} %select_maximum_fusion.refs_4_), channel_id=1, source_target_pairs={{0,2},{2,4},{4,6},{6,0},{1,3},{3,5},{5,7},{7,1},{8,10},{10,12},{12... | collective-permute-start | bytes 1585160 | tf_op jit(solution)/shard_map/ppermute | solution.py:254
  3.5 3.9 %collective-permute-start.3 = (f32[1032,128]{1,0:T(8,128)S(1)}, f32[1032,128]{1,0:T(8,128)S(1)}, u32[]{:S(2)}, u32[]{:S(2)}) collective-permute-start(f32[1032,128]{1,0:T(8,128)S(1)} %select_maximum_fusion.refs_4_), channel_id=1, source_target_pairs={{0,8},{8,0},{1,9},{9,1},{2,10},{10,2},{3,11},{11,3},{4,12},{12,4},... | collective-permute-start | bytes 1585160 | tf_op jit(solution)/shard_map/ppermute | solution.py:256
  7.3 1.7 %collective-permute-start.2 = (f32[1032,128]{1,0:T(8,128)S(1)}, f32[1032,128]{1,0:T(8,128)S(1)}, u32[]{:S(2)}, u32[]{:S(2)}) collective-permute-start(f32[1032,128]{1,0:T(8,128)S(1)} %select_maximum_fusion.refs_4_), channel_id=1, source_target_pairs={{0,6},{2,0},{4,2},{6,4},{1,7},{3,1},{5,3},{7,5},{8,14},{10,8},{12,... | collective-permute-start | bytes 1585160 | tf_op jit(solution)/shard_map/ppermute | solution.py:255
  9.0 2.9 %shard_map.73 = (s32[288]{0:T(512)}, s32[1]{0:T(128)}) custom-call(s32[16,16]{1,0:T(8,128)} %bitcast.13, s32[16,16]{1,0:T(8,128)} %bitcast.14), custom_call_target="tpu_custom_call" | custom-call | flops 100000 | bytes 10000 | tf_op jit(solution)/shard_map/pallas_call | solution.py:262
  11.9 5.0 %collective-permute-done.1.refs_6_ = f32[1032,128]{1,0:T(8,128)S(1)} collective-permute-done((f32[1032,128]{1,0:T(8,128)S(1)}, f32[1032,128]{1,0:T(8,128)S(1)}, u32[]{:S(2)}, u32[]{:S(2)}) %collective-permute-start.1) | collective-permute-done | bytes 528416 | tf_op jit(solution)/shard_map/ppermute | solution.py:254
  16.9 3.9 %collective-permute-start.7 = (f32[1032,128]{1,0:T(8,128)S(1)}, f32[1032,128]{1,0:T(8,128)S(1)}, u32[]{:S(2)}, u32[]{:S(2)}) collective-permute-start(f32[1032,128]{1,0:T(8,128)S(1)} %collective-permute-done.1.refs_6_), channel_id=1, source_target_pairs={{0,8},{8,0},{1,9},{9,1},{2,10},{10,2},{3,11},{11,3},{4,12},{12,4},... | collective-permute-start | bytes 1585160 | tf_op jit(solution)/shard_map/ppermute | solution.py:276
  20.8 0.3 collective-permute-start.5
  21.1 2.9 %collective-permute-start.6 = (f32[1032,128]{1,0:T(8,128)S(1)}, f32[1032,128]{1,0:T(8,128)S(1)}, u32[]{:S(2)}, u32[]{:S(2)}) collective-permute-start(f32[1032,128]{1,0:T(8,128)S(1)} %collective-permute-done.3.refs_8_), channel_id=1, source_target_pairs={{0,6},{2,0},{4,2},{6,4},{1,7},{3,1},{5,3},{7,5},{8,14},{10,8},{12,... | collective-permute-start | bytes 1585160 | tf_op jit(solution)/shard_map/ppermute | solution.py:275
  24.0 0.1 pad_add_fusion.refs_0_
  24.1 0.1 pad_maximum_fusion
  24.2 0.1 collective-permute-start.4
  24.3 0.5 copy-done.1
  24.8 8.3 %shard_map.74 = (f32[65,128,128]{2,1,0:T(8,128)S(1)}, s32[288]{0:T(512)S(1)}, s32[1]{0:T(128)}) custom-call(s32[2]{0:T(128)S(1)} %pad_add_fusion.refs_0_, s32[288]{0:T(512)S(1)} %copy-done.1, s32[1]{0:T(128)} %get-tuple-element.32.refs_2_, f32[256,128,128]{2,1,0:T(8,128)} %bitcast.9, f32[1032,128]{1,0:T(8,128)S(1)} %select_maximum_fusion.refs_4_, ...), custom_call_target="tpu_custom_call" | custom-call | flops 100000 | bytes 10000 | tf_op jit(solution)/shard_map/pallas_call | solution.py:220
  33.1 0.8 collective-permute-done.6.refs_4_
  33.9 0.7 collective-permute-done.5.refs_5_
  34.7 0.1 pad_maximum_fusion.1
  34.8 0.1 collective-permute-start.10
  34.9 3.0 %collective-permute-start.9 = (f32[520,128]{1,0:T(8,128)S(1)}, f32[520,128]{1,0:T(8,128)S(1)}, u32[]{:S(2)}, u32[]{:S(2)}) collective-permute-start(f32[520,128]{1,0:T(8,128)S(1)} %slice.31), channel_id=1, source_target_pairs={{0,6},{2,0},{4,2},{6,4},{1,7},{3,1},{5,3},{7,5},{8,14},{10,8},{12,... | collective-permute-start | bytes 798728 | tf_op jit(solution)/shard_map/ppermute | solution.py:283
  38.0 8.1 %shard_map.75 = (f32[65,128,128]{2,1,0:T(8,128)S(1)}, s32[288]{0:T(512)S(1)}, s32[1]{0:T(128)}, s32[288]{0:T(512)S(1)}, s32[1]{0:T(128)}) custom-call(s32[2]{0:T(128)S(1)} %pad_add_fusion.refs_0_, s32[288]{0:T(512)S(1)} %get-tuple-element.34.refs_1_, s32[1]{0:T(128)} %get-tuple-element.35.refs_2_, f32[256,128,128]{2,1,0:T(8,128)} %bitcast.10, ...), custom_call_target="tpu_custom_call" | custom-call | flops 100000 | bytes 10000 | tf_op jit(solution)/shard_map/pallas_call | solution.py:220
  46.1 1.4 %collective-permute-done.8.refs_6_ = f32[512,128]{1,0:T(8,128)S(1)} collective-permute-done((f32[512,128]{1,0:T(8,128)S(1)}, f32[512,128]{1,0:T(8,128)S(1)}, u32[]{:S(2)}, u32[]{:S(2)}) %collective-permute-start.8) | collective-permute-done | bytes 262176 | tf_op jit(solution)/shard_map/ppermute | solution.py:283
  47.6 0.5 collective-permute-start.11
  48.1 1.4 %collective-permute-done.11.refs_9_ = f32[512,128]{1,0:T(8,128)S(1)} collective-permute-done((f32[512,128]{1,0:T(8,128)S(1)}, f32[512,128]{1,0:T(8,128)S(1)}, u32[]{:S(2)}, u32[]{:S(2)}) %collective-permute-start.11) | collective-permute-done | bytes 262176 | tf_op jit(solution)/shard_map/ppermute | solution.py:294
  49.5 5.6 %shard_map.76 = (f32[8,128,128]{2,1,0:T(8,128)S(1)}, f32[8,128,128]{2,1,0:T(8,128)S(1)}, f32[8,128,128]{2,1,0:T(8,128)S(1)}) custom-call(s32[2]{0:T(128)S(1)} %pad_add_fusion.refs_0_, s32[288]{0:T(512)S(1)} %get-tuple-element.46.refs_1_, s32[1]{0:T(128)} %get-tuple-element.47.refs_2_, f32[256,128,128]{2,1,0:T(8,128)} %bitcast.11, ...), custom_call_target="tpu_custom_call" | custom-call | flops 100000 | bytes 10000 | tf_op jit(solution)/shard_map/pallas_call | solution.py:220
  55.1 0.3 collective-permute-start.13
  55.4 1.9 %collective-permute-start.18 = (f32[8,128,128]{2,1,0:T(8,128)S(1)}, f32[8,128,128]{2,1,0:T(8,128)S(1)}, u32[]{:S(2)}, u32[]{:S(2)}) collective-permute-start(f32[8,128,128]{2,1,0:T(8,128)S(1)} %get-tuple-element.55), channel_id=1, source_target_pairs={{0,16},{16,32},{32,48},{48,0},{1,17},{17,33},{33,49},{49,1},{2,18}... | collective-permute-start | bytes 1572872 | tf_op jit(solution)/shard_map/ppermute | solution.py:303
  57.3 1.3 %collective-permute-start.19 = (f32[8,128,128]{2,1,0:T(8,128)S(1)}, f32[8,128,128]{2,1,0:T(8,128)S(1)}, u32[]{:S(2)}, u32[]{:S(2)}) collective-permute-start(f32[8,128,128]{2,1,0:T(8,128)S(1)} %get-tuple-element.56), channel_id=1, source_target_pairs={{0,48},{16,0},{32,16},{48,32},{1,49},{17,1},{33,17},{49,33},{2,50}... | collective-permute-start | bytes 1572872 | tf_op jit(solution)/shard_map/ppermute | solution.py:304
  58.6 6.0 %shard_map.77 = (f32[8,128,128]{2,1,0:T(8,128)S(1)}, f32[8,128,128]{2,1,0:T(8,128)S(1)}, f32[8,128,128]{2,1,0:T(8,128)S(1)}, f32[8,128,128]{2,1,0:T(8,128)S(1)}, f32[8,128,128]{2,1,0:T(8,128)S(1)}) custom-call(s32[2]{0:T(128)S(1)} %pad_add_fusion.refs_0_, s32[288]{0:T(512)S(1)} %get-tuple-element.38.refs_1_, s32[1]{0:T(128)} %get-tuple-element.39.refs_2_, ...), custom_call_target="tpu_custom_call" | custom-call | flops 100000 | bytes 10000 | tf_op jit(solution)/shard_map/pallas_call | solution.py:220
  64.6 4.5 %collective-permute-done.13 = f32[8,128,128]{2,1,0:T(8,128)S(1)} collective-permute-done((f32[8,128,128]{2,1,0:T(8,128)S(1)}, f32[8,128,128]{2,1,0:T(8,128)S(1)}, u32[]{:S(2)}, u32[]{:S(2)}) %collective-permute-start.13) | collective-permute-done | bytes 524320 | tf_op jit(solution)/shard_map/ppermute | solution.py:302
  69.2 0.1 slice_add_fusion
  69.2 1.2 %collective-permute-start.14 = (f32[4,128,128]{2,1,0:T(8,128)S(1)}, f32[4,128,128]{2,1,0:T(8,128)S(1)}, u32[]{:S(2)}, u32[]{:S(2)}) collective-permute-start(f32[4,128,128]{2,1,0:T(8,128)S(1)} %get-tuple-element.58), channel_id=1, source_target_pairs={{0,16},{16,32},{32,48},{48,0},{1,17},{17,33},{33,49},{49,1},{2,18}... | collective-permute-start | bytes 786440 | tf_op jit(solution)/shard_map/ppermute | solution.py:305
  70.4 0.7 collective-permute-done.18
  71.1 0.1 add_add_fusion
  71.2 1.1 %collective-permute-start.20 = (f32[8,128,128]{2,1,0:T(8,128)S(1)}, f32[8,128,128]{2,1,0:T(8,128)S(1)}, u32[]{:S(2)}, u32[]{:S(2)}) collective-permute-start(f32[8,128,128]{2,1,0:T(8,128)S(1)} %add_add_fusion), channel_id=1, source_target_pairs={{0,64},{64,0},{1,65},{65,1},{2,66},{66,2},{3,67},{67,3},{4,68},{68... | collective-permute-start | bytes 1572872 | tf_op jit(solution)/shard_map/ppermute | solution.py:307
  72.3 3.0 %collective-permute-start.16 = (f32[4,128,128]{2,1,0:T(8,128)S(1)}, f32[4,128,128]{2,1,0:T(8,128)S(1)}, u32[]{:S(2)}, u32[]{:S(2)}) collective-permute-start(f32[4,128,128]{2,1,0:T(8,128)S(1)} %get-tuple-element.57), channel_id=1, source_target_pairs={{0,48},{16,0},{32,16},{48,32},{1,49},{17,1},{33,17},{49,33},{2,50}... | collective-permute-start | bytes 786440 | tf_op jit(solution)/shard_map/ppermute | solution.py:306
  75.3 2.7 %collective-permute-done.14 = f32[4,128,128]{2,1,0:T(8,128)S(1)} collective-permute-done((f32[4,128,128]{2,1,0:T(8,128)S(1)}, f32[4,128,128]{2,1,0:T(8,128)S(1)}, u32[]{:S(2)}, u32[]{:S(2)}) %collective-permute-start.14) | collective-permute-done | bytes 262176 | tf_op jit(solution)/shard_map/ppermute | solution.py:305
  78.0 0.1 slice_add_fusion.3
  78.1 0.0 copy-start
  78.1 0.0 copy-start.2
  78.2 0.8 collective-permute-start.15
  78.9 0.8 collective-permute-done.16
  79.8 0.1 fusion
  79.9 3.8 %collective-permute-start.17 = (f32[8,128,128]{2,1,0:T(8,128)S(1)}, f32[8,128,128]{2,1,0:T(8,128)S(1)}, u32[]{:S(2)}, u32[]{:S(2)}) collective-permute-start(f32[8,128,128]{2,1,0:T(8,128)S(1)} %pad_maximum_fusion.3), channel_id=1, source_target_pairs={{0,48},{16,0},{32,16},{48,32},{1,49},{17,1},{33,17},{49,33},{2,50}... | collective-permute-start | bytes 1572872 | tf_op jit(solution)/shard_map/ppermute | solution.py:309
  83.6 1.4 %collective-permute-done.20.d = f32[8,128,128]{2,1,0:T(8,128)S(1)} collective-permute-done((f32[8,128,128]{2,1,0:T(8,128)S(1)}, f32[8,128,128]{2,1,0:T(8,128)S(1)}, u32[]{:S(2)}, u32[]{:S(2)}) %collective-permute-start.20) | collective-permute-done | bytes 524320 | tf_op jit(solution)/shard_map/ppermute | solution.py:307
  85.0 6.6 %collective-permute-done.15.b = f32[8,128,128]{2,1,0:T(8,128)S(1)} collective-permute-done((f32[8,128,128]{2,1,0:T(8,128)S(1)}, f32[8,128,128]{2,1,0:T(8,128)S(1)}, u32[]{:S(2)}, u32[]{:S(2)}) %collective-permute-start.15) | collective-permute-done | bytes 524320 | tf_op jit(solution)/shard_map/ppermute | solution.py:308
  91.6 1.1 %collective-permute-done.17.c = f32[8,128,128]{2,1,0:T(8,128)S(1)} collective-permute-done((f32[8,128,128]{2,1,0:T(8,128)S(1)}, f32[8,128,128]{2,1,0:T(8,128)S(1)}, u32[]{:S(2)}, u32[]{:S(2)}) %collective-permute-start.17) | collective-permute-done | bytes 524320 | tf_op jit(solution)/shard_map/ppermute | solution.py:309
  92.8 1.1 %shard_map.78 = f32[1024,128]{1,0:T(8,128)} custom-call(f32[8,128,128]{2,1,0:T(8,128)S(1)} %get-tuple-element.50.a, f32[8,128,128]{2,1,0:T(8,128)S(1)} %collective-permute-done.15.b, f32[8,128,128]{2,1,0:T(8,128)S(1)} %collective-permute-done.17.c, f32[8,128,128]{2,1,0:T(8,128)S(1)} %collective-permute-done.20.d, f32[128,128]{1,0:T(8,128)S(1)} %copy-done, ...), custom_call_target="tpu_custom_call" | custom-call | tf_op jit(solution)/shard_map/pallas_call | solution.py:311
  (19 shorter events, 0.1 us)
Async XLA Ops:
  1.7 15.2 %collective-permute-start.1 = (f32[1032,128]{1,0:T(8,128)S(1)}, f32[1032,128]{1,0:T(8,128)S(1)}, u32[]{:S(2)}, u32[]{:S(2)}) collective-permute-start(f32[1032,128]{1,0:T(8,128)S(1)} %select_maximum_fusion.refs_4_), channel_id=1, source_target_pairs={{0,2},{2,4},{4,6},{6,0},{1,3},{3,5},{5,7},{7,1},{8,10},{10,12},{12... | collective-permute-start | bytes 1585160 | tf_op jit(solution)/shard_map/ppermute | solution.py:254
  3.5 17.6 %collective-permute-start.3 = (f32[1032,128]{1,0:T(8,128)S(1)}, f32[1032,128]{1,0:T(8,128)S(1)}, u32[]{:S(2)}, u32[]{:S(2)}) collective-permute-start(f32[1032,128]{1,0:T(8,128)S(1)} %select_maximum_fusion.refs_4_), channel_id=1, source_target_pairs={{0,8},{8,0},{1,9},{9,1},{2,10},{10,2},{3,11},{11,3},{4,12},{12,4},... | collective-permute-start | bytes 1585160 | tf_op jit(solution)/shard_map/ppermute | solution.py:256
  7.3 16.8 %collective-permute-start.2 = (f32[1032,128]{1,0:T(8,128)S(1)}, f32[1032,128]{1,0:T(8,128)S(1)}, u32[]{:S(2)}, u32[]{:S(2)}) collective-permute-start(f32[1032,128]{1,0:T(8,128)S(1)} %select_maximum_fusion.refs_4_), channel_id=1, source_target_pairs={{0,6},{2,0},{4,2},{6,4},{1,7},{3,1},{5,3},{7,5},{8,14},{10,8},{12,... | collective-permute-start | bytes 1585160 | tf_op jit(solution)/shard_map/ppermute | solution.py:255
  9.0 15.3 %collective-permute-start = (f32[1032,128]{1,0:T(8,128)S(1)}, f32[1032,128]{1,0:T(8,128)S(1)}, u32[]{:S(2)}, u32[]{:S(2)}) collective-permute-start(f32[1032,128]{1,0:T(8,128)S(1)} %select_maximum_fusion.refs_4_), channel_id=1, source_target_pairs={{0,1},{1,0},{2,3},{3,2},{4,5},{5,4},{6,7},{7,6},{8,9},{9,8},{10,11... | collective-permute-start | bytes 1585160 | tf_op jit(solution)/shard_map/ppermute | solution.py:257
  16.9 17.0 %collective-permute-start.7 = (f32[1032,128]{1,0:T(8,128)S(1)}, f32[1032,128]{1,0:T(8,128)S(1)}, u32[]{:S(2)}, u32[]{:S(2)}) collective-permute-start(f32[1032,128]{1,0:T(8,128)S(1)} %collective-permute-done.1.refs_6_), channel_id=1, source_target_pairs={{0,8},{8,0},{1,9},{9,1},{2,10},{10,2},{3,11},{11,3},{4,12},{12,4},... | collective-permute-start | bytes 1585160 | tf_op jit(solution)/shard_map/ppermute | solution.py:276
  20.8 13.9 %collective-permute-start.5 = (f32[1032,128]{1,0:T(8,128)S(1)}, f32[1032,128]{1,0:T(8,128)S(1)}, u32[]{:S(2)}, u32[]{:S(2)}) collective-permute-start(f32[1032,128]{1,0:T(8,128)S(1)} %collective-permute-done.1.refs_6_), channel_id=1, source_target_pairs={{0,2},{2,4},{4,6},{6,0},{1,3},{3,5},{5,7},{7,1},{8,10},{10,12},{12... | collective-permute-start | bytes 1585160 | tf_op jit(solution)/shard_map/ppermute | solution.py:274
  21.1 12.8 %collective-permute-start.6 = (f32[1032,128]{1,0:T(8,128)S(1)}, f32[1032,128]{1,0:T(8,128)S(1)}, u32[]{:S(2)}, u32[]{:S(2)}) collective-permute-start(f32[1032,128]{1,0:T(8,128)S(1)} %collective-permute-done.3.refs_8_), channel_id=1, source_target_pairs={{0,6},{2,0},{4,2},{6,4},{1,7},{3,1},{5,3},{7,5},{8,14},{10,8},{12,... | collective-permute-start | bytes 1585160 | tf_op jit(solution)/shard_map/ppermute | solution.py:275
  24.1 0.7 copy-start.1
  24.2 13.8 %collective-permute-start.4 = (f32[3096,128]{1,0:T(8,128)S(1)}, f32[3096,128]{1,0:T(8,128)S(1)}, u32[]{:S(2)}, u32[]{:S(2)}) collective-permute-start(f32[3096,128]{1,0:T(8,128)S(1)} %pad_maximum_fusion), channel_id=1, source_target_pairs={{0,1},{1,0},{2,3},{3,2},{4,5},{5,4},{6,7},{7,6},{8,9},{9,8},{10,11... | collective-permute-start | bytes 4755464 | tf_op jit(solution)/shard_map/ppermute | solution.py:277
  34.8 14.6 %collective-permute-start.10 = (f32[3096,128]{1,0:T(8,128)S(1)}, f32[3096,128]{1,0:T(8,128)S(1)}, u32[]{:S(2)}, u32[]{:S(2)}) collective-permute-start(f32[3096,128]{1,0:T(8,128)S(1)} %pad_maximum_fusion.1), channel_id=1, source_target_pairs={{0,1},{1,0},{2,3},{3,2},{4,5},{5,4},{6,7},{7,6},{8,9},{9,8},{10,11... | collective-permute-start | bytes 4755464 | tf_op jit(solution)/shard_map/ppermute | solution.py:293
  34.9 12.6 %collective-permute-start.9 = (f32[520,128]{1,0:T(8,128)S(1)}, f32[520,128]{1,0:T(8,128)S(1)}, u32[]{:S(2)}, u32[]{:S(2)}) collective-permute-start(f32[520,128]{1,0:T(8,128)S(1)} %slice.31), channel_id=1, source_target_pairs={{0,6},{2,0},{4,2},{6,4},{1,7},{3,1},{5,3},{7,5},{8,14},{10,8},{12,... | collective-permute-start | bytes 798728 | tf_op jit(solution)/shard_map/ppermute | solution.py:283
  38.0 9.6 %collective-permute-start.8 = (f32[512,128]{1,0:T(8,128)S(1)}, f32[512,128]{1,0:T(8,128)S(1)}, u32[]{:S(2)}, u32[]{:S(2)}) collective-permute-start(f32[512,128]{1,0:T(8,128)S(1)} %slice.30), channel_id=1, source_target_pairs={{0,2},{2,4},{4,6},{6,0},{1,3},{3,5},{5,7},{7,1},{8,10},{10,12},{12... | collective-permute-start | bytes 786440 | tf_op jit(solution)/shard_map/ppermute | solution.py:283
  47.6 1.9 %collective-permute-start.12 = (f32[520,128]{1,0:T(8,128)S(1)}, f32[520,128]{1,0:T(8,128)S(1)}, u32[]{:S(2)}, u32[]{:S(2)}) collective-permute-start(f32[520,128]{1,0:T(8,128)S(1)} %collective-permute-done.9.refs_7_), channel_id=1, source_target_pairs={{0,1},{1,0},{2,3},{3,2},{4,5},{5,4},{6,7},{7,6},{8,9},{9,8},{10,11... | collective-permute-start | bytes 798728 | tf_op jit(solution)/shard_map/ppermute | solution.py:294
  47.6 1.9 %collective-permute-start.11 = (f32[512,128]{1,0:T(8,128)S(1)}, f32[512,128]{1,0:T(8,128)S(1)}, u32[]{:S(2)}, u32[]{:S(2)}) collective-permute-start(f32[512,128]{1,0:T(8,128)S(1)} %collective-permute-done.8.refs_6_), channel_id=1, source_target_pairs={{0,1},{1,0},{2,3},{3,2},{4,5},{5,4},{6,7},{7,6},{8,9},{9,8},{10,11... | collective-permute-start | bytes 786440 | tf_op jit(solution)/shard_map/ppermute | solution.py:294
  55.1 14.0 %collective-permute-start.13 = (f32[8,128,128]{2,1,0:T(8,128)S(1)}, f32[8,128,128]{2,1,0:T(8,128)S(1)}, u32[]{:S(2)}, u32[]{:S(2)}) collective-permute-start(f32[8,128,128]{2,1,0:T(8,128)S(1)} %get-tuple-element.48), channel_id=1, source_target_pairs={{0,64},{64,0},{1,65},{65,1},{2,66},{66,2},{3,67},{67,3},{4,68},{68... | collective-permute-start | bytes 1572872 | tf_op jit(solution)/shard_map/ppermute | solution.py:302
  55.4 15.7 %collective-permute-start.18 = (f32[8,128,128]{2,1,0:T(8,128)S(1)}, f32[8,128,128]{2,1,0:T(8,128)S(1)}, u32[]{:S(2)}, u32[]{:S(2)}) collective-permute-start(f32[8,128,128]{2,1,0:T(8,128)S(1)} %get-tuple-element.55), channel_id=1, source_target_pairs={{0,16},{16,32},{32,48},{48,0},{1,17},{17,33},{33,49},{49,1},{2,18}... | collective-permute-start | bytes 1572872 | tf_op jit(solution)/shard_map/ppermute | solution.py:303
  57.3 13.8 %collective-permute-start.19 = (f32[8,128,128]{2,1,0:T(8,128)S(1)}, f32[8,128,128]{2,1,0:T(8,128)S(1)}, u32[]{:S(2)}, u32[]{:S(2)}) collective-permute-start(f32[8,128,128]{2,1,0:T(8,128)S(1)} %get-tuple-element.56), channel_id=1, source_target_pairs={{0,48},{16,0},{32,16},{48,32},{1,49},{17,1},{33,17},{49,33},{2,50}... | collective-permute-start | bytes 1572872 | tf_op jit(solution)/shard_map/ppermute | solution.py:304
  69.2 8.8 %collective-permute-start.14 = (f32[4,128,128]{2,1,0:T(8,128)S(1)}, f32[4,128,128]{2,1,0:T(8,128)S(1)}, u32[]{:S(2)}, u32[]{:S(2)}) collective-permute-start(f32[4,128,128]{2,1,0:T(8,128)S(1)} %get-tuple-element.58), channel_id=1, source_target_pairs={{0,16},{16,32},{32,48},{48,0},{1,17},{17,33},{33,49},{49,1},{2,18}... | collective-permute-start | bytes 786440 | tf_op jit(solution)/shard_map/ppermute | solution.py:305
  71.2 13.7 %collective-permute-start.20 = (f32[8,128,128]{2,1,0:T(8,128)S(1)}, f32[8,128,128]{2,1,0:T(8,128)S(1)}, u32[]{:S(2)}, u32[]{:S(2)}) collective-permute-start(f32[8,128,128]{2,1,0:T(8,128)S(1)} %add_add_fusion), channel_id=1, source_target_pairs={{0,64},{64,0},{1,65},{65,1},{2,66},{66,2},{3,67},{67,3},{4,68},{68... | collective-permute-start | bytes 1572872 | tf_op jit(solution)/shard_map/ppermute | solution.py:307
  72.3 7.4 %collective-permute-start.16 = (f32[4,128,128]{2,1,0:T(8,128)S(1)}, f32[4,128,128]{2,1,0:T(8,128)S(1)}, u32[]{:S(2)}, u32[]{:S(2)}) collective-permute-start(f32[4,128,128]{2,1,0:T(8,128)S(1)} %get-tuple-element.57), channel_id=1, source_target_pairs={{0,48},{16,0},{32,16},{48,32},{1,49},{17,1},{33,17},{49,33},{2,50}... | collective-permute-start | bytes 786440 | tf_op jit(solution)/shard_map/ppermute | solution.py:306
  78.1 14.7 %copy-start = (f32[128,128]{1,0:T(8,128)S(1)}, f32[128,128]{1,0:T(8,128)}, u32[]{:S(2)}) copy-start(f32[128,128]{1,0:T(8,128)} %weight.1) | copy-start | bytes 196612
  78.1 14.7 %copy-start.2 = (f32[128]{0:T(128)S(1)}, f32[128]{0:T(128)}, u32[]{:S(2)}) copy-start(f32[128]{0:T(128)} %param.13) | copy-start | bytes 1540
  78.2 13.5 %collective-permute-start.15 = (f32[8,128,128]{2,1,0:T(8,128)S(1)}, f32[8,128,128]{2,1,0:T(8,128)S(1)}, u32[]{:S(2)}, u32[]{:S(2)}) collective-permute-start(f32[8,128,128]{2,1,0:T(8,128)S(1)} %pad_maximum_fusion.2), channel_id=1, source_target_pairs={{0,16},{16,32},{32,48},{48,0},{1,17},{17,33},{33,49},{49,1},{2,18}... | collective-permute-start | bytes 1572872 | tf_op jit(solution)/shard_map/ppermute | solution.py:308
  79.9 12.9 %collective-permute-start.17 = (f32[8,128,128]{2,1,0:T(8,128)S(1)}, f32[8,128,128]{2,1,0:T(8,128)S(1)}, u32[]{:S(2)}, u32[]{:S(2)}) collective-permute-start(f32[8,128,128]{2,1,0:T(8,128)S(1)} %pad_maximum_fusion.3), channel_id=1, source_target_pairs={{0,48},{16,0},{32,16},{48,32},{1,49},{17,1},{33,17},{49,33},{2,50}... | collective-permute-start | bytes 1572872 | tf_op jit(solution)/shard_map/ppermute | solution.py:309

commit v12 on v11

--- a/solution.py
+++ b/solution.py
@@ -304,7 +304,7 @@
     got_down = move(z_down, "x", DOWN)
     two_up = move(two[:half] + got_two[:half], "x", UP)
     two_down = move(two[half:] + got_two[half:], "x", DOWN)
-    end_z = move(z_mine + got_up + got_down, "z_lo", SWAP)
+    end_z = move(after(z_mine + got_up + got_down, two_up), "z_lo", SWAP)
     end_up = move(jnp.concatenate([up[:half] + two_up, up[half:]]), "x", UP)
     end_down = move(jnp.concatenate([down[:half], down[half:] + two_down]), "x", DOWN)
 

time: 94.7 us -> 96 us (1.014); the launches traced: 93.9 us -> 96.2 us
  waiting for transfers between devices: 27.4 us -> 34.2 us
  starting transfers between devices: 31.3 us -> 29 us
  Pallas kernels: 32.1 us -> 29.9 us
    ppermute x1, waiting for transfers between devices: 1.37 us -> 9.17 us  [body(): end_z = move(after(z_mine + got_up + got_down, two_up), 'z_lo', SWAP)]
    ppermute x1, waiting for transfers between devices: 2.75 us -> 9.11 us  [body(): two_up = move(two[:half] + got_two[:half], 'x', UP)]
    ppermute x1, waiting for transfers between devices: 6.65 us -> 1.41 us  [body(): end_up = move(jnp.concatenate([up[:half] + two_up, up[half:]]), 'x', UP)]
    pallas_call x4, Pallas kernels: 28.1 us -> 26 us  [tile_products(): pl.pallas_call(functools.partial(tile_kernel, len(pieces), first, split_r...]
    ppermute x1, waiting for transfers between devices: 0.81 us -> 2.22 us  [body(): far_above = move(far, 'y', DOWN)]
    ppermute x1, starting transfers between devices: 1.15 us -> 0.01 us  [body(): two_up = move(two[:half] + got_two[:half], 'x', UP)]
    ppermute x1, waiting for transfers between devices: 1.15 us -> 0.01 us  [body(): move(jnp.concatenate([down[:half], down[half:] + two_down]), 'x', DOWN)]
    ppermute x1, starting transfers between devices: 1.08 us -> 0.01 us  [body(): end_z = move(after(z_mine + got_up + got_down, two_up), 'z_lo', SWAP)]
  transfers between devices with their start and end apart: 21 -> 21, of which waited for: 12 -> 9; matrix products, arithmetic and copies ran while one was open for 1% -> 1% of each run, Pallas kernels for 27% -> 25%
where the time goes in v12:
time: 96 us; the launch traced here: 96.2 us
  waiting for transfers between devices  34.2 us (36%)
  Pallas kernels  29.9 us (31%)
  starting transfers between devices  29 us (30%)
  other arithmetic  2.4 us (2%)
    pallas_call x4, Pallas kernels, tile_products(): pl.pallas_call(functools.partial(tile_kernel, len(pieces), first, split_r...  26 us
    ppermute x1, waiting for transfers between devices, body(): end_z = move(after(z_mine + got_up + got_down, two_up), 'z_lo', SWAP)  9.17 us
    ppermute x1, waiting for transfers between devices, body(): two_up = move(two[:half] + got_two[:half], 'x', UP)  9.11 us
    ppermute x1, waiting for transfers between devices, body(): below = move(own, 'y', UP)  5.03 us
    ppermute x1, starting transfers between devices, body(): far = move(own, 'z_hi', SWAP)  3.88 us
    ppermute x1, starting transfers between devices, body(): far_below = move(below, 'z_hi', SWAP)  3.88 us
    ppermute x1, waiting for transfers between devices, body(): got_two = move(z_two, 'z_lo', SWAP)  3.71 us
    ppermute x1, starting transfers between devices, body(): move(jnp.concatenate([down[:half], down[half:] + two_down]), 'x', DOWN)  3.28 us
  transfers between devices with their start and end apart: 21, of which 9 were waited for; matrix products, arithmetic and copies ran while one was open for 1% of the time, Pallas kernels for 25%

profile of v12, /device:TPU:0, one launch (start us, length us, event | category | flops | bytes accessed | tf_op | source)
XLA Modules:
  0.0 96.2 jit_solution(16176893054569521907)
XLA Ops:
  0.0 0.7 convert_bitcast_fusion
  0.7 1.1 %select_maximum_fusion.refs_4_ = f32[1032,128]{1,0:T(8,128)S(1)} fusion(f32[1,8]{1,0:T(1,128)S(1)} %convert_bitcast_fusion, f32[1024,128]{1,0:T(8,128)} %param.7), kind=kLoop, calls=%fused_computation.2 | loop fusion | flops 396288 | bytes 1052704 | tf_op jit(solution)/shard_map/concatenate | solution.py:253
  1.7 1.7 %collective-permute-start.1 = (f32[1032,128]{1,0:T(8,128)S(1)}, f32[1032,128]{1,0:T(8,128)S(1)}, u32[]{:S(2)}, u32[]{:S(2)}) collective-permute-start(f32[1032,128]{1,0:T(8,128)S(1)} %select_maximum_fusion.refs_4_), channel_id=1, source_target_pairs={{0,2},{2,4},{4,6},{6,0},{1,3},{3,5},{5,7},{7,1},{8,10},{10,12},{12... | collective-permute-start | bytes 1585160 | tf_op jit(solution)/shard_map/ppermute | solution.py:254
  3.5 3.9 %collective-permute-start.3 = (f32[1032,128]{1,0:T(8,128)S(1)}, f32[1032,128]{1,0:T(8,128)S(1)}, u32[]{:S(2)}, u32[]{:S(2)}) collective-permute-start(f32[1032,128]{1,0:T(8,128)S(1)} %select_maximum_fusion.refs_4_), channel_id=1, source_target_pairs={{0,8},{8,0},{1,9},{9,1},{2,10},{10,2},{3,11},{11,3},{4,12},{12,4},... | collective-permute-start | bytes 1585160 | tf_op jit(solution)/shard_map/ppermute | solution.py:256
  7.3 1.7 %collective-permute-start.2 = (f32[1032,128]{1,0:T(8,128)S(1)}, f32[1032,128]{1,0:T(8,128)S(1)}, u32[]{:S(2)}, u32[]{:S(2)}) collective-permute-start(f32[1032,128]{1,0:T(8,128)S(1)} %select_maximum_fusion.refs_4_), channel_id=1, source_target_pairs={{0,6},{2,0},{4,2},{6,4},{1,7},{3,1},{5,3},{7,5},{8,14},{10,8},{12,... | collective-permute-start | bytes 1585160 | tf_op jit(solution)/shard_map/ppermute | solution.py:255
  9.0 0.0 collective-permute-start
  9.0 2.9 %shard_map.73 = (s32[288]{0:T(512)}, s32[1]{0:T(128)}) custom-call(s32[16,16]{1,0:T(8,128)} %bitcast.13, s32[16,16]{1,0:T(8,128)} %bitcast.14), custom_call_target="tpu_custom_call" | custom-call | flops 100000 | bytes 10000 | tf_op jit(solution)/shard_map/pallas_call | solution.py:262
  11.9 5.0 %collective-permute-done.1.refs_6_ = f32[1032,128]{1,0:T(8,128)S(1)} collective-permute-done((f32[1032,128]{1,0:T(8,128)S(1)}, f32[1032,128]{1,0:T(8,128)S(1)}, u32[]{:S(2)}, u32[]{:S(2)}) %collective-permute-start.1) | collective-permute-done | bytes 528416 | tf_op jit(solution)/shard_map/ppermute | solution.py:254
  16.9 3.9 %collective-permute-start.7 = (f32[1032,128]{1,0:T(8,128)S(1)}, f32[1032,128]{1,0:T(8,128)S(1)}, u32[]{:S(2)}, u32[]{:S(2)}) collective-permute-start(f32[1032,128]{1,0:T(8,128)S(1)} %collective-permute-done.1.refs_6_), channel_id=1, source_target_pairs={{0,8},{8,0},{1,9},{9,1},{2,10},{10,2},{3,11},{11,3},{4,12},{12,4},... | collective-permute-start | bytes 1585160 | tf_op jit(solution)/shard_map/ppermute | solution.py:276
  20.8 0.3 collective-permute-start.5
  21.1 2.9 %collective-permute-start.6 = (f32[1032,128]{1,0:T(8,128)S(1)}, f32[1032,128]{1,0:T(8,128)S(1)}, u32[]{:S(2)}, u32[]{:S(2)}) collective-permute-start(f32[1032,128]{1,0:T(8,128)S(1)} %collective-permute-done.3.refs_8_), channel_id=1, source_target_pairs={{0,6},{2,0},{4,2},{6,4},{1,7},{3,1},{5,3},{7,5},{8,14},{10,8},{12,... | collective-permute-start | bytes 1585160 | tf_op jit(solution)/shard_map/ppermute | solution.py:275
  24.0 0.1 pad_add_fusion.refs_0_
  24.1 0.0 collective-permute-done.2.refs_7_
  24.1 0.1 pad_maximum_fusion
  24.2 0.1 collective-permute-start.4
  24.3 0.5 copy-done.1
  24.8 6.9 %shard_map.74 = (f32[65,128,128]{2,1,0:T(8,128)S(1)}, s32[288]{0:T(512)S(1)}, s32[1]{0:T(128)}) custom-call(s32[2]{0:T(128)S(1)} %pad_add_fusion.refs_0_, s32[288]{0:T(512)S(1)} %copy-done.1, s32[1]{0:T(128)} %get-tuple-element.33.refs_2_, f32[256,128,128]{2,1,0:T(8,128)} %bitcast.9, f32[1032,128]{1,0:T(8,128)S(1)} %select_maximum_fusion.refs_4_, ...), custom_call_target="tpu_custom_call" | custom-call | flops 100000 | bytes 10000 | tf_op jit(solution)/shard_map/pallas_call | solution.py:220
  31.7 2.2 %collective-permute-done.6.refs_4_ = f32[1032,128]{1,0:T(8,128)S(1)} collective-permute-done((f32[1032,128]{1,0:T(8,128)S(1)}, f32[1032,128]{1,0:T(8,128)S(1)}, u32[]{:S(2)}, u32[]{:S(2)}) %collective-permute-start.6) | collective-permute-done | bytes 528416 | tf_op jit(solution)/shard_map/ppermute | solution.py:275
  33.9 0.7 collective-permute-done.5.refs_5_
  34.7 0.1 pad_maximum_fusion.1
  34.8 0.1 collective-permute-start.10
  34.9 3.0 %collective-permute-start.9 = (f32[520,128]{1,0:T(8,128)S(1)}, f32[520,128]{1,0:T(8,128)S(1)}, u32[]{:S(2)}, u32[]{:S(2)}) collective-permute-start(f32[520,128]{1,0:T(8,128)S(1)} %slice.31), channel_id=1, source_target_pairs={{0,6},{2,0},{4,2},{6,4},{1,7},{3,1},{5,3},{7,5},{8,14},{10,8},{12,... | collective-permute-start | bytes 798728 | tf_op jit(solution)/shard_map/ppermute | solution.py:283
  38.0 0.0 collective-permute-start.8
  38.0 0.0 collective-permute-done.4.refs_4_
  38.0 8.2 %shard_map.75 = (f32[65,128,128]{2,1,0:T(8,128)S(1)}, s32[288]{0:T(512)S(1)}, s32[1]{0:T(128)}, s32[288]{0:T(512)S(1)}, s32[1]{0:T(128)}) custom-call(s32[2]{0:T(128)S(1)} %pad_add_fusion.refs_0_, s32[288]{0:T(512)S(1)} %get-tuple-element.35.refs_1_, s32[1]{0:T(128)} %get-tuple-element.36.refs_2_, f32[256,128,128]{2,1,0:T(8,128)} %bitcast.10, ...), custom_call_target="tpu_custom_call" | custom-call | flops 100000 | bytes 10000 | tf_op jit(solution)/shard_map/pallas_call | solution.py:220
  46.2 1.4 %collective-permute-done.8.refs_6_ = f32[512,128]{1,0:T(8,128)S(1)} collective-permute-done((f32[512,128]{1,0:T(8,128)S(1)}, f32[512,128]{1,0:T(8,128)S(1)}, u32[]{:S(2)}, u32[]{:S(2)}) %collective-permute-start.8) | collective-permute-done | bytes 262176 | tf_op jit(solution)/shard_map/ppermute | solution.py:283
  47.6 0.5 collective-permute-start.11
  48.1 1.4 %collective-permute-done.11.refs_9_ = f32[512,128]{1,0:T(8,128)S(1)} collective-permute-done((f32[512,128]{1,0:T(8,128)S(1)}, f32[512,128]{1,0:T(8,128)S(1)}, u32[]{:S(2)}, u32[]{:S(2)}) %collective-permute-start.11) | collective-permute-done | bytes 262176 | tf_op jit(solution)/shard_map/ppermute | solution.py:294
  49.5 0.0 collective-permute-done.12.refs_10_
  49.5 4.8 %shard_map.76 = (f32[8,128,128]{2,1,0:T(8,128)S(1)}, f32[8,128,128]{2,1,0:T(8,128)S(1)}, f32[8,128,128]{2,1,0:T(8,128)S(1)}) custom-call(s32[2]{0:T(128)S(1)} %pad_add_fusion.refs_0_, s32[288]{0:T(512)S(1)} %get-tuple-element.47.refs_1_, s32[1]{0:T(128)} %get-tuple-element.48.refs_2_, f32[256,128,128]{2,1,0:T(8,128)} %bitcast.11, ...), custom_call_target="tpu_custom_call" | custom-call | flops 100000 | bytes 10000 | tf_op jit(solution)/shard_map/pallas_call | solution.py:220
  54.3 1.1 %collective-permute-start.13 = (f32[8,128,128]{2,1,0:T(8,128)S(1)}, f32[8,128,128]{2,1,0:T(8,128)S(1)}, u32[]{:S(2)}, u32[]{:S(2)}) collective-permute-start(f32[8,128,128]{2,1,0:T(8,128)S(1)} %get-tuple-element.49), channel_id=1, source_target_pairs={{0,64},{64,0},{1,65},{65,1},{2,66},{66,2},{3,67},{67,3},{4,68},{68... | collective-permute-start | bytes 1572872 | tf_op jit(solution)/shard_map/ppermute | solution.py:302
  55.4 1.1 %collective-permute-start.18 = (f32[8,128,128]{2,1,0:T(8,128)S(1)}, f32[8,128,128]{2,1,0:T(8,128)S(1)}, u32[]{:S(2)}, u32[]{:S(2)}) collective-permute-start(f32[8,128,128]{2,1,0:T(8,128)S(1)} %get-tuple-element.56), channel_id=1, source_target_pairs={{0,16},{16,32},{32,48},{48,0},{1,17},{17,33},{33,49},{49,1},{2,18}... | collective-permute-start | bytes 1572872 | tf_op jit(solution)/shard_map/ppermute | solution.py:303
  56.5 2.2 %collective-permute-start.19 = (f32[8,128,128]{2,1,0:T(8,128)S(1)}, f32[8,128,128]{2,1,0:T(8,128)S(1)}, u32[]{:S(2)}, u32[]{:S(2)}) collective-permute-start(f32[8,128,128]{2,1,0:T(8,128)S(1)} %get-tuple-element.57), channel_id=1, source_target_pairs={{0,48},{16,0},{32,16},{48,32},{1,49},{17,1},{33,17},{49,33},{2,50}... | collective-permute-start | bytes 1572872 | tf_op jit(solution)/shard_map/ppermute | solution.py:304
  58.6 6.0 %shard_map.77 = (f32[8,128,128]{2,1,0:T(8,128)S(1)}, f32[8,128,128]{2,1,0:T(8,128)S(1)}, f32[8,128,128]{2,1,0:T(8,128)S(1)}, f32[8,128,128]{2,1,0:T(8,128)S(1)}, f32[8,128,128]{2,1,0:T(8,128)S(1)}) custom-call(s32[2]{0:T(128)S(1)} %pad_add_fusion.refs_0_, s32[288]{0:T(512)S(1)} %get-tuple-element.39.refs_1_, s32[1]{0:T(128)} %get-tuple-element.40.refs_2_, ...), custom_call_target="tpu_custom_call" | custom-call | flops 100000 | bytes 10000 | tf_op jit(solution)/shard_map/pallas_call | solution.py:220
  64.6 3.7 %collective-permute-done.13 = f32[8,128,128]{2,1,0:T(8,128)S(1)} collective-permute-done((f32[8,128,128]{2,1,0:T(8,128)S(1)}, f32[8,128,128]{2,1,0:T(8,128)S(1)}, u32[]{:S(2)}, u32[]{:S(2)}) %collective-permute-start.13) | collective-permute-done | bytes 524320 | tf_op jit(solution)/shard_map/ppermute | solution.py:302
  68.3 0.1 slice_add_fusion
  68.4 3.2 %collective-permute-start.16 = (f32[4,128,128]{2,1,0:T(8,128)S(1)}, f32[4,128,128]{2,1,0:T(8,128)S(1)}, u32[]{:S(2)}, u32[]{:S(2)}) collective-permute-start(f32[4,128,128]{2,1,0:T(8,128)S(1)} %get-tuple-element.59), channel_id=1, source_target_pairs={{0,48},{16,0},{32,16},{48,32},{1,49},{17,1},{33,17},{49,33},{2,50}... | collective-permute-start | bytes 786440 | tf_op jit(solution)/shard_map/ppermute | solution.py:306
  71.7 0.1 add_add_fusion
  71.8 9.1 %collective-permute-done.14 = f32[4,128,128]{2,1,0:T(8,128)S(1)} collective-permute-done((f32[4,128,128]{2,1,0:T(8,128)S(1)}, f32[4,128,128]{2,1,0:T(8,128)S(1)}, u32[]{:S(2)}, u32[]{:S(2)}) %collective-permute-start.14) | collective-permute-done | bytes 262176 | tf_op jit(solution)/shard_map/ppermute | solution.py:305
  80.9 0.1 slice_add_fusion.3
  81.0 0.0 copy-start
  81.0 0.0 copy-start.2
  81.0 0.1 collective-permute-start.15
  81.1 0.1 fusion
  81.2 3.3 %collective-permute-start.17 = (f32[8,128,128]{2,1,0:T(8,128)S(1)}, f32[8,128,128]{2,1,0:T(8,128)S(1)}, u32[]{:S(2)}, u32[]{:S(2)}) collective-permute-start(f32[8,128,128]{2,1,0:T(8,128)S(1)} %pad_maximum_fusion.3), channel_id=1, source_target_pairs={{0,48},{16,0},{32,16},{48,32},{1,49},{17,1},{33,17},{49,33},{2,50}... | collective-permute-start | bytes 1572872 | tf_op jit(solution)/shard_map/ppermute | solution.py:309
  84.5 9.2 %collective-permute-done.20.d = f32[8,128,128]{2,1,0:T(8,128)S(1)} collective-permute-done((f32[8,128,128]{2,1,0:T(8,128)S(1)}, f32[8,128,128]{2,1,0:T(8,128)S(1)}, u32[]{:S(2)}, u32[]{:S(2)}) %collective-permute-start.20) | collective-permute-done | bytes 524320 | tf_op jit(solution)/shard_map/ppermute | solution.py:307
  93.7 1.4 %collective-permute-done.15.b = f32[8,128,128]{2,1,0:T(8,128)S(1)} collective-permute-done((f32[8,128,128]{2,1,0:T(8,128)S(1)}, f32[8,128,128]{2,1,0:T(8,128)S(1)}, u32[]{:S(2)}, u32[]{:S(2)}) %collective-permute-start.15) | collective-permute-done | bytes 524320 | tf_op jit(solution)/shard_map/ppermute | solution.py:308
  95.1 1.1 %shard_map.78 = f32[1024,128]{1,0:T(8,128)} custom-call(f32[8,128,128]{2,1,0:T(8,128)S(1)} %get-tuple-element.51.a, f32[8,128,128]{2,1,0:T(8,128)S(1)} %collective-permute-done.15.b, f32[8,128,128]{2,1,0:T(8,128)S(1)} %collective-permute-done.17.c, f32[8,128,128]{2,1,0:T(8,128)S(1)} %collective-permute-done.20.d, f32[128,128]{1,0:T(8,128)S(1)} %copy-done, ...), custom_call_target="tpu_custom_call" | custom-call | tf_op jit(solution)/shard_map/pallas_call | solution.py:311
  (19 shorter events, 0.1 us)
Async XLA Ops:
  1.7 15.2 %collective-permute-start.1 = (f32[1032,128]{1,0:T(8,128)S(1)}, f32[1032,128]{1,0:T(8,128)S(1)}, u32[]{:S(2)}, u32[]{:S(2)}) collective-permute-start(f32[1032,128]{1,0:T(8,128)S(1)} %select_maximum_fusion.refs_4_), channel_id=1, source_target_pairs={{0,2},{2,4},{4,6},{6,0},{1,3},{3,5},{5,7},{7,1},{8,10},{10,12},{12... | collective-permute-start | bytes 1585160 | tf_op jit(solution)/shard_map/ppermute | solution.py:254
  3.5 17.6 %collective-permute-start.3 = (f32[1032,128]{1,0:T(8,128)S(1)}, f32[1032,128]{1,0:T(8,128)S(1)}, u32[]{:S(2)}, u32[]{:S(2)}) collective-permute-start(f32[1032,128]{1,0:T(8,128)S(1)} %select_maximum_fusion.refs_4_), channel_id=1, source_target_pairs={{0,8},{8,0},{1,9},{9,1},{2,10},{10,2},{3,11},{11,3},{4,12},{12,4},... | collective-permute-start | bytes 1585160 | tf_op jit(solution)/shard_map/ppermute | solution.py:256
  7.3 16.8 %collective-permute-start.2 = (f32[1032,128]{1,0:T(8,128)S(1)}, f32[1032,128]{1,0:T(8,128)S(1)}, u32[]{:S(2)}, u32[]{:S(2)}) collective-permute-start(f32[1032,128]{1,0:T(8,128)S(1)} %select_maximum_fusion.refs_4_), channel_id=1, source_target_pairs={{0,6},{2,0},{4,2},{6,4},{1,7},{3,1},{5,3},{7,5},{8,14},{10,8},{12,... | collective-permute-start | bytes 1585160 | tf_op jit(solution)/shard_map/ppermute | solution.py:255
  9.0 15.3 %collective-permute-start = (f32[1032,128]{1,0:T(8,128)S(1)}, f32[1032,128]{1,0:T(8,128)S(1)}, u32[]{:S(2)}, u32[]{:S(2)}) collective-permute-start(f32[1032,128]{1,0:T(8,128)S(1)} %select_maximum_fusion.refs_4_), channel_id=1, source_target_pairs={{0,1},{1,0},{2,3},{3,2},{4,5},{5,4},{6,7},{7,6},{8,9},{9,8},{10,11... | collective-permute-start | bytes 1585160 | tf_op jit(solution)/shard_map/ppermute | solution.py:257
  16.9 17.0 %collective-permute-start.7 = (f32[1032,128]{1,0:T(8,128)S(1)}, f32[1032,128]{1,0:T(8,128)S(1)}, u32[]{:S(2)}, u32[]{:S(2)}) collective-permute-start(f32[1032,128]{1,0:T(8,128)S(1)} %collective-permute-done.1.refs_6_), channel_id=1, source_target_pairs={{0,8},{8,0},{1,9},{9,1},{2,10},{10,2},{3,11},{11,3},{4,12},{12,4},... | collective-permute-start | bytes 1585160 | tf_op jit(solution)/shard_map/ppermute | solution.py:276
  20.8 13.9 %collective-permute-start.5 = (f32[1032,128]{1,0:T(8,128)S(1)}, f32[1032,128]{1,0:T(8,128)S(1)}, u32[]{:S(2)}, u32[]{:S(2)}) collective-permute-start(f32[1032,128]{1,0:T(8,128)S(1)} %collective-permute-done.1.refs_6_), channel_id=1, source_target_pairs={{0,2},{2,4},{4,6},{6,0},{1,3},{3,5},{5,7},{7,1},{8,10},{10,12},{12... | collective-permute-start | bytes 1585160 | tf_op jit(solution)/shard_map/ppermute | solution.py:274
  21.1 12.8 %collective-permute-start.6 = (f32[1032,128]{1,0:T(8,128)S(1)}, f32[1032,128]{1,0:T(8,128)S(1)}, u32[]{:S(2)}, u32[]{:S(2)}) collective-permute-start(f32[1032,128]{1,0:T(8,128)S(1)} %collective-permute-done.3.refs_8_), channel_id=1, source_target_pairs={{0,6},{2,0},{4,2},{6,4},{1,7},{3,1},{5,3},{7,5},{8,14},{10,8},{12,... | collective-permute-start | bytes 1585160 | tf_op jit(solution)/shard_map/ppermute | solution.py:275
  24.1 0.7 copy-start.1
  24.2 13.8 %collective-permute-start.4 = (f32[3096,128]{1,0:T(8,128)S(1)}, f32[3096,128]{1,0:T(8,128)S(1)}, u32[]{:S(2)}, u32[]{:S(2)}) collective-permute-start(f32[3096,128]{1,0:T(8,128)S(1)} %pad_maximum_fusion), channel_id=1, source_target_pairs={{0,1},{1,0},{2,3},{3,2},{4,5},{5,4},{6,7},{7,6},{8,9},{9,8},{10,11... | collective-permute-start | bytes 4755464 | tf_op jit(solution)/shard_map/ppermute | solution.py:277
  34.8 14.6 %collective-permute-start.10 = (f32[3096,128]{1,0:T(8,128)S(1)}, f32[3096,128]{1,0:T(8,128)S(1)}, u32[]{:S(2)}, u32[]{:S(2)}) collective-permute-start(f32[3096,128]{1,0:T(8,128)S(1)} %pad_maximum_fusion.1), channel_id=1, source_target_pairs={{0,1},{1,0},{2,3},{3,2},{4,5},{5,4},{6,7},{7,6},{8,9},{9,8},{10,11... | collective-permute-start | bytes 4755464 | tf_op jit(solution)/shard_map/ppermute | solution.py:293
  34.9 12.6 %collective-permute-start.9 = (f32[520,128]{1,0:T(8,128)S(1)}, f32[520,128]{1,0:T(8,128)S(1)}, u32[]{:S(2)}, u32[]{:S(2)}) collective-permute-start(f32[520,128]{1,0:T(8,128)S(1)} %slice.31), channel_id=1, source_target_pairs={{0,6},{2,0},{4,2},{6,4},{1,7},{3,1},{5,3},{7,5},{8,14},{10,8},{12,... | collective-permute-start | bytes 798728 | tf_op jit(solution)/shard_map/ppermute | solution.py:283
  38.0 9.6 %collective-permute-start.8 = (f32[512,128]{1,0:T(8,128)S(1)}, f32[512,128]{1,0:T(8,128)S(1)}, u32[]{:S(2)}, u32[]{:S(2)}) collective-permute-start(f32[512,128]{1,0:T(8,128)S(1)} %slice.30), channel_id=1, source_target_pairs={{0,2},{2,4},{4,6},{6,0},{1,3},{3,5},{5,7},{7,1},{8,10},{10,12},{12... | collective-permute-start | bytes 786440 | tf_op jit(solution)/shard_map/ppermute | solution.py:283
  47.6 1.9 %collective-permute-start.12 = (f32[520,128]{1,0:T(8,128)S(1)}, f32[520,128]{1,0:T(8,128)S(1)}, u32[]{:S(2)}, u32[]{:S(2)}) collective-permute-start(f32[520,128]{1,0:T(8,128)S(1)} %collective-permute-done.9.refs_7_), channel_id=1, source_target_pairs={{0,1},{1,0},{2,3},{3,2},{4,5},{5,4},{6,7},{7,6},{8,9},{9,8},{10,11... | collective-permute-start | bytes 798728 | tf_op jit(solution)/shard_map/ppermute | solution.py:294
  47.6 1.9 %collective-permute-start.11 = (f32[512,128]{1,0:T(8,128)S(1)}, f32[512,128]{1,0:T(8,128)S(1)}, u32[]{:S(2)}, u32[]{:S(2)}) collective-permute-start(f32[512,128]{1,0:T(8,128)S(1)} %collective-permute-done.8.refs_6_), channel_id=1, source_target_pairs={{0,1},{1,0},{2,3},{3,2},{4,5},{5,4},{6,7},{7,6},{8,9},{9,8},{10,11... | collective-permute-start | bytes 786440 | tf_op jit(solution)/shard_map/ppermute | solution.py:294
  54.3 14.0 %collective-permute-start.13 = (f32[8,128,128]{2,1,0:T(8,128)S(1)}, f32[8,128,128]{2,1,0:T(8,128)S(1)}, u32[]{:S(2)}, u32[]{:S(2)}) collective-permute-start(f32[8,128,128]{2,1,0:T(8,128)S(1)} %get-tuple-element.49), channel_id=1, source_target_pairs={{0,64},{64,0},{1,65},{65,1},{2,66},{66,2},{3,67},{67,3},{4,68},{68... | collective-permute-start | bytes 1572872 | tf_op jit(solution)/shard_map/ppermute | solution.py:302
  55.4 16.3 %collective-permute-start.18 = (f32[8,128,128]{2,1,0:T(8,128)S(1)}, f32[8,128,128]{2,1,0:T(8,128)S(1)}, u32[]{:S(2)}, u32[]{:S(2)}) collective-permute-start(f32[8,128,128]{2,1,0:T(8,128)S(1)} %get-tuple-element.56), channel_id=1, source_target_pairs={{0,16},{16,32},{32,48},{48,0},{1,17},{17,33},{33,49},{49,1},{2,18}... | collective-permute-start | bytes 1572872 | tf_op jit(solution)/shard_map/ppermute | solution.py:303
  56.5 15.2 %collective-permute-start.19 = (f32[8,128,128]{2,1,0:T(8,128)S(1)}, f32[8,128,128]{2,1,0:T(8,128)S(1)}, u32[]{:S(2)}, u32[]{:S(2)}) collective-permute-start(f32[8,128,128]{2,1,0:T(8,128)S(1)} %get-tuple-element.57), channel_id=1, source_target_pairs={{0,48},{16,0},{32,16},{48,32},{1,49},{17,1},{33,17},{49,33},{2,50}... | collective-permute-start | bytes 1572872 | tf_op jit(solution)/shard_map/ppermute | solution.py:304
  68.4 12.7 %collective-permute-start.16 = (f32[4,128,128]{2,1,0:T(8,128)S(1)}, f32[4,128,128]{2,1,0:T(8,128)S(1)}, u32[]{:S(2)}, u32[]{:S(2)}) collective-permute-start(f32[4,128,128]{2,1,0:T(8,128)S(1)} %get-tuple-element.59), channel_id=1, source_target_pairs={{0,48},{16,0},{32,16},{48,32},{1,49},{17,1},{33,17},{49,33},{2,50}... | collective-permute-start | bytes 786440 | tf_op jit(solution)/shard_map/ppermute | solution.py:306
  71.7 9.2 %collective-permute-start.14 = (f32[4,128,128]{2,1,0:T(8,128)S(1)}, f32[4,128,128]{2,1,0:T(8,128)S(1)}, u32[]{:S(2)}, u32[]{:S(2)}) collective-permute-start(f32[4,128,128]{2,1,0:T(8,128)S(1)} %get-tuple-element.60), channel_id=1, source_target_pairs={{0,16},{16,32},{32,48},{48,0},{1,17},{17,33},{33,49},{49,1},{2,18}... | collective-permute-start | bytes 786440 | tf_op jit(solution)/shard_map/ppermute | solution.py:305
  80.9 12.8 %collective-permute-start.20 = (f32[8,128,128]{2,1,0:T(8,128)S(1)}, f32[8,128,128]{2,1,0:T(8,128)S(1)}, u32[]{:S(2)}, u32[]{:S(2)}) collective-permute-start(f32[8,128,128]{2,1,0:T(8,128)S(1)} %add_add_fusion), channel_id=1, source_target_pairs={{0,64},{64,0},{1,65},{65,1},{2,66},{66,2},{3,67},{67,3},{4,68},{68... | collective-permute-start | bytes 1572872 | tf_op jit(solution)/shard_map/ppermute | solution.py:307
  81.0 14.1 %copy-start = (f32[128,128]{1,0:T(8,128)S(1)}, f32[128,128]{1,0:T(8,128)}, u32[]{:S(2)}) copy-start(f32[128,128]{1,0:T(8,128)} %weight.1) | copy-start | bytes 196612
  81.0 14.1 %copy-start.2 = (f32[128]{0:T(128)S(1)}, f32[128]{0:T(128)}, u32[]{:S(2)}) copy-start(f32[128]{0:T(128)} %param.13) | copy-start | bytes 1540
  81.0 14.1 %collective-permute-start.15 = (f32[8,128,128]{2,1,0:T(8,128)S(1)}, f32[8,128,128]{2,1,0:T(8,128)S(1)}, u32[]{:S(2)}, u32[]{:S(2)}) collective-permute-start(f32[8,128,128]{2,1,0:T(8,128)S(1)} %pad_maximum_fusion.2), channel_id=1, source_target_pairs={{0,16},{16,32},{32,48},{48,0},{1,17},{17,33},{33,49},{49,1},{2,18}... | collective-permute-start | bytes 1572872 | tf_op jit(solution)/shard_map/ppermute | solution.py:308
  81.2 13.9 %collective-permute-start.17 = (f32[8,128,128]{2,1,0:T(8,128)S(1)}, f32[8,128,128]{2,1,0:T(8,128)S(1)}, u32[]{:S(2)}, u32[]{:S(2)}) collective-permute-start(f32[8,128,128]{2,1,0:T(8,128)S(1)} %pad_maximum_fusion.3), channel_id=1, source_target_pairs={{0,48},{16,0},{32,16},{48,32},{1,49},{17,1},{33,17},{49,33},{2,50}... | collective-permute-start | bytes 1572872 | tf_op jit(solution)/shard_map/ppermute | solution.py:309
